TPU v7x, 32 devices: a whole 2x2x4 slice. The times are simulated.
32 devices in a mesh: wide: 8 (over z, y), narrow: 4 (over x, core).
Axes of the slice: x: 2, y: 2, z: 4, core: 2. Of those that a mesh axis runs over, the one named last changes fastest.
Arguments:
- observed: bfloat16 [96, 121, 256], P(('wide', 'narrow')), may hold values from -4 to 4
- following: bfloat16 [96, 121, 256], P(('wide', 'narrow')), may hold values from -4 to 4
- game_ids: int32 [96], P(('wide', 'narrow')), may hold values from 0 to 3
- actions: int32 [96, 2], P(('wide', 'narrow')), may hold values from 0 to 17, as said below
- legal_mask: int32 [96, 18], P(('wide', 'narrow')), may hold values from 0 to 1
- rewards: float32 [96], P(('wide', 'narrow')), may hold values from -1 to 1
- discounts: float32 [96], P(('wide', 'narrow')), may hold values from 0.5 to 0.99
- done_flags: int32 [96], P(('wide', 'narrow')), may hold values 0 or 1
- params_top: float32 [3700736], P(('wide', 'narrow')), may hold values from -8 to 8
- params_blocks: float32 [2, 4462592], P(None, ('wide', 'narrow')), may hold values from -8 to 8
- first_top: float32 [3700736], P(('wide', 'narrow')), may hold values from -1 to 1
- first_blocks: float32 [2, 4462592], P(None, ('wide', 'narrow')), may hold values from -1 to 1
- second_top: float32 [3700736], P(('wide', 'narrow')), may hold values from 0 to 1, as said below
- second_blocks: float32 [2, 4462592], P(None, ('wide', 'narrow')), may hold values from 0 to 1, as said below
- average_top: float32 [3700736], P(('wide', 'narrow')), may hold values from -8 to 8
- average_blocks: float32 [2, 4462592], P(None, ('wide', 'narrow')), may hold values from -8 to 8
- target_top: bfloat16 [3700736], P(('wide', 'narrow')), may hold values from -8 to 8
- target_blocks: bfloat16 [2, 4462592], P(None, ('wide', 'narrow')), may hold values from -8 to 8
Outputs:
- loss_total: float32 [], replicated
- matrix_norms: float32 [2, 12], replicated
- updated_top: float32 [3700736], P(('wide', 'narrow'))
- half_top: bfloat16 [3700736], P(('wide', 'narrow'))
- momentum_top: float32 [3700736], P(('wide', 'narrow'))
- variance_top: float32 [3700736], P(('wide', 'narrow'))
- averaged_top: float32 [3700736], P(('wide', 'narrow'))
- updated_blocks: float32 [2, 4462592], P(None, ('wide', 'narrow'))
- half_blocks: bfloat16 [2, 4462592], P(None, ('wide', 'narrow'))
- momentum_blocks: float32 [2, 4462592], P(None, ('wide', 'narrow'))
- variance_blocks: float32 [2, 4462592], P(None, ('wide', 'narrow'))
- averaged_blocks: float32 [2, 4462592], P(None, ('wide', 'narrow'))
- gain_grads: float32 [2, 6144], P(None, ('wide', 'narrow'))
Inputs may be any that keep to these rules, and one draw needn't show every extreme that they name: `actions`: column 0 is legal in legal_mask; column 1 is any action. `second_top`: positive. `second_blocks`: positive.
All inputs are finite; a program needn't handle non-finite values. No bound on the sum of `done_flags` on one device may be relied on, other than what follows from the above.
Results may differ from a plain program's by a relative error of at most 0.025.
Values may be sent and summed in bfloat16 or wider, within the bound.
No kernel may reach another device: no remote copies, remote signals or barrier semaphores. Data moves between devices by JAX's collectives and lax.ppermute only.
A program may use at most 320 MiB of HBM per device.

v0:
```python
import jax
import jax.numpy as jnp
from jax import lax
from jax.sharding import PartitionSpec as P

D = 2048
BOT = 512
GROUPS = 32
PATCH_IN = 256
DPROJ = 512
ACTIONS = 18
ATOMS = 51
GAMES = 4
BLOCKS = 2
SIDE = 11
STEP = 5
PIX = 121


FULL_PRECISION = lax.Precision.HIGHEST
CQL_WEIGHT = 0.05
BETA_ONE = 0.5
BETA_TWO = 0.5
LEARNING_RATE = 0.25
WEIGHT_DECAY = 0.01


def average_decay():
    return min(0.99, (1.0 + STEP) / (10.0 + STEP))


def segment_lengths():
    top = [PATCH_IN * D, D * PIX, D * DPROJ, DPROJ * GAMES * ACTIONS * ATOMS]
    block = [D * BOT, 9 * BOT * BOT, BOT * D, 2 * (2 * BOT + D)]
    return (top, block)


def cut_points(lengths, devices):
    cuts = []
    offset = 0
    for length in lengths:
        width = length // devices
        cuts.append((offset, width))
        offset += width
    return cuts


def unpack(flat, lengths, devices):
    grid = flat.reshape(devices, -1)
    return [
        grid[:, start : start + width].reshape(-1) for start, width in cut_points(lengths, devices)
    ]


def to_grid(pieces, devices):
    return jnp.concatenate([piece.reshape(devices, -1) for piece in pieces], axis=1)


def product(left, right):
    return jnp.dot(left, right, preferred_element_type=jnp.float32)


def product_left(left, right):
    return lax.dot_general(
        left, right, (((0,), (0,)), ((), ())), preferred_element_type=jnp.float32
    )


def product_right(left, right):
    return lax.dot_general(
        left, right, (((1,), (1,)), ((), ())), preferred_element_type=jnp.float32
    )


def shape_top(flats):
    return (
        flats[0].reshape(PATCH_IN, D),
        flats[1].reshape(D, PIX),
        flats[2].reshape(D, DPROJ),
        flats[3].reshape(DPROJ, GAMES * ACTIONS * ATOMS),
    )


def shape_block(flats):
    return (
        flats[0].reshape(D, BOT),
        flats[1].reshape(9 * BOT, BOT),
        flats[2].reshape(BOT, D),
        flats[3].astype(jnp.float32),
    )


def split_gains(gains):
    pieces = []
    offset = 0
    for width in [BOT, BOT, BOT, BOT, D, D]:
        pieces.append(gains[offset : offset + width])
        offset += width
    return pieces


def group_norm(hidden, gain, bias):
    chans = hidden.shape[-1]
    split = hidden.reshape(-1, PIX, GROUPS, chans // GROUPS)
    mean = jnp.mean(split, axis=(1, 3), keepdims=True)
    centered = split - mean
    var = jnp.mean(centered * centered, axis=(1, 3), keepdims=True)
    return (centered * lax.rsqrt(var + 1e-05)).reshape(hidden.shape) * gain + bias


def norm_act(hidden, gain, bias):
    return jax.nn.silu(group_norm(hidden, gain, bias))


def closing(stream, hidden, gain, bias):
    return jax.nn.silu(stream + group_norm(hidden, gain, bias))


def columns(acts):
    chans = acts.shape[-1]
    grid = jnp.pad(acts.reshape(-1, SIDE, SIDE, chans), ((0, 0), (1, 1), (1, 1), (0, 0)))
    taps = [grid[:, row : row + SIDE, col : col + SIDE, :] for row in range(3) for col in range(3)]
    return jnp.concatenate(taps, axis=-1).reshape(-1, 9 * chans)


def uncolumns(grads, chans):
    grid = grads.reshape(-1, SIDE, SIDE, 9, chans)
    total = jnp.zeros((grid.shape[0], SIDE + 2, SIDE + 2, chans), jnp.float32)
    for tap in range(9):
        row, col = (tap // 3, tap % 3)
        total = total + jnp.pad(
            grid[:, :, :, tap, :], ((0, 0), (row, 2 - row), (col, 2 - col), (0, 0))
        )
    return total[:, 1 : SIDE + 1, 1 : SIDE + 1, :].reshape(-1, chans)


def fetch_block(shard, block_lengths, devices, again):
    if again:
        whole = lax.all_gather(shard, ("wide", "narrow"), axis=0, tiled=True)
    else:
        whole = lax.all_gather(shard, ("wide", "narrow"), axis=0, tiled=True)
    return shape_block(unpack(whole, block_lengths, devices))


def block_forward(stream, weights):
    weight_in, weight_mid, weight_out, gains = weights
    gain_one, bias_one, gain_two, bias_two, gain_three, bias_three = split_gains(gains)
    first_act = norm_act(
        product(stream.astype(jnp.bfloat16), weight_in), gain_one, bias_one
    ).astype(jnp.bfloat16)
    second_act = norm_act(product(columns(first_act), weight_mid), gain_two, bias_two).astype(
        jnp.bfloat16
    )
    return closing(stream, product(second_act, weight_out), gain_three, bias_three)


def block_backward(stream, weights, grad_out):
    weight_in, weight_mid, weight_out, gains = weights
    gain_one, bias_one, gain_two, bias_two, gain_three, bias_three = split_gains(gains)
    stream_low = stream.astype(jnp.bfloat16)
    first_act, back_one = jax.vjp(norm_act, product(stream_low, weight_in), gain_one, bias_one)
    windows = columns(first_act.astype(jnp.bfloat16))
    second_act, back_two = jax.vjp(norm_act, product(windows, weight_mid), gain_two, bias_two)
    second_low = second_act.astype(jnp.bfloat16)
    ignored, back_three = jax.vjp(
        closing, stream, product(second_low, weight_out), gain_three, bias_three
    )
    grad_res, grad_third, grad_g3, grad_b3 = back_three(grad_out)
    grad_third = grad_third.astype(jnp.bfloat16)
    grad_wout = product_left(second_low, grad_third)
    grad_second, grad_g2, grad_b2 = back_two(product_right(grad_third, weight_out))
    grad_second = grad_second.astype(jnp.bfloat16)
    grad_wmid = product_left(windows, grad_second)
    grad_first, grad_g1, grad_b1 = back_one(uncolumns(product_right(grad_second, weight_mid), BOT))
    grad_first = grad_first.astype(jnp.bfloat16)
    grad_win = product_left(stream_low, grad_first)
    grad_stream = grad_res + product_right(grad_first, weight_in)
    grad_gains = jnp.concatenate([grad_g1, grad_b1, grad_g2, grad_b2, grad_g3, grad_b3])
    return (
        grad_stream,
        (grad_win.reshape(-1), grad_wmid.reshape(-1), grad_wout.reshape(-1), grad_gains),
    )


def head_logits(stream, pool_w, proj_w, heads_w):
    count = stream.shape[0] // PIX
    stream_low = stream.astype(jnp.bfloat16).reshape(count, PIX, D)
    pooled_low = jnp.einsum(
        "npc,cp->nc", stream_low, pool_w, preferred_element_type=jnp.float32
    ).astype(jnp.bfloat16)
    before = product(pooled_low, proj_w)
    hidden_low = jax.nn.silu(before).astype(jnp.bfloat16)
    return (product(hidden_low, heads_w), (stream_low, pooled_low, before, hidden_low))


def select(scores, game_hot):
    count = scores.shape[0]
    picked = jnp.einsum(
        "ng,ngk->nk",
        game_hot,
        scores.reshape(count, GAMES, ACTIONS * ATOMS),
        precision=FULL_PRECISION,
    )
    return picked.reshape(count, ACTIONS, ATOMS)


def support():
    return -10.0 + 20.0 / (ATOMS - 1) * jnp.arange(ATOMS, dtype=jnp.float32)


def target_dist(logits_next, next_hot, rewards, discounts, done_flags):
    chosen = jnp.einsum("na,naz->nz", next_hot, logits_next, precision=FULL_PRECISION)
    probs = jax.nn.softmax(chosen, axis=-1)
    atoms = support()
    spacing = 20.0 / (ATOMS - 1)
    keep = discounts * (1.0 - done_flags.astype(jnp.float32))
    moved = jnp.clip(rewards[:, None] + keep[:, None] * atoms[None, :], -10.0, 10.0)
    kernel = jnp.clip(1.0 - jnp.abs(moved[:, :, None] - atoms[None, None, :]) / spacing, 0.0, 1.0)
    return jnp.einsum("nj,nji->ni", probs, kernel, precision=FULL_PRECISION)


def frame_losses(logits, target, taken_hot, legal_now):
    logp = jax.nn.log_softmax(logits, axis=-1)
    action_values = jnp.sum(jnp.exp(logp) * support(), axis=-1)
    taken_logp = jnp.sum(taken_hot[:, :, None] * logp, axis=1)
    cross = -jnp.sum(target * taken_logp, axis=-1)
    masked = jnp.where(legal_now > 0, action_values, -1e30)
    largest = jnp.max(masked, axis=-1, keepdims=True)
    spread = jnp.log(jnp.sum(jnp.exp(masked - largest), axis=-1)) + largest[:, 0]
    return cross + CQL_WEIGHT * (spread - jnp.sum(taken_hot * action_values, axis=-1))


def lamb_parts(params, grads, first, second):
    momentum = BETA_ONE * first + (1.0 - BETA_ONE) * grads
    variance = BETA_TWO * second + (1.0 - BETA_TWO) * grads * grads
    direction = (
        momentum / (1.0 - BETA_ONE**STEP) / (jnp.sqrt(variance / (1.0 - BETA_TWO**STEP)) + 1e-06)
        + WEIGHT_DECAY * params
    )
    return (momentum, variance, direction)


def squares(flat, cuts):
    return jnp.stack(
        [jnp.sum(jnp.square(flat[..., start : start + width]), axis=-1) for start, width in cuts],
        axis=-1,
    )


def spread_ratio(ratio, flat, cuts):
    parts = [
        jnp.broadcast_to(ratio[..., index : index + 1], flat.shape[:-1] + (width,))
        for index, (start, width) in enumerate(cuts)
    ]
    return jnp.concatenate(parts, axis=-1)


def on_device(
    observed,
    following,
    game_ids,
    actions,
    legal_mask,
    rewards,
    discounts,
    done_flags,
    params_top,
    params_blocks,
    first_top,
    first_blocks,
    second_top,
    second_blocks,
    average_top,
    average_blocks,
    target_top,
    target_blocks,
):
    devices = lax.axis_size(("wide", "narrow"))
    count = observed.shape[0]
    frames_all = count * devices
    top_lengths, block_lengths = segment_lengths()
    top_cuts = cut_points(top_lengths, devices)
    block_cuts = cut_points(block_lengths, devices)
    weight_parts = jnp.concatenate(
        [squares(params_top, top_cuts), squares(params_blocks, block_cuts).reshape(-1)]
    )
    weight_sq = lax.psum(weight_parts, ("wide", "narrow"))
    online_full, target_full, target_mids = (
        lax.all_gather(params_top.astype(jnp.bfloat16), ("wide", "narrow"), axis=0, tiled=True),
        lax.all_gather(target_top, ("wide", "narrow"), axis=0, tiled=True),
        lax.all_gather(target_blocks, ("wide", "narrow"), axis=1, tiled=True),
    )
    patch_w, pool_w, proj_w, heads_w = shape_top(unpack(online_full, top_lengths, devices))
    game_hot = (game_ids[:, None] == jnp.arange(GAMES)[None, :]).astype(jnp.float32)
    taken_hot = (actions[:, 0:1] == jnp.arange(ACTIONS)[None, :]).astype(jnp.float32)
    next_hot = (actions[:, 1:2] == jnp.arange(ACTIONS)[None, :]).astype(jnp.float32)
    target_patch, target_pool, target_proj, target_heads = shape_top(
        unpack(target_full, top_lengths, devices)
    )
    stream = product(following.reshape(-1, PATCH_IN), target_patch)
    for index in range(BLOCKS):
        stream = block_forward(
            stream, shape_block(unpack(target_mids[index], block_lengths, devices))
        )
    target_scores, ignored = head_logits(stream, target_pool, target_proj, target_heads)
    target = target_dist(select(target_scores, game_hot), next_hot, rewards, discounts, done_flags)
    rows = observed.reshape(-1, PATCH_IN)
    stream = product(rows, patch_w)
    inputs = []
    stored = []
    for index in range(BLOCKS):
        inputs.append(stream)
        weights = fetch_block(
            params_blocks[index].astype(jnp.bfloat16), block_lengths, devices, False
        )
        stored.append(weights)
        stream = block_forward(stream, weights)
    scores, kept = head_logits(stream, pool_w, proj_w, heads_w)
    stream_low, pooled_low, before, hidden_low = kept

    def objective(scores_in):
        return jnp.sum(frame_losses(select(scores_in, game_hot), target, taken_hot, legal_mask))

    loss_part, back_loss = jax.vjp(objective, scores)
    grad_scores = back_loss(jnp.float32(1.0 / frames_all))[0].astype(jnp.bfloat16)
    grad_heads = product_left(hidden_low, grad_scores)
    grad_hidden = product_right(grad_scores, heads_w)
    grad_before = jax.vjp(jax.nn.silu, before)[1](grad_hidden)[0].astype(jnp.bfloat16)
    grad_proj = product_left(pooled_low, grad_before)
    grad_pooled = product_right(grad_before, proj_w).astype(jnp.bfloat16)
    grad_pool = jnp.einsum(
        "npc,nc->cp", stream_low, grad_pooled, preferred_element_type=jnp.float32
    )
    grad_stream = jnp.einsum(
        "nc,cp->npc", grad_pooled, pool_w, preferred_element_type=jnp.float32
    ).reshape(-1, D)
    block_grads = [None] * BLOCKS
    for index in reversed(range(BLOCKS)):
        weights = fetch_block(
            params_blocks[index].astype(jnp.bfloat16), block_lengths, devices, True
        )
        grad_stream, flats = block_backward(inputs[index], weights, grad_stream)
        grid = to_grid(flats, devices)
        block_grads[index] = lax.psum_scatter(
            grid, ("wide", "narrow"), scatter_dimension=0, tiled=True
        ).reshape(-1)
    grad_patch = product_left(rows, grad_stream.astype(jnp.bfloat16))
    top_grid = to_grid((grad_patch, grad_pool, grad_proj, grad_heads), devices)
    grad_top = lax.psum_scatter(
        top_grid, ("wide", "narrow"), scatter_dimension=0, tiled=True
    ).reshape(-1)
    grad_blocks = jnp.stack(block_grads)
    momentum_top, variance_top, direction_top = lamb_parts(
        params_top, grad_top, first_top, second_top
    )
    momentum_blocks, variance_blocks, direction_blocks = lamb_parts(
        params_blocks, grad_blocks, first_blocks, second_blocks
    )
    update_parts = jnp.concatenate(
        [squares(direction_top, top_cuts), squares(direction_blocks, block_cuts).reshape(-1)]
    )
    update_sq, loss_total = lax.psum((update_parts, loss_part), ("wide", "narrow"))
    weight_norm = jnp.sqrt(weight_sq)
    update_norm = jnp.sqrt(update_sq)
    ratio = weight_norm / (update_norm + 1e-06)
    scale_top = spread_ratio(ratio[:4], params_top, top_cuts)
    scale_blocks = spread_ratio(ratio[4:].reshape(BLOCKS, 4), params_blocks, block_cuts)
    updated_top = params_top - LEARNING_RATE * scale_top * direction_top
    updated_blocks = params_blocks - LEARNING_RATE * scale_blocks * direction_blocks
    decay = average_decay()
    averaged_top = decay * average_top + (1.0 - decay) * updated_top
    averaged_blocks = decay * average_blocks + (1.0 - decay) * updated_blocks
    matrix_norms = jnp.stack([weight_norm, update_norm])
    gain_start, gain_width = block_cuts[3]
    gain_grads = grad_blocks[:, gain_start : gain_start + gain_width]
    return (
        loss_total,
        matrix_norms,
        updated_top,
        updated_top.astype(jnp.bfloat16),
        momentum_top,
        variance_top,
        averaged_top,
        updated_blocks,
        updated_blocks.astype(jnp.bfloat16),
        momentum_blocks,
        variance_blocks,
        averaged_blocks,
        gain_grads,
    )


def solution(mesh):
    return jax.shard_map(
        on_device,
        mesh=mesh,
        in_specs=(
            P(("wide", "narrow"), None, None),
            P(("wide", "narrow"), None, None),
            P(("wide", "narrow")),
            P(("wide", "narrow"), None),
            P(("wide", "narrow"), None),
            P(("wide", "narrow")),
            P(("wide", "narrow")),
            P(("wide", "narrow")),
            P(("wide", "narrow")),
            P(None, ("wide", "narrow")),
            P(("wide", "narrow")),
            P(None, ("wide", "narrow")),
            P(("wide", "narrow")),
            P(None, ("wide", "narrow")),
            P(("wide", "narrow")),
            P(None, ("wide", "narrow")),
            P(("wide", "narrow")),
            P(None, ("wide", "narrow")),
        ),
        out_specs=(
            P(),
            P(),
            P(("wide", "narrow")),
            P(("wide", "narrow")),
            P(("wide", "narrow")),
            P(("wide", "narrow")),
            P(("wide", "narrow")),
            P(None, ("wide", "narrow")),
            P(None, ("wide", "narrow")),
            P(None, ("wide", "narrow")),
            P(None, ("wide", "narrow")),
            P(None, ("wide", "narrow")),
            P(None, ("wide", "narrow")),
        ),
        check_vma=False,
    )
```

profile of v0, /device:TPU:0, one launch (start us, length us, event | category | flops | bytes accessed | tf_op | source)
XLA Modules:
  0.0 2721.9 jit_solution(9175684755115947043)
XLA Ops:
  55.6 492.9 %all-reduce.37.cloned.1.call-done = (bf16[3700736]{0:T(1024)(128)(2,1)}, bf16[4462592]{0:T(1024)(128)(2,1)}, bf16[4462592]{0:T(1024)(128)(2,1)}, bf16[3700736]{0:T(1024)(128)(2,1)}) async-done(((bf16[3700736]{0:T(1024)(128)(2,1)}, bf16[4462592]{0:T(1024)(128)(2,1)}, bf16[4462592]{0:T(1024)(128)(2,1)}, bf16[3700736]{0:T(1024)(128)(2,1)}), (bf16[3700736]{0:T(1024)(128)(2,1)}, bf16[4462592]{0:T(1024)(128)(2,1)}, ...) | async-done | bytes 32653328
  548.6 9.5 reshape.1058
  573.6 9.5 reshape.1048
  591.7 16.1 reshape.1059
  636.7 6.1 reshape.1153
  681.5 6.8 copy.490
  697.3 16.3 reshape.1063
  735.0 6.0 reshape.1178
  810.4 7.0 copy.505
  830.0 7.9 reshape_reshape.103
  838.0 11.7 reshape.1171
  857.9 8.0 reshape_reshape.93
  865.9 12.0 reshape.1164
  929.2 7.4 copy.648
  936.6 6.0 reshape.1179
  986.9 17.4 copy.766
  1004.3 37.4 %reshape.1192 = bf16[8925184]{0:T(1024)(128)(2,1)} reshape(bf16[2,32,139456]{2,1,0:T(8,128)(2,1)} %bitcast.414) | data formatting | bytes 35700736
  1041.7 18.6 reshape.1193
  1060.3 15.7 bitcast_bitcast_fusion
  1076.0 195.1 %slice_reduce_fusion.1 = (bf16[4462592]{0:T(1024)(128)(2,1)}, bf16[4462592]{0:T(1024)(128)(2,1)}) fusion(bf16[2,4462592]{1,0:T(2,128)(2,1)} %bitcast_bitcast_fusion), kind=kLoop, calls=%fused_computation.3 | loop fusion | bytes 35700736 | tf_op jit(solution)/shard_map/slice | solution.py:303
  1271.1 16.0 reshape_squeeze.6
  1311.8 6.7 copy.623
  1318.5 16.0 reshape_squeeze.7
  1348.1 6.1 reshape_reshape.86
  1354.2 6.6 copy.459
  1371.3 6.4 reshape.1157
  1411.4 7.8 copy.626
  1419.2 6.1 reshape.1158
  1446.5 6.8 copy.627
  1461.4 6.7 copy.474
  1478.6 6.6 reshape.1160
  1519.0 7.4 copy.630
  1526.4 6.1 reshape.1161
  1575.5 7.1 copy.518
  1637.3 7.4 fusion.149
  1653.0 6.9 copy.543
  1709.1 7.2 fusion.201
  1716.3 8.2 reshape_reshape.108
  1753.4 7.3 fusion.198
  1760.6 8.2 reshape_reshape.105
  1803.6 8.3 reshape.1082
  1817.2 14.8 dynamic-update-slice.36
  1832.1 23.0 dynamic-update-slice.37
  1855.1 16.3 pad_maximum_fusion.1
  1871.5 14.9 pad_maximum_fusion
  1895.2 734.9 %all-reduce.35.cloned.1.call-done = (f32[32,115648]{1,0:T(8,128)}, f32[32,139456]{1,0:T(8,128)}, f32[32,139456]{1,0:T(8,128)}) async-done(((f32[32,115648]{1,0:T(8,128)}, f32[32,139456]{1,0:T(8,128)}, f32[32,139456]{1,0:T(8,128)}), (f32[32,115648]{1,0:T(8,128)}, f32[32,139456]{1,0:T(8,128)}, f32[32,139456]{1,0:T(8,128)})) %all-reduce.35.cloned.1.call-update) | async-done | bytes 50503696
  2653.4 40.0 %all-reduce.29 = (f32[]{:T(128)}, f32[12]{0:T(128)S(1)}, f32[12]{0:T(128)S(1)}) all-reduce(f32[]{:T(128)} %add_reduce_fusion.1, f32[12]{0:T(128)S(1)} %concatenate.209, f32[12]{0:T(128)S(1)} %concatenate.185), channel_id=1, replica_groups=mesh['wide'=8,'narrow'=4] {'wide','narrow'}, use_global_device_ids=true, to_apply=%region_35.36 | all-reduce | flops 25 | bytes 200 | tf_op jit(solution)/shard_map/psum | solution.py:362
  2705.4 7.7 multiply_add_fusion.1
  (1033 shorter events, 779.4 us)
Async XLA Ops:
  7.2 541.4 %all-reduce.37.cloned.1.call-start = ((), (), s32[]{:S(2)}) async-start(), calls=%async_computation.2 | async-start | bytes 65306624
  50.1 936.8 %all-gather.5.cloned.1.call-start = ((), (), s32[]{:S(2)}) async-start(), calls=%async_computation | async-start | bytes 18416640 | tf_op jit(solution)/shard_map/all_gather | solution.py:291
  50.9 2579.2 %all-reduce.35.cloned.1.call-start = ((), (), s32[]{:S(2)}) async-start(), calls=%async_computation.1 | async-start | bytes 101056512
  51.5 497.1 %copy-start.216 = (f32[51]{0:T(128)}, f32[51]{0:T(128)S(1)}, u32[]{:S(2)}) copy-start(f32[51]{0:T(128)S(1)} %multiply_add_fusion.15) | copy-start | bytes 616
  54.2 560.8 %copy-start.67 = (bf16[363,256]{1,0:T(8,128)(2,1)}, bf16[363,256]{1,0:T(8,128)(2,1)S(1)}, u32[]{:S(2)}) copy-start(bf16[363,256]{1,0:T(8,128)(2,1)S(1)} %reshape.1057) | copy-start | bytes 557572
  632.8 10.0 copy-start.129
  633.0 9.7 copy-start.197
  633.6 9.1 copy-start.157
  661.2 27.4 %copy-start.145 = (f32[512]{0:T(512)}, f32[512]{0:T(512)S(1)}, u32[]{:S(2)}) copy-start(f32[512]{0:T(512)S(1)} %get-tuple-element.152) | copy-start | bytes 6148
  661.2 27.4 %copy-start.148 = (f32[512]{0:T(512)}, f32[512]{0:T(512)S(1)}, u32[]{:S(2)}) copy-start(f32[512]{0:T(512)S(1)} %get-tuple-element.153) | copy-start | bytes 6148
  663.3 9.7 copy-start.42
  694.2 19.4 copy-start.199
  694.8 18.8 copy-start.179
  761.9 10.0 copy-start.133
  762.2 9.7 copy-start.203
  762.8 9.1 copy-start.159
  790.1 192.6 %copy-start.151 = (f32[512]{0:T(512)}, f32[512]{0:T(512)S(1)}, u32[]{:S(2)}) copy-start(f32[512]{0:T(512)S(1)} %get-tuple-element.156) | copy-start | bytes 6148
  790.1 192.6 %copy-start.153 = (f32[512]{0:T(512)}, f32[512]{0:T(512)S(1)}, u32[]{:S(2)}) copy-start(f32[512]{0:T(512)S(1)} %get-tuple-element.157) | copy-start | bytes 6148
  792.2 9.7 copy-start.43
  838.0 11.7 slice-start.4
  838.0 14.5 slice-start.5
  889.6 9.5 copy-start.144
  889.6 10.1 copy-start.143
  962.2 13.7 copy-start.146
  962.2 13.7 copy-start.149
  962.2 14.7 copy-start.90
  963.1 14.6 copy-start.104
  963.2 14.5 copy-start.155
  964.0 14.6 copy-start.177
  965.4 13.2 copy-start.211
  967.7 10.1 copy-start.91
  969.6 9.0 copy-start.92
  1318.5 59.2 %copy-start.193 = (f32[512]{0:T(512)}, f32[512]{0:T(512)S(1)}, u32[]{:S(2)}) copy-start(f32[512]{0:T(512)S(1)} %get-tuple-element.164) | copy-start | bytes 6148
  1318.5 59.2 %copy-start.195 = (f32[512]{0:T(512)}, f32[512]{0:T(512)S(1)}, u32[]{:S(2)}) copy-start(f32[512]{0:T(512)S(1)} %get-tuple-element.165) | copy-start | bytes 6148
  1716.3 8.4 copy-start.188
  1716.3 8.4 copy-start.219
  1716.3 8.4 copy-start.237
  1716.3 8.5 copy-start.236
  1716.3 8.5 copy-start.184
  1716.3 8.5 copy-start.183
  1832.1 39.4 %slice-start = ((s8[9437184]{0:T(1024)(128)(4,1)}), s8[1048576]{0:T(1024)(128)(4,1)S(1)}, s32[]{:S(2)}) async-start(s8[9437184]{0:T(1024)(128)(4,1)} %bitcast.415), calls=%async_computation.3 | async-start | bytes 2097152
  1855.1 16.4 slice-start.1
  1855.1 16.4 slice-start.2
  1855.1 16.4 copy-start.23
  1886.4 746.0 %copy-start.108 = (f32[115648]{0:T(1024)S(1)}, f32[115648]{0:T(1024)}, u32[]{:S(2)}) copy-start(f32[115648]{0:T(1024)} %param.28) | copy-start | bytes 1387780
  2632.4 10.2 copy-start.101
  2632.4 10.2 copy-start.102
  2704.1 9.0 copy-start.66
  (209 other events, 900.9 us)
Sparse Core Ops, SparseCore 0:
  50.2 498.2 all-reduce.36
  551.4 118.5 all-gather.4
  1886.6 743.4 all-reduce.34
where the time goes:
time: 2740 us; the launch traced here: 2720 us
  waiting for transfers between devices  1230 us (45%)
  local copies, waits for them, and re-layouts  1160 us (42%)
  other arithmetic  147 us (5%)
  matrix products  131 us (5%)
  blocking collectives  40 us (1%)
    unnamed x5, waiting for transfers between devices  1230 us
    slice x1, local copies, waits for them, and re-layouts, on_device(): target_mids[index]  195 us
    unnamed x571, local copies, waits for them, and re-layouts  178 us
    reshape x34, local copies, waits for them, and re-layouts, group_norm(): (centered * lax.rsqrt(var + 1e-05)).reshape(hidden.shape) * gain + bias  151 us
    dot_general x14, local copies, waits for them, and re-layouts, product(): return jnp.dot(left, right, preferred_element_type=jnp.float32)  66.8 us
    concatenate x54, local copies, waits for them, and re-layouts, columns(): return jnp.concatenate(taps, axis=-1).reshape(-1, 9 * chans)  63.3 us
    slice x19, local copies, waits for them, and re-layouts, unpack(): grid[:, start:start + width].reshape(-1)  56.4 us
  transfers between devices with their start and end apart: 3, of which 2 were waited for; matrix products, arithmetic and copies ran while one was open for 16% of the time, Pallas kernels for 0%

commit v1 on v0

v1 whole, which is shorter than its diff:
```python
import functools

import jax
import jax.numpy as jnp
from jax import lax
from jax.experimental import pallas as pl
from jax.experimental.pallas import tpu as pltpu
from jax.sharding import PartitionSpec as P

D = 2048
BOT = 512
GROUPS = 32
SIDE = 11
PIX = 121
TAPS = 9

ROWS = 128
LANES = 256
VMEM_LIMIT = 60 * 1024 * 1024


def shifts():
    pixel = jnp.arange(ROWS)
    row, col = (pixel // SIDE, pixel % SIDE)
    mats = []
    for tap in range(TAPS):
        at_row, at_col = (row + tap // 3 - 1, col + tap % 3 - 1)
        inside = (at_row >= 0) & (at_row < SIDE) & (at_col >= 0) & (at_col < SIDE) & (pixel < PIX)
        mats.append((inside[:, None] & (pixel[None, :] == (at_row * SIDE + at_col)[:, None])))
    return jnp.concatenate(mats, axis=0).astype(jnp.bfloat16)


def dot(left, right):
    return jnp.dot(left, right, preferred_element_type=jnp.float32)


def dot_rows(left, right):
    return lax.dot_general(
        left, right, (((0,), (0,)), ((), ())), preferred_element_type=jnp.float32
    )


def dot_lanes(left, right):
    return lax.dot_general(
        left, right, (((1,), (1,)), ((), ())), preferred_element_type=jnp.float32
    )


def each_chunk(count, chans, body, unroll=1):
    per = chans // LANES

    def step(index, carry):
        frame = index // per
        rows = pl.ds(pl.multiple_of(frame * ROWS, ROWS), ROWS)
        lanes = pl.ds(pl.multiple_of((index % per) * LANES, LANES), LANES)
        body(pl.ds(frame, 1), rows, lanes)
        return carry

    lax.fori_loop(0, count * per, step, 0, unroll=unroll)


def real_rows():
    return lax.broadcasted_iota(jnp.int32, (ROWS, LANES), 0) < PIX


def group_mean(sums):
    chans = sums.shape[1]
    width = chans // GROUPS
    lane = lax.broadcasted_iota(jnp.int32, sums.shape, 1)
    step = 1
    while step < width:
        ahead = pltpu.roll(sums, chans - step, 1)
        behind = pltpu.roll(sums, step, 1)
        sums = sums + jnp.where((lane & step) == 0, ahead, behind)
        step *= 2
    return sums * (1.0 / (PIX * width))


def silu(value):
    return value / (1.0 + jnp.exp(-value))


def silu_slope(value):
    gate = 1.0 / (1.0 + jnp.exp(-value))
    return gate * (1.0 + value * (1.0 - gate))


def normalise(count, chans, hid, sums, rstd, rstd_at):
    whole = pl.ds(0, chans)
    sums[:, whole] = jnp.zeros((sums.shape[0], chans), jnp.float32)

    def add(frame, rows, lanes):
        sums[frame, lanes] = jnp.sum(hid[rows, lanes], axis=0, keepdims=True)

    each_chunk(count, chans, add, unroll=2)
    sums[:, whole] = group_mean(sums[:, whole])

    def center(frame, rows, lanes):
        value = jnp.where(real_rows(), hid[rows, lanes] - sums[frame, lanes], 0.0)
        hid[rows, lanes] = value
        sums[frame, lanes] = jnp.sum(value * value, axis=0, keepdims=True)

    each_chunk(count, chans, center, unroll=2)
    at = pl.ds(rstd_at, chans)
    rstd[:, at] = lax.rsqrt(group_mean(sums[:, whole]) + 1e-05)


def forward_kernel(count, keep, *refs):
    x, w_in, w_mid, w_out, gains, shift, out = refs[:7]
    hid_one, hid_two, hid_three, rstd, low, act, cols, sums = refs[7:]

    def cast(frame, rows, lanes):
        low[rows, lanes] = x[rows, lanes].astype(jnp.bfloat16)

    def activate(hid, at, offset):
        def body(frame, rows, lanes):
            gain = gains[:, pl.ds(offset + lanes.start, LANES)]
            bias = gains[:, pl.ds(offset + BOT + lanes.start, LANES)]
            value = hid[rows, lanes] * rstd[frame, pl.ds(at + lanes.start, LANES)]
            hid[rows, lanes] = value
            value = jnp.where(real_rows(), silu(value * gain + bias), 0.0)
            act[rows, lanes] = value.astype(jnp.bfloat16)

        return body

    each_chunk(count, D, cast)
    hid_one[...] = dot(low[...], w_in[...])
    normalise(count, BOT, hid_one, sums, rstd, 0)
    each_chunk(count, BOT, activate(hid_one, 0, 0))
    for frame in range(count):
        rows = pl.ds(frame * ROWS, ROWS)
        for tap in range(TAPS):
            picked = dot(shift[pl.ds(tap * ROWS, ROWS), :], act[rows, :])
            cols[rows, pl.ds(tap * BOT, BOT)] = picked.astype(jnp.bfloat16)
    hid_two[...] = dot(cols[...], w_mid[...])
    normalise(count, BOT, hid_two, sums, rstd, BOT)
    each_chunk(count, BOT, activate(hid_two, BOT, 2 * BOT))
    for part in range(D // BOT):
        lanes = pl.ds(part * BOT, BOT)
        hid_three[:, lanes] = dot(act[...], w_out[:, lanes])
    normalise(count, D, hid_three, sums, rstd, 2 * BOT)

    def finish(frame, rows, lanes):
        gain = gains[:, pl.ds(4 * BOT + lanes.start, LANES)]
        bias = gains[:, pl.ds(4 * BOT + D + lanes.start, LANES)]
        value = hid_three[rows, lanes] * rstd[frame, pl.ds(2 * BOT + lanes.start, LANES)]
        if keep:
            hid_three[rows, lanes] = value
        value = silu(x[rows, lanes] + value * gain + bias)
        out[rows, lanes] = jnp.where(real_rows(), value, 0.0)

    each_chunk(count, D, finish)


def in_vmem(number):
    return [pl.BlockSpec(memory_space=pltpu.VMEM)] * number


def f32(*shape):
    return jax.ShapeDtypeStruct(shape, jnp.float32)


def bf16(*shape):
    return jax.ShapeDtypeStruct(shape, jnp.bfloat16)


def stat_rows(count):
    return -(-count // 8) * 8


def block_forward(stream, w_in, w_mid, w_out, gains, shift, keep):
    rows = stream.shape[0]
    count = rows // ROWS
    stats = stat_rows(count)
    kept = [
        ((rows, BOT), jnp.float32),
        ((rows, BOT), jnp.float32),
        ((rows, D), jnp.float32),
        ((stats, 2 * BOT + D), jnp.float32),
    ]
    scratch = [
        ((rows, D), jnp.bfloat16),
        ((rows, BOT), jnp.bfloat16),
        ((rows, TAPS * BOT), jnp.bfloat16),
        ((stats, D), jnp.float32),
    ]
    out_shape = [f32(rows, D)]
    if keep:
        out_shape += [jax.ShapeDtypeStruct(*item) for item in kept]
    else:
        scratch = kept + scratch
    return pl.pallas_call(
        functools.partial(forward_kernel, count, keep),
        out_shape=out_shape,
        in_specs=in_vmem(6),
        out_specs=in_vmem(len(out_shape)),
        scratch_shapes=[pltpu.VMEM(*item) for item in scratch],
        compiler_params=pltpu.CompilerParams(vmem_limit_bytes=VMEM_LIMIT),
        cost_estimate=pl.CostEstimate(
            flops=2 * rows * BOT * (2 * D + 9 * BOT), bytes_accessed=20_000_000, transcendentals=0
        ),
        name="block_forward",
    )(stream, w_in, w_mid, w_out, gains, shift)


def norm_back(count, chans, slope, hid, sums, more, rstd, rstd_at, gain, grad_gain, grad_bias, store):
    whole = pl.ds(0, chans)
    sums[:, whole] = jnp.zeros((sums.shape[0], chans), jnp.float32)
    more[:, whole] = jnp.zeros((sums.shape[0], chans), jnp.float32)

    def add(frame, rows, lanes):
        value = slope(frame, rows, lanes)
        sums[frame, lanes] = jnp.sum(value, axis=0, keepdims=True)
        more[frame, lanes] = jnp.sum(value * hid[rows, lanes], axis=0, keepdims=True)

    each_chunk(count, chans, add)
    grad_bias[...] = jnp.sum(sums[:, whole], axis=0, keepdims=True)
    grad_gain[...] = jnp.sum(more[:, whole], axis=0, keepdims=True)
    sums[:, whole] = group_mean(sums[:, whole] * gain[...])
    more[:, whole] = group_mean(more[:, whole] * gain[...])

    def spread(frame, rows, lanes):
        store(
            rows,
            lanes,
            lambda value: jnp.where(
                real_rows(),
                rstd[frame, pl.ds(rstd_at + lanes.start, LANES)]
                * (value * gain[:, lanes] - sums[frame, lanes] - hid[rows, lanes] * more[frame, lanes]),
                0.0,
            ).astype(jnp.bfloat16),
        )

    each_chunk(count, chans, spread)


def back_out_kernel(count, *refs):
    grad, x, hid_two, hid_three, rstd, w_out, gains = refs[:7]
    dres, dlow, dw_out, dgains = refs[7:11]
    third, act, dact, sums, more = refs[11:]
    gain_three, bias_three = (gains.at[:, pl.ds(4 * BOT, D)], gains.at[:, pl.ds(4 * BOT + D, D)])

    def slope_three(frame, rows, lanes):
        value = x[rows, lanes] + hid_three[rows, lanes] * gain_three[:, lanes] + bias_three[:, lanes]
        value = jnp.where(real_rows(), grad[rows, lanes] * silu_slope(value), 0.0)
        dres[rows, lanes] = value
        return value

    def store_three(rows, lanes, back):
        third[rows, lanes] = back(dres[rows, lanes])

    norm_back(
        count, D, slope_three, hid_three, sums, more, rstd, 2 * BOT, gain_three,
        dgains.at[:, pl.ds(2 * BOT, D)], dgains.at[:, pl.ds(2 * BOT + D, D)], store_three,
    )
    total = None
    for part in range(D // BOT):
        lanes = pl.ds(part * BOT, BOT)
        term = dot_lanes(third[:, lanes], w_out[:, lanes])
        total = term if total is None else total + term
    dact[...] = total
    gain_two, bias_two = (gains.at[:, pl.ds(2 * BOT, BOT)], gains.at[:, pl.ds(3 * BOT, BOT)])

    def slope_two(frame, rows, lanes):
        value = hid_two[rows, lanes] * gain_two[:, lanes] + bias_two[:, lanes]
        gate = 1.0 / (1.0 + jnp.exp(-value))
        act[rows, lanes] = jnp.where(real_rows(), value * gate, 0.0).astype(jnp.bfloat16)
        value = dact[rows, lanes] * (gate * (1.0 + value * (1.0 - gate)))
        value = jnp.where(real_rows(), value, 0.0)
        dact[rows, lanes] = value
        return value

    def store_two(rows, lanes, back):
        dlow[rows, lanes] = back(dact[rows, lanes])

    norm_back(
        count, BOT, slope_two, hid_two, sums, more, rstd, BOT, gain_two,
        dgains.at[:, pl.ds(0, BOT)], dgains.at[:, pl.ds(BOT, BOT)], store_two,
    )
    for part in range(D // BOT):
        lanes = pl.ds(part * BOT, BOT)
        dw_out[:, lanes] = dot_rows(act[...], third[:, lanes]).astype(jnp.bfloat16)


def back_out(grad, stream, hid_two, hid_three, rstd, w_out, gains):
    rows = stream.shape[0]
    count = rows // ROWS
    stats = stat_rows(count)
    return pl.pallas_call(
        functools.partial(back_out_kernel, count),
        out_shape=[f32(rows, D), bf16(rows, BOT), bf16(BOT, D), f32(1, 2 * BOT + 2 * D)],
        in_specs=in_vmem(7),
        out_specs=in_vmem(4),
        scratch_shapes=[
            pltpu.VMEM((rows, D), jnp.bfloat16),
            pltpu.VMEM((rows, BOT), jnp.bfloat16),
            pltpu.VMEM((rows, BOT), jnp.float32),
            pltpu.VMEM((stats, D), jnp.float32),
            pltpu.VMEM((stats, D), jnp.float32),
        ],
        compiler_params=pltpu.CompilerParams(vmem_limit_bytes=VMEM_LIMIT),
        cost_estimate=pl.CostEstimate(
            flops=4 * rows * BOT * D, bytes_accessed=20_000_000, transcendentals=0
        ),
        name="back_out",
    )(grad, stream, hid_two, hid_three, rstd, w_out, gains)


def back_mid_kernel(count, *refs):
    grad, hid_one, rstd, w_mid, gains, shift = refs[:6]
    dlow, dw_mid, dgains = refs[6:9]
    act, cols, dact, sums, more = refs[9:]
    gain_one, bias_one = (gains.at[:, pl.ds(0, BOT)], gains.at[:, pl.ds(BOT, BOT)])
    for frame in range(count):
        rows = pl.ds(frame * ROWS, ROWS)
        for tap in range(TAPS):
            picked = dot(shift[pl.ds((TAPS - 1 - tap) * ROWS, ROWS), :], grad[rows, :])
            cols[rows, pl.ds(tap * BOT, BOT)] = picked.astype(jnp.bfloat16)
    total = None
    for tap in range(TAPS):
        lanes = pl.ds(tap * BOT, BOT)
        term = dot_lanes(cols[:, lanes], w_mid[lanes, :])
        total = term if total is None else total + term
    dact[...] = total

    def slope_one(frame, rows, lanes):
        value = hid_one[rows, lanes] * gain_one[:, lanes] + bias_one[:, lanes]
        gate = 1.0 / (1.0 + jnp.exp(-value))
        act[rows, lanes] = jnp.where(real_rows(), value * gate, 0.0).astype(jnp.bfloat16)
        value = dact[rows, lanes] * (gate * (1.0 + value * (1.0 - gate)))
        value = jnp.where(real_rows(), value, 0.0)
        dact[rows, lanes] = value
        return value

    def store_one(rows, lanes, back):
        dlow[rows, lanes] = back(dact[rows, lanes])

    norm_back(
        count, BOT, slope_one, hid_one, sums, more, rstd, 0, gain_one,
        dgains.at[:, pl.ds(0, BOT)], dgains.at[:, pl.ds(BOT, BOT)], store_one,
    )
    for tap in range(TAPS):
        lanes = pl.ds(tap * BOT, BOT)
        dw_mid[lanes, :] = dot_rows(act[...], cols[:, lanes]).astype(jnp.bfloat16)


def back_mid(grad, hid_one, rstd, w_mid, gains, shift):
    rows = grad.shape[0]
    count = rows // ROWS
    stats = stat_rows(count)
    return pl.pallas_call(
        functools.partial(back_mid_kernel, count),
        out_shape=[bf16(rows, BOT), bf16(TAPS * BOT, BOT), f32(1, 2 * BOT)],
        in_specs=in_vmem(6),
        out_specs=in_vmem(3),
        scratch_shapes=[
            pltpu.VMEM((rows, BOT), jnp.bfloat16),
            pltpu.VMEM((rows, TAPS * BOT), jnp.bfloat16),
            pltpu.VMEM((rows, BOT), jnp.float32),
            pltpu.VMEM((stats, BOT), jnp.float32),
            pltpu.VMEM((stats, BOT), jnp.float32),
        ],
        compiler_params=pltpu.CompilerParams(vmem_limit_bytes=VMEM_LIMIT),
        cost_estimate=pl.CostEstimate(
            flops=4 * rows * BOT * TAPS * BOT, bytes_accessed=12_000_000, transcendentals=0
        ),
        name="back_mid",
    )(grad, hid_one, rstd, w_mid, gains, shift)


def back_in_kernel(count, *refs):
    grad, x, dres, w_in, dw_in, dx, low = refs

    def cast(frame, rows, lanes):
        low[rows, lanes] = x[rows, lanes].astype(jnp.bfloat16)

    each_chunk(count, D, cast)
    for part in range(D // BOT):
        lanes = pl.ds(part * BOT, BOT)
        dw_in[lanes, :] = dot_rows(low[:, lanes], grad[...]).astype(jnp.bfloat16)
        dx[:, lanes] = dres[:, lanes] + dot_lanes(grad[...], w_in[lanes, :])


def back_in(grad, stream, dres, w_in):
    rows = grad.shape[0]
    return pl.pallas_call(
        functools.partial(back_in_kernel, rows // ROWS),
        out_shape=[bf16(D, BOT), f32(rows, D)],
        in_specs=in_vmem(4),
        out_specs=in_vmem(2),
        scratch_shapes=[pltpu.VMEM((rows, D), jnp.bfloat16)],
        compiler_params=pltpu.CompilerParams(vmem_limit_bytes=VMEM_LIMIT),
        cost_estimate=pl.CostEstimate(
            flops=4 * rows * BOT * D, bytes_accessed=15_000_000, transcendentals=0
        ),
        name="back_in",
    )(grad, stream, dres, w_in)


FULL_PRECISION = lax.Precision.HIGHEST
CQL_WEIGHT = 0.05
BETA_ONE = 0.5
BETA_TWO = 0.5
LEARNING_RATE = 0.25
WEIGHT_DECAY = 0.01
PATCH_IN = 256
DPROJ = 512
ACTIONS = 18
ATOMS = 51
GAMES = 4
BLOCKS = 2
STEP = 5
AXES = ("wide", "narrow")
SCORES = GAMES * ACTIONS * ATOMS


def average_decay():
    return min(0.99, (1.0 + STEP) / (10.0 + STEP))


def segment_lengths():
    top = [PATCH_IN * D, D * PIX, D * DPROJ, DPROJ * SCORES]
    block = [D * BOT, 9 * BOT * BOT, BOT * D, 2 * (2 * BOT + D)]
    return (top, block)


def cut_points(lengths, devices):
    cuts = []
    offset = 0
    for length in lengths:
        width = length // devices
        cuts.append((offset, width))
        offset += width
    return cuts


def rows_of(flat, cuts, widths):
    return [
        flat[start : start + size].reshape(-1, width)
        for (start, size), width in zip(cuts, widths)
    ]


def whole(rows):
    return lax.all_gather(rows, AXES, axis=0, tiled=True)


def own_sum(matrix):
    return lax.psum_scatter(matrix, AXES, scatter_dimension=0, tiled=True)


def select(scores, game_hot):
    count = scores.shape[0]
    picked = jnp.einsum(
        "ng,ngk->nk",
        game_hot,
        scores.reshape(count, GAMES, ACTIONS * ATOMS),
        precision=FULL_PRECISION,
    )
    return picked.reshape(count, ACTIONS, ATOMS)


def support():
    return -10.0 + 20.0 / (ATOMS - 1) * jnp.arange(ATOMS, dtype=jnp.float32)


def target_dist(logits_next, next_hot, rewards, discounts, done_flags):
    chosen = jnp.einsum("na,naz->nz", next_hot, logits_next, precision=FULL_PRECISION)
    probs = jax.nn.softmax(chosen, axis=-1)
    atoms = support()
    spacing = 20.0 / (ATOMS - 1)
    keep = discounts * (1.0 - done_flags.astype(jnp.float32))
    moved = jnp.clip(rewards[:, None] + keep[:, None] * atoms[None, :], -10.0, 10.0)
    kernel = jnp.clip(1.0 - jnp.abs(moved[:, :, None] - atoms[None, None, :]) / spacing, 0.0, 1.0)
    return jnp.einsum("nj,nji->ni", probs, kernel, precision=FULL_PRECISION)


def frame_losses(logits, target, taken_hot, legal_now):
    logp = jax.nn.log_softmax(logits, axis=-1)
    action_values = jnp.sum(jnp.exp(logp) * support(), axis=-1)
    taken_logp = jnp.sum(taken_hot[:, :, None] * logp, axis=1)
    cross = -jnp.sum(target * taken_logp, axis=-1)
    masked = jnp.where(legal_now > 0, action_values, -1e30)
    largest = jnp.max(masked, axis=-1, keepdims=True)
    spread = jnp.log(jnp.sum(jnp.exp(masked - largest), axis=-1)) + largest[:, 0]
    return cross + CQL_WEIGHT * (spread - jnp.sum(taken_hot * action_values, axis=-1))


def head_scores(stream, pool_w, proj_w, heads_w):
    low = stream.astype(jnp.bfloat16).reshape(-1, ROWS, D)
    pooled = jnp.einsum("npc,cp->nc", low, pool_w, preferred_element_type=jnp.float32)
    pooled = pooled.astype(jnp.bfloat16)
    before = dot(pooled, proj_w)
    hidden = jax.nn.silu(before).astype(jnp.bfloat16)
    return (dot(hidden, heads_w), (low, pooled, before, hidden))


def lamb_parts(params, grads, first, second):
    momentum = BETA_ONE * first + (1.0 - BETA_ONE) * grads
    variance = BETA_TWO * second + (1.0 - BETA_TWO) * grads * grads
    direction = (
        momentum / (1.0 - BETA_ONE**STEP) / (jnp.sqrt(variance / (1.0 - BETA_TWO**STEP)) + 1e-06)
        + WEIGHT_DECAY * params
    )
    return (momentum, variance, direction)


def squares(flat, cuts):
    return jnp.stack(
        [jnp.sum(jnp.square(flat[..., start : start + width]), axis=-1) for start, width in cuts],
        axis=-1,
    )


def spread_ratio(ratio, flat, cuts):
    parts = [
        jnp.broadcast_to(ratio[..., index : index + 1], flat.shape[:-1] + (width,))
        for index, (start, width) in enumerate(cuts)
    ]
    return jnp.concatenate(parts, axis=-1)


def frame_rows(frames):
    count = frames.shape[0]
    return jnp.pad(frames, ((0, 0), (0, ROWS - PIX), (0, 0))).reshape(count * ROWS, PATCH_IN)


def on_device(
    observed,
    following,
    game_ids,
    actions,
    legal_mask,
    rewards,
    discounts,
    done_flags,
    params_top,
    params_blocks,
    first_top,
    first_blocks,
    second_top,
    second_blocks,
    average_top,
    average_blocks,
    target_top,
    target_blocks,
):
    devices = lax.axis_size(AXES)
    frames_all = observed.shape[0] * devices
    top_lengths, block_lengths = segment_lengths()
    top_cuts = cut_points(top_lengths, devices)
    block_cuts = cut_points(block_lengths, devices)
    top_widths = (D, PIX, DPROJ, SCORES)
    block_widths = (BOT, BOT, D)
    shift = shifts()
    weight_parts = jnp.concatenate(
        [squares(params_top, top_cuts), squares(params_blocks, block_cuts).reshape(-1)]
    )
    weight_sq = lax.psum(weight_parts, AXES)

    game_hot = (game_ids[:, None] == jnp.arange(GAMES)[None, :]).astype(jnp.float32)
    taken_hot = (actions[:, 0:1] == jnp.arange(ACTIONS)[None, :]).astype(jnp.float32)
    next_hot = (actions[:, 1:2] == jnp.arange(ACTIONS)[None, :]).astype(jnp.float32)

    low_top = params_top.astype(jnp.bfloat16)
    low_blocks = params_blocks.astype(jnp.bfloat16)
    gain_start, gain_width = block_cuts[3]
    gain_rows = jnp.concatenate([target_blocks, low_blocks])[:, gain_start:]
    gains = lax.all_gather(gain_rows, AXES, axis=1, tiled=True).astype(jnp.float32)

    def fetch_top(flat):
        patch, pool, proj, heads = rows_of(flat, top_cuts, top_widths)
        pool = jnp.pad(pool, ((0, 0), (0, ROWS - PIX)))
        return (whole(patch), whole(pool), whole(proj), whole(heads))

    def fetch_block(flat):
        return [whole(rows) for rows in rows_of(flat, block_cuts[:3], block_widths)]

    target_patch, target_pool, target_proj, target_heads = fetch_top(target_top)
    stream = dot(frame_rows(following), target_patch)
    for index in range(BLOCKS):
        stream = block_forward(
            stream, *fetch_block(target_blocks[index]), gains[index : index + 1], shift, False
        )[0]
    target_scores, ignored = head_scores(stream, target_pool, target_proj, target_heads)
    target = target_dist(select(target_scores, game_hot), next_hot, rewards, discounts, done_flags)

    patch_w, pool_w, proj_w, heads_w = fetch_top(low_top)
    rows = frame_rows(observed)
    stream = dot(rows, patch_w)
    kept = []
    for index in range(BLOCKS):
        weights = fetch_block(low_blocks[index])
        gain = gains[BLOCKS + index : BLOCKS + index + 1]
        out, hid_one, hid_two, hid_three, rstd = block_forward(stream, *weights, gain, shift, True)
        kept.append((stream, hid_one, hid_two, hid_three, rstd, weights, gain))
        stream = out
    scores, (low, pooled, before, hidden) = head_scores(stream, pool_w, proj_w, heads_w)

    def objective(scores_in):
        return jnp.sum(frame_losses(select(scores_in, game_hot), target, taken_hot, legal_mask))

    loss_part, back_loss = jax.vjp(objective, scores)
    grad_scores = back_loss(jnp.float32(1.0 / frames_all))[0].astype(jnp.bfloat16)
    grad_heads = dot_rows(hidden, grad_scores).astype(jnp.bfloat16)
    grad_hidden = dot_lanes(grad_scores, heads_w)
    grad_before = jax.vjp(jax.nn.silu, before)[1](grad_hidden)[0].astype(jnp.bfloat16)
    grad_proj = dot_rows(pooled, grad_before).astype(jnp.bfloat16)
    grad_pooled = dot_lanes(grad_before, proj_w).astype(jnp.bfloat16)
    grad_pool = jnp.einsum(
        "npc,nc->cp", low, grad_pooled, preferred_element_type=jnp.float32
    ).astype(jnp.bfloat16)
    grad_stream = jnp.einsum(
        "nc,cp->npc", grad_pooled, pool_w, preferred_element_type=jnp.float32
    ).reshape(-1, D)

    grad_blocks = [None] * BLOCKS
    for index in reversed(range(BLOCKS)):
        stream, hid_one, hid_two, hid_three, rstd, weights, gain = kept[index]
        w_in, w_mid, w_out = weights
        dres, dsecond, dw_out, dgains_late = back_out(
            grad_stream, stream, hid_two, hid_three, rstd, w_out, gain
        )
        dfirst, dw_mid, dgains_early = back_mid(dsecond, hid_one, rstd, w_mid, gain, shift)
        dw_in, grad_stream = back_in(dfirst, stream, dres, w_in)
        dgains = jnp.concatenate([dgains_early, dgains_late], axis=1).reshape(devices, -1)
        parts = [own_sum(part).astype(jnp.float32) for part in (dw_in, dw_mid, dw_out, dgains)]
        grad_blocks[index] = jnp.concatenate([part.reshape(-1) for part in parts])
    grad_patch = dot_rows(rows, grad_stream.astype(jnp.bfloat16)).astype(jnp.bfloat16)
    grad_blocks = jnp.stack(grad_blocks)
    parts = [
        own_sum(part).astype(jnp.float32)
        for part in (grad_patch, grad_pool, grad_proj, grad_heads)
    ]
    parts[1] = parts[1][:, :PIX]
    grad_top = jnp.concatenate([part.reshape(-1) for part in parts])

    momentum_top, variance_top, direction_top = lamb_parts(
        params_top, grad_top, first_top, second_top
    )
    momentum_blocks, variance_blocks, direction_blocks = lamb_parts(
        params_blocks, grad_blocks, first_blocks, second_blocks
    )
    update_parts = jnp.concatenate(
        [squares(direction_top, top_cuts), squares(direction_blocks, block_cuts).reshape(-1)]
    )
    update_sq, loss_total = lax.psum((update_parts, loss_part), AXES)
    weight_norm = jnp.sqrt(weight_sq)
    update_norm = jnp.sqrt(update_sq)
    ratio = weight_norm / (update_norm + 1e-06)
    scale_top = spread_ratio(ratio[:4], params_top, top_cuts)
    scale_blocks = spread_ratio(ratio[4:].reshape(BLOCKS, 4), params_blocks, block_cuts)
    updated_top = params_top - LEARNING_RATE * scale_top * direction_top
    updated_blocks = params_blocks - LEARNING_RATE * scale_blocks * direction_blocks
    decay = average_decay()
    averaged_top = decay * average_top + (1.0 - decay) * updated_top
    averaged_blocks = decay * average_blocks + (1.0 - decay) * updated_blocks
    matrix_norms = jnp.stack([weight_norm, update_norm])
    gain_grads = grad_blocks[:, gain_start : gain_start + gain_width]
    return (
        loss_total,
        matrix_norms,
        updated_top,
        updated_top.astype(jnp.bfloat16),
        momentum_top,
        variance_top,
        averaged_top,
        updated_blocks,
        updated_blocks.astype(jnp.bfloat16),
        momentum_blocks,
        variance_blocks,
        averaged_blocks,
        gain_grads,
    )


def solution(mesh):
    one = P(AXES)
    flat = P(None, AXES)
    return jax.shard_map(
        on_device,
        mesh=mesh,
        in_specs=(P(AXES, None, None),) * 2
        + (one, P(AXES, None), P(AXES, None))
        + (one,) * 3
        + (one, flat) * 5,
        out_specs=(P(), P()) + (one,) * 5 + (flat,) * 6,
        check_vma=False,
    )
```

time: 2740 us -> 2500 us (0.912)
  local copies, waits for them, and re-layouts: 1160 us -> 60.5 us
  waiting for transfers between devices: 1230 us -> 1980 us
  blocking collectives: 40 us -> 202 us
  Pallas kernels: 0 us -> 144 us
  other arithmetic: 147 us -> 50.3 us
  matrix products: 131 us -> 38.1 us
    unnamed x5 -> x28, waiting for transfers between devices: 1230 us -> 3.97 us
    reduce_scatter x0 -> x10, waiting for transfers between devices: none -> 1150 us  [own_sum(): return lax.psum_scatter(matrix, AXES, scatter_dimension=0, tiled=True)]
    all_gather x1 -> x18, waiting for transfers between devices: 0.01 us -> 824 us  [whole(): return lax.all_gather(rows, AXES, axis=0, tiled=True)]
    slice x48 -> x13, local copies, waits for them, and re-layouts: 277 us -> 9.06 us  [the longest x12 8.37 us: rows_of(): flat[start:start + size].reshape(-1, width)]
    reshape x55 -> x28, local copies, waits for them, and re-layouts: 257 us -> 21.4 us  [the longest x20 12.9 us: rows_of(): flat[start:start + size].reshape(-1, width)]
    unnamed x571 -> x56, local copies, waits for them, and re-layouts: 178 us -> 2.68 us
    another operation x34 -> x3, local copies, waits for them, and re-layouts: 177 us -> 6.46 us  [the longest x2 5.26 us: on_device(): grad_blocks = jnp.stack(grad_blocks)]
    pallas_call x0 -> x10, Pallas kernels: none -> 144 us  [the longest x4 76.7 us: block_forward(): pl.pallas_call(functools.partial(forward_kernel, count, keep), out_shape=...]
  transfers between devices with their start and end apart: 3 -> 28, of which waited for: 2 -> 26; matrix products, arithmetic and copies ran while one was open for 16% -> 4% of each run, Pallas kernels for 0% -> 6%
where the time goes in v1:
time: 2500 us; the launch traced here: 2490 us
  waiting for transfers between devices  1980 us (79%)
  blocking collectives  202 us (8%)
  Pallas kernels  144 us (6%)
  local copies, waits for them, and re-layouts  60.5 us (2%)
  other arithmetic  50.3 us (2%)
  matrix products  38.1 us (2%)
    reduce_scatter x10, waiting for transfers between devices, own_sum(): return lax.psum_scatter(matrix, AXES, scatter_dimension=0, tiled=True)  1150 us
    all_gather x18, waiting for transfers between devices, whole(): return lax.all_gather(rows, AXES, axis=0, tiled=True)  824 us
    all_gather x2, blocking collectives, whole(): return lax.all_gather(rows, AXES, axis=0, tiled=True)  87.5 us
    pallas_call x4, Pallas kernels, block_forward(): pl.pallas_call(functools.partial(forward_kernel, count, keep), out_shape=...  76.7 us
  transfers between devices with their start and end apart: 28, of which 26 were waited for; matrix products, arithmetic and copies ran while one was open for 4% of the time, Pallas kernels for 6%

profile of v1, /device:TPU:0, one launch (start us, length us, event | category | flops | bytes accessed | tf_op | source)
XLA Modules:
  0.0 2488.4 jit_solution(9722589328756047986)
XLA Ops:
  34.0 44.8 %all_gather.74 = bf16[2048,128]{1,0:T(8,128)(2,1)S(1)} all-gather(bf16[64,128]{1,0:T(8,128)(2,1)S(1)} %pad.16), channel_id=1, replica_groups=mesh['wide'=8,'narrow'=4] {'wide','narrow'}, dimensions={0}, use_global_device_ids=true | all-gather | bytes 540672 | tf_op jit(solution)/shard_map/all_gather | solution.py:445
  78.8 36.9 %all-gather = bf16[32,192,4]{1,2,0:T(4,128)(2,1)S(1)} all-gather(bf16[1,192,4]{1,2,0:T(4,128)(2,1)S(1)} %fusion.70), channel_id=1, replica_groups=mesh['wide'=8,'narrow'=4] {'wide','narrow'}, dimensions={0}, use_global_device_ids=true | all-gather | bytes 50688 | tf_op jit(solution)/shard_map/all_gather | solution.py:569
  117.3 42.7 %all_gather.63 = bf16[2048,128]{1,0:T(8,128)(2,1)} all-gather(bf16[64,128]{1,0:T(8,128)(2,1)S(1)} %pad.14), channel_id=1, replica_groups=mesh['wide'=8,'narrow'=4] {'wide','narrow'}, dimensions={0}, use_global_device_ids=true | all-gather | bytes 540672 | tf_op jit(solution)/shard_map/all_gather | solution.py:445
  167.6 13.9 all-gather.26.cloned.1.call-done.refs_3_
  181.5 58.0 %all-gather.22.cloned.1.call-done.refs_1_ = bf16[2048,512]{1,0:T(8,128)(2,1)} async-done(((bf16[64,512]{1,0:T(8,128)(2,1)}), bf16[2048,512]{1,0:T(8,128)(2,1)}) %all-gather.22.cloned.1.call-update) | async-done | bytes 2097168 | tf_op jit(solution)/shard_map/all_gather | solution.py:445
  239.5 65.9 %all-gather.24.cloned.1.call-done.refs_2_ = bf16[4608,512]{1,0:T(8,128)(2,1)} async-done(((bf16[144,512]{1,0:T(8,128)(2,1)}), bf16[4608,512]{1,0:T(8,128)(2,1)}) %all-gather.24.cloned.1.call-update) | async-done | bytes 4718608 | tf_op jit(solution)/shard_map/all_gather | solution.py:445
  305.3 18.4 block_forward.4.refs_0_
  323.7 39.6 %all-gather.32.cloned.1.call-done.refs_3_ = bf16[512,2048]{1,0:T(8,128)(2,1)} async-done(((bf16[16,2048]{1,0:T(8,128)(2,1)}), bf16[512,2048]{1,0:T(8,128)(2,1)}) %all-gather.32.cloned.1.call-update) | async-done | bytes 2097168 | tf_op jit(solution)/shard_map/all_gather | solution.py:445
  363.3 58.1 %all-gather.28.cloned.1.call-done.refs_1_ = bf16[2048,512]{1,0:T(8,128)(2,1)} async-done(((bf16[64,512]{1,0:T(8,128)(2,1)}), bf16[2048,512]{1,0:T(8,128)(2,1)}) %all-gather.28.cloned.1.call-update) | async-done | bytes 2097168 | tf_op jit(solution)/shard_map/all_gather | solution.py:445
  421.4 66.0 %all-gather.30.cloned.1.call-done.refs_2_ = bf16[4608,512]{1,0:T(8,128)(2,1)} async-done(((bf16[144,512]{1,0:T(8,128)(2,1)}), bf16[4608,512]{1,0:T(8,128)(2,1)}) %all-gather.30.cloned.1.call-update) | async-done | bytes 4718608 | tf_op jit(solution)/shard_map/all_gather | solution.py:445
  487.4 18.4 block_forward.5
  510.8 4.1 fusion.6
  514.9 30.6 %all-gather.34.cloned.1.call-done = bf16[2048,512]{1,0:T(8,128)(2,1)} async-done(((bf16[64,512]{1,0:T(8,128)(2,1)}), bf16[2048,512]{1,0:T(8,128)(2,1)}) %all-gather.34.cloned.1.call-update) | async-done | bytes 2097168 | tf_op jit(solution)/shard_map/all_gather | solution.py:445
  545.5 63.0 %all-gather.36.cloned.1.call-done = bf16[512,3672]{1,0:T(8,128)(2,1)} async-done(((bf16[16,3672]{1,0:T(8,128)(2,1)}), bf16[512,3672]{1,0:T(8,128)(2,1)}) %all-gather.36.cloned.1.call-update) | async-done | bytes 3760144 | tf_op jit(solution)/shard_map/all_gather | solution.py:445
  608.5 3.8 fusion.59
  612.7 54.4 %all-gather.44.cloned.1.call-done.refs_3_.refs_5_ = bf16[512,2048]{1,0:T(8,128)(2,1)} async-done(((bf16[16,2048]{1,0:T(8,128)(2,1)}), bf16[512,2048]{1,0:T(8,128)(2,1)}) %all-gather.44.cloned.1.call-update) | async-done | bytes 2097168 | tf_op jit(solution)/shard_map/all_gather | solution.py:445
  667.1 58.5 %all-gather.40.cloned.1.call-done.refs_1_.refs_3_ = bf16[2048,512]{1,0:T(8,128)(2,1)} async-done(((bf16[64,512]{1,0:T(8,128)(2,1)}), bf16[2048,512]{1,0:T(8,128)(2,1)}) %all-gather.40.cloned.1.call-update) | async-done | bytes 2097168 | tf_op jit(solution)/shard_map/all_gather | solution.py:445
  725.7 66.0 %all-gather.42.cloned.1.call-done.refs_2_.refs_3_ = bf16[4608,512]{1,0:T(8,128)(2,1)} async-done(((bf16[144,512]{1,0:T(8,128)(2,1)}), bf16[4608,512]{1,0:T(8,128)(2,1)}) %all-gather.42.cloned.1.call-update) | async-done | bytes 4718608 | tf_op jit(solution)/shard_map/all_gather | solution.py:445
  791.7 19.9 block_forward.6
  811.5 38.1 %all-gather.50.cloned.1.call-done.refs_3_.refs_5_ = bf16[512,2048]{1,0:T(8,128)(2,1)} async-done(((bf16[16,2048]{1,0:T(8,128)(2,1)}), bf16[512,2048]{1,0:T(8,128)(2,1)}) %all-gather.50.cloned.1.call-update) | async-done | bytes 2097168 | tf_op jit(solution)/shard_map/all_gather | solution.py:445
  849.6 58.0 %all-gather.46.cloned.1.call-done.refs_1_.refs_3_ = bf16[2048,512]{1,0:T(8,128)(2,1)} async-done(((bf16[64,512]{1,0:T(8,128)(2,1)}), bf16[2048,512]{1,0:T(8,128)(2,1)}) %all-gather.46.cloned.1.call-update) | async-done | bytes 2097168 | tf_op jit(solution)/shard_map/all_gather | solution.py:445
  907.6 65.9 %all-gather.48.cloned.1.call-done.refs_2_.refs_3_ = bf16[4608,512]{1,0:T(8,128)(2,1)} async-done(((bf16[144,512]{1,0:T(8,128)(2,1)}), bf16[4608,512]{1,0:T(8,128)(2,1)}) %all-gather.48.cloned.1.call-update) | async-done | bytes 4718608 | tf_op jit(solution)/shard_map/all_gather | solution.py:445
  973.4 20.1 block_forward.7
  999.0 4.9 fusion.4
  1003.9 27.5 %all-gather.52.cloned.1.call-done = bf16[2048,512]{1,0:T(8,128)(2,1)} async-done(((bf16[64,512]{1,0:T(8,128)(2,1)}), bf16[2048,512]{1,0:T(8,128)(2,1)}) %all-gather.52.cloned.1.call-update) | async-done | bytes 2097168 | tf_op jit(solution)/shard_map/all_gather | solution.py:445
  1033.7 60.7 %all-gather.54.cloned.1.call-done = bf16[512,3672]{1,0:T(8,128)(2,1)} async-done(((bf16[16,3672]{1,0:T(8,128)(2,1)}), bf16[512,3672]{1,0:T(8,128)(2,1)}) %all-gather.54.cloned.1.call-update) | async-done | bytes 3760144 | tf_op jit(solution)/shard_map/all_gather | solution.py:445
  1108.5 13.6 back_out.2
  1122.1 11.7 back_mid.2
  1133.8 8.3 back_in.2
  1142.1 13.8 back_out.3
  1155.9 11.6 back_mid.3
  1167.5 8.3 back_in.3
  1175.8 3.7 convolution_convert_fusion.2
  1192.7 39.9 %all-reduce.7 = (f32[32,192]{1,0:T(8,128)S(1)}, f32[32,192]{1,0:T(8,128)S(1)}) all-reduce(f32[32,192]{1,0:T(8,128)S(1)} %reshape.486, f32[32,192]{1,0:T(8,128)S(1)} %reshape.478), channel_id=13, replica_groups=mesh['wide'=8,'narrow'=4] {'wide','narrow'}, use_global_device_ids=true, to_apply=%region_39.40.clone | all-reduce | flops 12288 | bytes 98304
  1239.1 132.6 %reduce-scatter.11.cloned.1.call-done = bf16[8,2048]{1,0:T(8,128)(2,1)} async-done(((bf16[256,2048]{1,0:T(8,128)(2,1)}), bf16[8,2048]{1,0:T(8,128)(2,1)}) %reduce-scatter.11.cloned.1.call-update) | async-done | bytes 32784 | tf_op jit(solution)/shard_map/reduce_scatter | solution.py:449
  1372.5 134.1 %reduce-scatter.15.cloned.1.call-done = bf16[64,512]{1,0:T(8,128)(2,1)} async-done(((bf16[2048,512]{1,0:T(8,128)(2,1)}), bf16[64,512]{1,0:T(8,128)(2,1)}) %reduce-scatter.15.cloned.1.call-update) | async-done | bytes 65552 | tf_op jit(solution)/shard_map/reduce_scatter | solution.py:449
  1508.1 133.5 %reduce-scatter.29.cloned.1.call-done = bf16[16,2048]{1,0:T(8,128)(2,1)} async-done(((bf16[512,2048]{1,0:T(8,128)(2,1)}), bf16[16,2048]{1,0:T(8,128)(2,1)}) %reduce-scatter.29.cloned.1.call-update) | async-done | bytes 65552 | tf_op jit(solution)/shard_map/reduce_scatter | solution.py:449
  1642.4 133.9 %reduce-scatter.25.cloned.1.call-done = bf16[64,512]{1,0:T(8,128)(2,1)} async-done(((bf16[2048,512]{1,0:T(8,128)(2,1)}), bf16[64,512]{1,0:T(8,128)(2,1)}) %reduce-scatter.25.cloned.1.call-update) | async-done | bytes 65552 | tf_op jit(solution)/shard_map/reduce_scatter | solution.py:449
  1777.3 133.9 %reduce-scatter.23.cloned.1.call-done = bf16[16,2048]{1,0:T(8,128)(2,1)} async-done(((bf16[512,2048]{1,0:T(8,128)(2,1)}), bf16[16,2048]{1,0:T(8,128)(2,1)}) %reduce-scatter.23.cloned.1.call-update) | async-done | bytes 65552 | tf_op jit(solution)/shard_map/reduce_scatter | solution.py:449
  1912.0 133.9 %reduce-scatter.19.cloned.1.call-done = bf16[64,512]{1,0:T(8,128)(2,1)} async-done(((bf16[2048,512]{1,0:T(8,128)(2,1)}), bf16[64,512]{1,0:T(8,128)(2,1)}) %reduce-scatter.19.cloned.1.call-update) | async-done | bytes 65552 | tf_op jit(solution)/shard_map/reduce_scatter | solution.py:449
  2046.9 108.2 %reduce-scatter.27.cloned.1.call-done = bf16[144,512]{1,0:T(8,128)(2,1)} async-done(((bf16[4608,512]{1,0:T(8,128)(2,1)}), bf16[144,512]{1,0:T(8,128)(2,1)}) %reduce-scatter.27.cloned.1.call-update) | async-done | bytes 147472 | tf_op jit(solution)/shard_map/reduce_scatter | solution.py:449
  2158.8 107.8 %reduce-scatter.21.cloned.1.call-done = bf16[144,512]{1,0:T(8,128)(2,1)} async-done(((bf16[4608,512]{1,0:T(8,128)(2,1)}), bf16[144,512]{1,0:T(8,128)(2,1)}) %reduce-scatter.21.cloned.1.call-update) | async-done | bytes 147472 | tf_op jit(solution)/shard_map/reduce_scatter | solution.py:449
  2270.3 6.8 multiply_add_fusion.2
  2278.6 129.5 %reduce-scatter.17.cloned.1.call-done = bf16[16,3672]{1,0:T(8,128)(2,1)} async-done(((bf16[512,3672]{1,0:T(8,128)(2,1)}), bf16[16,3672]{1,0:T(8,128)(2,1)}) %reduce-scatter.17.cloned.1.call-update) | async-done | bytes 117520 | tf_op jit(solution)/shard_map/reduce_scatter | solution.py:449
  2409.8 3.8 concatenate.39
  2422.6 37.3 %all-reduce.6 = (f32[]{:T(128)}, f32[12]{0:T(128)S(1)}, f32[12]{0:T(128)S(1)}) all-reduce(f32[]{:T(128)} %add_reduce_fusion.1, f32[12]{0:T(128)S(1)} %concatenate.45, f32[12]{0:T(128)S(1)} %concatenate.38), channel_id=1, replica_groups=mesh['wide'=8,'narrow'=4] {'wide','narrow'}, use_global_device_ids=true, to_apply=%region_11.12 | all-reduce | flops 25 | bytes 200 | tf_op jit(solution)/shard_map/psum | solution.py:647
  2464.8 3.6 concatenate.46
  2471.9 7.7 multiply_add_fusion.1
  (307 shorter events, 117.4 us)
Async XLA Ops:
  7.2 7.5 copy-start.4
  7.2 153.5 %all-gather.20.cloned.1.call-start = ((), (), s32[]{:S(2)}) async-start(), calls=%async_computation.10 | async-start | bytes 1081344 | tf_op jit(solution)/shard_map/all_gather | solution.py:445
  8.7 10.7 copy-start.10
  8.7 155.4 %all-gather.38.cloned.1.call-start = ((), (), s32[]{:S(2)}) async-start(), calls=%async_computation.19 | async-start | bytes 1081344 | tf_op jit(solution)/shard_map/all_gather | solution.py:445
  10.5 10.8 copy-start
  10.5 171.0 %all-gather.26.cloned.1.call-start = ((), (), s32[]{:S(2)}) async-start(), calls=%async_computation.13 | async-start | bytes 2162688 | tf_op jit(solution)/shard_map/all_gather | solution.py:445
  13.9 225.6 %all-gather.22.cloned.1.call-start = ((), (), s32[]{:S(2)}) async-start(), calls=%async_computation.11 | async-start | bytes 2162688 | tf_op jit(solution)/shard_map/all_gather | solution.py:445
  14.6 290.7 %all-gather.24.cloned.1.call-start = ((), (), s32[]{:S(2)}) async-start(), calls=%async_computation.12 | async-start | bytes 4866048 | tf_op jit(solution)/shard_map/all_gather | solution.py:445
  17.0 346.2 %all-gather.32.cloned.1.call-start = ((), (), s32[]{:S(2)}) async-start(), calls=%async_computation.16 | async-start | bytes 2162688 | tf_op jit(solution)/shard_map/all_gather | solution.py:445
  17.7 403.6 %all-gather.28.cloned.1.call-start = ((), (), s32[]{:S(2)}) async-start(), calls=%async_computation.14 | async-start | bytes 2162688 | tf_op jit(solution)/shard_map/all_gather | solution.py:445
  18.5 468.9 %all-gather.30.cloned.1.call-start = ((), (), s32[]{:S(2)}) async-start(), calls=%async_computation.15 | async-start | bytes 4866048 | tf_op jit(solution)/shard_map/all_gather | solution.py:445
  19.3 526.2 %all-gather.34.cloned.1.call-start = ((), (), s32[]{:S(2)}) async-start(), calls=%async_computation.17 | async-start | bytes 2162688 | tf_op jit(solution)/shard_map/all_gather | solution.py:445
  20.2 588.4 %all-gather.36.cloned.1.call-start = ((), (), s32[]{:S(2)}) async-start(), calls=%async_computation.18 | async-start | bytes 3919872 | tf_op jit(solution)/shard_map/all_gather | solution.py:445
  21.2 645.9 %all-gather.44.cloned.1.call-start = ((), (), s32[]{:S(2)}) async-start(), calls=%async_computation.22 | async-start | bytes 2162688 | tf_op jit(solution)/shard_map/all_gather | solution.py:445
  23.8 701.9 %all-gather.40.cloned.1.call-start = ((), (), s32[]{:S(2)}) async-start(), calls=%async_computation.20 | async-start | bytes 2162688 | tf_op jit(solution)/shard_map/all_gather | solution.py:445
  24.6 7.1 copy-start.18
  24.6 767.1 %all-gather.42.cloned.1.call-start = ((), (), s32[]{:S(2)}) async-start(), calls=%async_computation.21 | async-start | bytes 4866048 | tf_op jit(solution)/shard_map/all_gather | solution.py:445
  26.2 7.6 copy-start.11
  26.9 6.8 copy-start.12
  27.0 822.6 %all-gather.50.cloned.1.call-start = ((), (), s32[]{:S(2)}) async-start(), calls=%async_computation.25 | async-start | bytes 2162688 | tf_op jit(solution)/shard_map/all_gather | solution.py:445
  27.7 879.9 %all-gather.46.cloned.1.call-start = ((), (), s32[]{:S(2)}) async-start(), calls=%async_computation.23 | async-start | bytes 2162688 | tf_op jit(solution)/shard_map/all_gather | solution.py:445
  28.4 945.0 %all-gather.48.cloned.1.call-start = ((), (), s32[]{:S(2)}) async-start(), calls=%async_computation.24 | async-start | bytes 4866048 | tf_op jit(solution)/shard_map/all_gather | solution.py:445
  29.3 1002.1 %all-gather.52.cloned.1.call-start = ((), (), s32[]{:S(2)}) async-start(), calls=%async_computation.26 | async-start | bytes 2162688 | tf_op jit(solution)/shard_map/all_gather | solution.py:445
  30.1 1064.3 %all-gather.54.cloned.1.call-start = ((), (), s32[]{:S(2)}) async-start(), calls=%async_computation.27 | async-start | bytes 3919872 | tf_op jit(solution)/shard_map/all_gather | solution.py:445
  31.2 1207.1 %reduce-scatter.13.cloned.1.call-start = ((), (), s32[]{:S(2)}) async-start(), calls=%async_computation.29 | async-start | bytes 540672 | tf_op jit(solution)/shard_map/reduce_scatter | solution.py:449
  31.6 85.4 %copy-start.21 = (f32[3]{0:T(128)S(1)}, f32[3]{0:T(128)}, u32[]{:S(2)}) copy-start(f32[3]{0:T(128)} %param.24) | copy-start | bytes 40
  31.6 85.4 %copy-start.22 = (s32[3]{0:T(128)S(1)}, s32[3]{0:T(128)}, u32[]{:S(2)}) copy-start(s32[3]{0:T(128)} %param.25) | copy-start | bytes 40
  31.6 85.5 %copy-start.20 = (s32[3]{0:T(128)S(1)}, s32[3]{0:T(128)}, u32[]{:S(2)}) copy-start(s32[3]{0:T(128)} %param.20) | copy-start | bytes 40
  31.6 85.6 %copy-start.19 = (f32[3]{0:T(128)S(1)}, f32[3]{0:T(128)}, u32[]{:S(2)}) copy-start(f32[3]{0:T(128)} %param.23) | copy-start | bytes 40
  1033.7 64.3 %copy-start.17 = (s32[3,18]{1,0:T(4,128)S(1)}, s32[3,18]{1,0:T(4,128)}, u32[]{:S(2)}) copy-start(s32[3,18]{1,0:T(4,128)} %param.22) | copy-start | bytes 652
  1099.9 3.3 copy-start.1
  1105.2 266.5 %reduce-scatter.11.cloned.1.call-start = ((), (), s32[]{:S(2)}) async-start(), calls=%async_computation.28 | async-start | bytes 1081344 | tf_op jit(solution)/shard_map/reduce_scatter | solution.py:449
  1175.8 3.8 copy-start.6
  1179.5 327.1 %reduce-scatter.15.cloned.1.call-start = ((), (), s32[]{:S(2)}) async-start(), calls=%async_computation.30 | async-start | bytes 2162688 | tf_op jit(solution)/shard_map/reduce_scatter | solution.py:449
  1181.6 460.0 %reduce-scatter.29.cloned.1.call-start = ((), (), s32[]{:S(2)}) async-start(), calls=%async_computation.37 | async-start | bytes 2162688 | tf_op jit(solution)/shard_map/reduce_scatter | solution.py:449
  1182.4 594.0 %reduce-scatter.25.cloned.1.call-start = ((), (), s32[]{:S(2)}) async-start(), calls=%async_computation.35 | async-start | bytes 2162688 | tf_op jit(solution)/shard_map/reduce_scatter | solution.py:449
  1183.1 728.1 %reduce-scatter.23.cloned.1.call-start = ((), (), s32[]{:S(2)}) async-start(), calls=%async_computation.34 | async-start | bytes 2162688 | tf_op jit(solution)/shard_map/reduce_scatter | solution.py:449
  1183.7 862.3 %reduce-scatter.19.cloned.1.call-start = ((), (), s32[]{:S(2)}) async-start(), calls=%async_computation.32 | async-start | bytes 2162688 | tf_op jit(solution)/shard_map/reduce_scatter | solution.py:449
  1184.4 970.7 %reduce-scatter.27.cloned.1.call-start = ((), (), s32[]{:S(2)}) async-start(), calls=%async_computation.36 | async-start | bytes 4866048 | tf_op jit(solution)/shard_map/reduce_scatter | solution.py:449
  1185.0 1081.6 %reduce-scatter.21.cloned.1.call-start = ((), (), s32[]{:S(2)}) async-start(), calls=%async_computation.33 | async-start | bytes 4866048 | tf_op jit(solution)/shard_map/reduce_scatter | solution.py:449
  1185.1 7.4 copy-start.13
  1185.1 7.4 copy-start.15
  1185.1 7.5 copy-start.14
  1185.1 7.5 copy-start.16
  1185.6 1222.5 %reduce-scatter.17.cloned.1.call-start = ((), (), s32[]{:S(2)}) async-start(), calls=%async_computation.31 | async-start | bytes 3919872 | tf_op jit(solution)/shard_map/reduce_scatter | solution.py:449
  2270.3 6.8 copy-start.3
  2468.4 3.5 copy-start.9
  2470.6 9.0 copy-start.8
  (3 other events, 5.8 us)
Sparse Core Ops, SparseCore 0:
  10.9 56.9 all-gather.19
  70.8 52.3 all-gather.37
  126.0 55.4 all-gather.25
  184.2 55.2 all-gather.21
  242.8 62.4 all-gather.23
  308.0 55.1 all-gather.31
  366.1 55.2 all-gather.27
  424.9 62.4 all-gather.29
  490.3 55.1 all-gather.33
  548.8 59.7 all-gather.35
  612.0 55.1 all-gather.43
  670.4 55.2 all-gather.39
  729.2 62.4 all-gather.41
  794.4 55.1 all-gather.49
  852.3 55.2 all-gather.45
  910.9 62.4 all-gather.47
  976.1 55.1 all-gather.51
  1034.6 59.7 all-gather.53
  1105.3 132.9 reduce-scatter.12
  1241.0 130.6 reduce-scatter.10
  1374.0 132.5 reduce-scatter.14
  1508.9 132.5 reduce-scatter.28
  1643.8 132.5 reduce-scatter.24
  1778.6 132.5 reduce-scatter.22
  1913.4 132.5 reduce-scatter.18
  2052.2 102.8 reduce-scatter.26
  2160.5 106.0 reduce-scatter.20
  2269.0 139.0 reduce-scatter.16

commit v2 on v1

--- a/solution.py
+++ b/solution.py
@@ -1,4 +1,5 @@
 import functools
+import itertools
 
 import jax
 import jax.numpy as jnp
@@ -137,7 +138,7 @@
     each_chunk(count, BOT, activate(hid_two, BOT, 2 * BOT))
     for part in range(D // BOT):
         lanes = pl.ds(part * BOT, BOT)
-        hid_three[:, lanes] = dot(act[...], w_out[:, lanes])
+        hid_three[:, lanes] = dot(act[...], w_out[lanes, :])
     normalise(count, D, hid_three, sums, rstd, 2 * BOT)
 
     def finish(frame, rows, lanes):
@@ -150,10 +151,6 @@
         out[rows, lanes] = jnp.where(real_rows(), value, 0.0)
 
     each_chunk(count, D, finish)
-
-
-def in_vmem(number):
-    return [pl.BlockSpec(memory_space=pltpu.VMEM)] * number
 
 
 def f32(*shape):
@@ -256,7 +253,7 @@
     total = None
     for part in range(D // BOT):
         lanes = pl.ds(part * BOT, BOT)
-        term = dot_lanes(third[:, lanes], w_out[:, lanes])
+        term = dot_lanes(third[:, lanes], w_out[lanes, :])
         total = term if total is None else total + term
     dact[...] = total
     gain_two, bias_two = (gains.at[:, pl.ds(2 * BOT, BOT)], gains.at[:, pl.ds(3 * BOT, BOT)])
@@ -279,7 +276,7 @@
     )
     for part in range(D // BOT):
         lanes = pl.ds(part * BOT, BOT)
-        dw_out[:, lanes] = dot_rows(act[...], third[:, lanes]).astype(jnp.bfloat16)
+        dw_out[lanes, :] = dot_rows(act[...], third[:, lanes]).astype(jnp.bfloat16)
 
 
 def back_out(grad, stream, hid_two, hid_three, rstd, w_out, gains):
@@ -288,7 +285,7 @@
     stats = stat_rows(count)
     return pl.pallas_call(
         functools.partial(back_out_kernel, count),
-        out_shape=[f32(rows, D), bf16(rows, BOT), bf16(BOT, D), f32(1, 2 * BOT + 2 * D)],
+        out_shape=[f32(rows, D), bf16(rows, BOT), bf16(D, BOT), f32(1, 2 * BOT + 2 * D)],
         in_specs=in_vmem(7),
         out_specs=in_vmem(4),
         scratch_shapes=[
@@ -397,6 +394,365 @@
     )(grad, stream, dres, w_in)
 
 
+def spread_pixels(devices):
+    rows = PATCH_IN // devices
+    value = jnp.arange(PATCH_IN)
+    at = value // rows * 2 * rows + value % rows
+    return jnp.stack(
+        [jnp.arange(2 * PATCH_IN)[None, :] == (at + half * rows)[:, None] for half in range(2)]
+    ).astype(jnp.bfloat16)
+
+
+def embed_kernel(pixels, spread, patch, out):
+    for half in range(2):
+        wide = dot(pixels[...], spread[half]).astype(jnp.bfloat16)
+        for block in range(2):
+            lanes = pl.ds((2 * half + block) * WIDTH, WIDTH)
+            out[:, lanes] = dot(wide, patch[block])
+
+
+def embed(pixels, spread, patch):
+    return pl.pallas_call(
+        embed_kernel,
+        out_shape=f32(pixels.shape[0], D),
+        in_specs=in_vmem(3),
+        out_specs=in_vmem(1)[0],
+        compiler_params=pltpu.CompilerParams(vmem_limit_bytes=VMEM_LIMIT),
+        name="embed",
+    )(pixels, spread, patch)
+
+
+def embed_back_kernel(pixels, spread, grad, out):
+    wide = [dot(pixels[...], spread[half]).astype(jnp.bfloat16) for half in range(2)]
+    for block in range(2):
+        total = None
+        for half in range(2):
+            lanes = pl.ds((2 * half + block) * WIDTH, WIDTH)
+            term = dot_rows(wide[half], grad[:, lanes].astype(jnp.bfloat16))
+            total = term if total is None else total + term
+        out[block] = total.astype(jnp.bfloat16)
+
+
+def embed_back(pixels, spread, grad):
+    return pl.pallas_call(
+        embed_back_kernel,
+        out_shape=bf16(2, 2 * PATCH_IN, WIDTH),
+        in_specs=in_vmem(3),
+        out_specs=in_vmem(1)[0],
+        compiler_params=pltpu.CompilerParams(vmem_limit_bytes=VMEM_LIMIT),
+        name="embed_back",
+    )(pixels, spread, grad)
+
+
+WIDTH = 512
+TILE = 16
+AXES = ("wide", "narrow")
+
+
+def grid_sizes():
+    return (lax.axis_size("wide") // 2, 2, lax.axis_size("narrow") // 2, 2)
+
+
+def spot():
+    sizes = grid_sizes()
+    wide, narrow = (lax.axis_index("wide"), lax.axis_index("narrow"))
+    return jnp.stack(
+        [wide // sizes[1], wide % sizes[1], narrow // sizes[3], narrow % sizes[3]]
+    ).astype(jnp.int32)
+
+
+def hop(array, axis_of_core, step=1):
+    sizes = grid_sizes()
+    pairs = []
+    for place in itertools.product(*[range(size) for size in sizes]):
+        axis = axis_of_core[place[3]]
+        other = list(place)
+        other[axis] = (place[axis] + step) % sizes[axis]
+        source, target = [
+            ((z * sizes[1] + y) * sizes[2] + x) * sizes[3] + core for z, y, x, core in (place, other)
+        ]
+        pairs.append((source, target))
+    return lax.ppermute(array, AXES, pairs)
+
+
+ALONG_Z = (0, 0)
+ACROSS = (3, 3)
+NEAR = (2, 1)
+FAR = (1, 2)
+
+
+def hbm(number):
+    return [pl.BlockSpec(memory_space=pl.ANY)] * number
+
+
+def in_vmem(number):
+    return [pl.BlockSpec(memory_space=pltpu.VMEM)] * number
+
+
+def in_smem():
+    return [pl.BlockSpec(memory_space=pltpu.SMEM)]
+
+
+def copies(pairs, sems):
+    started = [
+        pltpu.make_async_copy(source, target, sems.at[index])
+        for index, (source, target) in enumerate(pairs)
+    ]
+    for copy in started:
+        copy.start()
+    for copy in started:
+        copy.wait()
+
+
+class Part:
+    def __init__(self, blocks, rows, lanes):
+        self.blocks, self.rows, self.lanes = (blocks, rows, lanes)
+        self.across = WIDTH // lanes
+        self.travel = blocks * rows // self.across
+
+    def moves(self):
+        if self.across > 1:
+            deep = self.rows // self.across
+            return [(0, part * self.lanes, deep, 0, part * deep) for part in range(self.across)]
+        return [(block * self.rows, 0, self.rows, block, 0) for block in range(self.blocks)]
+
+    def pack(self, piece):
+        if self.across > 1:
+            piece = piece.reshape(self.across, self.rows // self.across, self.lanes)
+            return piece.transpose(1, 0, 2).reshape(self.travel, WIDTH)
+        return piece.reshape(self.travel, WIDTH)
+
+    def unpack(self, rows):
+        if self.across > 1:
+            rows = rows.reshape(self.rows // self.across, self.across, self.lanes)
+            return rows.transpose(1, 0, 2).reshape(1, self.rows, self.lanes)
+        return rows.reshape(self.blocks, self.rows, self.lanes)
+
+    def full(self, depth):
+        return (self.blocks, depth, 2, 2, 2, self.rows, self.lanes)
+
+
+def half_rows(parts):
+    total = sum(part.travel for part in parts)
+    return -(-total // (2 * TILE)) * TILE
+
+
+def half_moves(parts):
+    cut = half_rows(parts)
+    halves = ([], [])
+    offset = 0
+    for index, part in enumerate(parts):
+        for row, lane, rows, block, inner in part.moves():
+            row = row + offset
+            before = max(0, min(rows, cut - row))
+            if before:
+                halves[0].append((index, row, lane, before, block, inner))
+            if rows - before:
+                halves[1].append((index, row + before - cut, lane, rows - before, block, inner + before))
+        offset += part.travel
+    return halves
+
+
+def unit(parts, depth):
+    return (depth, 2, half_rows(parts), WIDTH)
+
+
+def pack(parts, pieces):
+    rows = jnp.concatenate([part.pack(piece) for part, piece in zip(parts, pieces)])
+    return jnp.pad(rows, ((0, 2 * half_rows(parts) - rows.shape[0]), (0, 0)))
+
+
+def stack_kernel(size, place, *refs):
+    pairs = [
+        (refs[step], refs[size].at[lax.rem(place[0] - step + size, size)]) for step in range(size)
+    ]
+    copies(pairs, refs[size + 1])
+
+
+def stack_z(arrays, place):
+    size = len(arrays)
+    return pl.pallas_call(
+        functools.partial(stack_kernel, size),
+        out_shape=jax.ShapeDtypeStruct((size,) + arrays[0].shape, arrays[0].dtype),
+        in_specs=in_smem() + hbm(size),
+        out_specs=in_vmem(1)[0],
+        scratch_shapes=[pltpu.SemaphoreType.DMA((size,))],
+        name="stack_z",
+    )(place, *arrays)
+
+
+def assemble_pairs(parts, core, y, x, ins, outs):
+    pairs = []
+    for number, (other, far, near) in enumerate(itertools.product((0, 1), repeat=3)):
+        half = core ^ other
+        step = [0, 0, 0, 0]
+        step[NEAR[half]], step[FAR[half]] = (near, far)
+        at_y, at_x = (lax.rem(y + step[1], 2), lax.rem(x + step[2], 2))
+        for index, row, lane, rows, block, inner in half_moves(parts)[half]:
+            pairs.append(
+                (
+                    ins[number].at[:, :, pl.ds(row, rows), pl.ds(lane, parts[index].lanes)],
+                    outs[index].at[block, :, at_y, at_x, :, pl.ds(inner, rows)],
+                )
+            )
+    return pairs
+
+
+def assemble_copies(parts):
+    return 4 * sum(len(moves) for moves in half_moves(parts))
+
+
+def assemble_kernel(parts, place, *refs):
+    for core in (0, 1):
+
+        @pl.when(place[3] == core)
+        def _():
+            copies(
+                assemble_pairs(parts, core, place[1], place[2], refs[:8], refs[8:-1]), refs[-1]
+            )
+
+
+def assemble(parts, buffers, place):
+    depth = buffers[0].shape[0]
+    full = pl.pallas_call(
+        functools.partial(assemble_kernel, parts),
+        out_shape=[jax.ShapeDtypeStruct(part.full(depth), jnp.bfloat16) for part in parts],
+        in_specs=in_smem() + hbm(8),
+        out_specs=in_vmem(len(parts)),
+        scratch_shapes=[pltpu.SemaphoreType.DMA((assemble_copies(parts),))],
+        compiler_params=pltpu.CompilerParams(vmem_limit_bytes=VMEM_LIMIT),
+        name="assemble",
+    )(place, *buffers)
+    return [item.reshape(item.shape[0], -1, item.shape[-1]) for item in full]
+
+
+def both_cores(own, other, core):
+    first = jnp.where(core == 0, own, other)
+    second = jnp.where(core == 0, other, own)
+    return jnp.stack([first, second])
+
+
+def gather_all(groups, pieces, place):
+    depth = grid_sizes()[0]
+    core = place[3]
+    packed = [pack(parts, items) for parts, items in zip(groups, pieces)]
+    halves = [half_rows(parts) for parts in groups]
+    kept = [lax.dynamic_slice_in_dim(rows, core * half, half) for rows, half in zip(packed, halves)]
+    sent = [
+        lax.dynamic_slice_in_dim(rows, (1 - core) * half, half) for rows, half in zip(packed, halves)
+    ]
+    got = hop(jnp.concatenate(sent), ACROSS)
+    held = []
+    offset = 0
+    for keep, half in zip(kept, halves):
+        held.append([both_cores(keep, got[offset : offset + half], core)])
+        offset += half
+    count = len(groups)
+    ready = {}
+    for tick in range(count + 3):
+        live = [index for index in range(tick - 3, tick + 1) if 0 <= index < count]
+        flat, tree = jax.tree.flatten([held[index] for index in live])
+        for index, items in zip(live, jax.tree.unflatten(tree, lax.optimization_barrier(flat))):
+            held[index] = items
+        for index in live:
+            items = held[index]
+            stage = tick - index
+            if stage == 0:
+                held[index] = items + [hop(items[0], ALONG_Z, step) for step in range(1, depth)]
+            elif stage == 1:
+                stacked = stack_z(items, place)
+                held[index] = [stacked, hop(stacked, NEAR)]
+            elif stage == 2:
+                held[index] = items + [hop(item, FAR) for item in items]
+            else:
+                held[index] = items + [hop(item, ACROSS) for item in items]
+    return held
+
+
+def deal_kernel(parts, place, *refs):
+    number = len(parts)
+    ins, outs, sems = (refs[:number], refs[number:-1], refs[-1])
+    to_core, to_far, to_near, own = outs
+    y, x = (place[1], place[2])
+    for core in (0, 1):
+
+        @pl.when(place[3] == core)
+        def _():
+            pairs = []
+            for other, far, near in itertools.product((0, 1), repeat=3):
+                half = core ^ other
+                step = [0, 0, 0, 0]
+                step[NEAR[half]], step[FAR[half]] = (near, far)
+                at_y, at_x = (lax.rem(y + step[1], 2), lax.rem(x + step[2], 2))
+                if other:
+                    target = to_core.at[far, near]
+                elif far:
+                    target = to_far.at[near]
+                else:
+                    target = to_near if near else own
+                for index, row, lane, rows, block, inner in half_moves(parts)[half]:
+                    pairs.append(
+                        (
+                            ins[index].at[block, :, at_y, at_x, :, pl.ds(inner, rows)],
+                            target.at[:, :, pl.ds(row, rows), pl.ds(lane, parts[index].lanes)],
+                        )
+                    )
+            copies(pairs, sems)
+
+
+def deal(parts, arrays, place):
+    depth = arrays[0].shape[1]
+    size = unit(parts, depth)
+    return pl.pallas_call(
+        functools.partial(deal_kernel, parts),
+        out_shape=[
+            jax.ShapeDtypeStruct(lead + size, jnp.bfloat16) for lead in ((2, 2), (2,), (), ())
+        ],
+        in_specs=in_smem() + in_vmem(len(parts)),
+        out_specs=hbm(4),
+        scratch_shapes=[pltpu.SemaphoreType.DMA((assemble_copies(parts),))],
+        compiler_params=pltpu.CompilerParams(vmem_limit_bytes=VMEM_LIMIT),
+        name="deal",
+    )(place, *arrays)
+
+
+def add_up(*terms):
+    total = terms[0].astype(jnp.float32)
+    for term in terms[1:]:
+        total = total + term.astype(jnp.float32)
+    return total
+
+
+def low_add(*terms):
+    return add_up(*terms).astype(jnp.bfloat16)
+
+
+def scatter(parts, arrays, place):
+    depth = grid_sizes()[0]
+    arrays = [array.reshape(part.full(depth)) for part, array in zip(parts, arrays)]
+    to_core, to_far, to_near, own = deal(parts, arrays, place)
+    z, core = (place[0], place[3])
+    from_core = hop(to_core, ACROSS)
+    from_far = hop(low_add(to_far, from_core[1]), FAR)
+    from_near = hop(low_add(to_near, from_core[0, 1], from_far[1]), NEAR)
+
+    def mine(at):
+        pick = [own, from_core[0, 0], from_far[0], from_near]
+        return [lax.dynamic_index_in_dim(item, at, 0, False) for item in pick]
+
+    along = [hop(low_add(*mine(lax.rem(z + step, depth))), ALONG_Z, step) for step in range(1, depth)]
+    total = add_up(*mine(z), *along)
+    keep = lax.dynamic_index_in_dim(total, core, 0, False)
+    other = hop(lax.dynamic_index_in_dim(total, 1 - core, 0, False), ACROSS)
+    rows = both_cores(keep, other, core).reshape(-1, WIDTH)
+    pieces = []
+    offset = 0
+    for part in parts:
+        pieces.append(part.unpack(rows[offset : offset + part.travel]))
+        offset += part.travel
+    return pieces
+
+
 FULL_PRECISION = lax.Precision.HIGHEST
 CQL_WEIGHT = 0.05
 BETA_ONE = 0.5
@@ -410,8 +766,7 @@
 GAMES = 4
 BLOCKS = 2
 STEP = 5
-AXES = ("wide", "narrow")
-SCORES = GAMES * ACTIONS * ATOMS
+PLAYS = ACTIONS * ATOMS
 
 
 def average_decay():
@@ -419,7 +774,7 @@
 
 
 def segment_lengths():
-    top = [PATCH_IN * D, D * PIX, D * DPROJ, DPROJ * SCORES]
+    top = [PATCH_IN * D, D * PIX, D * DPROJ, DPROJ * GAMES * PLAYS]
     block = [D * BOT, 9 * BOT * BOT, BOT * D, 2 * (2 * BOT + D)]
     return (top, block)
 
@@ -434,19 +789,67 @@
     return cuts
 
 
-def rows_of(flat, cuts, widths):
-    return [
-        flat[start : start + size].reshape(-1, width)
-        for (start, size), width in zip(cuts, widths)
-    ]
-
-
-def whole(rows):
-    return lax.all_gather(rows, AXES, axis=0, tiled=True)
-
-
-def own_sum(matrix):
-    return lax.psum_scatter(matrix, AXES, scatter_dimension=0, tiled=True)
+def pack_top(flat, cuts):
+    patch, pool, proj, heads = [flat[start : start + size] for start, size in cuts]
+    patch = patch.reshape(-1, 2, 2, WIDTH).transpose(2, 1, 0, 3).reshape(2, -1, WIDTH)
+    pool = jnp.pad(pool.reshape(1, -1, PIX), ((0, 0), (0, 0), (0, ROWS - PIX)))
+    heads = jnp.pad(heads.reshape(-1, GAMES, PLAYS), ((0, 0), (0, 0), (0, 2 * WIDTH - PLAYS)))
+    heads = heads.reshape(-1, 2 * GAMES, WIDTH).transpose(1, 0, 2)
+    return [patch, pool, proj.reshape(1, -1, WIDTH), heads]
+
+
+def flat_top(patch, pool, proj, heads):
+    patch = patch.reshape(2, 2, -1, WIDTH).transpose(2, 1, 0, 3)
+    heads = heads.transpose(1, 0, 2).reshape(-1, GAMES, 2 * WIDTH)[:, :, :PLAYS]
+    return jnp.concatenate(
+        [item.reshape(-1) for item in (patch, pool[:, :, :PIX], proj, heads)]
+    )
+
+
+def pack_block(flat, cuts):
+    w_in, w_mid, w_out = [flat[start : start + size] for start, size in cuts[:3]]
+    w_out = w_out.reshape(-1, D // BOT, BOT).transpose(1, 0, 2)
+    return [w_in.reshape(1, -1, BOT), w_mid.reshape(1, -1, BOT), w_out]
+
+
+def flat_block(w_in, w_mid, w_out, gains):
+    return jnp.concatenate(
+        [item.reshape(-1) for item in (w_in, w_mid, w_out.transpose(1, 0, 2), gains)]
+    )
+
+
+def parts_for(devices):
+    rows = {"patch": 2 * PATCH_IN, "pool": D, "proj": D, "heads": DPROJ}
+    rows |= {"w_in": D, "w_mid": TAPS * BOT, "w_out": BOT, "gains": TILE * devices}
+    blocks = {"patch": 2, "heads": 2 * GAMES, "w_out": D // BOT}
+    return {
+        name: Part(blocks.get(name, 1), count // devices, ROWS if name == "pool" else WIDTH)
+        for name, count in rows.items()
+    }
+
+
+def is_tuned(devices):
+    parts = parts_for(devices).values()
+    whole = all(part.rows // part.across % TILE == 0 for part in parts)
+    return whole and lax.axis_size("wide") == 8 and lax.axis_size("narrow") == 4
+
+
+def plain_gather(piece):
+    return lax.all_gather(piece, AXES, axis=1, tiled=True)
+
+
+def plain_scatter(array):
+    return lax.psum_scatter(array, AXES, scatter_dimension=1, tiled=True).astype(jnp.float32)
+
+
+def total(array):
+    if lax.axis_size("wide") != 8 or lax.axis_size("narrow") != 4:
+        return lax.psum(array, AXES)
+    array = array + hop(array, ACROSS)
+    array = array + hop(array, (2, 2))
+    array = array + hop(array, (1, 1))
+    one, two, three = [hop(array, ALONG_Z, step) for step in (1, 2, 3)]
+    return (array + two) + (one + three)
 
 
 def select(scores, game_hot):
@@ -454,7 +857,7 @@
     picked = jnp.einsum(
         "ng,ngk->nk",
         game_hot,
-        scores.reshape(count, GAMES, ACTIONS * ATOMS),
+        scores,
         precision=FULL_PRECISION,
     )
     return picked.reshape(count, ACTIONS, ATOMS)
@@ -492,7 +895,9 @@
     pooled = pooled.astype(jnp.bfloat16)
     before = dot(pooled, proj_w)
     hidden = jax.nn.silu(before).astype(jnp.bfloat16)
-    return (dot(hidden, heads_w), (low, pooled, before, hidden))
+    scores = jnp.einsum("nk,bkl->nbl", hidden, heads_w, preferred_element_type=jnp.float32)
+    scores = scores.reshape(-1, GAMES, 2 * WIDTH)[:, :, :PLAYS]
+    return (scores, (low, pooled, before, hidden))
 
 
 def lamb_parts(params, grads, first, second):
@@ -550,51 +955,86 @@
     top_lengths, block_lengths = segment_lengths()
     top_cuts = cut_points(top_lengths, devices)
     block_cuts = cut_points(block_lengths, devices)
-    top_widths = (D, PIX, DPROJ, SCORES)
-    block_widths = (BOT, BOT, D)
+    gain_start, gain_width = block_cuts[3]
+    parts = parts_for(devices)
+    tuned = is_tuned(devices)
+    place = spot()
     shift = shifts()
+    spread = spread_pixels(devices)
     weight_parts = jnp.concatenate(
         [squares(params_top, top_cuts), squares(params_blocks, block_cuts).reshape(-1)]
     )
-    weight_sq = lax.psum(weight_parts, AXES)
 
     game_hot = (game_ids[:, None] == jnp.arange(GAMES)[None, :]).astype(jnp.float32)
     taken_hot = (actions[:, 0:1] == jnp.arange(ACTIONS)[None, :]).astype(jnp.float32)
     next_hot = (actions[:, 1:2] == jnp.arange(ACTIONS)[None, :]).astype(jnp.float32)
 
-    low_top = params_top.astype(jnp.bfloat16)
     low_blocks = params_blocks.astype(jnp.bfloat16)
-    gain_start, gain_width = block_cuts[3]
+    own = {}
+    for net, top, blocks in (
+        ("target", target_top, target_blocks),
+        ("online", params_top.astype(jnp.bfloat16), low_blocks),
+    ):
+        for name, piece in zip(("patch", "pool", "proj", "heads"), pack_top(top, top_cuts)):
+            own[net, name] = piece
+        for index in range(BLOCKS):
+            for name, piece in zip(("w_in", "w_mid", "w_out"), pack_block(blocks[index], block_cuts)):
+                own[net, name, index] = piece
     gain_rows = jnp.concatenate([target_blocks, low_blocks])[:, gain_start:]
-    gains = lax.all_gather(gain_rows, AXES, axis=1, tiled=True).astype(jnp.float32)
-
-    def fetch_top(flat):
-        patch, pool, proj, heads = rows_of(flat, top_cuts, top_widths)
-        pool = jnp.pad(pool, ((0, 0), (0, ROWS - PIX)))
-        return (whole(patch), whole(pool), whole(proj), whole(heads))
-
-    def fetch_block(flat):
-        return [whole(rows) for rows in rows_of(flat, block_cuts[:3], block_widths)]
-
-    target_patch, target_pool, target_proj, target_heads = fetch_top(target_top)
-    stream = dot(frame_rows(following), target_patch)
+    own["gains",] = jnp.pad(
+        gain_rows, ((0, TILE - 2 * BLOCKS), (0, WIDTH - gain_width))
+    ).reshape(1, TILE, WIDTH)
+    block_names = ("w_in", "w_mid", "w_out")
+    keys = []
+    for net in ("target", "online"):
+        ends = [(net, name) for name in ("pool", "proj")]
+        if net == "target":
+            keys.append([("gains",)] + ends)
+        keys.append([(net, "patch")] + [(net, name, 0) for name in block_names])
+        for index in range(1, BLOCKS):
+            keys.append([(net, name, index) for name in block_names])
+        keys.append([(net, "heads")] + (ends if net == "online" else []))
+
+    def part_of(key):
+        return parts[key[0] if key[0] == "gains" else key[1]]
+
+    full = {}
+    if tuned:
+        groups = [[part_of(key) for key in group] for group in keys]
+        held = gather_all(groups, [[own[key] for key in group] for group in keys], place)
+        for group, kinds, buffers in zip(keys, groups, held):
+            full |= dict(zip(group, assemble(kinds, buffers, place)))
+    else:
+        for key, piece in own.items():
+            full[key] = plain_gather(piece)
+    gains = full["gains",].reshape(devices, TILE, WIDTH)[:, : 2 * BLOCKS, :gain_width]
+    gains = gains.transpose(1, 0, 2).reshape(2 * BLOCKS, -1).astype(jnp.float32)
+
+    def block_weights(net, index):
+        w_in, w_mid, w_out = [full[net, name, index] for name in block_names]
+        return (w_in[0], w_mid[0], w_out.reshape(D, BOT))
+
+    def top_weights(net):
+        return (full[net, "pool"][0], full[net, "proj"][0], full[net, "heads"])
+
+    stream = embed(frame_rows(following), spread, full["target", "patch"])
     for index in range(BLOCKS):
         stream = block_forward(
-            stream, *fetch_block(target_blocks[index]), gains[index : index + 1], shift, False
+            stream, *block_weights("target", index), gains[index : index + 1], shift, False
         )[0]
-    target_scores, ignored = head_scores(stream, target_pool, target_proj, target_heads)
+    target_scores, ignored = head_scores(stream, *top_weights("target"))
     target = target_dist(select(target_scores, game_hot), next_hot, rewards, discounts, done_flags)
 
-    patch_w, pool_w, proj_w, heads_w = fetch_top(low_top)
-    rows = frame_rows(observed)
-    stream = dot(rows, patch_w)
+    pixels = frame_rows(observed)
+    stream = embed(pixels, spread, full["online", "patch"])
     kept = []
     for index in range(BLOCKS):
-        weights = fetch_block(low_blocks[index])
+        weights = block_weights("online", index)
         gain = gains[BLOCKS + index : BLOCKS + index + 1]
         out, hid_one, hid_two, hid_three, rstd = block_forward(stream, *weights, gain, shift, True)
         kept.append((stream, hid_one, hid_two, hid_three, rstd, weights, gain))
         stream = out
+    pool_w, proj_w, heads_w = top_weights("online")
     scores, (low, pooled, before, hidden) = head_scores(stream, pool_w, proj_w, heads_w)
 
     def objective(scores_in):
@@ -602,38 +1042,63 @@
 
     loss_part, back_loss = jax.vjp(objective, scores)
     grad_scores = back_loss(jnp.float32(1.0 / frames_all))[0].astype(jnp.bfloat16)
-    grad_heads = dot_rows(hidden, grad_scores).astype(jnp.bfloat16)
-    grad_hidden = dot_lanes(grad_scores, heads_w)
+    grad_scores = jnp.pad(grad_scores, ((0, 0), (0, 0), (0, 2 * WIDTH - PLAYS)))
+    grad_scores = grad_scores.reshape(-1, 2 * GAMES, WIDTH)
+    grads = {}
+    grads["heads",] = jnp.einsum(
+        "nk,nbl->bkl", hidden, grad_scores, preferred_element_type=jnp.float32
+    ).astype(jnp.bfloat16)
+    grad_hidden = jnp.einsum(
+        "nbl,bkl->nk", grad_scores, heads_w, preferred_element_type=jnp.float32
+    )
     grad_before = jax.vjp(jax.nn.silu, before)[1](grad_hidden)[0].astype(jnp.bfloat16)
-    grad_proj = dot_rows(pooled, grad_before).astype(jnp.bfloat16)
+    grads["proj",] = dot_rows(pooled, grad_before).astype(jnp.bfloat16)[None]
     grad_pooled = dot_lanes(grad_before, proj_w).astype(jnp.bfloat16)
-    grad_pool = jnp.einsum(
+    grads["pool",] = jnp.einsum(
         "npc,nc->cp", low, grad_pooled, preferred_element_type=jnp.float32
-    ).astype(jnp.bfloat16)
+    ).astype(jnp.bfloat16)[None]
     grad_stream = jnp.einsum(
         "nc,cp->npc", grad_pooled, pool_w, preferred_element_type=jnp.float32
     ).reshape(-1, D)
 
-    grad_blocks = [None] * BLOCKS
+    dgains = [None] * BLOCKS
     for index in reversed(range(BLOCKS)):
         stream, hid_one, hid_two, hid_three, rstd, weights, gain = kept[index]
         w_in, w_mid, w_out = weights
-        dres, dsecond, dw_out, dgains_late = back_out(
+        dres, dsecond, dw_out, late = back_out(
             grad_stream, stream, hid_two, hid_three, rstd, w_out, gain
         )
-        dfirst, dw_mid, dgains_early = back_mid(dsecond, hid_one, rstd, w_mid, gain, shift)
+        dfirst, dw_mid, early = back_mid(dsecond, hid_one, rstd, w_mid, gain, shift)
         dw_in, grad_stream = back_in(dfirst, stream, dres, w_in)
-        dgains = jnp.concatenate([dgains_early, dgains_late], axis=1).reshape(devices, -1)
-        parts = [own_sum(part).astype(jnp.float32) for part in (dw_in, dw_mid, dw_out, dgains)]
-        grad_blocks[index] = jnp.concatenate([part.reshape(-1) for part in parts])
-    grad_patch = dot_rows(rows, grad_stream.astype(jnp.bfloat16)).astype(jnp.bfloat16)
-    grad_blocks = jnp.stack(grad_blocks)
-    parts = [
-        own_sum(part).astype(jnp.float32)
-        for part in (grad_patch, grad_pool, grad_proj, grad_heads)
-    ]
-    parts[1] = parts[1][:, :PIX]
-    grad_top = jnp.concatenate([part.reshape(-1) for part in parts])
+        dgains[index] = jnp.concatenate([early, late], axis=1)
+        grads["w_in", index] = dw_in[None]
+        grads["w_mid", index] = dw_mid[None]
+        grads["w_out", index] = dw_out.reshape(D // BOT, BOT, BOT)
+    grads["patch",] = embed_back(pixels, spread, grad_stream)
+    dgains = jnp.concatenate(dgains).reshape(BLOCKS, devices, gain_width).transpose(1, 0, 2)
+    dgains = jnp.pad(dgains, ((0, 0), (0, TILE - BLOCKS), (0, WIDTH - gain_width)))
+    grads["gains",] = dgains.reshape(1, -1, WIDTH).astype(jnp.bfloat16)
+
+    keys = [[("heads",), ("proj",)], [("w_out", BLOCKS - 1), ("pool",)]]
+    for index in reversed(range(BLOCKS)):
+        keys.append([("w_mid", index)])
+        keys.append([("w_in", index)])
+        keys[-1] += [("w_out", index - 1)] if index else [("patch",), ("gains",)]
+    mine = {}
+    for group in keys:
+        arrays = [grads[key] for key in group]
+        if tuned:
+            sums = scatter([parts[key[0]] for key in group], arrays, place)
+        else:
+            sums = [plain_scatter(array) for array in arrays]
+        mine |= dict(zip(group, sums))
+    grad_top = flat_top(*[mine[name,] for name in ("patch", "pool", "proj", "heads")])
+    grad_blocks = jnp.stack(
+        [
+            flat_block(*[mine[name, index] for name in block_names], mine["gains",][0, index, :gain_width])
+            for index in range(BLOCKS)
+        ]
+    )
 
     momentum_top, variance_top, direction_top = lamb_parts(
         params_top, grad_top, first_top, second_top
@@ -644,7 +1109,9 @@
     update_parts = jnp.concatenate(
         [squares(direction_top, top_cuts), squares(direction_blocks, block_cuts).reshape(-1)]
     )
-    update_sq, loss_total = lax.psum((update_parts, loss_part), AXES)
+    sums = total(jnp.concatenate([weight_parts, update_parts, loss_part[None]])[None])[0]
+    count = weight_parts.shape[0]
+    weight_sq, update_sq, loss_total = (sums[:count], sums[count : 2 * count], sums[2 * count])
     weight_norm = jnp.sqrt(weight_sq)
     update_norm = jnp.sqrt(update_sq)
     ratio = weight_norm / (update_norm + 1e-06)

time: 2500 us -> 850 us (0.34)
  waiting for transfers between devices: 1980 us -> 219 us
  blocking collectives: 202 us -> 0 us
  starting transfers between devices: 1.15 us -> 150 us
  Pallas kernels: 144 us -> 256 us
  other arithmetic: 50.3 us -> 91.4 us
  local copies, waits for them, and re-layouts: 60.5 us -> 94 us
    reduce_scatter x10 -> x0, waiting for transfers between devices: 1150 us -> none  [own_sum(): return lax.psum_scatter(matrix, AXES, scatter_dimension=0, tiled=True)]
    all_gather x18 -> x0, waiting for transfers between devices: 824 us -> none  [whole(): return lax.all_gather(rows, AXES, axis=0, tiled=True)]
    ppermute x0 -> x119, waiting for transfers between devices: none -> 219 us  [hop(): return lax.ppermute(array, AXES, pairs)]
    ppermute x0 -> x119, starting transfers between devices: none -> 150 us  [hop(): return lax.ppermute(array, AXES, pairs)]
    all_gather x3 -> x0, blocking collectives: 124 us -> none  [the longest x2 87.5 us: whole(): return lax.all_gather(rows, AXES, axis=0, tiled=True)]
    pallas_call x0 -> x23, Pallas kernels: none -> 112 us  [the longest x7 50.9 us: assemble(): pl.pallas_call(functools.partial(assemble_kernel, parts), out_shape=[jax....]
    unnamed x1 -> x0, blocking collectives: 39.9 us -> none
    psum x1 -> x0, blocking collectives: 37.3 us -> none  [on_device(): update_sq, loss_total = lax.psum((update_parts, loss_part), AXES)]
  transfers between devices with their start and end apart: 28 -> 119, of which waited for: 26 -> 47; matrix products, arithmetic and copies ran while one was open for 4% -> 14% of each run, Pallas kernels for 6% -> 27%
where the time goes in v2:
time: 850 us; the launch traced here: 840 us
  Pallas kernels  256 us (30%)
  waiting for transfers between devices  219 us (26%)
  starting transfers between devices  150 us (18%)
  local copies, waits for them, and re-layouts  94 us (11%)
  other arithmetic  91.4 us (11%)
  matrix products  25.3 us (3%)
    ppermute x119, waiting for transfers between devices, hop(): return lax.ppermute(array, AXES, pairs)  219 us
    ppermute x119, starting transfers between devices, hop(): return lax.ppermute(array, AXES, pairs)  150 us
    pallas_call x4, Pallas kernels, block_forward(): pl.pallas_call(functools.partial(forward_kernel, count, keep), out_shape=...  76.9 us
    pallas_call x7, Pallas kernels, assemble(): pl.pallas_call(functools.partial(assemble_kernel, parts), out_shape=[jax....  50.9 us
    convert_element_type x18, other arithmetic, low_add(): return add_up(*terms).astype(jnp.bfloat16)  27.8 us
    pallas_call x6, Pallas kernels, deal(): pl.pallas_call(functools.partial(deal_kernel, parts), out_shape=[jax.Shap...  27 us
    pallas_call x2, Pallas kernels, back_out(): pl.pallas_call(functools.partial(back_out_kernel, count), out_shape=[f32(...  26.7 us
    pallas_call x2, Pallas kernels, back_mid(): pl.pallas_call(functools.partial(back_mid_kernel, count), out_shape=[bf16...  23.6 us
  transfers between devices with their start and end apart: 119, of which 47 were waited for; matrix products, arithmetic and copies ran while one was open for 14% of the time, Pallas kernels for 27%

profile of v2, /device:TPU:0, one launch (start us, length us, event | category | flops | bytes accessed | tf_op | source)
XLA Modules:
  0.0 839.7 jit_solution(14487912837409709013)
XLA Ops:
  43.0 7.3 collective-permute-done.5.refs_1_
  50.3 12.7 %collective-permute-done.6.refs_2_ = bf16[2,160,512]{2,1,0:T(8,128)(2,1)S(1)} collective-permute-done((bf16[2,160,512]{2,1,0:T(8,128)(2,1)S(1)}, bf16[2,160,512]{2,1,0:T(8,128)(2,1)S(1)}, u32[]{:S(2)}, u32[]{:S(2)}) %collective-permute-start.6) | collective-permute-done | bytes 327712 | tf_op jit(solution)/shard_map/ppermute | solution.py:475
  69.1 6.8 collective-permute-start.11
  79.5 5.3 collective-permute-done.11.refs_1_
  85.7 8.8 %collective-permute-done.12.refs_2_ = bf16[2,144,512]{2,1,0:T(8,128)(2,1)S(1)} collective-permute-done((bf16[2,144,512]{2,1,0:T(8,128)(2,1)S(1)}, bf16[2,144,512]{2,1,0:T(8,128)(2,1)S(1)}, u32[]{:S(2)}, u32[]{:S(2)}) %collective-permute-start.12) | collective-permute-done | bytes 294944 | tf_op jit(solution)/shard_map/ppermute | solution.py:475
  94.5 6.0 collective-permute-done.13.refs_3_
  120.1 14.9 %collective-permute-done.16.refs_1_ = bf16[4,2,144,512]{3,2,1,0:T(8,128)(2,1)} collective-permute-done((bf16[4,2,144,512]{3,2,1,0:T(8,128)(2,1)}, bf16[4,2,144,512]{3,2,1,0:T(8,128)(2,1)}, u32[]{:S(2)}, u32[]{:S(2)}) %collective-permute-start.16) | collective-permute-done | bytes 1179680 | tf_op jit(solution)/shard_map/ppermute | solution.py:475
  135.0 10.3 %collective-permute-done.15.refs_3_ = bf16[4,2,160,512]{3,2,1,0:T(8,128)(2,1)} collective-permute-done((bf16[4,2,160,512]{3,2,1,0:T(8,128)(2,1)S(1)}, bf16[4,2,160,512]{3,2,1,0:T(8,128)(2,1)}, u32[]{:S(2)}, u32[]{:S(2)}) %collective-permute-start.15) | collective-permute-done | bytes 1310752 | tf_op jit(solution)/shard_map/ppermute | solution.py:475
  161.2 9.7 %collective-permute-done.24.refs_2_ = bf16[2,160,512]{2,1,0:T(8,128)(2,1)S(1)} collective-permute-done((bf16[2,160,512]{2,1,0:T(8,128)(2,1)S(1)}, bf16[2,160,512]{2,1,0:T(8,128)(2,1)S(1)}, u32[]{:S(2)}, u32[]{:S(2)}) %collective-permute-start.24) | collective-permute-done | bytes 327712 | tf_op jit(solution)/shard_map/ppermute | solution.py:475
  173.4 4.9 collective-permute-done.25.refs_3_
  196.7 11.9 %collective-permute-done.30.refs_2_ = bf16[2,144,512]{2,1,0:T(8,128)(2,1)S(1)} collective-permute-done((bf16[2,144,512]{2,1,0:T(8,128)(2,1)}, bf16[2,144,512]{2,1,0:T(8,128)(2,1)S(1)}, u32[]{:S(2)}, u32[]{:S(2)}) %collective-permute-start.30) | collective-permute-done | bytes 294944 | tf_op jit(solution)/shard_map/ppermute | solution.py:475
  211.0 7.1 collective-permute-done.27.refs_3_
  226.0 4.9 collective-permute-start.35
  235.0 5.4 collective-permute-done.35.refs_1_
  241.8 7.0 collective-permute-done.36.refs_2_
  256.1 11.1 %collective-permute-done.33.refs_3_ = bf16[4,2,160,512]{3,2,1,0:T(8,128)(2,1)S(1)} collective-permute-done((bf16[4,2,160,512]{3,2,1,0:T(8,128)(2,1)}, bf16[4,2,160,512]{3,2,1,0:T(8,128)(2,1)S(1)}, u32[]{:S(2)}, u32[]{:S(2)}) %collective-permute-start.33) | collective-permute-done | bytes 1310752 | tf_op jit(solution)/shard_map/ppermute | solution.py:475
  288.1 10.0 %collective-permute-done.40.refs_1_ = bf16[4,2,112,512]{3,2,1,0:T(8,128)(2,1)S(1)} collective-permute-done((bf16[4,2,112,512]{3,2,1,0:T(8,128)(2,1)}, bf16[4,2,112,512]{3,2,1,0:T(8,128)(2,1)S(1)}, u32[]{:S(2)}, u32[]{:S(2)}) %collective-permute-start.40) | collective-permute-done | bytes 917536 | tf_op jit(solution)/shard_map/ppermute | solution.py:475
  298.6 8.6 %collective-permute-done.39.refs_3_ = bf16[4,2,144,512]{3,2,1,0:T(8,128)(2,1)} collective-permute-done((bf16[4,2,144,512]{3,2,1,0:T(8,128)(2,1)}, bf16[4,2,144,512]{3,2,1,0:T(8,128)(2,1)}, u32[]{:S(2)}, u32[]{:S(2)}) %collective-permute-start.39) | collective-permute-done | bytes 1179680 | tf_op jit(solution)/shard_map/ppermute | solution.py:475
  310.0 8.8 %assemble.9 = (bf16[2,4,2,2,2,16,512]{6,5,4,3,2,1,0:T(8,128)(2,1)}, bf16[1,4,2,2,2,64,512]{6,5,4,3,2,1,0:T(8,128)(2,1)}, bf16[1,4,2,2,2,144,512]{6,5,4,3,2,1,0:T(8,128)(2,1)}, bf16[4,4,2,2,2,16,512]{6,5,4,3,2,1,0:T(8,128)(2,1)}) custom-call(s32[4]{0:T(128)} %pad_add_fusion.place, bf16[4,2,160,512]{3,2,1,0:T(8,128)(2,1)} %stack_z.8.refs_0_, ...), custom_call_target="tpu_custom_call" | custom-call | tf_op jit(solution)/shard_map/assemble/pallas_call | solution.py:617
  324.7 18.4 %block_forward.4.refs_0_ = f32[384,2048]{1,0:T(8,128)} custom-call(f32[384,2048]{1,0:T(8,128)} %embed.2.refs_0_, bf16[2048,512]{1,0:T(8,128)(2,1)} %bitcast.730, bf16[4608,512]{1,0:T(8,128)(2,1)} %bitcast.725, bf16[2048,512]{1,0:T(8,128)(2,1)} %bitcast.731, f32[1,6144]{1,0:T(1,128)} %slice.464.refs_4_, bf16[1152,128]{1,0:T(8,128)(2,1)} %convert_element_type.987.refs_5_), custom_call_target="tpu_custom_call" | custom-call | flops 3422552064 | bytes 20000000 | tf_op jit(solution)/shard_map/block_forward/pallas_call | solution.py:189
  343.1 8.2 assemble.10
  351.3 18.5 %block_forward.5 = f32[384,2048]{1,0:T(8,128)} custom-call(f32[384,2048]{1,0:T(8,128)} %block_forward.4.refs_0_, bf16[2048,512]{1,0:T(8,128)(2,1)} %bitcast.732, bf16[4608,512]{1,0:T(8,128)(2,1)} %bitcast.726, bf16[2048,512]{1,0:T(8,128)(2,1)} %bitcast.733, f32[1,6144]{1,0:T(1,128)} %slice.466.refs_4_, bf16[1152,128]{1,0:T(8,128)(2,1)} %convert_element_type.987.refs_5_), custom_call_target="tpu_custom_call" | custom-call | flops 3422552064 | bytes 20000000 | tf_op jit(solution)/shard_map/block_forward/pallas_call | solution.py:189
  375.6 5.0 fusion.20
  380.6 5.3 assemble.11
  385.9 6.6 copy.97
  401.3 9.0 %assemble.12 = (bf16[2,4,2,2,2,16,512]{6,5,4,3,2,1,0:T(8,128)(2,1)}, bf16[1,4,2,2,2,64,512]{6,5,4,3,2,1,0:T(8,128)(2,1)}, bf16[1,4,2,2,2,144,512]{6,5,4,3,2,1,0:...) custom-call(s32[4]{0:T(128)} %pad_add_fusion.place, bf16[4,2,160,512]{3,2,1,0:T(8,128)(2,1)} %stack_z.11.refs_0_, ...), custom_call_target="tpu_custom_call" | custom-call | tf_op jit(solution)/shard_map/assemble/pallas_call | solution.py:617
  414.7 20.2 %block_forward.6 = (f32[384,2048]{1,0:T(8,128)}, f32[384,512]{1,0:T(8,128)}, f32[384,512]{1,0:T(8,128)}, f32[384,2048]{1,0:T(8,128)}, f32[8,3072]{1,0:T(8,128)}) custom-call(f32[384,2048]{1,0:T(8,128)} %embed.3.refs_0_.refs_1_, bf16[2048,512]{1,0:T(8,128)(2,1)} %bitcast.741, bf16[4608,512]{1,0:T(8,128)(2,1)} %bitcast.815, bf16[2048,512]{1,0:T(8,128)(2,1)} %bitcast.743, ...), custom_call_target="tpu_custom_call" | custom-call | flops 3422552064 | bytes 20000000 | tf_op jit(solution)/shard_map/block_forward/pallas_call | solution.py:189
  434.9 7.8 assemble.13
  442.7 19.9 %block_forward.7 = (f32[384,2048]{1,0:T(8,128)}, f32[384,512]{1,0:T(8,128)}, f32[384,512]{1,0:T(8,128)}, f32[384,2048]{1,0:T(8,128)}, f32[8,3072]{1,0:T(8,128)}) custom-call(f32[384,2048]{1,0:T(8,128)} %get-tuple-element.248.refs_0_.refs_1_, bf16[2048,512]{1,0:T(8,128)(2,1)} %bitcast.745, bf16[4608,512]{1,0:T(8,128)(2,1)} %bitcast.817, ...), custom_call_target="tpu_custom_call" | custom-call | flops 3422552064 | bytes 20000000 | tf_op jit(solution)/shard_map/block_forward/pallas_call | solution.py:189
  467.3 7.3 assemble.7
  474.6 6.5 copy.98
  504.1 13.4 %back_out.2 = (f32[384,2048]{1,0:T(8,128)}, bf16[384,512]{1,0:T(8,128)(2,1)}, bf16[2048,512]{1,0:T(8,128)(2,1)}, f32[1,5120]{1,0:T(1,128)}) custom-call(f32[384,2048]{1,0:T(8,128)} %bitcast.718, f32[384,2048]{1,0:T(8,128)} %get-tuple-element.248.refs_0_.refs_1_, f32[384,512]{1,0:T(8,128)} %get-tuple-element.259.refs_2_, ...), custom_call_target="tpu_custom_call" | custom-call | flops 1610612736 | bytes 20000000 | tf_op jit(solution)/shard_map/back_out/pallas_call | solution.py:286
  521.4 12.1 %back_mid.2 = (bf16[384,512]{1,0:T(8,128)(2,1)}, bf16[4608,512]{1,0:T(8,128)(2,1)}, f32[1,1024]{1,0:T(1,128)}) custom-call(bf16[384,512]{1,0:T(8,128)(2,1)} %get-tuple-element.262.refs_0_, f32[384,512]{1,0:T(8,128)} %get-tuple-element.263.refs_1_, f32[8,3072]{1,0:T(8,128)} %get-tuple-element.261.refs_4_.refs_2_, bf16[4608,512]{1,0:T(8,128)(2,1)} %bitcast.818, ...), custom_call_target="tpu_custom_call" | custom-call | flops 3623878656 | bytes 12000000 | tf_op jit(solution)/shard_map/back_mid/pallas_call | solution.py:348
  533.4 8.3 back_in.2
  541.7 13.3 %back_out.3 = (f32[384,2048]{1,0:T(8,128)}, bf16[384,512]{1,0:T(8,128)(2,1)}, bf16[2048,512]{1,0:T(8,128)(2,1)}, f32[1,5120]{1,0:T(1,128)}) custom-call(f32[384,2048]{1,0:T(8,128)} %get-tuple-element.266.refs_0_, f32[384,2048]{1,0:T(8,128)} %embed.3.refs_0_.refs_1_, f32[384,512]{1,0:T(8,128)} %get-tuple-element.267.refs_2_, ...), custom_call_target="tpu_custom_call" | custom-call | flops 1610612736 | bytes 20000000 | tf_op jit(solution)/shard_map/back_out/pallas_call | solution.py:286
  555.1 11.6 %back_mid.3 = (bf16[384,512]{1,0:T(8,128)(2,1)}, bf16[4608,512]{1,0:T(8,128)(2,1)}, f32[1,1024]{1,0:T(1,128)}) custom-call(bf16[384,512]{1,0:T(8,128)(2,1)} %get-tuple-element.270.refs_0_, f32[384,512]{1,0:T(8,128)} %get-tuple-element.271.refs_1_, f32[8,3072]{1,0:T(8,128)} %get-tuple-element.269.refs_4_.refs_2_, bf16[4608,512]{1,0:T(8,128)(2,1)} %bitcast.816, ...), custom_call_target="tpu_custom_call" | custom-call | flops 3623878656 | bytes 12000000 | tf_op jit(solution)/shard_map/back_mid/pallas_call | solution.py:348
  577.6 8.5 %back_in.3 = (bf16[2048,512]{1,0:T(8,128)(2,1)}, f32[384,2048]{1,0:T(8,128)}) custom-call(bf16[384,512]{1,0:T(8,128)(2,1)} %get-tuple-element.272.refs_0_, f32[384,2048]{1,0:T(8,128)} %embed.3.refs_0_.refs_1_, f32[384,2048]{1,0:T(8,128)} %get-tuple-element.273.refs_2_, bf16[2048,512]{1,0:T(8,128)(2,1)} %bitcast.742), custom_call_target="tpu_custom_call" | custom-call | flops 1610612736 | bytes 15000000 | tf_op jit(solution)/shard_map/back_in/pallas_call | solution.py:383
  611.0 6.0 deal.8
  627.5 5.9 collective-permute-start.81
  679.8 7.5 collective-permute-start.104
  712.7 9.0 %collective-permute-done.94 = bf16[4,2,80,512]{3,2,1,0:T(8,128)(2,1)S(1)} collective-permute-done((bf16[4,2,80,512]{3,2,1,0:T(8,128)(2,1)S(1)}, bf16[4,2,80,512]{3,2,1,0:T(8,128)(2,1)S(1)}, u32[]{:S(2)}, u32[]{:S(2)}) %collective-permute-start.94) | collective-permute-done | bytes 655392 | tf_op jit(solution)/shard_map/ppermute | solution.py:475
  738.1 6.8 collective-permute-start.98
  744.9 5.4 collective-permute-done.110
  758.0 5.4 multiply_add_fusion.2
  773.4 7.5 collective-permute-done.89
  783.4 5.5 concatenate.69
  794.3 5.9 concatenate.72
  821.9 7.6 multiply_add_fusion.1
  (734 shorter events, 402.3 us)
Async XLA Ops:
  36.2 28.3 %collective-permute-start.4 = (bf16[4,2,48,512]{3,2,1,0:T(8,128)(2,1)}, bf16[4,2,48,512]{3,2,1,0:T(8,128)(2,1)}, u32[]{:S(2)}, u32[]{:S(2)}) collective-permute-start(bf16[4,2,48,512]{3,2,1,0:T(8,128)(2,1)} %stack_z.7.refs_0_), channel_id=1, source_target_pairs={{0,2},{1,5},{2,0},{3,7},{4,6},{5,1},{6,4},{7,3},{8,10},{9,13},{10,... | collective-permute-start | bytes 1179656 | tf_op jit(solution)/shard_map/ppermute | solution.py:475
  39.7 23.3 %collective-permute-start.6 = (bf16[2,160,512]{2,1,0:T(8,128)(2,1)S(1)}, bf16[2,160,512]{2,1,0:T(8,128)(2,1)S(1)}, u32[]{:S(2)}, u32[]{:S(2)}) collective-permute-start(bf16[2,160,512]{2,1,0:T(8,128)(2,1)S(1)} %pad_maximum_fusion.4.refs_0_), channel_id=1, source_target_pairs={{0,16},{1,17},{2,18},{3,19},{4,20},{5,21},{6,22},{7,23},{8,24},{9,... | collective-permute-start | bytes 983048 | tf_op jit(solution)/shard_map/ppermute | solution.py:475
  67.6 33.0 %collective-permute-start.10 = (bf16[4,2,160,512]{3,2,1,0:T(8,128)(2,1)}, bf16[4,2,160,512]{3,2,1,0:T(8,128)(2,1)S(1)}, u32[]{:S(2)}, u32[]{:S(2)}) collective-permute-start(bf16[4,2,160,512]{3,2,1,0:T(8,128)(2,1)} %stack_z.8.refs_0_), channel_id=1, source_target_pairs={{0,2},{1,5},{2,0},{3,7},{4,6},{5,1},{6,4},{7,3},{8,10},{9,13},{10,... | collective-permute-start | bytes 3932168 | tf_op jit(solution)/shard_map/ppermute | solution.py:475
  75.9 24.7 %collective-permute-start.8 = (bf16[4,2,48,512]{3,2,1,0:T(8,128)(2,1)S(1)}, bf16[4,2,48,512]{3,2,1,0:T(8,128)(2,1)}, u32[]{:S(2)}, u32[]{:S(2)}) collective-permute-start(bf16[4,2,48,512]{3,2,1,0:T(8,128)(2,1)S(1)} %copy-done.22), channel_id=1, source_target_pairs={{0,4},{1,3},{2,6},{3,1},{4,0},{5,7},{6,2},{7,5},{8,12},{9,11},{10,... | collective-permute-start | bytes 1179656 | tf_op jit(solution)/shard_map/ppermute | solution.py:475
  76.4 24.2 %collective-permute-start.9 = (bf16[4,2,48,512]{3,2,1,0:T(8,128)(2,1)}, bf16[4,2,48,512]{3,2,1,0:T(8,128)(2,1)}, u32[]{:S(2)}, u32[]{:S(2)}) collective-permute-start(bf16[4,2,48,512]{3,2,1,0:T(8,128)(2,1)} %collective-permute-done.4.refs_1_), channel_id=1, source_target_pairs={{0,4},{1,3},{2,6},{3,1},{4,0},{5,7},{6,2},{7,5},{8,12},{9,11},{10,... | collective-permute-start | bytes 1179656 | tf_op jit(solution)/shard_map/ppermute | solution.py:475
  100.6 34.3 %collective-permute-start.14 = (bf16[4,2,160,512]{3,2,1,0:T(8,128)(2,1)}, bf16[4,2,160,512]{3,2,1,0:T(8,128)(2,1)}, u32[]{:S(2)}, u32[]{:S(2)}) collective-permute-start(bf16[4,2,160,512]{3,2,1,0:T(8,128)(2,1)} %stack_z.8.refs_0_), channel_id=1, source_target_pairs={{0,4},{1,3},{2,6},{3,1},{4,0},{5,7},{6,2},{7,5},{8,12},{9,11},{10,... | collective-permute-start | bytes 3932168 | tf_op jit(solution)/shard_map/ppermute | solution.py:475
  101.3 44.0 %collective-permute-start.15 = (bf16[4,2,160,512]{3,2,1,0:T(8,128)(2,1)S(1)}, bf16[4,2,160,512]{3,2,1,0:T(8,128)(2,1)}, u32[]{:S(2)}, u32[]{:S(2)}) collective-permute-start(bf16[4,2,160,512]{3,2,1,0:T(8,128)(2,1)S(1)} %collective-permute-done.10.refs_1_), channel_id=1, source_target_pairs={{0,4},{1,3},{2,6},{3,1},{4,0},{5,7},{6,2},{7,5},{8,12},{9,11},{10,... | collective-permute-start | bytes 3932168 | tf_op jit(solution)/shard_map/ppermute | solution.py:475
  105.7 29.3 %collective-permute-start.16 = (bf16[4,2,144,512]{3,2,1,0:T(8,128)(2,1)}, bf16[4,2,144,512]{3,2,1,0:T(8,128)(2,1)}, u32[]{:S(2)}, u32[]{:S(2)}) collective-permute-start(bf16[4,2,144,512]{3,2,1,0:T(8,128)(2,1)} %stack_z.9.refs_0_), channel_id=1, source_target_pairs={{0,2},{1,5},{2,0},{3,7},{4,6},{5,1},{6,4},{7,3},{8,10},{9,13},{10,... | collective-permute-start | bytes 3538952 | tf_op jit(solution)/shard_map/ppermute | solution.py:475
  145.3 33.8 %collective-permute-start.20 = (bf16[4,2,144,512]{3,2,1,0:T(8,128)(2,1)}, bf16[4,2,144,512]{3,2,1,0:T(8,128)(2,1)}, u32[]{:S(2)}, u32[]{:S(2)}) collective-permute-start(bf16[4,2,144,512]{3,2,1,0:T(8,128)(2,1)} %stack_z.9.refs_0_), channel_id=1, source_target_pairs={{0,4},{1,3},{2,6},{3,1},{4,0},{5,7},{6,2},{7,5},{8,12},{9,11},{10,... | collective-permute-start | bytes 3538952 | tf_op jit(solution)/shard_map/ppermute | solution.py:475
  145.3 34.8 %collective-permute-start.21 = (bf16[4,2,144,512]{3,2,1,0:T(8,128)(2,1)}, bf16[4,2,144,512]{3,2,1,0:T(8,128)(2,1)}, u32[]{:S(2)}, u32[]{:S(2)}) collective-permute-start(bf16[4,2,144,512]{3,2,1,0:T(8,128)(2,1)} %collective-permute-done.16.refs_1_), channel_id=1, source_target_pairs={{0,4},{1,3},{2,6},{3,1},{4,0},{5,7},{6,2},{7,5},{8,12},{9,11},{10,... | collective-permute-start | bytes 3538952 | tf_op jit(solution)/shard_map/ppermute | solution.py:475
  155.1 24.0 %collective-permute-start.22 = (bf16[4,2,64,512]{3,2,1,0:T(8,128)(2,1)}, bf16[4,2,64,512]{3,2,1,0:T(8,128)(2,1)}, u32[]{:S(2)}, u32[]{:S(2)}) collective-permute-start(bf16[4,2,64,512]{3,2,1,0:T(8,128)(2,1)} %stack_z.10.refs_0_), channel_id=1, source_target_pairs={{0,2},{1,5},{2,0},{3,7},{4,6},{5,1},{6,4},{7,3},{8,10},{9,13},{10,... | collective-permute-start | bytes 1572872 | tf_op jit(solution)/shard_map/ppermute | solution.py:475
  183.1 35.7 %collective-permute-start.28 = (bf16[4,2,160,512]{3,2,1,0:T(8,128)(2,1)}, bf16[4,2,160,512]{3,2,1,0:T(8,128)(2,1)}, u32[]{:S(2)}, u32[]{:S(2)}) collective-permute-start(bf16[4,2,160,512]{3,2,1,0:T(8,128)(2,1)} %stack_z.11.refs_0_), channel_id=1, source_target_pairs={{0,2},{1,5},{2,0},{3,7},{4,6},{5,1},{6,4},{7,3},{8,10},{9,13},{10,... | collective-permute-start | bytes 3932168 | tf_op jit(solution)/shard_map/ppermute | solution.py:475
  196.7 29.3 %collective-permute-start.51 = (bf16[4,2,160,512]{3,2,1,0:T(8,128)(2,1)S(1)}, bf16[4,2,160,512]{3,2,1,0:T(8,128)(2,1)}, u32[]{:S(2)}, u32[]{:S(2)}) collective-permute-start(bf16[4,2,160,512]{3,2,1,0:T(8,128)(2,1)S(1)} %copy-done.5), channel_id=1, source_target_pairs={{0,1},{1,0},{2,3},{3,2},{4,5},{5,4},{6,7},{7,6},{8,9},{9,8},{10,11... | collective-permute-start | bytes 3932168 | tf_op jit(solution)/shard_map/ppermute | solution.py:475
  209.9 21.8 %collective-permute-start.52 = (bf16[4,2,160,512]{3,2,1,0:T(8,128)(2,1)}, bf16[4,2,160,512]{3,2,1,0:T(8,128)(2,1)}, u32[]{:S(2)}, u32[]{:S(2)}) collective-permute-start(bf16[4,2,160,512]{3,2,1,0:T(8,128)(2,1)} %copy-done.27), channel_id=1, source_target_pairs={{0,1},{1,0},{2,3},{3,2},{4,5},{5,4},{6,7},{7,6},{8,9},{9,8},{10,11... | collective-permute-start | bytes 3932168 | tf_op jit(solution)/shard_map/ppermute | solution.py:475
  210.7 24.2 %collective-permute-start.53 = (bf16[4,2,160,512]{3,2,1,0:T(8,128)(2,1)}, bf16[4,2,160,512]{3,2,1,0:T(8,128)(2,1)}, u32[]{:S(2)}, u32[]{:S(2)}) collective-permute-start(bf16[4,2,160,512]{3,2,1,0:T(8,128)(2,1)} %collective-permute-done.14.refs_2_), channel_id=1, source_target_pairs={{0,1},{1,0},{2,3},{3,2},{4,5},{5,4},{6,7},{7,6},{8,9},{9,8},{10,11... | collective-permute-start | bytes 3932168 | tf_op jit(solution)/shard_map/ppermute | solution.py:475
  223.6 29.2 %collective-permute-start.34 = (bf16[4,2,144,512]{3,2,1,0:T(8,128)(2,1)}, bf16[4,2,144,512]{3,2,1,0:T(8,128)(2,1)}, u32[]{:S(2)}, u32[]{:S(2)}) collective-permute-start(bf16[4,2,144,512]{3,2,1,0:T(8,128)(2,1)} %stack_z.12.refs_0_), channel_id=1, source_target_pairs={{0,2},{1,5},{2,0},{3,7},{4,6},{5,1},{6,4},{7,3},{8,10},{9,13},{10,... | collective-permute-start | bytes 3538952 | tf_op jit(solution)/shard_map/ppermute | solution.py:475
  225.4 28.7 %collective-permute-start.32 = (bf16[4,2,160,512]{3,2,1,0:T(8,128)(2,1)}, bf16[4,2,160,512]{3,2,1,0:T(8,128)(2,1)}, u32[]{:S(2)}, u32[]{:S(2)}) collective-permute-start(bf16[4,2,160,512]{3,2,1,0:T(8,128)(2,1)} %stack_z.11.refs_0_), channel_id=1, source_target_pairs={{0,4},{1,3},{2,6},{3,1},{4,0},{5,7},{6,2},{7,5},{8,12},{9,11},{10,... | collective-permute-start | bytes 3932168 | tf_op jit(solution)/shard_map/ppermute | solution.py:475
  240.3 26.9 %collective-permute-start.33 = (bf16[4,2,160,512]{3,2,1,0:T(8,128)(2,1)}, bf16[4,2,160,512]{3,2,1,0:T(8,128)(2,1)S(1)}, u32[]{:S(2)}, u32[]{:S(2)}) collective-permute-start(bf16[4,2,160,512]{3,2,1,0:T(8,128)(2,1)} %collective-permute-done.28.refs_1_), channel_id=1, source_target_pairs={{0,4},{1,3},{2,6},{3,1},{4,0},{5,7},{6,2},{7,5},{8,12},{9,11},{10,... | collective-permute-start | bytes 3932168 | tf_op jit(solution)/shard_map/ppermute | solution.py:475
  254.1 25.4 %collective-permute-start.57 = (bf16[4,2,144,512]{3,2,1,0:T(8,128)(2,1)}, bf16[4,2,144,512]{3,2,1,0:T(8,128)(2,1)}, u32[]{:S(2)}, u32[]{:S(2)}) collective-permute-start(bf16[4,2,144,512]{3,2,1,0:T(8,128)(2,1)} %collective-permute-done.20.refs_2_), channel_id=1, source_target_pairs={{0,1},{1,0},{2,3},{3,2},{4,5},{5,4},{6,7},{7,6},{8,9},{9,8},{10,11... | collective-permute-start | bytes 3538952 | tf_op jit(solution)/shard_map/ppermute | solution.py:475
  268.2 29.9 %collective-permute-start.38 = (bf16[4,2,144,512]{3,2,1,0:T(8,128)(2,1)}, bf16[4,2,144,512]{3,2,1,0:T(8,128)(2,1)}, u32[]{:S(2)}, u32[]{:S(2)}) collective-permute-start(bf16[4,2,144,512]{3,2,1,0:T(8,128)(2,1)} %stack_z.12.refs_0_), channel_id=1, source_target_pairs={{0,4},{1,3},{2,6},{3,1},{4,0},{5,7},{6,2},{7,5},{8,12},{9,11},{10,... | collective-permute-start | bytes 3538952 | tf_op jit(solution)/shard_map/ppermute | solution.py:475
  269.1 38.1 %collective-permute-start.39 = (bf16[4,2,144,512]{3,2,1,0:T(8,128)(2,1)}, bf16[4,2,144,512]{3,2,1,0:T(8,128)(2,1)}, u32[]{:S(2)}, u32[]{:S(2)}) collective-permute-start(bf16[4,2,144,512]{3,2,1,0:T(8,128)(2,1)} %collective-permute-done.34.refs_1_), channel_id=1, source_target_pairs={{0,4},{1,3},{2,6},{3,1},{4,0},{5,7},{6,2},{7,5},{8,12},{9,11},{10,... | collective-permute-start | bytes 3538952 | tf_op jit(solution)/shard_map/ppermute | solution.py:475
  274.5 23.6 %collective-permute-start.40 = (bf16[4,2,112,512]{3,2,1,0:T(8,128)(2,1)}, bf16[4,2,112,512]{3,2,1,0:T(8,128)(2,1)S(1)}, u32[]{:S(2)}, u32[]{:S(2)}) collective-permute-start(bf16[4,2,112,512]{3,2,1,0:T(8,128)(2,1)} %stack_z.13.refs_0_), channel_id=1, source_target_pairs={{0,2},{1,5},{2,0},{3,7},{4,6},{5,1},{6,4},{7,3},{8,10},{9,13},{10,... | collective-permute-start | bytes 2752520 | tf_op jit(solution)/shard_map/ppermute | solution.py:475
  280.4 42.8 %collective-permute-start.60 = (bf16[4,2,64,512]{3,2,1,0:T(8,128)(2,1)}, bf16[4,2,64,512]{3,2,1,0:T(8,128)(2,1)}, u32[]{:S(2)}, u32[]{:S(2)}) collective-permute-start(bf16[4,2,64,512]{3,2,1,0:T(8,128)(2,1)} %collective-permute-done.22.refs_1_), channel_id=1, source_target_pairs={{0,1},{1,0},{2,3},{3,2},{4,5},{5,4},{6,7},{7,6},{8,9},{9,8},{10,11... | collective-permute-start | bytes 1572872 | tf_op jit(solution)/shard_map/ppermute | solution.py:475
  282.4 41.4 %collective-permute-start.61 = (bf16[4,2,64,512]{3,2,1,0:T(8,128)(2,1)}, bf16[4,2,64,512]{3,2,1,0:T(8,128)(2,1)S(1)}, u32[]{:S(2)}, u32[]{:S(2)}) collective-permute-start(bf16[4,2,64,512]{3,2,1,0:T(8,128)(2,1)} %copy-done.48), channel_id=1, source_target_pairs={{0,1},{1,0},{2,3},{3,2},{4,5},{5,4},{6,7},{7,6},{8,9},{9,8},{10,11... | collective-permute-start | bytes 1572872 | tf_op jit(solution)/shard_map/ppermute | solution.py:475
  298.1 94.4 %collective-permute-start.63 = (bf16[4,2,160,512]{3,2,1,0:T(8,128)(2,1)}, bf16[4,2,160,512]{3,2,1,0:T(8,128)(2,1)}, u32[]{:S(2)}, u32[]{:S(2)}) collective-permute-start(bf16[4,2,160,512]{3,2,1,0:T(8,128)(2,1)} %stack_z.11.refs_0_), channel_id=1, source_target_pairs={{0,1},{1,0},{2,3},{3,2},{4,5},{5,4},{6,7},{7,6},{8,9},{9,8},{10,11... | collective-permute-start | bytes 3932168 | tf_op jit(solution)/shard_map/ppermute | solution.py:475
  298.1 94.4 %collective-permute-start.64 = (bf16[4,2,160,512]{3,2,1,0:T(8,128)(2,1)}, bf16[4,2,160,512]{3,2,1,0:T(8,128)(2,1)}, u32[]{:S(2)}, u32[]{:S(2)}) collective-permute-start(bf16[4,2,160,512]{3,2,1,0:T(8,128)(2,1)} %collective-permute-done.28.refs_1_), channel_id=1, source_target_pairs={{0,1},{1,0},{2,3},{3,2},{4,5},{5,4},{6,7},{7,6},{8,9},{9,8},{10,11... | collective-permute-start | bytes 3932168 | tf_op jit(solution)/shard_map/ppermute | solution.py:475
  307.1 85.9 %collective-permute-start.65 = (bf16[4,2,160,512]{3,2,1,0:T(8,128)(2,1)}, bf16[4,2,160,512]{3,2,1,0:T(8,128)(2,1)}, u32[]{:S(2)}, u32[]{:S(2)}) collective-permute-start(bf16[4,2,160,512]{3,2,1,0:T(8,128)(2,1)} %collective-permute-done.32.refs_2_), channel_id=1, source_target_pairs={{0,1},{1,0},{2,3},{3,2},{4,5},{5,4},{6,7},{7,6},{8,9},{9,8},{10,11... | collective-permute-start | bytes 3932168 | tf_op jit(solution)/shard_map/ppermute | solution.py:475
  323.2 51.3 %collective-permute-start.62 = (bf16[4,2,64,512]{3,2,1,0:T(8,128)(2,1)}, bf16[4,2,64,512]{3,2,1,0:T(8,128)(2,1)}, u32[]{:S(2)}, u32[]{:S(2)}) collective-permute-start(bf16[4,2,64,512]{3,2,1,0:T(8,128)(2,1)} %collective-permute-done.27.refs_3_), channel_id=1, source_target_pairs={{0,1},{1,0},{2,3},{3,2},{4,5},{5,4},{6,7},{7,6},{8,9},{9,8},{10,11... | collective-permute-start | bytes 1572872 | tf_op jit(solution)/shard_map/ppermute | solution.py:475
  323.7 69.3 %collective-permute-start.41 = (bf16[4,2,112,512]{3,2,1,0:T(8,128)(2,1)}, bf16[4,2,112,512]{3,2,1,0:T(8,128)(2,1)}, u32[]{:S(2)}, u32[]{:S(2)}) collective-permute-start(bf16[4,2,112,512]{3,2,1,0:T(8,128)(2,1)} %stack_z.13.refs_0_), channel_id=1, source_target_pairs={{0,4},{1,3},{2,6},{3,1},{4,0},{5,7},{6,2},{7,5},{8,12},{9,11},{10,... | collective-permute-start | bytes 2752520 | tf_op jit(solution)/shard_map/ppermute | solution.py:475
  374.5 24.0 %collective-permute-start.42 = (bf16[4,2,112,512]{3,2,1,0:T(8,128)(2,1)}, bf16[4,2,112,512]{3,2,1,0:T(8,128)(2,1)}, u32[]{:S(2)}, u32[]{:S(2)}) collective-permute-start(bf16[4,2,112,512]{3,2,1,0:T(8,128)(2,1)} %copy-done.39), channel_id=1, source_target_pairs={{0,4},{1,3},{2,6},{3,1},{4,0},{5,7},{6,2},{7,5},{8,12},{9,11},{10,... | collective-permute-start | bytes 2752520 | tf_op jit(solution)/shard_map/ppermute | solution.py:475
  398.5 36.4 %collective-permute-start.70 = (bf16[4,2,144,512]{3,2,1,0:T(8,128)(2,1)}, bf16[4,2,144,512]{3,2,1,0:T(8,128)(2,1)}, u32[]{:S(2)}, u32[]{:S(2)}) collective-permute-start(bf16[4,2,144,512]{3,2,1,0:T(8,128)(2,1)} %collective-permute-done.39.refs_3_), channel_id=1, source_target_pairs={{0,1},{1,0},{2,3},{3,2},{4,5},{5,4},{6,7},{7,6},{8,9},{9,8},{10,11... | collective-permute-start | bytes 3538952 | tf_op jit(solution)/shard_map/ppermute | solution.py:475
  399.0 68.2 %collective-permute-start.43 = (bf16[4,2,112,512]{3,2,1,0:T(8,128)(2,1)}, bf16[4,2,112,512]{3,2,1,0:T(8,128)(2,1)}, u32[]{:S(2)}, u32[]{:S(2)}) collective-permute-start(bf16[4,2,112,512]{3,2,1,0:T(8,128)(2,1)} %stack_z.13.refs_0_), channel_id=1, source_target_pairs={{0,1},{1,0},{2,3},{3,2},{4,5},{5,4},{6,7},{7,6},{8,9},{9,8},{10,11... | collective-permute-start | bytes 2752520 | tf_op jit(solution)/shard_map/ppermute | solution.py:475
  399.5 67.8 %collective-permute-start.44 = (bf16[4,2,112,512]{3,2,1,0:T(8,128)(2,1)}, bf16[4,2,112,512]{3,2,1,0:T(8,128)(2,1)}, u32[]{:S(2)}, u32[]{:S(2)}) collective-permute-start(bf16[4,2,112,512]{3,2,1,0:T(8,128)(2,1)} %copy-done.39), channel_id=1, source_target_pairs={{0,1},{1,0},{2,3},{3,2},{4,5},{5,4},{6,7},{7,6},{8,9},{9,8},{10,11... | collective-permute-start | bytes 2752520 | tf_op jit(solution)/shard_map/ppermute | solution.py:475
  399.6 67.7 %collective-permute-start.45 = (bf16[4,2,112,512]{3,2,1,0:T(8,128)(2,1)}, bf16[4,2,112,512]{3,2,1,0:T(8,128)(2,1)}, u32[]{:S(2)}, u32[]{:S(2)}) collective-permute-start(bf16[4,2,112,512]{3,2,1,0:T(8,128)(2,1)} %collective-permute-done.41.refs_2_), channel_id=1, source_target_pairs={{0,1},{1,0},{2,3},{3,2},{4,5},{5,4},{6,7},{7,6},{8,9},{9,8},{10,11... | collective-permute-start | bytes 2752520 | tf_op jit(solution)/shard_map/ppermute | solution.py:475
  400.9 66.3 %collective-permute-start.46 = (bf16[4,2,112,512]{3,2,1,0:T(8,128)(2,1)}, bf16[4,2,112,512]{3,2,1,0:T(8,128)(2,1)}, u32[]{:S(2)}, u32[]{:S(2)}) collective-permute-start(bf16[4,2,112,512]{3,2,1,0:T(8,128)(2,1)} %collective-permute-done.42.refs_3_), channel_id=1, source_target_pairs={{0,1},{1,0},{2,3},{3,2},{4,5},{5,4},{6,7},{7,6},{8,9},{9,8},{10,11... | collective-permute-start | bytes 2752520 | tf_op jit(solution)/shard_map/ppermute | solution.py:475
  520.9 74.4 %collective-permute-start.78 = (bf16[2,2,4,2,48,512]{5,4,3,2,1,0:T(8,128)(2,1)}, bf16[2,2,4,2,48,512]{5,4,3,2,1,0:T(8,128)(2,1)S(1)}, u32[]{:S(2)}, u32[]{:S(2)}) collective-permute-start(bf16[2,2,4,2,48,512]{5,4,3,2,1,0:T(8,128)(2,1)} %get-tuple-element.286), channel_id=1, source_target_pairs={{0,1},{1,0},{2,3},{3,2},{4,5},{5,4},{6,7},{7,6},{8,9},{9,8},{10,11... | collective-permute-start | bytes 4718600 | tf_op jit(solution)/shard_map/ppermute | solution.py:475
  571.3 63.6 %collective-permute-start.92 = (bf16[2,2,4,2,80,512]{5,4,3,2,1,0:T(8,128)(2,1)}, bf16[2,2,4,2,80,512]{5,4,3,2,1,0:T(8,128)(2,1)}, u32[]{:S(2)}, u32[]{:S(2)}) collective-permute-start(bf16[2,2,4,2,80,512]{5,4,3,2,1,0:T(8,128)(2,1)} %get-tuple-element.295), channel_id=1, source_target_pairs={{0,1},{1,0},{2,3},{3,2},{4,5},{5,4},{6,7},{7,6},{8,9},{9,8},{10,11... | collective-permute-start | bytes 7864328 | tf_op jit(solution)/shard_map/ppermute | solution.py:475
  575.9 42.5 %collective-permute-start.99 = (bf16[2,2,4,2,64,512]{5,4,3,2,1,0:T(8,128)(2,1)}, bf16[2,2,4,2,64,512]{5,4,3,2,1,0:T(8,128)(2,1)}, u32[]{:S(2)}, u32[]{:S(2)}) collective-permute-start(bf16[2,2,4,2,64,512]{5,4,3,2,1,0:T(8,128)(2,1)} %get-tuple-element.301), channel_id=1, source_target_pairs={{0,1},{1,0},{2,3},{3,2},{4,5},{5,4},{6,7},{7,6},{8,9},{9,8},{10,11... | collective-permute-start | bytes 6291464 | tf_op jit(solution)/shard_map/ppermute | solution.py:475
  594.8 32.7 %collective-permute-start.71 = (bf16[2,2,4,2,64,512]{5,4,3,2,1,0:T(8,128)(2,1)}, bf16[2,2,4,2,64,512]{5,4,3,2,1,0:T(8,128)(2,1)}, u32[]{:S(2)}, u32[]{:S(2)}) collective-permute-start(bf16[2,2,4,2,64,512]{5,4,3,2,1,0:T(8,128)(2,1)} %get-tuple-element.281), channel_id=1, source_target_pairs={{0,1},{1,0},{2,3},{3,2},{4,5},{5,4},{6,7},{7,6},{8,9},{9,8},{10,11... | collective-permute-start | bytes 6291464 | tf_op jit(solution)/shard_map/ppermute | solution.py:475
  604.7 51.5 %collective-permute-start.106 = (bf16[2,2,4,2,80,512]{5,4,3,2,1,0:T(8,128)(2,1)}, bf16[2,2,4,2,80,512]{5,4,3,2,1,0:T(8,128)(2,1)}, u32[]{:S(2)}, u32[]{:S(2)}) collective-permute-start(bf16[2,2,4,2,80,512]{5,4,3,2,1,0:T(8,128)(2,1)} %get-tuple-element.306), channel_id=1, source_target_pairs={{0,1},{1,0},{2,3},{3,2},{4,5},{5,4},{6,7},{7,6},{8,9},{9,8},{10,11... | collective-permute-start | bytes 7864328 | tf_op jit(solution)/shard_map/ppermute | solution.py:475
  617.0 57.8 %collective-permute-start.85 = (bf16[2,2,4,2,96,512]{5,4,3,2,1,0:T(8,128)(2,1)}, bf16[2,2,4,2,96,512]{5,4,3,2,1,0:T(8,128)(2,1)}, u32[]{:S(2)}, u32[]{:S(2)}) collective-permute-start(bf16[2,2,4,2,96,512]{5,4,3,2,1,0:T(8,128)(2,1)} %get-tuple-element.290), channel_id=1, source_target_pairs={{0,1},{1,0},{2,3},{3,2},{4,5},{5,4},{6,7},{7,6},{8,9},{9,8},{10,11... | collective-permute-start | bytes 9437192 | tf_op jit(solution)/shard_map/ppermute | solution.py:475
  626.3 24.5 %collective-permute-start.100 = (bf16[2,4,2,64,512]{4,3,2,1,0:T(8,128)(2,1)S(1)}, bf16[2,4,2,64,512]{4,3,2,1,0:T(8,128)(2,1)S(1)}, u32[]{:S(2)}, u32[]{:S(2)}) collective-permute-start(bf16[2,4,2,64,512]{4,3,2,1,0:T(8,128)(2,1)S(1)} %fusion.7), channel_id=1, source_target_pairs={{0,4},{1,3},{2,6},{3,1},{4,0},{5,7},{6,2},{7,5},{8,12},{9,11},{10,... | collective-permute-start | bytes 3145736 | tf_op jit(solution)/shard_map/ppermute | solution.py:475
  649.6 54.4 %collective-permute-start.93 = (bf16[2,4,2,80,512]{4,3,2,1,0:T(8,128)(2,1)}, bf16[2,4,2,80,512]{4,3,2,1,0:T(8,128)(2,1)}, u32[]{:S(2)}, u32[]{:S(2)}) collective-permute-start(bf16[2,4,2,80,512]{4,3,2,1,0:T(8,128)(2,1)} %fusion.6), channel_id=1, source_target_pairs={{0,4},{1,3},{2,6},{3,1},{4,0},{5,7},{6,2},{7,5},{8,12},{9,11},{10,... | collective-permute-start | bytes 3932168 | tf_op jit(solution)/shard_map/ppermute | solution.py:475
  656.2 23.6 %collective-permute-start.73 = (bf16[4,2,64,512]{3,2,1,0:T(8,128)(2,1)}, bf16[4,2,64,512]{3,2,1,0:T(8,128)(2,1)}, u32[]{:S(2)}, u32[]{:S(2)}) collective-permute-start(bf16[4,2,64,512]{3,2,1,0:T(8,128)(2,1)} %fusion.17), channel_id=1, source_target_pairs={{0,2},{1,5},{2,0},{3,7},{4,6},{5,1},{6,4},{7,3},{8,10},{9,13},{10,... | collective-permute-start | bytes 1572872 | tf_op jit(solution)/shard_map/ppermute | solution.py:475
  662.5 44.2 %collective-permute-start.107 = (bf16[2,4,2,80,512]{4,3,2,1,0:T(8,128)(2,1)}, bf16[2,4,2,80,512]{4,3,2,1,0:T(8,128)(2,1)}, u32[]{:S(2)}, u32[]{:S(2)}) collective-permute-start(bf16[2,4,2,80,512]{4,3,2,1,0:T(8,128)(2,1)} %fusion.5), channel_id=1, source_target_pairs={{0,4},{1,3},{2,6},{3,1},{4,0},{5,7},{6,2},{7,5},{8,12},{9,11},{10,... | collective-permute-start | bytes 3932168 | tf_op jit(solution)/shard_map/ppermute | solution.py:475
  670.1 21.9 %collective-permute-start.102 = (bf16[2,64,512]{2,1,0:T(8,128)(2,1)S(1)}, bf16[2,64,512]{2,1,0:T(8,128)(2,1)S(1)}, u32[]{:S(2)}, u32[]{:S(2)}) collective-permute-start(bf16[2,64,512]{2,1,0:T(8,128)(2,1)S(1)} %get-tuple-element.358), channel_id=1, source_target_pairs={{0,8},{1,9},{2,10},{3,11},{4,12},{5,13},{6,14},{7,15},{8,16},{9,17... | collective-permute-start | bytes 393224 | tf_op jit(solution)/shard_map/ppermute | solution.py:475
  699.6 32.0 %collective-permute-start.86 = (bf16[2,4,2,96,512]{4,3,2,1,0:T(8,128)(2,1)S(1)}, bf16[2,4,2,96,512]{4,3,2,1,0:T(8,128)(2,1)S(1)}, u32[]{:S(2)}, u32[]{:S(2)}) collective-permute-start(bf16[2,4,2,96,512]{4,3,2,1,0:T(8,128)(2,1)S(1)} %fusion.4), channel_id=1, source_target_pairs={{0,4},{1,3},{2,6},{3,1},{4,0},{5,7},{6,2},{7,5},{8,12},{9,11},{10,... | collective-permute-start | bytes 4718600 | tf_op jit(solution)/shard_map/ppermute | solution.py:475
  737.6 25.7 %collective-permute-start.87 = (bf16[4,2,96,512]{3,2,1,0:T(8,128)(2,1)S(1)}, bf16[4,2,96,512]{3,2,1,0:T(8,128)(2,1)S(1)}, u32[]{:S(2)}, u32[]{:S(2)}) collective-permute-start(bf16[4,2,96,512]{3,2,1,0:T(8,128)(2,1)S(1)} %fusion.9), channel_id=1, source_target_pairs={{0,2},{1,5},{2,0},{3,7},{4,6},{5,1},{6,4},{7,3},{8,10},{9,13},{10,... | collective-permute-start | bytes 2359304 | tf_op jit(solution)/shard_map/ppermute | solution.py:475
  (169 other events, 1989.5 us)

commit v3 on v2

--- a/solution.py
+++ b/solution.py
@@ -18,6 +18,7 @@
 ROWS = 128
 LANES = 256
 VMEM_LIMIT = 60 * 1024 * 1024
+LIGHT = pl.CostEstimate(flops=1024, bytes_accessed=1024, transcendentals=0)
 
 
 def shifts():
@@ -106,9 +107,55 @@
     rstd[:, at] = lax.rsqrt(group_mean(sums[:, whole]) + 1e-05)
 
 
-def forward_kernel(count, keep, *refs):
-    x, w_in, w_mid, w_out, gains, shift, out = refs[:7]
-    hid_one, hid_two, hid_three, rstd, low, act, cols, sums = refs[7:]
+def forward_kernel(count, keep, parts, tuned, *refs):
+    refs = list(refs)
+    first = len(parts) > 3
+
+    def take(number):
+        taken = refs[:number]
+        del refs[:number]
+        return taken
+
+    (place,) = take(1)
+    x = take(2 if first else 1)
+    gains, shift = take(2)
+    sources = take(2 if tuned else len(parts))
+    (out,) = take(1)
+    if keep:
+        if first:
+            (start,) = take(1)
+        hid_one, hid_two, hid_three, rstd = take(4)
+        kept_weights = take(3)
+    weights = take(len(parts))
+    sems, back_sems, low, act, cols, sums = take(6)
+    if not keep:
+        hid_one, hid_two, hid_three, rstd = take(4)
+        if first:
+            (start,) = take(1)
+    fetch(parts, tuned, place, sources, weights, sems)
+
+    def arrived(index):
+        index += len(parts)
+        pltpu.make_async_copy(weights[index], weights[index], sems.at[index]).wait()
+        if keep and index >= len(parts) - 3:
+            number = index - len(parts) + 3
+            pltpu.make_async_copy(weights[index], kept_weights[number], back_sems.at[number]).start()
+        return weights[index]
+
+    def whole(value):
+        return value.reshape(-1, value.shape[-1])
+
+    if first:
+        pixels, spread = x
+        x = start
+        patch = arrived(-4)
+        for half in range(2):
+            wide = dot(pixels[...], spread[half]).astype(jnp.bfloat16)
+            for block in range(2):
+                lanes = pl.ds((2 * half + block) * WIDTH, WIDTH)
+                x[:, lanes] = dot(wide, whole(patch[block]))
+    else:
+        (x,) = x
 
     def cast(frame, rows, lanes):
         low[rows, lanes] = x[rows, lanes].astype(jnp.bfloat16)
@@ -125,7 +172,7 @@
         return body
 
     each_chunk(count, D, cast)
-    hid_one[...] = dot(low[...], w_in[...])
+    hid_one[...] = dot(low[...], whole(arrived(-3)[...]))
     normalise(count, BOT, hid_one, sums, rstd, 0)
     each_chunk(count, BOT, activate(hid_one, 0, 0))
     for frame in range(count):
@@ -133,12 +180,12 @@
         for tap in range(TAPS):
             picked = dot(shift[pl.ds(tap * ROWS, ROWS), :], act[rows, :])
             cols[rows, pl.ds(tap * BOT, BOT)] = picked.astype(jnp.bfloat16)
-    hid_two[...] = dot(cols[...], w_mid[...])
+    hid_two[...] = dot(cols[...], whole(arrived(-2)[...]))
     normalise(count, BOT, hid_two, sums, rstd, BOT)
     each_chunk(count, BOT, activate(hid_two, BOT, 2 * BOT))
+    w_out = arrived(-1)
     for part in range(D // BOT):
-        lanes = pl.ds(part * BOT, BOT)
-        hid_three[:, lanes] = dot(act[...], w_out[lanes, :])
+        hid_three[:, pl.ds(part * BOT, BOT)] = dot(act[...], whole(w_out[part]))
     normalise(count, D, hid_three, sums, rstd, 2 * BOT)
 
     def finish(frame, rows, lanes):
@@ -151,6 +198,10 @@
         out[rows, lanes] = jnp.where(real_rows(), value, 0.0)
 
     each_chunk(count, D, finish)
+    if keep:
+        for number in range(3):
+            weight = weights[len(parts) - 3 + number]
+            pltpu.make_async_copy(weight, kept_weights[number], back_sems.at[number]).wait()
 
 
 def f32(*shape):
@@ -165,8 +216,9 @@
     return -(-count // 8) * 8
 
 
-def block_forward(stream, w_in, w_mid, w_out, gains, shift, keep):
-    rows = stream.shape[0]
+def block_forward(stream, gains, shift, parts, buffers, place, keep, tuned):
+    first = len(parts) > 3
+    rows = stream[0].shape[0]
     count = rows // ROWS
     stats = stat_rows(count)
     kept = [
@@ -175,29 +227,35 @@
         ((rows, D), jnp.float32),
         ((stats, 2 * BOT + D), jnp.float32),
     ]
-    scratch = [
-        ((rows, D), jnp.bfloat16),
-        ((rows, BOT), jnp.bfloat16),
-        ((rows, TAPS * BOT), jnp.bfloat16),
-        ((stats, D), jnp.float32),
+    start = [((rows, D), jnp.float32)] if first else []
+    weights = weight_shapes(parts, buffers, tuned)
+    out_shape = [f32(rows, D)]
+    out_specs = in_vmem(1)
+    scratch = [pltpu.VMEM(shape, jnp.bfloat16) for shape in weights]
+    scratch += [
+        pltpu.SemaphoreType.DMA((len(parts),)),
+        pltpu.SemaphoreType.DMA((3,)),
+        pltpu.VMEM((rows, D), jnp.bfloat16),
+        pltpu.VMEM((rows, BOT), jnp.bfloat16),
+        pltpu.VMEM((rows, TAPS * BOT), jnp.bfloat16),
+        pltpu.VMEM((stats, D), jnp.float32),
     ]
-    out_shape = [f32(rows, D)]
     if keep:
-        out_shape += [jax.ShapeDtypeStruct(*item) for item in kept]
+        out_shape += [jax.ShapeDtypeStruct(*item) for item in start + kept]
+        out_shape += [jax.ShapeDtypeStruct(shape, jnp.bfloat16) for shape in weights[-3:]]
+        out_specs += in_vmem(len(start + kept)) + hbm(3)
     else:
-        scratch = kept + scratch
+        scratch += [pltpu.VMEM(*item) for item in kept + start]
     return pl.pallas_call(
-        functools.partial(forward_kernel, count, keep),
+        functools.partial(forward_kernel, count, keep, parts, tuned),
         out_shape=out_shape,
-        in_specs=in_vmem(6),
-        out_specs=in_vmem(len(out_shape)),
-        scratch_shapes=[pltpu.VMEM(*item) for item in scratch],
+        in_specs=in_smem() + in_vmem(len(stream) + 2) + hbm(len(buffers)),
+        out_specs=out_specs,
+        scratch_shapes=scratch,
         compiler_params=pltpu.CompilerParams(vmem_limit_bytes=VMEM_LIMIT),
-        cost_estimate=pl.CostEstimate(
-            flops=2 * rows * BOT * (2 * D + 9 * BOT), bytes_accessed=20_000_000, transcendentals=0
-        ),
+        cost_estimate=LIGHT,
         name="block_forward",
-    )(stream, w_in, w_mid, w_out, gains, shift)
+    )(place, *stream, gains, shift, *buffers)
 
 
 def norm_back(count, chans, slope, hid, sums, more, rstd, rstd_at, gain, grad_gain, grad_bias, store):
@@ -296,9 +354,7 @@
             pltpu.VMEM((stats, D), jnp.float32),
         ],
         compiler_params=pltpu.CompilerParams(vmem_limit_bytes=VMEM_LIMIT),
-        cost_estimate=pl.CostEstimate(
-            flops=4 * rows * BOT * D, bytes_accessed=20_000_000, transcendentals=0
-        ),
+        cost_estimate=LIGHT,
         name="back_out",
     )(grad, stream, hid_two, hid_three, rstd, w_out, gains)
 
@@ -358,9 +414,7 @@
             pltpu.VMEM((stats, BOT), jnp.float32),
         ],
         compiler_params=pltpu.CompilerParams(vmem_limit_bytes=VMEM_LIMIT),
-        cost_estimate=pl.CostEstimate(
-            flops=4 * rows * BOT * TAPS * BOT, bytes_accessed=12_000_000, transcendentals=0
-        ),
+        cost_estimate=LIGHT,
         name="back_mid",
     )(grad, hid_one, rstd, w_mid, gains, shift)
 
@@ -387,9 +441,7 @@
         out_specs=in_vmem(2),
         scratch_shapes=[pltpu.VMEM((rows, D), jnp.bfloat16)],
         compiler_params=pltpu.CompilerParams(vmem_limit_bytes=VMEM_LIMIT),
-        cost_estimate=pl.CostEstimate(
-            flops=4 * rows * BOT * D, bytes_accessed=15_000_000, transcendentals=0
-        ),
+        cost_estimate=LIGHT,
         name="back_in",
     )(grad, stream, dres, w_in)
 
@@ -401,25 +453,6 @@
     return jnp.stack(
         [jnp.arange(2 * PATCH_IN)[None, :] == (at + half * rows)[:, None] for half in range(2)]
     ).astype(jnp.bfloat16)
-
-
-def embed_kernel(pixels, spread, patch, out):
-    for half in range(2):
-        wide = dot(pixels[...], spread[half]).astype(jnp.bfloat16)
-        for block in range(2):
-            lanes = pl.ds((2 * half + block) * WIDTH, WIDTH)
-            out[:, lanes] = dot(wide, patch[block])
-
-
-def embed(pixels, spread, patch):
-    return pl.pallas_call(
-        embed_kernel,
-        out_shape=f32(pixels.shape[0], D),
-        in_specs=in_vmem(3),
-        out_specs=in_vmem(1)[0],
-        compiler_params=pltpu.CompilerParams(vmem_limit_bytes=VMEM_LIMIT),
-        name="embed",
-    )(pixels, spread, patch)
 
 
 def embed_back_kernel(pixels, spread, grad, out):
@@ -440,8 +473,173 @@
         in_specs=in_vmem(3),
         out_specs=in_vmem(1)[0],
         compiler_params=pltpu.CompilerParams(vmem_limit_bytes=VMEM_LIMIT),
+        cost_estimate=LIGHT,
         name="embed_back",
     )(pixels, spread, grad)
+
+
+def head_forward(count, stream, pool, proj, heads, games, pool_t, pooled):
+    for part in range(D // ROWS):
+        lanes = pl.ds(part * ROWS, ROWS)
+        pool_t[:, lanes] = pool[lanes, :].astype(jnp.float32).T
+    pooled[...] = jnp.zeros_like(pooled)
+
+    def weigh(frame, rows, lanes):
+        value = stream[rows, lanes].astype(jnp.bfloat16).astype(jnp.float32)
+        pooled[frame, lanes] = jnp.sum(value * pool_t[:, lanes], axis=0, keepdims=True)
+
+    each_chunk(count, D, weigh)
+    before = dot(pooled[...].astype(jnp.bfloat16), proj[...])
+    hidden = silu(before).astype(jnp.bfloat16)
+    scores = None
+    for game in range(GAMES):
+        pair = [dot(hidden, heads[2 * game + half]) for half in range(2)]
+        term = jnp.where(games == game, jnp.concatenate(pair, axis=1), 0.0)
+        scores = term if scores is None else scores + term
+    return ([pick_atoms(scores, action) for action in range(ACTIONS)], before, hidden)
+
+
+def atom_lanes():
+    return lax.broadcasted_iota(jnp.int32, (8, ROWS), 1)
+
+
+def pick_atoms(scores, action):
+    offset = action * ATOMS
+    moved = pltpu.roll(scores, 2 * WIDTH - offset, 1) if offset else scores
+    return jnp.where(atom_lanes() < ATOMS, moved[:, :ROWS], -1e30)
+
+
+def support_lanes():
+    return -10.0 + 20.0 / (ATOMS - 1) * atom_lanes().astype(jnp.float32)
+
+
+def lane_sum(value):
+    return jnp.sum(value, axis=1, keepdims=True)
+
+
+def target_kernel(count, stream, pool, proj, heads, whole, real, out, pool_t, pooled):
+    logits, _, _ = head_forward(
+        count, stream, pool, proj, heads, whole[:, 0:1], pool_t, pooled
+    )
+    chosen = None
+    for action in range(ACTIONS):
+        term = jnp.where(whole[:, 2:3] == action, logits[action], 0.0)
+        chosen = term if chosen is None else chosen + term
+    power = jnp.exp(chosen - jnp.max(chosen, axis=1, keepdims=True))
+    probs = power / lane_sum(power)
+    atoms = support_lanes()
+    spacing = 20.0 / (ATOMS - 1)
+    moved = jnp.clip(real[:, 0:1] + real[:, 1:2] * atoms, -10.0, 10.0)
+    total = jnp.zeros_like(probs)
+    for atom in range(ATOMS):
+        near = 1.0 - jnp.abs(moved[:, atom : atom + 1] - atoms) / spacing
+        total = total + probs[:, atom : atom + 1] * jnp.clip(near, 0.0, 1.0)
+    inside = (atom_lanes() < ATOMS) & (lax.broadcasted_iota(jnp.int32, total.shape, 0) < count)
+    out[...] = jnp.where(inside, total, 0.0)
+
+
+def head_target(stream, pool, proj, heads, whole, real):
+    count = stream.shape[0] // ROWS
+    return pl.pallas_call(
+        functools.partial(target_kernel, count),
+        out_shape=f32(8, ROWS),
+        in_specs=in_vmem(6),
+        out_specs=in_vmem(1)[0],
+        scratch_shapes=[pltpu.VMEM((ROWS, D), jnp.float32), pltpu.VMEM((8, D), jnp.float32)],
+        compiler_params=pltpu.CompilerParams(vmem_limit_bytes=VMEM_LIMIT),
+        cost_estimate=LIGHT,
+        name="head_target",
+    )(stream, pool, proj, heads, whole, real)
+
+
+def loss_kernel(count, frames_all, *refs):
+    stream, pool, proj, heads, target, whole, legal = refs[:7]
+    loss, dheads, dproj, dpool, dstream = refs[7:12]
+    pool_t, pooled, dpooled = refs[12:]
+    games, taken = (whole[:, 0:1], whole[:, 1:2])
+    logits, before, hidden = head_forward(count, stream, pool, proj, heads, games, pool_t, pooled)
+    atoms = support_lanes()
+    inside = atom_lanes() < ATOMS
+    logps, probs, values = ([], [], [])
+    for value in logits:
+        value = value - jnp.max(value, axis=1, keepdims=True)
+        power = jnp.where(inside, jnp.exp(value), 0.0)
+        mass = lane_sum(power)
+        logps.append(value - jnp.log(mass))
+        probs.append(power / mass)
+        values.append(lane_sum(probs[-1] * atoms))
+    masked = [
+        jnp.where(legal[:, action : action + 1] > 0, values[action], -1e30)
+        for action in range(ACTIONS)
+    ]
+    largest = functools.reduce(jnp.maximum, masked)
+    powers = [jnp.exp(value - largest) for value in masked]
+    mass = sum(powers[1:], powers[0])
+    goal = target[...]
+    goal_mass = lane_sum(goal)
+    cross = taken_value = 0.0
+    real = lax.broadcasted_iota(jnp.int32, (8, 1), 0) < count
+    scale = jnp.where(real, 1.0 / frames_all, 0.0)
+    spread = jnp.zeros((8, 2 * WIDTH), jnp.float32)
+    for action in range(ACTIONS):
+        here = jnp.where(taken == action, 1.0, 0.0)
+        cross = cross - here * lane_sum(jnp.where(inside, goal * logps[action], 0.0))
+        taken_value = taken_value + here * values[action]
+        grad = here * (probs[action] * goal_mass - goal)
+        pull = CQL_WEIGHT * (powers[action] / mass - here)
+        grad = grad + pull * probs[action] * (atoms - values[action])
+        grad = jnp.where(inside, grad * scale, 0.0)
+        grad = jnp.concatenate([grad, jnp.zeros((8, 2 * WIDTH - ROWS), jnp.float32)], axis=1)
+        offset = action * ATOMS
+        spread = spread + (pltpu.roll(grad, offset, 1) if offset else grad)
+    losses = cross + CQL_WEIGHT * (jnp.log(mass) + largest - taken_value)
+    loss[...] = jnp.sum(jnp.where(real, losses, 0.0), axis=0, keepdims=True)
+    dhidden = None
+    for game in range(GAMES):
+        mine = jnp.where(games == game, spread, 0.0).astype(jnp.bfloat16)
+        for half in range(2):
+            part = mine[:, half * WIDTH : (half + 1) * WIDTH]
+            dheads[2 * game + half] = dot_rows(hidden, part).astype(jnp.bfloat16)
+            term = dot_lanes(part, heads[2 * game + half])
+            dhidden = term if dhidden is None else dhidden + term
+    dbefore = (silu_slope(before) * dhidden).astype(jnp.bfloat16)
+    dproj[...] = dot_rows(pooled[...].astype(jnp.bfloat16), dbefore).astype(jnp.bfloat16)
+    dpooled[...] = dot_lanes(dbefore, proj[...]).astype(jnp.bfloat16).astype(jnp.float32)
+
+    def push(frame, rows, lanes):
+        dstream[rows, lanes] = dpooled[frame, lanes] * pool_t[:, lanes]
+
+    each_chunk(count, D, push)
+
+    def gather_pool(part, carry):
+        lanes = pl.ds(pl.multiple_of(part * ROWS, ROWS), ROWS)
+        total = None
+        for frame in range(count):
+            value = stream[pl.ds(frame * ROWS, ROWS), lanes].astype(jnp.bfloat16)
+            term = value.astype(jnp.float32) * dpooled[pl.ds(frame, 1), lanes]
+            total = term if total is None else total + term
+        dpool[lanes, :] = total.T.astype(jnp.bfloat16)
+        return carry
+
+    lax.fori_loop(0, D // ROWS, gather_pool, 0)
+
+
+def head_loss(stream, pool, proj, heads, target, whole, legal, frames_all):
+    rows = stream.shape[0]
+    return pl.pallas_call(
+        functools.partial(loss_kernel, rows // ROWS, frames_all),
+        out_shape=[f32(1, 1), bf16(2 * GAMES, DPROJ, WIDTH), bf16(D, DPROJ), bf16(D, ROWS), f32(rows, D)],
+        in_specs=in_vmem(7),
+        out_specs=in_vmem(5),
+        scratch_shapes=[
+            pltpu.VMEM((ROWS, D), jnp.float32),
+            pltpu.VMEM((8, D), jnp.float32),
+            pltpu.VMEM((8, D), jnp.float32),
+        ],
+        compiler_params=pltpu.CompilerParams(vmem_limit_bytes=VMEM_LIMIT),
+        cost_estimate=LIGHT,
+        name="head_loss",
+    )(stream, pool, proj, heads, target, whole, legal)
 
 
 WIDTH = 512
@@ -577,13 +775,14 @@
         in_specs=in_smem() + hbm(size),
         out_specs=in_vmem(1)[0],
         scratch_shapes=[pltpu.SemaphoreType.DMA((size,))],
+        cost_estimate=LIGHT,
         name="stack_z",
     )(place, *arrays)
 
 
 def assemble_pairs(parts, core, y, x, ins, outs):
     pairs = []
-    for number, (other, far, near) in enumerate(itertools.product((0, 1), repeat=3)):
+    for other, far, near in itertools.product((0, 1), repeat=3):
         half = core ^ other
         step = [0, 0, 0, 0]
         step[NEAR[half]], step[FAR[half]] = (near, far)
@@ -591,39 +790,61 @@
         for index, row, lane, rows, block, inner in half_moves(parts)[half]:
             pairs.append(
                 (
-                    ins[number].at[:, :, pl.ds(row, rows), pl.ds(lane, parts[index].lanes)],
+                    index,
+                    ins[other].at[far, near, :, :, pl.ds(row, rows), pl.ds(lane, parts[index].lanes)],
                     outs[index].at[block, :, at_y, at_x, :, pl.ds(inner, rows)],
                 )
             )
     return pairs
 
 
-def assemble_copies(parts):
+def deal_copies(parts):
     return 4 * sum(len(moves) for moves in half_moves(parts))
 
 
-def assemble_kernel(parts, place, *refs):
+def fetch(parts, tuned, place, sources, weights, sems):
+    if not tuned:
+        for index, (source, weight) in enumerate(zip(sources, weights)):
+            pltpu.make_async_copy(source, weight, sems.at[index]).start()
+        return
     for core in (0, 1):
 
         @pl.when(place[3] == core)
         def _():
-            copies(
-                assemble_pairs(parts, core, place[1], place[2], refs[:8], refs[8:-1]), refs[-1]
-            )
+            pairs = assemble_pairs(parts, core, place[1], place[2], sources, weights)
+            for index, source, target in sorted(pairs, key=lambda pair: pair[0]):
+                pltpu.make_async_copy(source, target, sems.at[index]).start()
+
+
+def weight_shapes(parts, buffers, tuned):
+    if tuned:
+        return [part.full(buffers[0].shape[2]) for part in parts]
+    return [item.shape for item in buffers]
+
+
+def assemble_kernel(parts, place, *refs):
+    outs, sems = (refs[2:-1], refs[-1])
+    fetch(parts, True, place, refs[:2], outs, sems)
+    for index, out in enumerate(outs):
+        pltpu.make_async_copy(out, out, sems.at[index]).wait()
 
 
 def assemble(parts, buffers, place):
-    depth = buffers[0].shape[0]
     full = pl.pallas_call(
         functools.partial(assemble_kernel, parts),
-        out_shape=[jax.ShapeDtypeStruct(part.full(depth), jnp.bfloat16) for part in parts],
-        in_specs=in_smem() + hbm(8),
+        out_shape=[bf16(*shape) for shape in weight_shapes(parts, buffers, True)],
+        in_specs=in_smem() + hbm(2),
         out_specs=in_vmem(len(parts)),
-        scratch_shapes=[pltpu.SemaphoreType.DMA((assemble_copies(parts),))],
+        scratch_shapes=[pltpu.SemaphoreType.DMA((len(parts),))],
         compiler_params=pltpu.CompilerParams(vmem_limit_bytes=VMEM_LIMIT),
+        cost_estimate=LIGHT,
         name="assemble",
     )(place, *buffers)
-    return [item.reshape(item.shape[0], -1, item.shape[-1]) for item in full]
+    return [merged(item) for item in full]
+
+
+def merged(array):
+    return array.reshape(array.shape[0], -1, array.shape[-1])
 
 
 def both_cores(own, other, core):
@@ -632,8 +853,12 @@
     return jnp.stack([first, second])
 
 
-def gather_all(groups, pieces, place):
-    depth = grid_sizes()[0]
+def together(*trees):
+    flat, tree = jax.tree.flatten(trees)
+    return jax.tree.unflatten(tree, lax.optimization_barrier(flat))
+
+
+def start_gather(groups, pieces, place):
     core = place[3]
     packed = [pack(parts, items) for parts, items in zip(groups, pieces)]
     halves = [half_rows(parts) for parts in groups]
@@ -645,28 +870,32 @@
     held = []
     offset = 0
     for keep, half in zip(kept, halves):
-        held.append([both_cores(keep, got[offset : offset + half], core)])
+        held.append(both_cores(keep, got[offset : offset + half], core))
         offset += half
+    return held
+
+
+def gather_hop(stage, item):
+    if stage == 0:
+        return [item] + [hop(item, ALONG_Z, step) for step in range(1, grid_sizes()[0])]
+    return [item, hop(item, (NEAR, FAR, ACROSS)[stage - 1])]
+
+
+def pipelined_gather(groups, pieces, place, state, arrived):
     count = len(groups)
-    ready = {}
+    held = start_gather(groups, pieces, place)
     for tick in range(count + 3):
         live = [index for index in range(tick - 3, tick + 1) if 0 <= index < count]
-        flat, tree = jax.tree.flatten([held[index] for index in live])
-        for index, items in zip(live, jax.tree.unflatten(tree, lax.optimization_barrier(flat))):
-            held[index] = items
-        for index in live:
-            items = held[index]
-            stage = tick - index
-            if stage == 0:
-                held[index] = items + [hop(items[0], ALONG_Z, step) for step in range(1, depth)]
-            elif stage == 1:
-                stacked = stack_z(items, place)
-                held[index] = [stacked, hop(stacked, NEAR)]
-            elif stage == 2:
-                held[index] = items + [hop(item, FAR) for item in items]
-            else:
-                held[index] = items + [hop(item, ACROSS) for item in items]
-    return held
+        items, state = together([held[index] for index in live], state)
+        for index, item in zip(live, items):
+            held[index] = gather_hop(tick - index, item)
+        if tick >= 3:
+            state = arrived(tick - 3, held[tick - 3], state)
+        live = [index for index in live if index > tick - 3]
+        items, state = together([held[index] for index in live], state)
+        for index, item in zip(live, items):
+            held[index] = stack_z(item, place) if index == tick else jnp.stack(item)
+    return state
 
 
 def deal_kernel(parts, place, *refs):
@@ -710,8 +939,9 @@
         ],
         in_specs=in_smem() + in_vmem(len(parts)),
         out_specs=hbm(4),
-        scratch_shapes=[pltpu.SemaphoreType.DMA((assemble_copies(parts),))],
+        scratch_shapes=[pltpu.SemaphoreType.DMA((deal_copies(parts),))],
         compiler_params=pltpu.CompilerParams(vmem_limit_bytes=VMEM_LIMIT),
+        cost_estimate=LIGHT,
         name="deal",
     )(place, *arrays)
 
@@ -727,21 +957,29 @@
     return add_up(*terms).astype(jnp.bfloat16)
 
 
-def scatter(parts, arrays, place):
+def scatter_stage(stage, parts, items, place):
     depth = grid_sizes()[0]
-    arrays = [array.reshape(part.full(depth)) for part, array in zip(parts, arrays)]
-    to_core, to_far, to_near, own = deal(parts, arrays, place)
     z, core = (place[0], place[3])
-    from_core = hop(to_core, ACROSS)
-    from_far = hop(low_add(to_far, from_core[1]), FAR)
-    from_near = hop(low_add(to_near, from_core[0, 1], from_far[1]), NEAR)
+    if stage == 0:
+        arrays = [array.reshape(part.full(depth)) for part, array in zip(parts, items)]
+        to_core, *rest = deal(parts, arrays, place)
+        return rest + [hop(to_core, ACROSS)]
+    to_far, to_near, own, from_core = items[:4]
+    if stage == 1:
+        return items + [hop(low_add(to_far, from_core[1]), FAR)]
+    from_far = items[4]
+    if stage == 2:
+        return items + [hop(low_add(to_near, from_core[0, 1], from_far[1]), NEAR)]
+    pick = [own, from_core[0, 0], from_far[0], items[5]]
 
     def mine(at):
-        pick = [own, from_core[0, 0], from_far[0], from_near]
         return [lax.dynamic_index_in_dim(item, at, 0, False) for item in pick]
 
-    along = [hop(low_add(*mine(lax.rem(z + step, depth))), ALONG_Z, step) for step in range(1, depth)]
-    total = add_up(*mine(z), *along)
+    if stage == 3:
+        return items + [
+            hop(low_add(*mine(lax.rem(z + step, depth))), ALONG_Z, step) for step in range(1, depth)
+        ]
+    total = add_up(*mine(z), *items[6:])
     keep = lax.dynamic_index_in_dim(total, core, 0, False)
     other = hop(lax.dynamic_index_in_dim(total, 1 - core, 0, False), ACROSS)
     rows = both_cores(keep, other, core).reshape(-1, WIDTH)
@@ -753,7 +991,22 @@
     return pieces
 
 
-FULL_PRECISION = lax.Precision.HIGHEST
+SCATTER_STAGES = 5
+
+
+def pipelined_scatter(groups, place, state, steps):
+    count = len(groups)
+    held = [None] * count
+    for tick in range(count + SCATTER_STAGES):
+        live = [index for index in range(tick - SCATTER_STAGES, tick) if 0 <= index < count]
+        items, state = together([held[index] for index in live], state)
+        for index, item in zip(live, items):
+            held[index] = scatter_stage(tick - 1 - index, groups[index], item, place)
+        if tick < count:
+            held[tick], state = steps[tick](state)
+    return (held, state)
+
+
 CQL_WEIGHT = 0.05
 BETA_ONE = 0.5
 BETA_TWO = 0.5
@@ -850,54 +1103,6 @@
     array = array + hop(array, (1, 1))
     one, two, three = [hop(array, ALONG_Z, step) for step in (1, 2, 3)]
     return (array + two) + (one + three)
-
-
-def select(scores, game_hot):
-    count = scores.shape[0]
-    picked = jnp.einsum(
-        "ng,ngk->nk",
-        game_hot,
-        scores,
-        precision=FULL_PRECISION,
-    )
-    return picked.reshape(count, ACTIONS, ATOMS)
-
-
-def support():
-    return -10.0 + 20.0 / (ATOMS - 1) * jnp.arange(ATOMS, dtype=jnp.float32)
-
-
-def target_dist(logits_next, next_hot, rewards, discounts, done_flags):
-    chosen = jnp.einsum("na,naz->nz", next_hot, logits_next, precision=FULL_PRECISION)
-    probs = jax.nn.softmax(chosen, axis=-1)
-    atoms = support()
-    spacing = 20.0 / (ATOMS - 1)
-    keep = discounts * (1.0 - done_flags.astype(jnp.float32))
-    moved = jnp.clip(rewards[:, None] + keep[:, None] * atoms[None, :], -10.0, 10.0)
-    kernel = jnp.clip(1.0 - jnp.abs(moved[:, :, None] - atoms[None, None, :]) / spacing, 0.0, 1.0)
-    return jnp.einsum("nj,nji->ni", probs, kernel, precision=FULL_PRECISION)
-
-
-def frame_losses(logits, target, taken_hot, legal_now):
-    logp = jax.nn.log_softmax(logits, axis=-1)
-    action_values = jnp.sum(jnp.exp(logp) * support(), axis=-1)
-    taken_logp = jnp.sum(taken_hot[:, :, None] * logp, axis=1)
-    cross = -jnp.sum(target * taken_logp, axis=-1)
-    masked = jnp.where(legal_now > 0, action_values, -1e30)
-    largest = jnp.max(masked, axis=-1, keepdims=True)
-    spread = jnp.log(jnp.sum(jnp.exp(masked - largest), axis=-1)) + largest[:, 0]
-    return cross + CQL_WEIGHT * (spread - jnp.sum(taken_hot * action_values, axis=-1))
-
-
-def head_scores(stream, pool_w, proj_w, heads_w):
-    low = stream.astype(jnp.bfloat16).reshape(-1, ROWS, D)
-    pooled = jnp.einsum("npc,cp->nc", low, pool_w, preferred_element_type=jnp.float32)
-    pooled = pooled.astype(jnp.bfloat16)
-    before = dot(pooled, proj_w)
-    hidden = jax.nn.silu(before).astype(jnp.bfloat16)
-    scores = jnp.einsum("nk,bkl->nbl", hidden, heads_w, preferred_element_type=jnp.float32)
-    scores = scores.reshape(-1, GAMES, 2 * WIDTH)[:, :, :PLAYS]
-    return (scores, (low, pooled, before, hidden))
 
 
 def lamb_parts(params, grads, first, second):
@@ -965,9 +1170,12 @@
         [squares(params_top, top_cuts), squares(params_blocks, block_cuts).reshape(-1)]
     )
 
-    game_hot = (game_ids[:, None] == jnp.arange(GAMES)[None, :]).astype(jnp.float32)
-    taken_hot = (actions[:, 0:1] == jnp.arange(ACTIONS)[None, :]).astype(jnp.float32)
-    next_hot = (actions[:, 1:2] == jnp.arange(ACTIONS)[None, :]).astype(jnp.float32)
+    count = observed.shape[0]
+    whole = jnp.concatenate([game_ids[:, None], actions], axis=1)
+    whole = jnp.pad(whole, ((0, 8 - count), (0, ROWS - 3)), constant_values=-1)
+    legal = jnp.pad(legal_mask, ((0, 8 - count), (0, ROWS - ACTIONS)), constant_values=1)
+    keep = discounts * (1.0 - done_flags.astype(jnp.float32))
+    real = jnp.pad(jnp.stack([rewards, keep], axis=1), ((0, 8 - count), (0, ROWS - 2)))
 
     low_blocks = params_blocks.astype(jnp.bfloat16)
     own = {}
@@ -985,113 +1193,137 @@
         gain_rows, ((0, TILE - 2 * BLOCKS), (0, WIDTH - gain_width))
     ).reshape(1, TILE, WIDTH)
     block_names = ("w_in", "w_mid", "w_out")
-    keys = []
+
+    def part_of(key):
+        return parts[key[0] if key[0] in parts else key[1]]
+
+    full = {}
+
+    def block_weight(index, name):
+        return merged(full["online", name, index]).reshape(-1, BOT)
+
+    def top_weights(net):
+        return (full[net, "pool"][0], full[net, "proj"][0], full[net, "heads"])
+
+    def keep_ends(group, buffers, state):
+        arrays = assemble([part_of(key) for key in keys[group]], buffers, place) if tuned else buffers
+        full.update(zip(keys[group], arrays))
+        if ("gains",) not in keys[group]:
+            return state
+        gains = full["gains",].reshape(devices, TILE, WIDTH)[:, : 2 * BLOCKS, :gain_width]
+        gains = gains.transpose(1, 0, 2).reshape(2 * BLOCKS, -1).astype(jnp.float32)
+        return state | {"gains": gains}
+
+    def run_block(net, index, group, buffers, state):
+        keep = net == "online"
+        row = index + (BLOCKS if keep else 0)
+        gain = state["gains"][row : row + 1]
+        stream = [state["pixels" if keep else "following"], spread]
+        if index:
+            stream = [state["stream"]]
+        kinds = [part_of(key) for key in keys[group]]
+        out, *kept = block_forward(stream, gain, shift, kinds, buffers, place, keep, tuned)
+        state = state | {"stream": out}
+        if keep:
+            start = kept.pop(0) if index == 0 else stream[0]
+            full.update(zip([(net, name, index) for name in block_names], kept[-3:]))
+            state |= {"kept%d" % index: [start, *kept[:-3]]}
+        elif index == BLOCKS - 1:
+            state |= {"target": head_target(state.pop("stream"), *top_weights(net), whole, real)}
+        return state
+
+    keys, then = ([], [])
+    ends = ("pool", "proj", "heads")
     for net in ("target", "online"):
-        ends = [(net, name) for name in ("pool", "proj")]
-        if net == "target":
-            keys.append([("gains",)] + ends)
-        keys.append([(net, "patch")] + [(net, name, 0) for name in block_names])
-        for index in range(1, BLOCKS):
+        for index in range(BLOCKS):
             keys.append([(net, name, index) for name in block_names])
-        keys.append([(net, "heads")] + (ends if net == "online" else []))
-
-    def part_of(key):
-        return parts[key[0] if key[0] == "gains" else key[1]]
-
-    full = {}
+            if index == 0:
+                keys[-1] = [(net, "patch")] + keys[-1]
+            then.append(functools.partial(run_block, net, index))
+    keys = [[("gains",)] + [("target", name) for name in ends]] + keys
+    keys.append([("online", name) for name in ends])
+    then = [keep_ends, *then, keep_ends]
+
+    def arrived(group, buffers, state):
+        return then[group](group, buffers, dict(state))
+
+    state = {"following": frame_rows(following), "pixels": frame_rows(observed)}
+    pieces = [[own[key] for key in group] for group in keys]
     if tuned:
         groups = [[part_of(key) for key in group] for group in keys]
-        held = gather_all(groups, [[own[key] for key in group] for group in keys], place)
-        for group, kinds, buffers in zip(keys, groups, held):
-            full |= dict(zip(group, assemble(kinds, buffers, place)))
+        state = pipelined_gather(groups, pieces, place, state, arrived)
     else:
-        for key, piece in own.items():
-            full[key] = plain_gather(piece)
-    gains = full["gains",].reshape(devices, TILE, WIDTH)[:, : 2 * BLOCKS, :gain_width]
-    gains = gains.transpose(1, 0, 2).reshape(2 * BLOCKS, -1).astype(jnp.float32)
-
-    def block_weights(net, index):
-        w_in, w_mid, w_out = [full[net, name, index] for name in block_names]
-        return (w_in[0], w_mid[0], w_out.reshape(D, BOT))
-
-    def top_weights(net):
-        return (full[net, "pool"][0], full[net, "proj"][0], full[net, "heads"])
-
-    stream = embed(frame_rows(following), spread, full["target", "patch"])
-    for index in range(BLOCKS):
-        stream = block_forward(
-            stream, *block_weights("target", index), gains[index : index + 1], shift, False
-        )[0]
-    target_scores, ignored = head_scores(stream, *top_weights("target"))
-    target = target_dist(select(target_scores, game_hot), next_hot, rewards, discounts, done_flags)
-
-    pixels = frame_rows(observed)
-    stream = embed(pixels, spread, full["online", "patch"])
-    kept = []
-    for index in range(BLOCKS):
-        weights = block_weights("online", index)
-        gain = gains[BLOCKS + index : BLOCKS + index + 1]
-        out, hid_one, hid_two, hid_three, rstd = block_forward(stream, *weights, gain, shift, True)
-        kept.append((stream, hid_one, hid_two, hid_three, rstd, weights, gain))
-        stream = out
-    pool_w, proj_w, heads_w = top_weights("online")
-    scores, (low, pooled, before, hidden) = head_scores(stream, pool_w, proj_w, heads_w)
-
-    def objective(scores_in):
-        return jnp.sum(frame_losses(select(scores_in, game_hot), target, taken_hot, legal_mask))
-
-    loss_part, back_loss = jax.vjp(objective, scores)
-    grad_scores = back_loss(jnp.float32(1.0 / frames_all))[0].astype(jnp.bfloat16)
-    grad_scores = jnp.pad(grad_scores, ((0, 0), (0, 0), (0, 2 * WIDTH - PLAYS)))
-    grad_scores = grad_scores.reshape(-1, 2 * GAMES, WIDTH)
-    grads = {}
-    grads["heads",] = jnp.einsum(
-        "nk,nbl->bkl", hidden, grad_scores, preferred_element_type=jnp.float32
-    ).astype(jnp.bfloat16)
-    grad_hidden = jnp.einsum(
-        "nbl,bkl->nk", grad_scores, heads_w, preferred_element_type=jnp.float32
-    )
-    grad_before = jax.vjp(jax.nn.silu, before)[1](grad_hidden)[0].astype(jnp.bfloat16)
-    grads["proj",] = dot_rows(pooled, grad_before).astype(jnp.bfloat16)[None]
-    grad_pooled = dot_lanes(grad_before, proj_w).astype(jnp.bfloat16)
-    grads["pool",] = jnp.einsum(
-        "npc,nc->cp", low, grad_pooled, preferred_element_type=jnp.float32
-    ).astype(jnp.bfloat16)[None]
-    grad_stream = jnp.einsum(
-        "nc,cp->npc", grad_pooled, pool_w, preferred_element_type=jnp.float32
-    ).reshape(-1, D)
-
-    dgains = [None] * BLOCKS
-    for index in reversed(range(BLOCKS)):
-        stream, hid_one, hid_two, hid_three, rstd, weights, gain = kept[index]
-        w_in, w_mid, w_out = weights
-        dres, dsecond, dw_out, late = back_out(
-            grad_stream, stream, hid_two, hid_three, rstd, w_out, gain
+        for group, items in enumerate(pieces):
+            state = arrived(group, [plain_gather(item) for item in items], state)
+
+    def loss_step(state):
+        loss, dheads, dproj, dpool, dstream = head_loss(
+            state.pop("stream"), *top_weights("online"), state.pop("target"), whole, legal, frames_all
         )
-        dfirst, dw_mid, early = back_mid(dsecond, hid_one, rstd, w_mid, gain, shift)
-        dw_in, grad_stream = back_in(dfirst, stream, dres, w_in)
-        dgains[index] = jnp.concatenate([early, late], axis=1)
-        grads["w_in", index] = dw_in[None]
-        grads["w_mid", index] = dw_mid[None]
-        grads["w_out", index] = dw_out.reshape(D // BOT, BOT, BOT)
-    grads["patch",] = embed_back(pixels, spread, grad_stream)
-    dgains = jnp.concatenate(dgains).reshape(BLOCKS, devices, gain_width).transpose(1, 0, 2)
-    dgains = jnp.pad(dgains, ((0, 0), (0, TILE - BLOCKS), (0, WIDTH - gain_width)))
-    grads["gains",] = dgains.reshape(1, -1, WIDTH).astype(jnp.bfloat16)
+        state |= {"loss": loss[0, 0], "pool": dpool[None], "grad": dstream}
+        return ([dheads, dproj[None]], state)
+
+    def back_out_step(index, state):
+        stream, hid_one, hid_two, hid_three, rstd = state["kept%d" % index]
+        gain = state["gains"][BLOCKS + index : BLOCKS + index + 1]
+        dres, dlow, dw_out, late = back_out(
+            state["grad"], stream, hid_two, hid_three, rstd, block_weight(index, "w_out"), gain
+        )
+        state = state | {"grad": dres, "low": dlow, "late%d" % index: late}
+        return (dw_out.reshape(D // BOT, BOT, BOT), state)
+
+    def back_mid_step(index, state):
+        stream, hid_one, hid_two, hid_three, rstd = state["kept%d" % index]
+        gain = state["gains"][BLOCKS + index : BLOCKS + index + 1]
+        dlow, dw_mid, early = back_mid(
+            state["low"], hid_one, rstd, block_weight(index, "w_mid"), gain, shift
+        )
+        return ([dw_mid[None]], state | {"low": dlow, "early%d" % index: early})
+
+    def back_in_step(index, state):
+        stream = state.pop("kept%d" % index)[0]
+        dw_in, dx = back_in(state["low"], stream, state["grad"], block_weight(index, "w_in"))
+        return (dw_in[None], state | {"grad": dx})
+
+    def first_step(state):
+        dw_out, state = back_out_step(BLOCKS - 1, dict(state))
+        return ([dw_out, state.pop("pool")], state)
+
+    def between_step(index, state):
+        dw_in, state = back_in_step(index, dict(state))
+        dw_out, state = back_out_step(index - 1, state)
+        return ([dw_in, dw_out], state)
+
+    def last_step(state):
+        dw_in, state = back_in_step(0, dict(state))
+        dpatch = embed_back(state.pop("pixels"), spread, state.pop("grad"))
+        dgains = [
+            jnp.concatenate([state.pop("early%d" % index), state.pop("late%d" % index)], axis=1)
+            for index in range(BLOCKS)
+        ]
+        dgains = jnp.concatenate(dgains).reshape(BLOCKS, devices, gain_width).transpose(1, 0, 2)
+        dgains = jnp.pad(dgains, ((0, 0), (0, TILE - BLOCKS), (0, WIDTH - gain_width)))
+        return ([dw_in, dpatch, dgains.reshape(1, -1, WIDTH).astype(jnp.bfloat16)], state)
 
     keys = [[("heads",), ("proj",)], [("w_out", BLOCKS - 1), ("pool",)]]
+    steps = [lambda state: loss_step(dict(state)), first_step]
     for index in reversed(range(BLOCKS)):
         keys.append([("w_mid", index)])
+        steps.append(functools.partial(back_mid_step, index))
         keys.append([("w_in", index)])
         keys[-1] += [("w_out", index - 1)] if index else [("patch",), ("gains",)]
+        steps.append(functools.partial(between_step, index) if index else last_step)
     mine = {}
-    for group in keys:
-        arrays = [grads[key] for key in group]
-        if tuned:
-            sums = scatter([parts[key[0]] for key in group], arrays, place)
-        else:
-            sums = [plain_scatter(array) for array in arrays]
-        mine |= dict(zip(group, sums))
+    if tuned:
+        groups = [[parts[key[0]] for key in group] for group in keys]
+        sums, state = pipelined_scatter(groups, place, state, steps)
+        for group, items in zip(keys, sums):
+            mine.update(zip(group, items))
+    else:
+        for group, step in zip(keys, steps):
+            arrays, state = step(state)
+            mine.update(zip(group, [plain_scatter(array) for array in arrays]))
+    loss_part = state["loss"]
     grad_top = flat_top(*[mine[name,] for name in ("patch", "pool", "proj", "heads")])
     grad_blocks = jnp.stack(
         [

time: 850 us -> 762 us (0.90)
  waiting for transfers between devices: 219 us -> 168 us
  other arithmetic: 91.4 us -> 120 us
  Pallas kernels: 256 us -> 230 us
  matrix products: 25.3 us -> 0 us
  starting transfers between devices: 150 us -> 134 us
    ppermute x119 -> x85, waiting for transfers between devices: 219 us -> 168 us  [hop(): return lax.ppermute(array, AXES, pairs)]
    another operation x6 -> x18, other arithmetic: 2.27 us -> 34.9 us  [the longest x12 34.2 us: pipelined_gather(): held[index] = stack_z(item, place) if index == tick else jnp.stack(item)]
    pallas_call x13 -> x8, Pallas kernels: 137 us -> 111 us  [the longest x4 74.4 us: block_forward(): pl.pallas_call(functools.partial(forward_kernel, count, keep, parts, tune...]
    dot_general x13 -> x0, matrix products: 25.3 us -> none  [the longest x2 9.09 us: head_scores(): jnp.einsum('npc,cp->nc', low, pool_w, preferred_element_type=jnp.float32)]
    reshape x9 -> x1, local copies, waits for them, and re-layouts: 18.6 us -> 0.09 us  [last_step(): jnp.concatenate(dgains).reshape(BLOCKS, devices, gain_width)]
    ppermute x119 -> x85, starting transfers between devices: 150 us -> 134 us  [hop(): return lax.ppermute(array, AXES, pairs)]
    slice x22 -> x43, local copies, waits for them, and re-layouts: 16.7 us -> 29.6 us  [the longest x30 20 us: scatter_stage(): pick = [own, from_core[0, 0], from_far[0], items[5]]]
    convert_element_type x18, other arithmetic: 27.8 us -> 37 us  [low_add(): return add_up(*terms).astype(jnp.bfloat16)]
  transfers between devices with their start and end apart: 119 -> 85, of which waited for: 47 -> 34; matrix products, arithmetic and copies ran while one was open for 14% -> 12% of each run, Pallas kernels for 27% -> 22%
where the time goes in v3:
time: 762 us; the launch traced here: 751 us
  Pallas kernels  230 us (30%)
  waiting for transfers between devices  168 us (22%)
  starting transfers between devices  134 us (18%)
  other arithmetic  120 us (16%)
  local copies, waits for them, and re-layouts  96.2 us (13%)
    ppermute x85, waiting for transfers between devices, hop(): return lax.ppermute(array, AXES, pairs)  168 us
    ppermute x85, starting transfers between devices, hop(): return lax.ppermute(array, AXES, pairs)  134 us
    pallas_call x4, Pallas kernels, block_forward(): pl.pallas_call(functools.partial(forward_kernel, count, keep, parts, tune...  74.4 us
    convert_element_type x18, other arithmetic, low_add(): return add_up(*terms).astype(jnp.bfloat16)  37 us
    another operation x12, other arithmetic, pipelined_gather(): held[index] = stack_z(item, place) if index == tick else jnp.stack(item)  34.2 us
    pallas_call x6, Pallas kernels, deal(): pl.pallas_call(functools.partial(deal_kernel, parts), out_shape=[jax.Shap...  29.7 us
    pallas_call x2, Pallas kernels, back_out(): pl.pallas_call(functools.partial(back_out_kernel, count), out_shape=[f32(...  26.8 us
    pallas_call x2, Pallas kernels, back_mid(): pl.pallas_call(functools.partial(back_mid_kernel, count), out_shape=[bf16...  23.3 us
  transfers between devices with their start and end apart: 85, of which 34 were waited for; matrix products, arithmetic and copies ran while one was open for 12% of the time, Pallas kernels for 22%

profile of v3, /device:TPU:0, one launch (start us, length us, event | category | flops | bytes accessed | tf_op | source)
XLA Modules:
  0.0 751.0 jit_solution(18343943056208040776)
XLA Ops:
  41.2 9.6 %collective-permute-done.2.refs_2_ = bf16[2,112,512]{2,1,0:T(8,128)(2,1)S(1)} collective-permute-done((bf16[2,112,512]{2,1,0:T(8,128)(2,1)S(1)}, bf16[2,112,512]{2,1,0:T(8,128)(2,1)S(1)}, u32[]{:S(2)}, u32[]{:S(2)}) %collective-permute-start.2) | collective-permute-done | bytes 229408 | tf_op jit(solution)/shard_map/ppermute | solution.py:673
  56.0 4.8 collective-permute-start.5
  65.1 6.0 collective-permute-done.5.refs_1_
  71.1 12.8 %collective-permute-done.6.refs_2_ = bf16[2,160,512]{2,1,0:T(8,128)(2,1)S(1)} collective-permute-done((bf16[2,160,512]{2,1,0:T(8,128)(2,1)S(1)}, bf16[2,160,512]{2,1,0:T(8,128)(2,1)S(1)}, u32[]{:S(2)}, u32[]{:S(2)}) %collective-permute-start.6) | collective-permute-done | bytes 327712 | tf_op jit(solution)/shard_map/ppermute | solution.py:673
  91.2 7.4 collective-permute-start.10
  101.4 6.0 collective-permute-done.10.refs_1_
  107.4 11.1 %collective-permute-done.11.refs_2_ = bf16[2,144,512]{2,1,0:T(8,128)(2,1)S(1)} collective-permute-done((bf16[2,144,512]{2,1,0:T(8,128)(2,1)}, bf16[2,144,512]{2,1,0:T(8,128)(2,1)S(1)}, u32[]{:S(2)}, u32[]{:S(2)}) %collective-permute-start.11) | collective-permute-done | bytes 294944 | tf_op jit(solution)/shard_map/ppermute | solution.py:673
  121.7 4.8 collective-permute-done.8
  136.2 7.5 collective-permute-start.15
  144.4 5.0 collective-permute-start.17
  149.4 6.9 assemble.2
  158.1 7.8 %collective-permute-done.16.refs_2_ = bf16[2,160,512]{2,1,0:T(8,128)(2,1)} collective-permute-done((bf16[2,160,512]{2,1,0:T(8,128)(2,1)S(1)}, bf16[2,160,512]{2,1,0:T(8,128)(2,1)}, u32[]{:S(2)}, u32[]{:S(2)}) %collective-permute-start.16) | collective-permute-done | bytes 327712 | tf_op jit(solution)/shard_map/ppermute | solution.py:673
  165.9 13.5 %collective-permute-done.13 = bf16[2,4,2,160,512]{4,3,2,1,0:T(8,128)(2,1)} collective-permute-done((bf16[2,4,2,160,512]{4,3,2,1,0:T(8,128)(2,1)}, bf16[2,4,2,160,512]{4,3,2,1,0:T(8,128)(2,1)}, u32[]{:S(2)}, u32[]{:S(2)}) %collective-permute-start.13) | collective-permute-done | bytes 2621472 | tf_op jit(solution)/shard_map/ppermute | solution.py:673
  193.2 7.5 %collective-permute-start.21 = (bf16[2,144,512]{2,1,0:T(8,128)(2,1)}, bf16[2,144,512]{2,1,0:T(8,128)(2,1)S(1)}, u32[]{:S(2)}, u32[]{:S(2)}) collective-permute-start(bf16[2,144,512]{2,1,0:T(8,128)(2,1)} %get-tuple-element.523.refs_0_), channel_id=1, source_target_pairs={{0,8},{1,9},{2,10},{3,11},{4,12},{5,13},{6,14},{7,15},{8,16},{9,17... | collective-permute-start | bytes 884744 | tf_op jit(solution)/shard_map/ppermute | solution.py:673
  201.5 4.9 collective-permute-start.23
  209.0 18.0 %block_forward.4.refs_1_ = f32[384,2048]{1,0:T(8,128)} custom-call(s32[4]{0:T(128)} %pad_add_fusion.1.place.refs_0_, bf16[384,256]{1,0:T(8,128)(2,1)} %bitcast.664, bf16[2,256,512]{2,1,0:T(8,128)(2,1)} %add_convert_fusion.refs_2_.spread, f32[1,6144]{1,0:T(1,128)} %slice.441.refs_3_, bf16[1152,128]{1,0:T(8,128)(2,1)} %convert_element_type.935.refs_4_.refs_3_.refs_5_, ...), custom_call_target="tpu_custom_call" | custom-call | flops 1024 | bytes 1024 | tf_op jit(solution)/shard_map/block_forward/pallas_call | solution.py:249
  227.0 6.0 collective-permute-done.19
  246.3 7.5 collective-permute-start.27
  254.5 5.6 collective-permute-start.29
  262.5 17.1 %block_forward.5.stream = f32[384,2048]{1,0:T(8,128)} custom-call(s32[4]{0:T(128)} %pad_add_fusion.1.place.refs_0_, f32[384,2048]{1,0:T(8,128)} %block_forward.4.refs_1_, f32[1,6144]{1,0:T(1,128)} %slice.443.refs_2_, bf16[1152,128]{1,0:T(8,128)(2,1)} %convert_element_type.935.refs_4_.refs_3_.refs_5_, ...), custom_call_target="tpu_custom_call" | custom-call | flops 1024 | bytes 1024 | tf_op jit(solution)/shard_map/block_forward/pallas_call | solution.py:249
  279.7 7.2 head_target.1.refs_4_
  301.6 6.0 collective-permute-done.33.refs_6_
  307.6 20.6 %block_forward.6 = (f32[384,2048]{1,0:T(8,128)}, f32[384,2048]{1,0:T(8,128)}, f32[384,512]{1,0:T(8,128)}, f32[384,512]{1,0:T(8,128)}, f32[384,2048]{1,0:T(8,128)...) custom-call(s32[4]{0:T(128)} %pad_add_fusion.1.place.refs_0_, ...), custom_call_target="tpu_custom_call" | custom-call | flops 1024 | bytes 1024 | tf_op jit(solution)/shard_map/block_forward/pallas_call | solution.py:249
  328.3 9.2 %collective-permute-done.31 = bf16[2,4,2,144,512]{4,3,2,1,0:T(8,128)(2,1)} collective-permute-done((bf16[2,4,2,144,512]{4,3,2,1,0:T(8,128)(2,1)S(1)}, bf16[2,4,2,144,512]{4,3,2,1,0:T(8,128)(2,1)}, u32[]{:S(2)}, u32[]{:S(2)}) %collective-permute-start.31) | collective-permute-done | bytes 2359328 | tf_op jit(solution)/shard_map/ppermute | solution.py:673
  346.7 6.0 collective-permute-done.35.refs_5_
  352.7 18.7 %block_forward.7 = (f32[384,2048]{1,0:T(8,128)}, f32[384,512]{1,0:T(8,128)}, f32[384,512]{1,0:T(8,128)}, f32[384,2048]{1,0:T(8,128)}, f32[8,3072]{1,0:T(8,128)},...) custom-call(s32[4]{0:T(128)} %pad_add_fusion.1.place.refs_0_, ...), custom_call_target="tpu_custom_call" | custom-call | flops 1024 | bytes 1024 | tf_op jit(solution)/shard_map/block_forward/pallas_call | solution.py:249
  375.9 5.8 collective-permute-done.36.refs_1_
  381.7 6.6 assemble.3
  388.3 16.2 %head_loss.1 = (f32[1,1]{1,0:T(1,128)}, bf16[8,512,512]{2,1,0:T(8,128)(2,1)}, bf16[2048,512]{1,0:T(8,128)(2,1)}, bf16[2048,128]{1,0:T(8,128)(2,1)}, f32[384,2048]{1,0:T(8,128)}) custom-call(f32[384,2048]{1,0:T(8,128)} %get-tuple-element.626.refs_0_, bf16[2048,128]{1,0:T(8,128)(2,1)} %bitcast.682, bf16[2048,512]{1,0:T(8,128)(2,1)} %bitcast.648, ...), custom_call_target="tpu_custom_call" | custom-call | flops 1024 | bytes 1024 | tf_op jit(solution)/shard_map/head_loss/pallas_call | solution.py:629
  404.5 6.2 deal.6
  411.6 13.4 %back_out.2 = (f32[384,2048]{1,0:T(8,128)}, bf16[384,512]{1,0:T(8,128)(2,1)}, bf16[2048,512]{1,0:T(8,128)(2,1)}, f32[1,5120]{1,0:T(1,128)}) custom-call(f32[384,2048]{1,0:T(8,128)} %get-tuple-element.655.refs_0_, f32[384,2048]{1,0:T(8,128)} %get-tuple-element.717.refs_1_, f32[384,512]{1,0:T(8,128)} %get-tuple-element.657.refs_2_, ...), custom_call_target="tpu_custom_call" | custom-call | flops 1024 | bytes 1024 | tf_op jit(solution)/shard_map/back_out/pallas_call | solution.py:344
  433.4 11.7 %back_mid.2 = (bf16[384,512]{1,0:T(8,128)(2,1)}, bf16[4608,512]{1,0:T(8,128)(2,1)}, f32[1,1024]{1,0:T(1,128)}) custom-call(bf16[384,512]{1,0:T(8,128)(2,1)} %get-tuple-element.685.refs_0_, f32[384,512]{1,0:T(8,128)} %get-tuple-element.686.refs_1_, f32[8,3072]{1,0:T(8,128)} %get-tuple-element.687.refs_4_.refs_2_, bf16[4608,512]{1,0:T(8,128)(2,1)} %bitcast.626, ...), custom_call_target="tpu_custom_call" | custom-call | flops 1024 | bytes 1024 | tf_op jit(solution)/shard_map/back_mid/pallas_call | solution.py:404
  445.0 7.8 %collective-permute-done.38 = bf16[2,4,2,96,512]{4,3,2,1,0:T(8,128)(2,1)S(1)} collective-permute-done((bf16[2,4,2,96,512]{4,3,2,1,0:T(8,128)(2,1)}, bf16[2,4,2,96,512]{4,3,2,1,0:T(8,128)(2,1)S(1)}, u32[]{:S(2)}, u32[]{:S(2)}) %collective-permute-start.38) | collective-permute-done | bytes 1572896 | tf_op jit(solution)/shard_map/ppermute | solution.py:673
  452.9 5.4 deal.8
  464.7 8.2 %back_in.2 = (bf16[2048,512]{1,0:T(8,128)(2,1)}, f32[384,2048]{1,0:T(8,128)}) custom-call(bf16[384,512]{1,0:T(8,128)(2,1)} %get-tuple-element.716.refs_0_, f32[384,2048]{1,0:T(8,128)} %get-tuple-element.717.refs_1_, f32[384,2048]{1,0:T(8,128)} %get-tuple-element.718.refs_2_, bf16[2048,512]{1,0:T(8,128)(2,1)} %bitcast.646), custom_call_target="tpu_custom_call" | custom-call | flops 1024 | bytes 1024 | tf_op jit(solution)/shard_map/back_in/pallas_call | solution.py:437
  473.6 13.3 %back_out.3 = (f32[384,2048]{1,0:T(8,128)}, bf16[384,512]{1,0:T(8,128)(2,1)}, bf16[2048,512]{1,0:T(8,128)(2,1)}, f32[1,5120]{1,0:T(1,128)}) custom-call(f32[384,2048]{1,0:T(8,128)} %get-tuple-element.721.refs_0_, f32[384,2048]{1,0:T(8,128)} %get-tuple-element.788.refs_1_, f32[384,512]{1,0:T(8,128)} %get-tuple-element.723.refs_2_, ...), custom_call_target="tpu_custom_call" | custom-call | flops 1024 | bytes 1024 | tf_op jit(solution)/shard_map/back_out/pallas_call | solution.py:344
  487.0 5.4 deal.9
  500.5 7.5 collective-permute-start.43
  515.7 11.6 %back_mid.3 = (bf16[384,512]{1,0:T(8,128)(2,1)}, bf16[4608,512]{1,0:T(8,128)(2,1)}, f32[1,1024]{1,0:T(1,128)}) custom-call(bf16[384,512]{1,0:T(8,128)(2,1)} %get-tuple-element.755.refs_0_, f32[384,512]{1,0:T(8,128)} %get-tuple-element.756.refs_1_, f32[8,3072]{1,0:T(8,128)} %get-tuple-element.757.refs_4_.refs_2_, bf16[4608,512]{1,0:T(8,128)(2,1)} %bitcast.625, ...), custom_call_target="tpu_custom_call" | custom-call | flops 1024 | bytes 1024 | tf_op jit(solution)/shard_map/back_mid/pallas_call | solution.py:404
  549.0 8.4 %back_in.3 = (bf16[2048,512]{1,0:T(8,128)(2,1)}, f32[384,2048]{1,0:T(8,128)}) custom-call(bf16[384,512]{1,0:T(8,128)(2,1)} %get-tuple-element.787.refs_0_, f32[384,2048]{1,0:T(8,128)} %get-tuple-element.788.refs_1_, f32[384,2048]{1,0:T(8,128)} %get-tuple-element.789.refs_2_, bf16[2048,512]{1,0:T(8,128)(2,1)} %bitcast.643), custom_call_target="tpu_custom_call" | custom-call | flops 1024 | bytes 1024 | tf_op jit(solution)/shard_map/back_in/pallas_call | solution.py:437
  598.8 6.9 collective-permute-done.56
  630.6 5.4 collective-permute-done.62
  653.6 6.6 collective-permute-done.67
  674.9 4.9 collective-permute-done.71
  689.1 5.4 multiply_add_fusion.2
  696.5 6.3 concatenate.73
  708.2 5.9 concatenate.76
  733.5 7.6 %multiply_add_fusion.1 = (f32[2,139456]{1,0:T(2,128)}, f32[2,139456]{1,0:T(2,128)S(1)}) fusion(f32[2,139456]{1,0:T(2,128)S(1)} %copy-done.27, f32[2,139456]{1,0:T(2,128)S(1)} %copy-done.1, f32[2,139456]{1,0:T(2,128)S(1)} %get-tuple-element.915, f32[2,192]{1,0:T(2,128)S(1)} %broadcast_in_dim.138, f32[2,32768]{1,0:T(2,128)S(1)} %broadcast_in_dim.136, ...), kind=kLoop, calls=%fused_computation.42 | loop fusion | flops 2510208 | bytes 6693888 | tf_op jit(solution)/shard_map/add | solution.py:1356
  (596 shorter events, 333.9 us)
Async XLA Ops:
  32.6 18.2 %collective-permute-start.2 = (bf16[2,112,512]{2,1,0:T(8,128)(2,1)S(1)}, bf16[2,112,512]{2,1,0:T(8,128)(2,1)S(1)}, u32[]{:S(2)}, u32[]{:S(2)}) collective-permute-start(bf16[2,112,512]{2,1,0:T(8,128)(2,1)S(1)} %get-tuple-element.461.refs_0_), channel_id=1, source_target_pairs={{0,16},{1,17},{2,18},{3,19},{4,20},{5,21},{6,22},{7,23},{8,24},{9,... | collective-permute-start | bytes 688136 | tf_op jit(solution)/shard_map/ppermute | solution.py:673
  35.1 16.3 %collective-permute-start.3 = (bf16[2,112,512]{2,1,0:T(8,128)(2,1)S(1)}, bf16[2,112,512]{2,1,0:T(8,128)(2,1)}, u32[]{:S(2)}, u32[]{:S(2)}) collective-permute-start(bf16[2,112,512]{2,1,0:T(8,128)(2,1)S(1)} %get-tuple-element.461.refs_0_), channel_id=1, source_target_pairs={{0,24},{1,25},{2,26},{3,27},{4,28},{5,29},{6,30},{7,31},{8,0},{9,1... | collective-permute-start | bytes 688136 | tf_op jit(solution)/shard_map/ppermute | solution.py:673
  54.4 29.5 %collective-permute-start.4 = (bf16[4,2,112,512]{3,2,1,0:T(8,128)(2,1)}, bf16[4,2,112,512]{3,2,1,0:T(8,128)(2,1)}, u32[]{:S(2)}, u32[]{:S(2)}) collective-permute-start(bf16[4,2,112,512]{3,2,1,0:T(8,128)(2,1)} %stack_z.6), channel_id=1, source_target_pairs={{0,2},{1,5},{2,0},{3,7},{4,6},{5,1},{6,4},{7,3},{8,10},{9,13},{10,... | collective-permute-start | bytes 2752520 | tf_op jit(solution)/shard_map/ppermute | solution.py:673
  56.0 15.2 %collective-permute-start.5 = (bf16[2,160,512]{2,1,0:T(8,128)(2,1)S(1)}, bf16[2,160,512]{2,1,0:T(8,128)(2,1)S(1)}, u32[]{:S(2)}, u32[]{:S(2)}) collective-permute-start(bf16[2,160,512]{2,1,0:T(8,128)(2,1)S(1)} %get-tuple-element.473.refs_0_), channel_id=1, source_target_pairs={{0,8},{1,9},{2,10},{3,11},{4,12},{5,13},{6,14},{7,15},{8,16},{9,17... | collective-permute-start | bytes 983048 | tf_op jit(solution)/shard_map/ppermute | solution.py:673
  60.8 23.1 %collective-permute-start.6 = (bf16[2,160,512]{2,1,0:T(8,128)(2,1)S(1)}, bf16[2,160,512]{2,1,0:T(8,128)(2,1)S(1)}, u32[]{:S(2)}, u32[]{:S(2)}) collective-permute-start(bf16[2,160,512]{2,1,0:T(8,128)(2,1)S(1)} %get-tuple-element.473.refs_0_), channel_id=1, source_target_pairs={{0,16},{1,17},{2,18},{3,19},{4,20},{5,21},{6,22},{7,23},{8,24},{9,... | collective-permute-start | bytes 983048 | tf_op jit(solution)/shard_map/ppermute | solution.py:673
  63.0 21.0 %collective-permute-start.7 = (bf16[2,160,512]{2,1,0:T(8,128)(2,1)S(1)}, bf16[2,160,512]{2,1,0:T(8,128)(2,1)S(1)}, u32[]{:S(2)}, u32[]{:S(2)}) collective-permute-start(bf16[2,160,512]{2,1,0:T(8,128)(2,1)S(1)} %get-tuple-element.473.refs_0_), channel_id=1, source_target_pairs={{0,24},{1,25},{2,26},{3,27},{4,28},{5,29},{6,30},{7,31},{8,0},{9,1... | collective-permute-start | bytes 983048 | tf_op jit(solution)/shard_map/ppermute | solution.py:673
  89.2 37.3 %collective-permute-start.8 = (bf16[2,4,2,112,512]{4,3,2,1,0:T(8,128)(2,1)S(1)}, bf16[2,4,2,112,512]{4,3,2,1,0:T(8,128)(2,1)S(1)}, u32[]{:S(2)}, u32[]{:S(2)}) collective-permute-start(bf16[2,4,2,112,512]{4,3,2,1,0:T(8,128)(2,1)S(1)} %pad_maximum_fusion.10), channel_id=1, source_target_pairs={{0,4},{1,3},{2,6},{3,1},{4,0},{5,7},{6,2},{7,5},{8,12},{9,11},{10,... | collective-permute-start | bytes 5505032 | tf_op jit(solution)/shard_map/ppermute | solution.py:673
  89.7 31.9 %collective-permute-start.9 = (bf16[4,2,160,512]{3,2,1,0:T(8,128)(2,1)}, bf16[4,2,160,512]{3,2,1,0:T(8,128)(2,1)S(1)}, u32[]{:S(2)}, u32[]{:S(2)}) collective-permute-start(bf16[4,2,160,512]{3,2,1,0:T(8,128)(2,1)} %stack_z.7), channel_id=1, source_target_pairs={{0,2},{1,5},{2,0},{3,7},{4,6},{5,1},{6,4},{7,3},{8,10},{9,13},{10,... | collective-permute-start | bytes 3932168 | tf_op jit(solution)/shard_map/ppermute | solution.py:673
  91.2 16.2 %collective-permute-start.10 = (bf16[2,144,512]{2,1,0:T(8,128)(2,1)}, bf16[2,144,512]{2,1,0:T(8,128)(2,1)S(1)}, u32[]{:S(2)}, u32[]{:S(2)}) collective-permute-start(bf16[2,144,512]{2,1,0:T(8,128)(2,1)} %get-tuple-element.488.refs_0_), channel_id=1, source_target_pairs={{0,8},{1,9},{2,10},{3,11},{4,12},{5,13},{6,14},{7,15},{8,16},{9,17... | collective-permute-start | bytes 884744 | tf_op jit(solution)/shard_map/ppermute | solution.py:673
  98.6 20.0 %collective-permute-start.11 = (bf16[2,144,512]{2,1,0:T(8,128)(2,1)}, bf16[2,144,512]{2,1,0:T(8,128)(2,1)S(1)}, u32[]{:S(2)}, u32[]{:S(2)}) collective-permute-start(bf16[2,144,512]{2,1,0:T(8,128)(2,1)} %get-tuple-element.488.refs_0_), channel_id=1, source_target_pairs={{0,16},{1,17},{2,18},{3,19},{4,20},{5,21},{6,22},{7,23},{8,24},{9,... | collective-permute-start | bytes 884744 | tf_op jit(solution)/shard_map/ppermute | solution.py:673
  99.7 18.8 %collective-permute-start.12 = (bf16[2,144,512]{2,1,0:T(8,128)(2,1)}, bf16[2,144,512]{2,1,0:T(8,128)(2,1)S(1)}, u32[]{:S(2)}, u32[]{:S(2)}) collective-permute-start(bf16[2,144,512]{2,1,0:T(8,128)(2,1)} %get-tuple-element.488.refs_0_), channel_id=1, source_target_pairs={{0,24},{1,25},{2,26},{3,27},{4,28},{5,29},{6,30},{7,31},{8,0},{9,1... | collective-permute-start | bytes 884744 | tf_op jit(solution)/shard_map/ppermute | solution.py:673
  134.7 44.7 %collective-permute-start.13 = (bf16[2,4,2,160,512]{4,3,2,1,0:T(8,128)(2,1)}, bf16[2,4,2,160,512]{4,3,2,1,0:T(8,128)(2,1)}, u32[]{:S(2)}, u32[]{:S(2)}) collective-permute-start(bf16[2,4,2,160,512]{4,3,2,1,0:T(8,128)(2,1)} %pad_maximum_fusion.6), channel_id=1, source_target_pairs={{0,4},{1,3},{2,6},{3,1},{4,0},{5,7},{6,2},{7,5},{8,12},{9,11},{10,... | collective-permute-start | bytes 7864328 | tf_op jit(solution)/shard_map/ppermute | solution.py:673
  135.3 30.6 %collective-permute-start.14 = (bf16[4,2,144,512]{3,2,1,0:T(8,128)(2,1)}, bf16[4,2,144,512]{3,2,1,0:T(8,128)(2,1)S(1)}, u32[]{:S(2)}, u32[]{:S(2)}) collective-permute-start(bf16[4,2,144,512]{3,2,1,0:T(8,128)(2,1)} %stack_z.8), channel_id=1, source_target_pairs={{0,2},{1,5},{2,0},{3,7},{4,6},{5,1},{6,4},{7,3},{8,10},{9,13},{10,... | collective-permute-start | bytes 3538952 | tf_op jit(solution)/shard_map/ppermute | solution.py:673
  136.2 21.9 %collective-permute-start.15 = (bf16[2,160,512]{2,1,0:T(8,128)(2,1)S(1)}, bf16[2,160,512]{2,1,0:T(8,128)(2,1)S(1)}, u32[]{:S(2)}, u32[]{:S(2)}) collective-permute-start(bf16[2,160,512]{2,1,0:T(8,128)(2,1)S(1)} %get-tuple-element.505.refs_0_), channel_id=1, source_target_pairs={{0,8},{1,9},{2,10},{3,11},{4,12},{5,13},{6,14},{7,15},{8,16},{9,17... | collective-permute-start | bytes 983048 | tf_op jit(solution)/shard_map/ppermute | solution.py:673
  143.7 22.2 %collective-permute-start.16 = (bf16[2,160,512]{2,1,0:T(8,128)(2,1)S(1)}, bf16[2,160,512]{2,1,0:T(8,128)(2,1)}, u32[]{:S(2)}, u32[]{:S(2)}) collective-permute-start(bf16[2,160,512]{2,1,0:T(8,128)(2,1)S(1)} %get-tuple-element.505.refs_0_), channel_id=1, source_target_pairs={{0,16},{1,17},{2,18},{3,19},{4,20},{5,21},{6,22},{7,23},{8,24},{9,... | collective-permute-start | bytes 983048 | tf_op jit(solution)/shard_map/ppermute | solution.py:673
  144.4 21.4 %collective-permute-start.17 = (bf16[2,160,512]{2,1,0:T(8,128)(2,1)S(1)}, bf16[2,160,512]{2,1,0:T(8,128)(2,1)}, u32[]{:S(2)}, u32[]{:S(2)}) collective-permute-start(bf16[2,160,512]{2,1,0:T(8,128)(2,1)S(1)} %get-tuple-element.505.refs_0_), channel_id=1, source_target_pairs={{0,24},{1,25},{2,26},{3,27},{4,28},{5,29},{6,30},{7,31},{8,0},{9,1... | collective-permute-start | bytes 983048 | tf_op jit(solution)/shard_map/ppermute | solution.py:673
  189.9 43.1 %collective-permute-start.19 = (bf16[2,4,2,144,512]{4,3,2,1,0:T(8,128)(2,1)S(1)}, bf16[2,4,2,144,512]{4,3,2,1,0:T(8,128)(2,1)}, u32[]{:S(2)}, u32[]{:S(2)}) collective-permute-start(bf16[2,4,2,144,512]{4,3,2,1,0:T(8,128)(2,1)S(1)} %pad_maximum_fusion.8), channel_id=1, source_target_pairs={{0,4},{1,3},{2,6},{3,1},{4,0},{5,7},{6,2},{7,5},{8,12},{9,11},{10,... | collective-permute-start | bytes 7077896 | tf_op jit(solution)/shard_map/ppermute | solution.py:673
  191.0 36.0 %collective-permute-start.20 = (bf16[4,2,160,512]{3,2,1,0:T(8,128)(2,1)}, bf16[4,2,160,512]{3,2,1,0:T(8,128)(2,1)}, u32[]{:S(2)}, u32[]{:S(2)}) collective-permute-start(bf16[4,2,160,512]{3,2,1,0:T(8,128)(2,1)} %stack_z.9), channel_id=1, source_target_pairs={{0,2},{1,5},{2,0},{3,7},{4,6},{5,1},{6,4},{7,3},{8,10},{9,13},{10,... | collective-permute-start | bytes 3932168 | tf_op jit(solution)/shard_map/ppermute | solution.py:673
  193.2 33.7 %collective-permute-start.21 = (bf16[2,144,512]{2,1,0:T(8,128)(2,1)}, bf16[2,144,512]{2,1,0:T(8,128)(2,1)S(1)}, u32[]{:S(2)}, u32[]{:S(2)}) collective-permute-start(bf16[2,144,512]{2,1,0:T(8,128)(2,1)} %get-tuple-element.523.refs_0_), channel_id=1, source_target_pairs={{0,8},{1,9},{2,10},{3,11},{4,12},{5,13},{6,14},{7,15},{8,16},{9,17... | collective-permute-start | bytes 884744 | tf_op jit(solution)/shard_map/ppermute | solution.py:673
  200.8 26.2 %collective-permute-start.22 = (bf16[2,144,512]{2,1,0:T(8,128)(2,1)}, bf16[2,144,512]{2,1,0:T(8,128)(2,1)}, u32[]{:S(2)}, u32[]{:S(2)}) collective-permute-start(bf16[2,144,512]{2,1,0:T(8,128)(2,1)} %get-tuple-element.523.refs_0_), channel_id=1, source_target_pairs={{0,16},{1,17},{2,18},{3,19},{4,20},{5,21},{6,22},{7,23},{8,24},{9,... | collective-permute-start | bytes 884744 | tf_op jit(solution)/shard_map/ppermute | solution.py:673
  201.5 25.5 %collective-permute-start.23 = (bf16[2,144,512]{2,1,0:T(8,128)(2,1)}, bf16[2,144,512]{2,1,0:T(8,128)(2,1)}, u32[]{:S(2)}, u32[]{:S(2)}) collective-permute-start(bf16[2,144,512]{2,1,0:T(8,128)(2,1)} %get-tuple-element.523.refs_0_), channel_id=1, source_target_pairs={{0,24},{1,25},{2,26},{3,27},{4,28},{5,29},{6,30},{7,31},{8,0},{9,1... | collective-permute-start | bytes 884744 | tf_op jit(solution)/shard_map/ppermute | solution.py:673
  244.0 44.7 %collective-permute-start.25 = (bf16[2,4,2,160,512]{4,3,2,1,0:T(8,128)(2,1)}, bf16[2,4,2,160,512]{4,3,2,1,0:T(8,128)(2,1)}, u32[]{:S(2)}, u32[]{:S(2)}) collective-permute-start(bf16[2,4,2,160,512]{4,3,2,1,0:T(8,128)(2,1)} %pad_maximum_fusion.7), channel_id=1, source_target_pairs={{0,4},{1,3},{2,6},{3,1},{4,0},{5,7},{6,2},{7,5},{8,12},{9,11},{10,... | collective-permute-start | bytes 7864328 | tf_op jit(solution)/shard_map/ppermute | solution.py:673
  244.5 42.4 %collective-permute-start.26 = (bf16[4,2,144,512]{3,2,1,0:T(8,128)(2,1)}, bf16[4,2,144,512]{3,2,1,0:T(8,128)(2,1)S(1)}, u32[]{:S(2)}, u32[]{:S(2)}) collective-permute-start(bf16[4,2,144,512]{3,2,1,0:T(8,128)(2,1)} %stack_z.10), channel_id=1, source_target_pairs={{0,2},{1,5},{2,0},{3,7},{4,6},{5,1},{6,4},{7,3},{8,10},{9,13},{10,... | collective-permute-start | bytes 3538952 | tf_op jit(solution)/shard_map/ppermute | solution.py:673
  246.3 40.6 %collective-permute-start.27 = (bf16[2,112,512]{2,1,0:T(8,128)(2,1)S(1)}, bf16[2,112,512]{2,1,0:T(8,128)(2,1)S(1)}, u32[]{:S(2)}, u32[]{:S(2)}) collective-permute-start(bf16[2,112,512]{2,1,0:T(8,128)(2,1)S(1)} %copy-done.29), channel_id=1, source_target_pairs={{0,8},{1,9},{2,10},{3,11},{4,12},{5,13},{6,14},{7,15},{8,16},{9,17... | collective-permute-start | bytes 688136 | tf_op jit(solution)/shard_map/ppermute | solution.py:673
  253.8 33.1 %collective-permute-start.28 = (bf16[2,112,512]{2,1,0:T(8,128)(2,1)S(1)}, bf16[2,112,512]{2,1,0:T(8,128)(2,1)S(1)}, u32[]{:S(2)}, u32[]{:S(2)}) collective-permute-start(bf16[2,112,512]{2,1,0:T(8,128)(2,1)S(1)} %copy-done.29), channel_id=1, source_target_pairs={{0,16},{1,17},{2,18},{3,19},{4,20},{5,21},{6,22},{7,23},{8,24},{9,... | collective-permute-start | bytes 688136 | tf_op jit(solution)/shard_map/ppermute | solution.py:673
  254.5 32.4 %collective-permute-start.29 = (bf16[2,112,512]{2,1,0:T(8,128)(2,1)S(1)}, bf16[2,112,512]{2,1,0:T(8,128)(2,1)S(1)}, u32[]{:S(2)}, u32[]{:S(2)}) collective-permute-start(bf16[2,112,512]{2,1,0:T(8,128)(2,1)S(1)} %copy-done.29), channel_id=1, source_target_pairs={{0,24},{1,25},{2,26},{3,27},{4,28},{5,29},{6,30},{7,31},{8,0},{9,1... | collective-permute-start | bytes 688136 | tf_op jit(solution)/shard_map/ppermute | solution.py:673
  298.6 38.8 %collective-permute-start.31 = (bf16[2,4,2,144,512]{4,3,2,1,0:T(8,128)(2,1)S(1)}, bf16[2,4,2,144,512]{4,3,2,1,0:T(8,128)(2,1)}, u32[]{:S(2)}, u32[]{:S(2)}) collective-permute-start(bf16[2,4,2,144,512]{4,3,2,1,0:T(8,128)(2,1)S(1)} %pad_maximum_fusion.9), channel_id=1, source_target_pairs={{0,4},{1,3},{2,6},{3,1},{4,0},{5,7},{6,2},{7,5},{8,12},{9,11},{10,... | collective-permute-start | bytes 7077896 | tf_op jit(solution)/shard_map/ppermute | solution.py:673
  299.2 29.1 %collective-permute-start.32 = (bf16[4,2,112,512]{3,2,1,0:T(8,128)(2,1)}, bf16[4,2,112,512]{3,2,1,0:T(8,128)(2,1)}, u32[]{:S(2)}, u32[]{:S(2)}) collective-permute-start(bf16[4,2,112,512]{3,2,1,0:T(8,128)(2,1)} %stack_z.11), channel_id=1, source_target_pairs={{0,2},{1,5},{2,0},{3,7},{4,6},{5,1},{6,4},{7,3},{8,10},{9,13},{10,... | collective-permute-start | bytes 2752520 | tf_op jit(solution)/shard_map/ppermute | solution.py:673
  344.7 26.7 %collective-permute-start.34 = (bf16[2,4,2,112,512]{4,3,2,1,0:T(8,128)(2,1)}, bf16[2,4,2,112,512]{4,3,2,1,0:T(8,128)(2,1)S(1)}, u32[]{:S(2)}, u32[]{:S(2)}) collective-permute-start(bf16[2,4,2,112,512]{4,3,2,1,0:T(8,128)(2,1)} %pad_maximum_fusion.11), channel_id=1, source_target_pairs={{0,4},{1,3},{2,6},{3,1},{4,0},{5,7},{6,2},{7,5},{8,12},{9,11},{10,... | collective-permute-start | bytes 5505032 | tf_op jit(solution)/shard_map/ppermute | solution.py:673
  428.6 16.4 %collective-permute-start.39 = (bf16[2,2,4,2,48,512]{5,4,3,2,1,0:T(8,128)(2,1)}, bf16[2,2,4,2,48,512]{5,4,3,2,1,0:T(8,128)(2,1)}, u32[]{:S(2)}, u32[]{:S(2)}) collective-permute-start(bf16[2,2,4,2,48,512]{5,4,3,2,1,0:T(8,128)(2,1)} %get-tuple-element.684), channel_id=1, source_target_pairs={{0,1},{1,0},{2,3},{3,2},{4,5},{5,4},{6,7},{7,6},{8,9},{9,8},{10,11... | collective-permute-start | bytes 4718600 | tf_op jit(solution)/shard_map/ppermute | solution.py:673
  432.2 20.6 %collective-permute-start.38 = (bf16[2,4,2,96,512]{4,3,2,1,0:T(8,128)(2,1)}, bf16[2,4,2,96,512]{4,3,2,1,0:T(8,128)(2,1)S(1)}, u32[]{:S(2)}, u32[]{:S(2)}) collective-permute-start(bf16[2,4,2,96,512]{4,3,2,1,0:T(8,128)(2,1)} %fusion), channel_id=1, source_target_pairs={{0,4},{1,3},{2,6},{3,1},{4,0},{5,7},{6,2},{7,5},{8,12},{9,11},{10,... | collective-permute-start | bytes 4718600 | tf_op jit(solution)/shard_map/ppermute | solution.py:673
  458.3 28.6 %collective-permute-start.42 = (bf16[2,2,4,2,80,512]{5,4,3,2,1,0:T(8,128)(2,1)}, bf16[2,2,4,2,80,512]{5,4,3,2,1,0:T(8,128)(2,1)S(1)}, u32[]{:S(2)}, u32[]{:S(2)}) collective-permute-start(bf16[2,2,4,2,80,512]{5,4,3,2,1,0:T(8,128)(2,1)} %get-tuple-element.715), channel_id=1, source_target_pairs={{0,1},{1,0},{2,3},{3,2},{4,5},{5,4},{6,7},{7,6},{8,9},{9,8},{10,11... | collective-permute-start | bytes 7864328 | tf_op jit(solution)/shard_map/ppermute | solution.py:673
  461.0 25.9 %collective-permute-start.41 = (bf16[2,4,2,48,512]{4,3,2,1,0:T(8,128)(2,1)}, bf16[2,4,2,48,512]{4,3,2,1,0:T(8,128)(2,1)}, u32[]{:S(2)}, u32[]{:S(2)}) collective-permute-start(bf16[2,4,2,48,512]{4,3,2,1,0:T(8,128)(2,1)} %fusion.5), channel_id=1, source_target_pairs={{0,4},{1,3},{2,6},{3,1},{4,0},{5,7},{6,2},{7,5},{8,12},{9,11},{10,... | collective-permute-start | bytes 2359304 | tf_op jit(solution)/shard_map/ppermute | solution.py:673
  463.8 23.1 %collective-permute-start.40 = (bf16[4,2,96,512]{3,2,1,0:T(8,128)(2,1)}, bf16[4,2,96,512]{3,2,1,0:T(8,128)(2,1)}, u32[]{:S(2)}, u32[]{:S(2)}) collective-permute-start(bf16[4,2,96,512]{3,2,1,0:T(8,128)(2,1)} %fusion.6), channel_id=1, source_target_pairs={{0,2},{1,5},{2,0},{3,7},{4,6},{5,1},{6,4},{7,3},{8,10},{9,13},{10,... | collective-permute-start | bytes 2359304 | tf_op jit(solution)/shard_map/ppermute | solution.py:673
  492.3 35.0 %collective-permute-start.48 = (bf16[2,2,4,2,64,512]{5,4,3,2,1,0:T(8,128)(2,1)}, bf16[2,2,4,2,64,512]{5,4,3,2,1,0:T(8,128)(2,1)}, u32[]{:S(2)}, u32[]{:S(2)}) collective-permute-start(bf16[2,2,4,2,64,512]{5,4,3,2,1,0:T(8,128)(2,1)} %get-tuple-element.754), channel_id=1, source_target_pairs={{0,1},{1,0},{2,3},{3,2},{4,5},{5,4},{6,7},{7,6},{8,9},{9,8},{10,11... | collective-permute-start | bytes 6291464 | tf_op jit(solution)/shard_map/ppermute | solution.py:673
  495.3 32.0 %collective-permute-start.47 = (bf16[2,4,2,80,512]{4,3,2,1,0:T(8,128)(2,1)}, bf16[2,4,2,80,512]{4,3,2,1,0:T(8,128)(2,1)S(1)}, u32[]{:S(2)}, u32[]{:S(2)}) collective-permute-start(bf16[2,4,2,80,512]{4,3,2,1,0:T(8,128)(2,1)} %fusion.2), channel_id=1, source_target_pairs={{0,4},{1,3},{2,6},{3,1},{4,0},{5,7},{6,2},{7,5},{8,12},{9,11},{10,... | collective-permute-start | bytes 3932168 | tf_op jit(solution)/shard_map/ppermute | solution.py:673
  509.2 18.1 %collective-permute-start.46 = (bf16[4,2,48,512]{3,2,1,0:T(8,128)(2,1)S(1)}, bf16[4,2,48,512]{3,2,1,0:T(8,128)(2,1)S(1)}, u32[]{:S(2)}, u32[]{:S(2)}) collective-permute-start(bf16[4,2,48,512]{3,2,1,0:T(8,128)(2,1)S(1)} %fusion.14), channel_id=1, source_target_pairs={{0,2},{1,5},{2,0},{3,7},{4,6},{5,1},{6,4},{7,3},{8,10},{9,13},{10,... | collective-permute-start | bytes 1179656 | tf_op jit(solution)/shard_map/ppermute | solution.py:673
  510.3 17.0 %collective-permute-start.44 = (bf16[2,96,512]{2,1,0:T(8,128)(2,1)}, bf16[2,96,512]{2,1,0:T(8,128)(2,1)S(1)}, u32[]{:S(2)}, u32[]{:S(2)}) collective-permute-start(bf16[2,96,512]{2,1,0:T(8,128)(2,1)} %get-tuple-element.922), channel_id=1, source_target_pairs={{0,16},{1,17},{2,18},{3,19},{4,20},{5,21},{6,22},{7,23},{8,24},{9,... | collective-permute-start | bytes 589832 | tf_op jit(solution)/shard_map/ppermute | solution.py:673
  533.4 38.0 %collective-permute-start.54 = (bf16[2,2,4,2,80,512]{5,4,3,2,1,0:T(8,128)(2,1)}, bf16[2,2,4,2,80,512]{5,4,3,2,1,0:T(8,128)(2,1)}, u32[]{:S(2)}, u32[]{:S(2)}) collective-permute-start(bf16[2,2,4,2,80,512]{5,4,3,2,1,0:T(8,128)(2,1)} %get-tuple-element.786), channel_id=1, source_target_pairs={{0,1},{1,0},{2,3},{3,2},{4,5},{5,4},{6,7},{7,6},{8,9},{9,8},{10,11... | collective-permute-start | bytes 7864328 | tf_op jit(solution)/shard_map/ppermute | solution.py:673
  539.0 32.5 %collective-permute-start.53 = (bf16[2,4,2,64,512]{4,3,2,1,0:T(8,128)(2,1)}, bf16[2,4,2,64,512]{4,3,2,1,0:T(8,128)(2,1)S(1)}, u32[]{:S(2)}, u32[]{:S(2)}) collective-permute-start(bf16[2,4,2,64,512]{4,3,2,1,0:T(8,128)(2,1)} %fusion.4), channel_id=1, source_target_pairs={{0,4},{1,3},{2,6},{3,1},{4,0},{5,7},{6,2},{7,5},{8,12},{9,11},{10,... | collective-permute-start | bytes 3145736 | tf_op jit(solution)/shard_map/ppermute | solution.py:673
  542.7 28.8 %collective-permute-start.52 = (bf16[4,2,80,512]{3,2,1,0:T(8,128)(2,1)}, bf16[4,2,80,512]{3,2,1,0:T(8,128)(2,1)}, u32[]{:S(2)}, u32[]{:S(2)}) collective-permute-start(bf16[4,2,80,512]{3,2,1,0:T(8,128)(2,1)} %fusion.8), channel_id=1, source_target_pairs={{0,2},{1,5},{2,0},{3,7},{4,6},{5,1},{6,4},{7,3},{8,10},{9,13},{10,... | collective-permute-start | bytes 1966088 | tf_op jit(solution)/shard_map/ppermute | solution.py:673
  546.1 18.2 %collective-permute-start.49 = (bf16[2,48,512]{2,1,0:T(8,128)(2,1)S(1)}, bf16[2,48,512]{2,1,0:T(8,128)(2,1)S(1)}, u32[]{:S(2)}, u32[]{:S(2)}) collective-permute-start(bf16[2,48,512]{2,1,0:T(8,128)(2,1)S(1)} %get-tuple-element.938), channel_id=1, source_target_pairs={{0,8},{1,9},{2,10},{3,11},{4,12},{5,13},{6,14},{7,15},{8,16},{9,17... | collective-permute-start | bytes 294920 | tf_op jit(solution)/shard_map/ppermute | solution.py:673
  575.9 31.5 %collective-permute-start.60 = (bf16[2,2,4,2,64,512]{5,4,3,2,1,0:T(8,128)(2,1)}, bf16[2,2,4,2,64,512]{5,4,3,2,1,0:T(8,128)(2,1)}, u32[]{:S(2)}, u32[]{:S(2)}) collective-permute-start(bf16[2,2,4,2,64,512]{5,4,3,2,1,0:T(8,128)(2,1)} %get-tuple-element.817), channel_id=1, source_target_pairs={{0,1},{1,0},{2,3},{3,2},{4,5},{5,4},{6,7},{7,6},{8,9},{9,8},{10,11... | collective-permute-start | bytes 6291464 | tf_op jit(solution)/shard_map/ppermute | solution.py:673
  581.2 26.1 %collective-permute-start.59 = (bf16[2,4,2,80,512]{4,3,2,1,0:T(8,128)(2,1)}, bf16[2,4,2,80,512]{4,3,2,1,0:T(8,128)(2,1)}, u32[]{:S(2)}, u32[]{:S(2)}) collective-permute-start(bf16[2,4,2,80,512]{4,3,2,1,0:T(8,128)(2,1)} %fusion.1), channel_id=1, source_target_pairs={{0,4},{1,3},{2,6},{3,1},{4,0},{5,7},{6,2},{7,5},{8,12},{9,11},{10,... | collective-permute-start | bytes 3932168 | tf_op jit(solution)/shard_map/ppermute | solution.py:673
  584.1 23.2 %collective-permute-start.58 = (bf16[4,2,64,512]{3,2,1,0:T(8,128)(2,1)}, bf16[4,2,64,512]{3,2,1,0:T(8,128)(2,1)}, u32[]{:S(2)}, u32[]{:S(2)}) collective-permute-start(bf16[4,2,64,512]{3,2,1,0:T(8,128)(2,1)} %fusion.13), channel_id=1, source_target_pairs={{0,2},{1,5},{2,0},{3,7},{4,6},{5,1},{6,4},{7,3},{8,10},{9,13},{10,... | collective-permute-start | bytes 1572872 | tf_op jit(solution)/shard_map/ppermute | solution.py:673
  610.2 25.8 %collective-permute-start.65 = (bf16[2,4,2,64,512]{4,3,2,1,0:T(8,128)(2,1)}, bf16[2,4,2,64,512]{4,3,2,1,0:T(8,128)(2,1)}, u32[]{:S(2)}, u32[]{:S(2)}) collective-permute-start(bf16[2,4,2,64,512]{4,3,2,1,0:T(8,128)(2,1)} %fusion.3), channel_id=1, source_target_pairs={{0,4},{1,3},{2,6},{3,1},{4,0},{5,7},{6,2},{7,5},{8,12},{9,11},{10,... | collective-permute-start | bytes 3145736 | tf_op jit(solution)/shard_map/ppermute | solution.py:673
  613.7 22.3 %collective-permute-start.64 = (bf16[4,2,80,512]{3,2,1,0:T(8,128)(2,1)}, bf16[4,2,80,512]{3,2,1,0:T(8,128)(2,1)}, u32[]{:S(2)}, u32[]{:S(2)}) collective-permute-start(bf16[4,2,80,512]{3,2,1,0:T(8,128)(2,1)} %fusion.7), channel_id=1, source_target_pairs={{0,2},{1,5},{2,0},{3,7},{4,6},{5,1},{6,4},{7,3},{8,10},{9,13},{10,... | collective-permute-start | bytes 1966088 | tf_op jit(solution)/shard_map/ppermute | solution.py:673
  637.5 22.7 %collective-permute-start.69 = (bf16[4,2,64,512]{3,2,1,0:T(8,128)(2,1)S(1)}, bf16[4,2,64,512]{3,2,1,0:T(8,128)(2,1)S(1)}, u32[]{:S(2)}, u32[]{:S(2)}) collective-permute-start(bf16[4,2,64,512]{3,2,1,0:T(8,128)(2,1)S(1)} %fusion.12), channel_id=1, source_target_pairs={{0,2},{1,5},{2,0},{3,7},{4,6},{5,1},{6,4},{7,3},{8,10},{9,13},{10,... | collective-permute-start | bytes 1572872 | tf_op jit(solution)/shard_map/ppermute | solution.py:673
  (124 other events, 990.8 us)

commit v4 on v3

--- a/solution.py
+++ b/solution.py
@@ -107,9 +107,10 @@
     rstd[:, at] = lax.rsqrt(group_mean(sums[:, whole]) + 1e-05)
 
 
-def forward_kernel(count, keep, parts, tuned, *refs):
+def forward_kernel(count, keep, parts, skip, tuned, *refs):
     refs = list(refs)
-    first = len(parts) > 3
+    number = len(parts) - skip
+    first = number > 3
 
     def take(number):
         taken = refs[:number]
@@ -119,28 +120,27 @@
     (place,) = take(1)
     x = take(2 if first else 1)
     gains, shift = take(2)
-    sources = take(2 if tuned else len(parts))
+    sources = take(4 if tuned else len(parts))
     (out,) = take(1)
     if keep:
         if first:
             (start,) = take(1)
         hid_one, hid_two, hid_three, rstd = take(4)
         kept_weights = take(3)
-    weights = take(len(parts))
+    weights = take(number)
     sems, back_sems, low, act, cols, sums = take(6)
     if not keep:
         hid_one, hid_two, hid_three, rstd = take(4)
         if first:
             (start,) = take(1)
-    fetch(parts, tuned, place, sources, weights, sems)
+    fetch(parts, tuned, place, sources, dict(enumerate(weights, skip)), sems)
 
     def arrived(index):
-        index += len(parts)
-        pltpu.make_async_copy(weights[index], weights[index], sems.at[index]).wait()
-        if keep and index >= len(parts) - 3:
-            number = index - len(parts) + 3
-            pltpu.make_async_copy(weights[index], kept_weights[number], back_sems.at[number]).start()
-        return weights[index]
+        weight = weights[index]
+        pltpu.make_async_copy(weight, weight, sems.at[len(parts) + index]).wait()
+        if keep and index >= -3:
+            pltpu.make_async_copy(weight, kept_weights[index], back_sems.at[3 + index]).start()
+        return weight
 
     def whole(value):
         return value.reshape(-1, value.shape[-1])
@@ -199,9 +199,8 @@
 
     each_chunk(count, D, finish)
     if keep:
-        for number in range(3):
-            weight = weights[len(parts) - 3 + number]
-            pltpu.make_async_copy(weight, kept_weights[number], back_sems.at[number]).wait()
+        for index in (-3, -2, -1):
+            pltpu.make_async_copy(weights[index], kept_weights[index], back_sems.at[3 + index]).wait()
 
 
 def f32(*shape):
@@ -216,8 +215,8 @@
     return -(-count // 8) * 8
 
 
-def block_forward(stream, gains, shift, parts, buffers, place, keep, tuned):
-    first = len(parts) > 3
+def block_forward(stream, gains, shift, parts, skip, buffers, place, keep, tuned):
+    first = len(parts) - skip > 3
     rows = stream[0].shape[0]
     count = rows // ROWS
     stats = stat_rows(count)
@@ -228,7 +227,7 @@
         ((stats, 2 * BOT + D), jnp.float32),
     ]
     start = [((rows, D), jnp.float32)] if first else []
-    weights = weight_shapes(parts, buffers, tuned)
+    weights = weight_shapes(parts, buffers, tuned)[skip:]
     out_shape = [f32(rows, D)]
     out_specs = in_vmem(1)
     scratch = [pltpu.VMEM(shape, jnp.bfloat16) for shape in weights]
@@ -247,7 +246,7 @@
     else:
         scratch += [pltpu.VMEM(*item) for item in kept + start]
     return pl.pallas_call(
-        functools.partial(forward_kernel, count, keep, parts, tuned),
+        functools.partial(forward_kernel, count, keep, parts, skip, tuned),
         out_shape=out_shape,
         in_specs=in_smem() + in_vmem(len(stream) + 2) + hbm(len(buffers)),
         out_specs=out_specs,
@@ -289,10 +288,8 @@
     each_chunk(count, chans, spread)
 
 
-def back_out_kernel(count, *refs):
-    grad, x, hid_two, hid_three, rstd, w_out, gains = refs[:7]
-    dres, dlow, dw_out, dgains = refs[7:11]
-    third, act, dact, sums, more = refs[11:]
+def back_out_body(count, grad, x, hid_two, hid_three, rstd, w_out, gains, dres, dlow, dgains, scratch, dw_out):
+    third, act, dact, sums, more = scratch
     gain_three, bias_three = (gains.at[:, pl.ds(4 * BOT, D)], gains.at[:, pl.ds(4 * BOT + D, D)])
 
     def slope_three(frame, rows, lanes):
@@ -334,35 +331,22 @@
     )
     for part in range(D // BOT):
         lanes = pl.ds(part * BOT, BOT)
-        dw_out[lanes, :] = dot_rows(act[...], third[:, lanes]).astype(jnp.bfloat16)
-
-
-def back_out(grad, stream, hid_two, hid_three, rstd, w_out, gains):
-    rows = stream.shape[0]
-    count = rows // ROWS
-    stats = stat_rows(count)
-    return pl.pallas_call(
-        functools.partial(back_out_kernel, count),
-        out_shape=[f32(rows, D), bf16(rows, BOT), bf16(D, BOT), f32(1, 2 * BOT + 2 * D)],
-        in_specs=in_vmem(7),
-        out_specs=in_vmem(4),
-        scratch_shapes=[
-            pltpu.VMEM((rows, D), jnp.bfloat16),
-            pltpu.VMEM((rows, BOT), jnp.bfloat16),
-            pltpu.VMEM((rows, BOT), jnp.float32),
-            pltpu.VMEM((stats, D), jnp.float32),
-            pltpu.VMEM((stats, D), jnp.float32),
-        ],
-        compiler_params=pltpu.CompilerParams(vmem_limit_bytes=VMEM_LIMIT),
-        cost_estimate=LIGHT,
-        name="back_out",
-    )(grad, stream, hid_two, hid_three, rstd, w_out, gains)
-
-
-def back_mid_kernel(count, *refs):
-    grad, hid_one, rstd, w_mid, gains, shift = refs[:6]
-    dlow, dw_mid, dgains = refs[6:9]
-    act, cols, dact, sums, more = refs[9:]
+        dw_out[part] = dot_rows(act[...], third[:, lanes]).astype(jnp.bfloat16)
+
+
+def out_scratch(rows):
+    stats = stat_rows(rows // ROWS)
+    return [
+        pltpu.VMEM((rows, D), jnp.bfloat16),
+        pltpu.VMEM((rows, BOT), jnp.bfloat16),
+        pltpu.VMEM((rows, BOT), jnp.float32),
+        pltpu.VMEM((stats, D), jnp.float32),
+        pltpu.VMEM((stats, D), jnp.float32),
+    ]
+
+
+def back_mid_body(count, grad, hid_one, rstd, w_mid, gains, shift, dlow, dgains, scratch, dw_mid):
+    act, cols, dact, sums, more = scratch
     gain_one, bias_one = (gains.at[:, pl.ds(0, BOT)], gains.at[:, pl.ds(BOT, BOT)])
     for frame in range(count):
         rows = pl.ds(frame * ROWS, ROWS)
@@ -394,56 +378,125 @@
     )
     for tap in range(TAPS):
         lanes = pl.ds(tap * BOT, BOT)
-        dw_mid[lanes, :] = dot_rows(act[...], cols[:, lanes]).astype(jnp.bfloat16)
-
-
-def back_mid(grad, hid_one, rstd, w_mid, gains, shift):
-    rows = grad.shape[0]
-    count = rows // ROWS
-    stats = stat_rows(count)
-    return pl.pallas_call(
-        functools.partial(back_mid_kernel, count),
-        out_shape=[bf16(rows, BOT), bf16(TAPS * BOT, BOT), f32(1, 2 * BOT)],
-        in_specs=in_vmem(6),
-        out_specs=in_vmem(3),
-        scratch_shapes=[
-            pltpu.VMEM((rows, BOT), jnp.bfloat16),
-            pltpu.VMEM((rows, TAPS * BOT), jnp.bfloat16),
-            pltpu.VMEM((rows, BOT), jnp.float32),
-            pltpu.VMEM((stats, BOT), jnp.float32),
-            pltpu.VMEM((stats, BOT), jnp.float32),
-        ],
-        compiler_params=pltpu.CompilerParams(vmem_limit_bytes=VMEM_LIMIT),
-        cost_estimate=LIGHT,
-        name="back_mid",
-    )(grad, hid_one, rstd, w_mid, gains, shift)
-
-
-def back_in_kernel(count, *refs):
-    grad, x, dres, w_in, dw_in, dx, low = refs
-
+        dw_mid[0, lanes, :] = dot_rows(act[...], cols[:, lanes]).astype(jnp.bfloat16)
+
+
+def back_in_body(count, grad, x, dres, w_in, dx, low, dw_in):
     def cast(frame, rows, lanes):
         low[rows, lanes] = x[rows, lanes].astype(jnp.bfloat16)
 
     each_chunk(count, D, cast)
     for part in range(D // BOT):
         lanes = pl.ds(part * BOT, BOT)
-        dw_in[lanes, :] = dot_rows(low[:, lanes], grad[...]).astype(jnp.bfloat16)
         dx[:, lanes] = dres[:, lanes] + dot_lanes(grad[...], w_in[lanes, :])
-
-
-def back_in(grad, stream, dres, w_in):
-    rows = grad.shape[0]
-    return pl.pallas_call(
-        functools.partial(back_in_kernel, rows // ROWS),
-        out_shape=[bf16(D, BOT), f32(rows, D)],
-        in_specs=in_vmem(4),
-        out_specs=in_vmem(2),
-        scratch_shapes=[pltpu.VMEM((rows, D), jnp.bfloat16)],
+        dw_in[0, lanes, :] = dot_rows(low[:, lanes], grad[...]).astype(jnp.bfloat16)
+
+
+def back_kernel(body, parts, tuned, counts, *refs):
+    place, refs = (refs[0], list(refs[1:]))
+    groups = []
+    for number in (*counts[:2], len(dealt_shapes(parts, tuned)), len(parts), 1, counts[2]):
+        groups.append(refs[:number])
+        refs = refs[number:]
+    ins, outs, dealt, made, sems, scratch = groups
+
+    def done(index):
+        start_deal(parts, tuned, place, index, made, dealt, sems[0])
+
+    body(ins, outs, made, scratch, done)
+    for index, array in enumerate(made):
+        pltpu.make_async_copy(array, array, sems[0].at[index]).wait()
+
+
+def back_call(name, body, ins, out_shape, scratch, parts, tuned, place):
+    dealt = dealt_shapes(parts, tuned)
+    counts = (len(ins), len(out_shape), len(scratch))
+    outs = pl.pallas_call(
+        functools.partial(back_kernel, body, parts, tuned, counts),
+        out_shape=out_shape + [bf16(*shape) for shape in dealt],
+        in_specs=in_smem() + in_vmem(len(ins)),
+        out_specs=in_vmem(len(out_shape)) + hbm(len(dealt)),
+        scratch_shapes=[pltpu.VMEM(whole_shape(part), jnp.bfloat16) for part in parts]
+        + [pltpu.SemaphoreType.DMA((len(parts),))]
+        + scratch,
         compiler_params=pltpu.CompilerParams(vmem_limit_bytes=VMEM_LIMIT),
         cost_estimate=LIGHT,
-        name="back_in",
-    )(grad, stream, dres, w_in)
+        name=name,
+    )(place, *ins)
+    return (list(outs[: len(out_shape)]), list(outs[len(out_shape) :]))
+
+
+def back_out(grad, stream, hid_two, hid_three, rstd, w_out, gains, parts, tuned, place):
+    rows = stream.shape[0]
+
+    def body(ins, outs, made, scratch, done):
+        back_out_body(rows // ROWS, *ins, *outs, scratch, made[0])
+        done(0)
+
+    ins = [grad, stream, hid_two, hid_three, rstd, w_out, gains]
+    out_shape = [f32(rows, D), bf16(rows, BOT), f32(1, 2 * BOT + 2 * D)]
+    return back_call("back_out", body, ins, out_shape, out_scratch(rows), parts, tuned, place)
+
+
+def back_mid(grad, hid_one, rstd, w_mid, gains, shift, parts, tuned, place):
+    rows = grad.shape[0]
+    stats = stat_rows(rows // ROWS)
+
+    def body(ins, outs, made, scratch, done):
+        back_mid_body(rows // ROWS, *ins, *outs, scratch, made[0])
+        done(0)
+
+    scratch = [
+        pltpu.VMEM((rows, BOT), jnp.bfloat16),
+        pltpu.VMEM((rows, TAPS * BOT), jnp.bfloat16),
+        pltpu.VMEM((rows, BOT), jnp.float32),
+        pltpu.VMEM((stats, BOT), jnp.float32),
+        pltpu.VMEM((stats, BOT), jnp.float32),
+    ]
+    ins = [grad, hid_one, rstd, w_mid, gains, shift]
+    out_shape = [bf16(rows, BOT), f32(1, 2 * BOT)]
+    return back_call("back_mid", body, ins, out_shape, scratch, parts, tuned, place)
+
+
+def back_between(grad, stream, dres, w_in, later, parts, tuned, place):
+    rows = stream.shape[0]
+
+    def body(ins, outs, made, scratch, done):
+        dx, low, *rest = scratch
+        back_in_body(rows // ROWS, *ins[:4], dx, low, made[0])
+        done(0)
+        back_out_body(rows // ROWS, dx, *ins[4:], *outs, rest, made[1])
+        done(1)
+
+    scratch = [pltpu.VMEM((rows, D), jnp.float32), pltpu.VMEM((rows, D), jnp.bfloat16)]
+    scratch += out_scratch(rows)
+    ins = [grad, stream, dres, w_in, *later]
+    out_shape = [f32(rows, D), bf16(rows, BOT), f32(1, 2 * BOT + 2 * D)]
+    return back_call("back_between", body, ins, out_shape, scratch, parts, tuned, place)
+
+
+def back_first(grad, stream, dres, w_in, pixels, spread, dgains, parts, tuned, place):
+    rows = stream.shape[0]
+
+    def body(ins, outs, made, scratch, done):
+        dx, low = scratch
+        made[2][...] = ins[6][...]
+        done(2)
+        back_in_body(rows // ROWS, *ins[:4], dx, low, made[0])
+        done(0)
+        wide = [dot(ins[4][...], ins[5][half]).astype(jnp.bfloat16) for half in range(2)]
+        for block in range(2):
+            total = None
+            for half in range(2):
+                lanes = pl.ds((2 * half + block) * WIDTH, WIDTH)
+                term = dot_rows(wide[half], dx[:, lanes].astype(jnp.bfloat16))
+                total = term if total is None else total + term
+            made[1][block] = total.astype(jnp.bfloat16)
+        done(1)
+
+    scratch = [pltpu.VMEM((rows, D), jnp.float32), pltpu.VMEM((rows, D), jnp.bfloat16)]
+    ins = [grad, stream, dres, w_in, pixels, spread, dgains]
+    return back_call("back_first", body, ins, [], scratch, parts, tuned, place)[1]
 
 
 def spread_pixels(devices):
@@ -453,29 +506,6 @@
     return jnp.stack(
         [jnp.arange(2 * PATCH_IN)[None, :] == (at + half * rows)[:, None] for half in range(2)]
     ).astype(jnp.bfloat16)
-
-
-def embed_back_kernel(pixels, spread, grad, out):
-    wide = [dot(pixels[...], spread[half]).astype(jnp.bfloat16) for half in range(2)]
-    for block in range(2):
-        total = None
-        for half in range(2):
-            lanes = pl.ds((2 * half + block) * WIDTH, WIDTH)
-            term = dot_rows(wide[half], grad[:, lanes].astype(jnp.bfloat16))
-            total = term if total is None else total + term
-        out[block] = total.astype(jnp.bfloat16)
-
-
-def embed_back(pixels, spread, grad):
-    return pl.pallas_call(
-        embed_back_kernel,
-        out_shape=bf16(2, 2 * PATCH_IN, WIDTH),
-        in_specs=in_vmem(3),
-        out_specs=in_vmem(1)[0],
-        compiler_params=pltpu.CompilerParams(vmem_limit_bytes=VMEM_LIMIT),
-        cost_estimate=LIGHT,
-        name="embed_back",
-    )(pixels, spread, grad)
 
 
 def head_forward(count, stream, pool, proj, heads, games, pool_t, pooled):
@@ -552,10 +582,11 @@
     )(stream, pool, proj, heads, whole, real)
 
 
-def loss_kernel(count, frames_all, *refs):
-    stream, pool, proj, heads, target, whole, legal = refs[:7]
-    loss, dheads, dproj, dpool, dstream = refs[7:12]
-    pool_t, pooled, dpooled = refs[12:]
+def loss_body(count, frames_all, ins, outs, made, scratch, done):
+    stream, pool, proj, heads, target, whole, legal = ins
+    loss, dstream = outs
+    dheads, dproj, dpool = made
+    pool_t, pooled, dpooled = scratch
     games, taken = (whole[:, 0:1], whole[:, 1:2])
     logits, before, hidden = head_forward(count, stream, pool, proj, heads, games, pool_t, pooled)
     atoms = support_lanes()
@@ -602,8 +633,10 @@
             dheads[2 * game + half] = dot_rows(hidden, part).astype(jnp.bfloat16)
             term = dot_lanes(part, heads[2 * game + half])
             dhidden = term if dhidden is None else dhidden + term
+    done(0)
     dbefore = (silu_slope(before) * dhidden).astype(jnp.bfloat16)
-    dproj[...] = dot_rows(pooled[...].astype(jnp.bfloat16), dbefore).astype(jnp.bfloat16)
+    dproj[0] = dot_rows(pooled[...].astype(jnp.bfloat16), dbefore).astype(jnp.bfloat16)
+    done(1)
     dpooled[...] = dot_lanes(dbefore, proj[...]).astype(jnp.bfloat16).astype(jnp.float32)
 
     def push(frame, rows, lanes):
@@ -618,28 +651,23 @@
             value = stream[pl.ds(frame * ROWS, ROWS), lanes].astype(jnp.bfloat16)
             term = value.astype(jnp.float32) * dpooled[pl.ds(frame, 1), lanes]
             total = term if total is None else total + term
-        dpool[lanes, :] = total.T.astype(jnp.bfloat16)
+        dpool[0, lanes, :] = total.T.astype(jnp.bfloat16)
         return carry
 
     lax.fori_loop(0, D // ROWS, gather_pool, 0)
-
-
-def head_loss(stream, pool, proj, heads, target, whole, legal, frames_all):
+    done(2)
+
+
+def head_loss(stream, pool, proj, heads, target, whole, legal, frames_all, parts, tuned, place):
     rows = stream.shape[0]
-    return pl.pallas_call(
-        functools.partial(loss_kernel, rows // ROWS, frames_all),
-        out_shape=[f32(1, 1), bf16(2 * GAMES, DPROJ, WIDTH), bf16(D, DPROJ), bf16(D, ROWS), f32(rows, D)],
-        in_specs=in_vmem(7),
-        out_specs=in_vmem(5),
-        scratch_shapes=[
-            pltpu.VMEM((ROWS, D), jnp.float32),
-            pltpu.VMEM((8, D), jnp.float32),
-            pltpu.VMEM((8, D), jnp.float32),
-        ],
-        compiler_params=pltpu.CompilerParams(vmem_limit_bytes=VMEM_LIMIT),
-        cost_estimate=LIGHT,
-        name="head_loss",
-    )(stream, pool, proj, heads, target, whole, legal)
+    scratch = [
+        pltpu.VMEM((ROWS, D), jnp.float32),
+        pltpu.VMEM((8, D), jnp.float32),
+        pltpu.VMEM((8, D), jnp.float32),
+    ]
+    ins = [stream, pool, proj, heads, target, whole, legal]
+    body = functools.partial(loss_body, rows // ROWS, frames_all)
+    return back_call("head_loss", body, ins, [f32(1, 1), f32(rows, D)], scratch, parts, tuned, place)
 
 
 WIDTH = 512
@@ -788,24 +816,22 @@
         step[NEAR[half]], step[FAR[half]] = (near, far)
         at_y, at_x = (lax.rem(y + step[1], 2), lax.rem(x + step[2], 2))
         for index, row, lane, rows, block, inner in half_moves(parts)[half]:
+            if index not in outs:
+                continue
             pairs.append(
                 (
                     index,
-                    ins[other].at[far, near, :, :, pl.ds(row, rows), pl.ds(lane, parts[index].lanes)],
+                    ins[2 * other + far].at[near, :, :, pl.ds(row, rows), pl.ds(lane, parts[index].lanes)],
                     outs[index].at[block, :, at_y, at_x, :, pl.ds(inner, rows)],
                 )
             )
     return pairs
 
 
-def deal_copies(parts):
-    return 4 * sum(len(moves) for moves in half_moves(parts))
-
-
 def fetch(parts, tuned, place, sources, weights, sems):
     if not tuned:
-        for index, (source, weight) in enumerate(zip(sources, weights)):
-            pltpu.make_async_copy(source, weight, sems.at[index]).start()
+        for index, weight in weights.items():
+            pltpu.make_async_copy(sources[index], weight, sems.at[index]).start()
         return
     for core in (0, 1):
 
@@ -818,23 +844,25 @@
 
 def weight_shapes(parts, buffers, tuned):
     if tuned:
-        return [part.full(buffers[0].shape[2]) for part in parts]
+        return [part.full(buffers[0].shape[1]) for part in parts]
     return [item.shape for item in buffers]
 
 
-def assemble_kernel(parts, place, *refs):
-    outs, sems = (refs[2:-1], refs[-1])
-    fetch(parts, True, place, refs[:2], outs, sems)
-    for index, out in enumerate(outs):
+def assemble_kernel(parts, some, place, *refs):
+    outs, sems = (dict(zip(some, refs[4:-1])), refs[-1])
+    fetch(parts, True, place, refs[:4], outs, sems)
+    for index, out in outs.items():
         pltpu.make_async_copy(out, out, sems.at[index]).wait()
 
 
-def assemble(parts, buffers, place):
+def assemble(parts, buffers, place, some=None):
+    some = range(len(parts)) if some is None else some
+    shapes = weight_shapes(parts, buffers, True)
     full = pl.pallas_call(
-        functools.partial(assemble_kernel, parts),
-        out_shape=[bf16(*shape) for shape in weight_shapes(parts, buffers, True)],
-        in_specs=in_smem() + hbm(2),
-        out_specs=in_vmem(len(parts)),
+        functools.partial(assemble_kernel, parts, some),
+        out_shape=[bf16(*shapes[index]) for index in some],
+        in_specs=in_smem() + hbm(4),
+        out_specs=in_vmem(len(some)),
         scratch_shapes=[pltpu.SemaphoreType.DMA((len(parts),))],
         compiler_params=pltpu.CompilerParams(vmem_limit_bytes=VMEM_LIMIT),
         cost_estimate=LIGHT,
@@ -875,44 +903,64 @@
     return held
 
 
-def gather_hop(stage, item):
-    if stage == 0:
-        return [item] + [hop(item, ALONG_Z, step) for step in range(1, grid_sizes()[0])]
-    return [item, hop(item, (NEAR, FAR, ACROSS)[stage - 1])]
-
-
 def pipelined_gather(groups, pieces, place, state, arrived):
     count = len(groups)
-    held = start_gather(groups, pieces, place)
+    depth = grid_sizes()[0]
+    held = start_gather(groups[:1], pieces(None)[:1], place) + [None] * (count - 1)
     for tick in range(count + 3):
-        live = [index for index in range(tick - 3, tick + 1) if 0 <= index < count]
+        if tick == 1:
+            held[1:] = start_gather(groups[1:], pieces(early)[1:], place)
+        near, far, last = [index if 0 <= index < count else None for index in range(tick - 1, tick - 4, -1)]
+        live = [index for index in (tick, near, far, last) if index is not None and index < count]
         items, state = together([held[index] for index in live], state)
         for index, item in zip(live, items):
-            held[index] = gather_hop(tick - index, item)
-        if tick >= 3:
-            state = arrived(tick - 3, held[tick - 3], state)
-        live = [index for index in live if index > tick - 3]
-        items, state = together([held[index] for index in live], state)
-        for index, item in zip(live, items):
-            held[index] = stack_z(item, place) if index == tick else jnp.stack(item)
+            held[index] = item
+        if last is not None:
+            held[last] = held[last] + [hop(item, ACROSS) for item in held[last]]
+        if far is not None:
+            held[far] = [held[far], hop(held[far], FAR)]
+        if near is not None:
+            held[near] = [held[near], hop(held[near], NEAR)]
+        if tick < count:
+            early = held[tick]
+            held[tick] = [held[tick]] + [hop(held[tick], ALONG_Z, step) for step in range(1, depth)]
+        if last is not None:
+            state = arrived(last, held[last], state)
+        if tick < count:
+            items, state = together(held[tick], state)
+            held[tick] = stack_z(items, place)
+        if near is not None:
+            items, state = together(held[near], state)
+            held[near] = jnp.stack(items)
     return state
 
 
-def deal_kernel(parts, place, *refs):
-    number = len(parts)
-    ins, outs, sems = (refs[:number], refs[number:-1], refs[-1])
-    to_core, to_far, to_near, own = outs
-    y, x = (place[1], place[2])
+def whole_shape(part):
+    return (part.blocks, part.rows * lax.axis_size(AXES), part.lanes)
+
+
+def dealt_shapes(parts, tuned):
+    if not tuned:
+        return [whole_shape(part) for part in parts]
+    size = (grid_sizes()[0], 2, half_rows(parts), WIDTH)
+    return [lead + size for lead in ((2, 2), (2,), (), ())]
+
+
+def start_deal(parts, tuned, place, wanted, arrays, dealt, sems):
+    if not tuned:
+        pltpu.make_async_copy(arrays[wanted], dealt[wanted], sems.at[wanted]).start()
+        return
+    array = arrays[wanted].reshape(*parts[wanted].full(grid_sizes()[0]))
+    to_core, to_far, to_near, own = dealt
     for core in (0, 1):
 
         @pl.when(place[3] == core)
         def _():
-            pairs = []
             for other, far, near in itertools.product((0, 1), repeat=3):
                 half = core ^ other
                 step = [0, 0, 0, 0]
                 step[NEAR[half]], step[FAR[half]] = (near, far)
-                at_y, at_x = (lax.rem(y + step[1], 2), lax.rem(x + step[2], 2))
+                at_y, at_x = (lax.rem(place[1] + step[1], 2), lax.rem(place[2] + step[2], 2))
                 if other:
                     target = to_core.at[far, near]
                 elif far:
@@ -920,30 +968,12 @@
                 else:
                     target = to_near if near else own
                 for index, row, lane, rows, block, inner in half_moves(parts)[half]:
-                    pairs.append(
-                        (
-                            ins[index].at[block, :, at_y, at_x, :, pl.ds(inner, rows)],
+                    if index == wanted:
+                        pltpu.make_async_copy(
+                            array.at[block, :, at_y, at_x, :, pl.ds(inner, rows)],
                             target.at[:, :, pl.ds(row, rows), pl.ds(lane, parts[index].lanes)],
-                        )
-                    )
-            copies(pairs, sems)
-
-
-def deal(parts, arrays, place):
-    depth = arrays[0].shape[1]
-    size = unit(parts, depth)
-    return pl.pallas_call(
-        functools.partial(deal_kernel, parts),
-        out_shape=[
-            jax.ShapeDtypeStruct(lead + size, jnp.bfloat16) for lead in ((2, 2), (2,), (), ())
-        ],
-        in_specs=in_smem() + in_vmem(len(parts)),
-        out_specs=hbm(4),
-        scratch_shapes=[pltpu.SemaphoreType.DMA((deal_copies(parts),))],
-        compiler_params=pltpu.CompilerParams(vmem_limit_bytes=VMEM_LIMIT),
-        cost_estimate=LIGHT,
-        name="deal",
-    )(place, *arrays)
+                            sems.at[index],
+                        ).start()
 
 
 def add_up(*terms):
@@ -961,34 +991,24 @@
     depth = grid_sizes()[0]
     z, core = (place[0], place[3])
     if stage == 0:
-        arrays = [array.reshape(part.full(depth)) for part, array in zip(parts, items)]
-        to_core, *rest = deal(parts, arrays, place)
+        to_core, *rest = items
         return rest + [hop(to_core, ACROSS)]
-    to_far, to_near, own, from_core = items[:4]
     if stage == 1:
-        return items + [hop(low_add(to_far, from_core[1]), FAR)]
-    from_far = items[4]
+        to_far, to_near, own, from_core = items
+        return [to_near, own, from_core, hop(low_add(to_far, from_core[1]), FAR)]
     if stage == 2:
-        return items + [hop(low_add(to_near, from_core[0, 1], from_far[1]), NEAR)]
-    pick = [own, from_core[0, 0], from_far[0], items[5]]
-
-    def mine(at):
-        return [lax.dynamic_index_in_dim(item, at, 0, False) for item in pick]
-
+        to_near, own, from_core, from_far = items
+        from_near = hop(low_add(to_near, from_core[0, 1], from_far[1]), NEAR)
+        return [add_up(own, from_core[0, 0], from_far[0]), from_near]
     if stage == 3:
-        return items + [
-            hop(low_add(*mine(lax.rem(z + step, depth))), ALONG_Z, step) for step in range(1, depth)
-        ]
-    total = add_up(*mine(z), *items[6:])
+        summed = lax.optimization_barrier(add_up(*items))
+        sent = [lax.dynamic_index_in_dim(summed, lax.rem(z + step, depth), 0, False) for step in range(1, depth)]
+        along = [hop(item.astype(jnp.bfloat16), ALONG_Z, step + 1) for step, item in enumerate(sent)]
+        return [lax.dynamic_index_in_dim(summed, z, 0, False)] + along
+    total = add_up(*items)
     keep = lax.dynamic_index_in_dim(total, core, 0, False)
     other = hop(lax.dynamic_index_in_dim(total, 1 - core, 0, False), ACROSS)
-    rows = both_cores(keep, other, core).reshape(-1, WIDTH)
-    pieces = []
-    offset = 0
-    for part in parts:
-        pieces.append(part.unpack(rows[offset : offset + part.travel]))
-        offset += part.travel
-    return pieces
+    return both_cores(keep, other, core).reshape(-1, WIDTH)
 
 
 SCATTER_STAGES = 5
@@ -999,9 +1019,12 @@
     held = [None] * count
     for tick in range(count + SCATTER_STAGES):
         live = [index for index in range(tick - SCATTER_STAGES, tick) if 0 <= index < count]
-        items, state = together([held[index] for index in live], state)
-        for index, item in zip(live, items):
-            held[index] = scatter_stage(tick - 1 - index, groups[index], item, place)
+        if tick <= count:
+            items, state = together([held[index] for index in live], state)
+            for index, item in zip(live, items):
+                held[index] = item
+        for index in live:
+            held[index] = scatter_stage(tick - 1 - index, groups[index], held[index], place)
         if tick < count:
             held[tick], state = steps[tick](state)
     return (held, state)
@@ -1026,6 +1049,203 @@
     return min(0.99, (1.0 + STEP) / (10.0 + STEP))
 
 
+SWEEP = 1024
+
+
+def lamb_parts(grads, params, first, second):
+    momentum = BETA_ONE * first + (1.0 - BETA_ONE) * grads
+    variance = BETA_TWO * second + (1.0 - BETA_TWO) * grads * grads
+    direction = (
+        momentum / (1.0 - BETA_ONE**STEP) / (jnp.sqrt(variance / (1.0 - BETA_TWO**STEP)) + 1e-06)
+        + WEIGHT_DECAY * params
+    )
+    return (momentum, variance, direction)
+
+
+def sweep(start, size, body, carry):
+    steps = size // SWEEP
+
+    def step(index, carry):
+        return body(pl.ds(pl.multiple_of(start + index * SWEEP, ROWS), SWEEP), carry)
+
+    if steps:
+        carry = lax.fori_loop(0, steps, step, carry, unroll=2)
+    return (carry, start + steps * SWEEP, size - steps * SWEEP)
+
+
+def row_sum(value):
+    return jnp.sum(value, axis=1, keepdims=True)
+
+
+def put_rows(target, row, source, steps):
+    for first, rows, lane, stride in steps:
+
+        def step(index, carry):
+            lanes = pl.ds(pl.multiple_of(lane + index * stride, ROWS), WIDTH)
+            target[row : row + 1, lanes] = source[pl.ds(first + index, 1), :]
+            return carry
+
+        lax.fori_loop(0, rows, step, 0, unroll=4)
+
+
+def block_rows(name, start, rows, first):
+    if name == "w_out":
+        count = rows // (D // BOT)
+        return [(first + part * count, count, start + part * BOT, D) for part in range(D // BOT)]
+    return [(first, rows, start, WIDTH)]
+
+
+def patch_rows(rows, first):
+    count = rows // 4
+    return [
+        (first + (2 * block + half) * count, count, half * (D // 2) + block * WIDTH, D)
+        for block in range(2)
+        for half in range(2)
+    ]
+
+
+def direction_kernel(cuts, moves, gain_at, *refs):
+    top_cuts, block_cuts = cuts
+    number = len(moves)
+    sources, refs = (refs[:number], refs[number:])
+    late, loss, *refs = refs
+    top_ins, block_ins, refs = (refs[:3], refs[3:6], refs[6:])
+    sums, *refs = refs
+    top_outs, block_outs, (top_grad, block_grad) = (refs[:3], refs[3:6], refs[6:])
+    for source, steps in zip(sources, moves):
+        for row, placed in steps:
+            put_rows(top_grad if row is None else block_grad, row or 0, source, placed)
+    patch = top_cuts[0][1]
+    top_grad[:, pl.ds(patch, late.shape[1])] = late[...]
+    gain_start, gain_width = block_cuts[3]
+    source, first = (sources[gain_at[0]], gain_at[1])
+    block_grad[:, pl.ds(gain_start, gain_width)] = source[pl.ds(first, 8), :][:BLOCKS, :gain_width]
+
+    def work(lanes, grad, ins, outs):
+        param, *moments = [ref[:, lanes] for ref in ins]
+        made = lamb_parts(grad[:, lanes], param, *moments)
+        for ref, value in zip(outs, made):
+            ref[:, lanes] = value
+        return (param * param, made[2] * made[2])
+
+    found = []
+    width = top_ins[0].shape[1]
+
+    def top_step(lanes, carry):
+        size = lanes.size
+        squares = work(lanes, top_grad, top_ins, top_outs)
+        at = lanes.start + lax.broadcasted_iota(jnp.int32, (1, size), 1)
+        masks = [(at >= start) & (at < start + count) for start, count in top_cuts]
+        terms = [jnp.where(mask, value, 0.0) for mask in masks for value in squares]
+        if size != SWEEP:
+            return [row_sum(held) + row_sum(term) for held, term in zip(carry, terms)]
+        return [held + term for held, term in zip(carry, terms)]
+
+    zeros = [jnp.zeros((1, SWEEP), jnp.float32)] * (2 * len(top_cuts))
+    carry, start, rest = sweep(0, width, top_step, zeros)
+    carry = top_step(pl.ds(start, rest), carry) if rest else [row_sum(value) for value in carry]
+    found += [(index // 2, index % 2, value) for index, value in enumerate(carry)]
+
+    def block_step(lanes, carry):
+        return [held + term for held, term in zip(carry, work(lanes, block_grad, block_ins, block_outs))]
+
+    zeros = [jnp.zeros((BLOCKS, SWEEP), jnp.float32)] * 2
+    for index, (start, size) in enumerate(block_cuts):
+        carry, start, rest = sweep(start, size, block_step, zeros)
+        carry = [row_sum(value) for value in carry]
+        if rest:
+            terms = work(pl.ds(start, rest), block_grad, block_ins, block_outs)
+            carry = [held + row_sum(term) for held, term in zip(carry, terms)]
+        for block in range(BLOCKS):
+            lane = len(top_cuts) + block * len(block_cuts) + index
+            found += [(lane, row, value[block : block + 1]) for row, value in enumerate(carry)]
+    rows = lax.broadcasted_iota(jnp.int32, sums.shape, 0)
+    lanes = lax.broadcasted_iota(jnp.int32, sums.shape, 1)
+    result = jnp.where((rows == 2) & (lanes == 0), loss[...], 0.0)
+    for lane, row, value in found:
+        result = jnp.where((rows == row) & (lanes == lane), value, result)
+    sums[...] = result
+
+
+def directions(cuts, rows, moves, gain_at, late, loss, top_ins, block_ins):
+    shapes = [f32(*top_ins[0].shape)] * 3 + [f32(*block_ins[0].shape)] * 3
+    ins = [*rows, late, loss, *top_ins, *block_ins]
+    return pl.pallas_call(
+        functools.partial(direction_kernel, cuts, moves, gain_at),
+        out_shape=[f32(8, ROWS)] + shapes,
+        in_specs=in_vmem(len(ins)),
+        out_specs=in_vmem(7),
+        scratch_shapes=[
+            pltpu.VMEM(top_ins[0].shape, jnp.float32),
+            pltpu.VMEM(block_ins[0].shape, jnp.float32),
+        ],
+        compiler_params=pltpu.CompilerParams(vmem_limit_bytes=VMEM_LIMIT),
+        cost_estimate=LIGHT,
+        name="directions",
+    )(*ins)
+
+
+def update_kernel(cuts, sums, *refs):
+    top_cuts, block_cuts = cuts
+    top_ins, block_ins, refs = (refs[:3], refs[3:6], refs[6:])
+    norms, *refs = refs
+    top_outs, block_outs = (refs[:3], refs[3:])
+    norm = jnp.sqrt(sums[...])
+    norms[...] = norm
+    ratio = LEARNING_RATE * (norm[0:1] / (norm[1:2] + 1e-06))
+    decay = average_decay()
+
+    def work(lanes, ins, outs, scale):
+        param, direction, average = [ref[:, lanes] for ref in ins]
+        updated, half, averaged = outs
+        value = param - scale * direction
+        updated[:, lanes] = value
+        half[:, lanes] = value.astype(jnp.bfloat16)
+        averaged[:, lanes] = decay * average + (1.0 - decay) * value
+
+    def top_step(lanes, carry):
+        at = lanes.start + lax.broadcasted_iota(jnp.int32, (1, lanes.size), 1)
+        scale = jnp.broadcast_to(ratio[:, 3:4], at.shape)
+        for index in (2, 1, 0):
+            scale = jnp.where(at < top_cuts[index + 1][0], ratio[:, index : index + 1], scale)
+        work(lanes, top_ins, top_outs, scale)
+        return carry
+
+    _, start, rest = sweep(0, top_ins[0].shape[1], top_step, 0)
+    if rest:
+        top_step(pl.ds(start, rest), 0)
+    for index, (start, size) in enumerate(block_cuts):
+        scale = jnp.concatenate(
+            [
+                ratio[:, lane : lane + 1]
+                for lane in [4 + block * len(block_cuts) + index for block in range(BLOCKS)]
+            ]
+        )
+
+        def block_step(lanes, carry):
+            work(lanes, block_ins, block_outs, scale)
+            return carry
+
+        _, start, rest = sweep(start, size, block_step, 0)
+        if rest:
+            block_step(pl.ds(start, rest), 0)
+
+
+def update(cuts, sums, top_ins, block_ins):
+    shapes = []
+    for array in (top_ins[0], block_ins[0]):
+        shapes += [f32(*array.shape), bf16(*array.shape), f32(*array.shape)]
+    return pl.pallas_call(
+        functools.partial(update_kernel, cuts),
+        out_shape=[f32(8, ROWS)] + shapes,
+        in_specs=in_vmem(7),
+        out_specs=in_vmem(7),
+        compiler_params=pltpu.CompilerParams(vmem_limit_bytes=VMEM_LIMIT),
+        cost_estimate=LIGHT,
+        name="update",
+    )(sums, *top_ins, *block_ins)
+
+
 def segment_lengths():
     top = [PATCH_IN * D, D * PIX, D * DPROJ, DPROJ * GAMES * PLAYS]
     block = [D * BOT, 9 * BOT * BOT, BOT * D, 2 * (2 * BOT + D)]
@@ -1051,24 +1271,15 @@
     return [patch, pool, proj.reshape(1, -1, WIDTH), heads]
 
 
-def flat_top(patch, pool, proj, heads):
-    patch = patch.reshape(2, 2, -1, WIDTH).transpose(2, 1, 0, 3)
+def flat_late(pool, proj, heads):
     heads = heads.transpose(1, 0, 2).reshape(-1, GAMES, 2 * WIDTH)[:, :, :PLAYS]
-    return jnp.concatenate(
-        [item.reshape(-1) for item in (patch, pool[:, :, :PIX], proj, heads)]
-    )
+    return jnp.concatenate([item.reshape(-1) for item in (pool[:, :, :PIX], proj, heads)])
 
 
 def pack_block(flat, cuts):
     w_in, w_mid, w_out = [flat[start : start + size] for start, size in cuts[:3]]
     w_out = w_out.reshape(-1, D // BOT, BOT).transpose(1, 0, 2)
     return [w_in.reshape(1, -1, BOT), w_mid.reshape(1, -1, BOT), w_out]
-
-
-def flat_block(w_in, w_mid, w_out, gains):
-    return jnp.concatenate(
-        [item.reshape(-1) for item in (w_in, w_mid, w_out.transpose(1, 0, 2), gains)]
-    )
 
 
 def parts_for(devices):
@@ -1103,31 +1314,6 @@
     array = array + hop(array, (1, 1))
     one, two, three = [hop(array, ALONG_Z, step) for step in (1, 2, 3)]
     return (array + two) + (one + three)
-
-
-def lamb_parts(params, grads, first, second):
-    momentum = BETA_ONE * first + (1.0 - BETA_ONE) * grads
-    variance = BETA_TWO * second + (1.0 - BETA_TWO) * grads * grads
-    direction = (
-        momentum / (1.0 - BETA_ONE**STEP) / (jnp.sqrt(variance / (1.0 - BETA_TWO**STEP)) + 1e-06)
-        + WEIGHT_DECAY * params
-    )
-    return (momentum, variance, direction)
-
-
-def squares(flat, cuts):
-    return jnp.stack(
-        [jnp.sum(jnp.square(flat[..., start : start + width]), axis=-1) for start, width in cuts],
-        axis=-1,
-    )
-
-
-def spread_ratio(ratio, flat, cuts):
-    parts = [
-        jnp.broadcast_to(ratio[..., index : index + 1], flat.shape[:-1] + (width,))
-        for index, (start, width) in enumerate(cuts)
-    ]
-    return jnp.concatenate(parts, axis=-1)
 
 
 def frame_rows(frames):
@@ -1166,10 +1352,6 @@
     place = spot()
     shift = shifts()
     spread = spread_pixels(devices)
-    weight_parts = jnp.concatenate(
-        [squares(params_top, top_cuts), squares(params_blocks, block_cuts).reshape(-1)]
-    )
-
     count = observed.shape[0]
     whole = jnp.concatenate([game_ids[:, None], actions], axis=1)
     whole = jnp.pad(whole, ((0, 8 - count), (0, ROWS - 3)), constant_values=-1)
@@ -1177,21 +1359,25 @@
     keep = discounts * (1.0 - done_flags.astype(jnp.float32))
     real = jnp.pad(jnp.stack([rewards, keep], axis=1), ((0, 8 - count), (0, ROWS - 2)))
 
-    low_blocks = params_blocks.astype(jnp.bfloat16)
-    own = {}
-    for net, top, blocks in (
-        ("target", target_top, target_blocks),
-        ("online", params_top.astype(jnp.bfloat16), low_blocks),
-    ):
-        for name, piece in zip(("patch", "pool", "proj", "heads"), pack_top(top, top_cuts)):
-            own[net, name] = piece
-        for index in range(BLOCKS):
-            for name, piece in zip(("w_in", "w_mid", "w_out"), pack_block(blocks[index], block_cuts)):
-                own[net, name, index] = piece
-    gain_rows = jnp.concatenate([target_blocks, low_blocks])[:, gain_start:]
-    own["gains",] = jnp.pad(
-        gain_rows, ((0, TILE - 2 * BLOCKS), (0, WIDTH - gain_width))
-    ).reshape(1, TILE, WIDTH)
+    def read_pieces(early):
+        sources = (target_top, target_blocks, params_top, params_blocks)
+        if early is not None:
+            early, sources = together(early, sources)
+        tops = (sources[0], sources[2].astype(jnp.bfloat16))
+        blocks = (sources[1], sources[3].astype(jnp.bfloat16))
+        own = {}
+        for net, top, flat in zip(("target", "online"), tops, blocks):
+            for name, piece in zip(("patch", "pool", "proj", "heads"), pack_top(top, top_cuts)):
+                own[net, name] = piece
+            for index in range(BLOCKS):
+                for name, piece in zip(block_names, pack_block(flat[index], block_cuts)):
+                    own[net, name, index] = piece
+        gain_rows = jnp.concatenate(blocks)[:, gain_start:]
+        own["gains",] = jnp.pad(
+            gain_rows, ((0, TILE - 2 * BLOCKS), (0, WIDTH - gain_width))
+        ).reshape(1, TILE, WIDTH)
+        return [[own[key] for key in group] for group in keys]
+
     block_names = ("w_in", "w_mid", "w_out")
 
     def part_of(key):
@@ -1205,14 +1391,25 @@
     def top_weights(net):
         return (full[net, "pool"][0], full[net, "proj"][0], full[net, "heads"])
 
-    def keep_ends(group, buffers, state):
-        arrays = assemble([part_of(key) for key in keys[group]], buffers, place) if tuned else buffers
+    def hold(net, index, group, buffers, state):
+        full["held", index] = (group, buffers)
+        return state
+
+    def read_gains(group, buffers, state):
+        gains = assemble(group_parts(group), buffers, place, [0])[0] if tuned else buffers[0]
+        gains = gains.reshape(devices, TILE, WIDTH)[:, : 2 * BLOCKS, :gain_width]
+        gains = gains.transpose(1, 0, 2).reshape(2 * BLOCKS, -1).astype(jnp.float32)
+        return run_block("target", 0, group, buffers, state | {"gains": gains})
+
+    def keep_ends(net, group, buffers, state):
+        arrays = assemble(group_parts(group), buffers, place) if tuned else buffers
         full.update(zip(keys[group], arrays))
-        if ("gains",) not in keys[group]:
-            return state
-        gains = full["gains",].reshape(devices, TILE, WIDTH)[:, : 2 * BLOCKS, :gain_width]
-        gains = gains.transpose(1, 0, 2).reshape(2 * BLOCKS, -1).astype(jnp.float32)
-        return state | {"gains": gains}
+        if net == "target":
+            for index in range(1, BLOCKS):
+                state = run_block(net, index, *full["held", index], state)
+            stream = state.pop("stream")
+            state |= {"target": head_target(stream, *top_weights(net), whole, real)}
+        return state
 
     def run_block(net, index, group, buffers, state):
         keep = net == "online"
@@ -1221,151 +1418,171 @@
         stream = [state["pixels" if keep else "following"], spread]
         if index:
             stream = [state["stream"]]
-        kinds = [part_of(key) for key in keys[group]]
-        out, *kept = block_forward(stream, gain, shift, kinds, buffers, place, keep, tuned)
+        skip = 1 if keys[group][0] == ("gains",) else 0
+        out, *kept = block_forward(
+            stream, gain, shift, group_parts(group), skip, buffers, place, keep, tuned
+        )
         state = state | {"stream": out}
         if keep:
             start = kept.pop(0) if index == 0 else stream[0]
             full.update(zip([(net, name, index) for name in block_names], kept[-3:]))
             state |= {"kept%d" % index: [start, *kept[:-3]]}
-        elif index == BLOCKS - 1:
-            state |= {"target": head_target(state.pop("stream"), *top_weights(net), whole, real)}
         return state
 
     keys, then = ([], [])
     ends = ("pool", "proj", "heads")
-    for net in ("target", "online"):
-        for index in range(BLOCKS):
-            keys.append([(net, name, index) for name in block_names])
-            if index == 0:
-                keys[-1] = [(net, "patch")] + keys[-1]
-            then.append(functools.partial(run_block, net, index))
-    keys = [[("gains",)] + [("target", name) for name in ends]] + keys
-    keys.append([("online", name) for name in ends])
-    then = [keep_ends, *then, keep_ends]
+
+    def add_group(group, run, *names):
+        keys.append(group)
+        then.append(functools.partial(run, *names))
+
+    def block_keys(net, index):
+        return [(net, name, index) for name in block_names]
+
+    for index in range(1, BLOCKS):
+        add_group(block_keys("target", index), hold, "target", index)
+    add_group([("gains",), ("target", "patch")] + block_keys("target", 0), read_gains)
+    add_group([("target", name) for name in ends], keep_ends, "target")
+    for index in range(BLOCKS):
+        start = [] if index else [("online", "patch")]
+        add_group(start + block_keys("online", index), run_block, "online", index)
+    add_group([("online", name) for name in ends], keep_ends, "online")
+
+    def group_parts(group):
+        return [part_of(key) for key in keys[group]]
 
     def arrived(group, buffers, state):
         return then[group](group, buffers, dict(state))
 
     state = {"following": frame_rows(following), "pixels": frame_rows(observed)}
-    pieces = [[own[key] for key in group] for group in keys]
     if tuned:
-        groups = [[part_of(key) for key in group] for group in keys]
-        state = pipelined_gather(groups, pieces, place, state, arrived)
+        groups = [group_parts(group) for group in range(len(keys))]
+        state = pipelined_gather(groups, read_pieces, place, state, arrived)
     else:
-        for group, items in enumerate(pieces):
+        for group, items in enumerate(read_pieces(None)):
             state = arrived(group, [plain_gather(item) for item in items], state)
 
-    def loss_step(state):
-        loss, dheads, dproj, dpool, dstream = head_loss(
-            state.pop("stream"), *top_weights("online"), state.pop("target"), whole, legal, frames_all
+    keys = []
+    steps = []
+
+    def loss_step(group, state):
+        (loss, dstream), dealt = head_loss(
+            state.pop("stream"), *top_weights("online"), state.pop("target"), whole, legal, frames_all,
+            group, tuned, place,
         )
-        state |= {"loss": loss[0, 0], "pool": dpool[None], "grad": dstream}
-        return ([dheads, dproj[None]], state)
-
-    def back_out_step(index, state):
+        return (dealt, state | {"loss": loss, "grad": dstream})
+
+    def out_inputs(index, state):
         stream, hid_one, hid_two, hid_three, rstd = state["kept%d" % index]
         gain = state["gains"][BLOCKS + index : BLOCKS + index + 1]
-        dres, dlow, dw_out, late = back_out(
-            state["grad"], stream, hid_two, hid_three, rstd, block_weight(index, "w_out"), gain
+        return [stream, hid_two, hid_three, rstd, block_weight(index, "w_out"), gain]
+
+    def out_step(index, group, state):
+        (dres, low, late), dealt = back_out(
+            state["grad"], *out_inputs(index, state), group, tuned, place
         )
-        state = state | {"grad": dres, "low": dlow, "late%d" % index: late}
-        return (dw_out.reshape(D // BOT, BOT, BOT), state)
-
-    def back_mid_step(index, state):
+        return (dealt, state | {"grad": dres, "low": low, "late%d" % index: late})
+
+    def mid_step(index, group, state):
         stream, hid_one, hid_two, hid_three, rstd = state["kept%d" % index]
         gain = state["gains"][BLOCKS + index : BLOCKS + index + 1]
-        dlow, dw_mid, early = back_mid(
-            state["low"], hid_one, rstd, block_weight(index, "w_mid"), gain, shift
+        (low, early), dealt = back_mid(
+            state["low"], hid_one, rstd, block_weight(index, "w_mid"), gain, shift, group, tuned, place
         )
-        return ([dw_mid[None]], state | {"low": dlow, "early%d" % index: early})
-
-    def back_in_step(index, state):
+        return (dealt, state | {"low": low, "early%d" % index: early})
+
+    def between_step(index, group, state):
         stream = state.pop("kept%d" % index)[0]
-        dw_in, dx = back_in(state["low"], stream, state["grad"], block_weight(index, "w_in"))
-        return (dw_in[None], state | {"grad": dx})
-
-    def first_step(state):
-        dw_out, state = back_out_step(BLOCKS - 1, dict(state))
-        return ([dw_out, state.pop("pool")], state)
-
-    def between_step(index, state):
-        dw_in, state = back_in_step(index, dict(state))
-        dw_out, state = back_out_step(index - 1, state)
-        return ([dw_in, dw_out], state)
-
-    def last_step(state):
-        dw_in, state = back_in_step(0, dict(state))
-        dpatch = embed_back(state.pop("pixels"), spread, state.pop("grad"))
+        (dres, low, late), dealt = back_between(
+            state["low"], stream, state["grad"], block_weight(index, "w_in"),
+            out_inputs(index - 1, state), group, tuned, place,
+        )
+        return (dealt, state | {"grad": dres, "low": low, "late%d" % (index - 1): late})
+
+    def first_step(group, state):
+        stream = state.pop("kept0")[0]
         dgains = [
             jnp.concatenate([state.pop("early%d" % index), state.pop("late%d" % index)], axis=1)
             for index in range(BLOCKS)
         ]
         dgains = jnp.concatenate(dgains).reshape(BLOCKS, devices, gain_width).transpose(1, 0, 2)
         dgains = jnp.pad(dgains, ((0, 0), (0, TILE - BLOCKS), (0, WIDTH - gain_width)))
-        return ([dw_in, dpatch, dgains.reshape(1, -1, WIDTH).astype(jnp.bfloat16)], state)
-
-    keys = [[("heads",), ("proj",)], [("w_out", BLOCKS - 1), ("pool",)]]
-    steps = [lambda state: loss_step(dict(state)), first_step]
+        dgains = dgains.reshape(1, -1, WIDTH).astype(jnp.bfloat16)
+        dealt = back_first(
+            state.pop("low"), stream, state.pop("grad"), block_weight(0, "w_in"),
+            state.pop("pixels"), spread, dgains, group, tuned, place,
+        )
+        return (dealt, state)
+
+    def add_step(group, run, *names):
+        keys.append(group)
+        steps.append(
+            lambda state: run(*names, [parts[key[0]] for key in group], dict(state))
+        )
+
+    add_step([("heads",), ("proj",), ("pool",)], loss_step)
+    add_step([("w_out", BLOCKS - 1)], out_step, BLOCKS - 1)
     for index in reversed(range(BLOCKS)):
-        keys.append([("w_mid", index)])
-        steps.append(functools.partial(back_mid_step, index))
-        keys.append([("w_in", index)])
-        keys[-1] += [("w_out", index - 1)] if index else [("patch",), ("gains",)]
-        steps.append(functools.partial(between_step, index) if index else last_step)
-    mine = {}
+        add_step([("w_mid", index)], mid_step, index)
+        if index:
+            add_step([("w_in", index), ("w_out", index - 1)], between_step, index)
+    add_step([("w_in", 0), ("patch",), ("gains",)], first_step)
+    groups = [[parts[key[0]] for key in group] for group in keys]
     if tuned:
-        groups = [[parts[key[0]] for key in group] for group in keys]
-        sums, state = pipelined_scatter(groups, place, state, steps)
-        for group, items in zip(keys, sums):
-            mine.update(zip(group, items))
+        mine, state = pipelined_scatter(groups, place, state, steps)
     else:
-        for group, step in zip(keys, steps):
+        mine = []
+        for group, step in zip(groups, steps):
             arrays, state = step(state)
-            mine.update(zip(group, [plain_scatter(array) for array in arrays]))
+            mine.append(pack(group, [plain_scatter(array) for array in arrays]))
     loss_part = state["loss"]
-    grad_top = flat_top(*[mine[name,] for name in ("patch", "pool", "proj", "heads")])
-    grad_blocks = jnp.stack(
-        [
-            flat_block(*[mine[name, index] for name in block_names], mine["gains",][0, index, :gain_width])
-            for index in range(BLOCKS)
-        ]
+    at = {}
+    moves = []
+    for number, group in enumerate(keys):
+        first = 0
+        steps = []
+        for key in group:
+            count = parts[key[0]].travel
+            at[key] = (number, first)
+            if len(key) > 1:
+                start = block_cuts[block_names.index(key[0])][0]
+                steps.append((key[1], block_rows(key[0], start, count, first)))
+            elif key[0] == "patch":
+                steps.append((None, patch_rows(count, first)))
+            first += count
+        moves.append(steps)
+    late = []
+    for name in ("pool", "proj", "heads"):
+        number, first = at[name,]
+        late.append(parts[name].unpack(mine[number][first : first + parts[name].travel]))
+    late = flat_late(*late)[None]
+    cuts = (top_cuts, block_cuts)
+    tops = [array[None] for array in (params_top, first_top, second_top, average_top)]
+    sums, *made = directions(
+        cuts, mine[1:], moves[1:], (at["gains",][0] - 1, at["gains",][1]), late, loss_part,
+        tops[:3], [params_blocks, first_blocks, second_blocks],
     )
-
-    momentum_top, variance_top, direction_top = lamb_parts(
-        params_top, grad_top, first_top, second_top
+    momentum_top, variance_top, direction_top, momentum_blocks, variance_blocks, direction_blocks = made
+    sums = total(sums)
+    norms, *made = update(
+        cuts, sums, [tops[0], direction_top, tops[3]],
+        [params_blocks, direction_blocks, average_blocks],
     )
-    momentum_blocks, variance_blocks, direction_blocks = lamb_parts(
-        params_blocks, grad_blocks, first_blocks, second_blocks
-    )
-    update_parts = jnp.concatenate(
-        [squares(direction_top, top_cuts), squares(direction_blocks, block_cuts).reshape(-1)]
-    )
-    sums = total(jnp.concatenate([weight_parts, update_parts, loss_part[None]])[None])[0]
-    count = weight_parts.shape[0]
-    weight_sq, update_sq, loss_total = (sums[:count], sums[count : 2 * count], sums[2 * count])
-    weight_norm = jnp.sqrt(weight_sq)
-    update_norm = jnp.sqrt(update_sq)
-    ratio = weight_norm / (update_norm + 1e-06)
-    scale_top = spread_ratio(ratio[:4], params_top, top_cuts)
-    scale_blocks = spread_ratio(ratio[4:].reshape(BLOCKS, 4), params_blocks, block_cuts)
-    updated_top = params_top - LEARNING_RATE * scale_top * direction_top
-    updated_blocks = params_blocks - LEARNING_RATE * scale_blocks * direction_blocks
-    decay = average_decay()
-    averaged_top = decay * average_top + (1.0 - decay) * updated_top
-    averaged_blocks = decay * average_blocks + (1.0 - decay) * updated_blocks
-    matrix_norms = jnp.stack([weight_norm, update_norm])
-    gain_grads = grad_blocks[:, gain_start : gain_start + gain_width]
+    updated_top, half_top, averaged_top, updated_blocks, half_blocks, averaged_blocks = made
+    loss_total = sums[2, 0]
+    matrix_norms = norms[:2, : len(top_cuts) + BLOCKS * len(block_cuts)]
+    number, first = at["gains",]
+    gain_grads = mine[number][first : first + BLOCKS, :gain_width]
     return (
         loss_total,
         matrix_norms,
-        updated_top,
-        updated_top.astype(jnp.bfloat16),
-        momentum_top,
-        variance_top,
-        averaged_top,
+        updated_top[0],
+        half_top[0],
+        momentum_top[0],
+        variance_top[0],
+        averaged_top[0],
         updated_blocks,
-        updated_blocks.astype(jnp.bfloat16),
+        half_blocks,
         momentum_blocks,
         variance_blocks,
         averaged_blocks,

time: 762 us -> 670 us (0.88)
  other arithmetic: 120 us -> 70.6 us
  local copies, waits for them, and re-layouts: 96.2 us -> 50.2 us
    another operation x20 -> x10, other arithmetic: 36.1 us -> 14.4 us  [the longest x6 14.4 us: pipelined_gather(): held[near] = jnp.stack(items)]
    slice x43 -> x10, local copies, waits for them, and re-layouts: 24.9 us -> 6.55 us  [the longest x2 1.3 us: mid_step(): gain = state['gains'][BLOCKS + index:BLOCKS + index + 1]]
    add x4 -> x0, other arithmetic: 16.5 us -> none  [the longest x2 7.91 us: lamb_parts(): momentum / (1.0 - BETA_ONE ** STEP)]
    convert_element_type x18 -> x12, other arithmetic: 37 us -> 24 us  [low_add(): return add_up(*terms).astype(jnp.bfloat16)]
    concatenate x3 -> x2, local copies, waits for them, and re-layouts: 14.3 us -> 4.07 us  [the longest x1 4.07 us: flat_late(): jnp.concatenate([item.reshape(-1) for item in (pool[:, :, :PIX], proj, he...]
    reduce_sum x14 -> x0, other arithmetic: 7.89 us -> none  [squares(): jnp.sum(jnp.square(flat[..., start:start + width]), axis=-1)]
    ppermute x85 -> x92, waiting for transfers between devices: 168 us -> 175 us  [hop(): return lax.ppermute(array, AXES, pairs)]
    ppermute x85 -> x92, starting transfers between devices: 134 us -> 129 us  [hop(): return lax.ppermute(array, AXES, pairs)]
  transfers between devices with their start and end apart: 85 -> 92, of which waited for: 34 -> 37; matrix products, arithmetic and copies ran while one was open for 12% -> 12% of each run, Pallas kernels for 22% -> 27%
where the time goes in v4:
time: 670 us; the launch traced here: 661 us
  Pallas kernels  232 us (35%)
  waiting for transfers between devices  175 us (26%)
  starting transfers between devices  129 us (19%)
  other arithmetic  70.6 us (11%)
  local copies, waits for them, and re-layouts  50.2 us (7%)
    ppermute x92, waiting for transfers between devices, hop(): return lax.ppermute(array, AXES, pairs)  175 us
    ppermute x92, starting transfers between devices, hop(): return lax.ppermute(array, AXES, pairs)  129 us
    pallas_call x6, Pallas kernels, back_call(): pl.pallas_call(functools.partial(back_kernel, body, parts, tuned, counts)...  84.2 us
    pallas_call x4, Pallas kernels, block_forward(): pl.pallas_call(functools.partial(forward_kernel, count, keep, parts, skip...  74.5 us
    convert_element_type x12, other arithmetic, low_add(): return add_up(*terms).astype(jnp.bfloat16)  24 us
    pallas_call x6, Pallas kernels, stack_z(): pl.pallas_call(functools.partial(stack_kernel, size), out_shape=jax.Shape...  17.8 us
    pallas_call x1, Pallas kernels, directions(): pl.pallas_call(functools.partial(direction_kernel, cuts, moves, gain_at),...  16.8 us
    pallas_call x1, Pallas kernels, update(): pl.pallas_call(functools.partial(update_kernel, cuts), out_shape=[f32(8,...  16.1 us
  transfers between devices with their start and end apart: 92, of which 37 were waited for; matrix products, arithmetic and copies ran while one was open for 12% of the time, Pallas kernels for 27%

profile of v4, /device:TPU:0, one launch (start us, length us, event | category | flops | bytes accessed | tf_op | source)
XLA Modules:
  0.0 660.9 jit_solution(13776409541769651616)
XLA Ops:
  25.4 5.4 collective-permute-done.2.refs_1_
  30.9 12.0 %collective-permute-done.3.refs_2_ = bf16[2,144,512]{2,1,0:T(8,128)(2,1)S(1)} collective-permute-done((bf16[2,144,512]{2,1,0:T(8,128)(2,1)S(1)}, bf16[2,144,512]{2,1,0:T(8,128)(2,1)S(1)}, u32[]{:S(2)}, u32[]{:S(2)}) %collective-permute-start.3) | collective-permute-done | bytes 294944 | tf_op jit(solution)/shard_map/ppermute | solution.py:701
  51.0 6.1 collective-permute-start.5
  61.2 6.4 collective-permute-done.5.refs_1_
  67.6 12.2 %collective-permute-done.6.refs_2_ = bf16[2,160,512]{2,1,0:T(8,128)(2,1)S(1)} collective-permute-done((bf16[2,160,512]{2,1,0:T(8,128)(2,1)S(1)}, bf16[2,160,512]{2,1,0:T(8,128)(2,1)S(1)}, u32[]{:S(2)}, u32[]{:S(2)}) %collective-permute-start.6) | collective-permute-done | bytes 327712 | tf_op jit(solution)/shard_map/ppermute | solution.py:701
  89.7 5.7 collective-permute-start.10
  95.4 3.5 collective-permute-start.11
  100.1 6.7 %collective-permute-done.10.refs_2_ = bf16[2,112,512]{2,1,0:T(8,128)(2,1)S(1)} collective-permute-done((bf16[2,112,512]{2,1,0:T(8,128)(2,1)S(1)}, bf16[2,112,512]{2,1,0:T(8,128)(2,1)S(1)}, u32[]{:S(2)}, u32[]{:S(2)}) %collective-permute-start.10) | collective-permute-done | bytes 229408 | tf_op jit(solution)/shard_map/ppermute | solution.py:701
  106.8 7.0 %collective-permute-done.9.refs_1_ = bf16[2,112,512]{2,1,0:T(8,128)(2,1)S(1)} collective-permute-done((bf16[2,112,512]{2,1,0:T(8,128)(2,1)S(1)}, bf16[2,112,512]{2,1,0:T(8,128)(2,1)S(1)}, u32[]{:S(2)}, u32[]{:S(2)}) %collective-permute-start.9) | collective-permute-done | bytes 229408 | tf_op jit(solution)/shard_map/ppermute | solution.py:701
  122.1 8.8 %collective-permute-done.13.refs_5_ = bf16[2,4,2,144,512]{4,3,2,1,0:T(8,128)(2,1)} collective-permute-done((bf16[2,4,2,144,512]{4,3,2,1,0:T(8,128)(2,1)}, bf16[2,4,2,144,512]{4,3,2,1,0:T(8,128)(2,1)}, u32[]{:S(2)}, u32[]{:S(2)}) %collective-permute-start.13) | collective-permute-done | bytes 2359328 | tf_op jit(solution)/shard_map/ppermute | solution.py:701
  135.8 7.0 %collective-permute-start.14 = (bf16[2,160,512]{2,1,0:T(8,128)(2,1)S(1)}, bf16[2,160,512]{2,1,0:T(8,128)(2,1)S(1)}, u32[]{:S(2)}, u32[]{:S(2)}) collective-permute-start(bf16[2,160,512]{2,1,0:T(8,128)(2,1)S(1)} %copy-done.20), channel_id=1, source_target_pairs={{0,8},{1,9},{2,10},{3,11},{4,12},{5,13},{6,14},{7,15},{8,16},{9,17... | collective-permute-start | bytes 983048 | tf_op jit(solution)/shard_map/ppermute | solution.py:701
  146.8 5.7 collective-permute-done.14.refs_1_
  152.5 12.9 %collective-permute-done.15.refs_2_ = bf16[2,160,512]{2,1,0:T(8,128)(2,1)S(1)} collective-permute-done((bf16[2,160,512]{2,1,0:T(8,128)(2,1)S(1)}, bf16[2,160,512]{2,1,0:T(8,128)(2,1)S(1)}, u32[]{:S(2)}, u32[]{:S(2)}) %collective-permute-start.15) | collective-permute-done | bytes 327712 | tf_op jit(solution)/shard_map/ppermute | solution.py:701
  175.9 6.9 %collective-permute-start.19 = (bf16[2,144,512]{2,1,0:T(8,128)(2,1)}, bf16[2,144,512]{2,1,0:T(8,128)(2,1)S(1)}, u32[]{:S(2)}, u32[]{:S(2)}) collective-permute-start(bf16[2,144,512]{2,1,0:T(8,128)(2,1)} %pad_maximum_fusion.12.refs_0_), channel_id=1, source_target_pairs={{0,8},{1,9},{2,10},{3,11},{4,12},{5,13},{6,14},{7,15},{8,16},{9,17... | collective-permute-start | bytes 884744 | tf_op jit(solution)/shard_map/ppermute | solution.py:701
  183.0 7.8 %collective-permute-done.19.refs_1_ = bf16[2,144,512]{2,1,0:T(8,128)(2,1)S(1)} collective-permute-done((bf16[2,144,512]{2,1,0:T(8,128)(2,1)}, bf16[2,144,512]{2,1,0:T(8,128)(2,1)S(1)}, u32[]{:S(2)}, u32[]{:S(2)}) %collective-permute-start.19) | collective-permute-done | bytes 294944 | tf_op jit(solution)/shard_map/ppermute | solution.py:701
  200.8 8.7 %collective-permute-done.20.refs_2_ = bf16[2,144,512]{2,1,0:T(8,128)(2,1)S(1)} collective-permute-done((bf16[2,144,512]{2,1,0:T(8,128)(2,1)}, bf16[2,144,512]{2,1,0:T(8,128)(2,1)S(1)}, u32[]{:S(2)}, u32[]{:S(2)}) %collective-permute-start.20) | collective-permute-done | bytes 294944 | tf_op jit(solution)/shard_map/ppermute | solution.py:701
  210.2 18.0 %block_forward.4.refs_1_ = f32[384,2048]{1,0:T(8,128)} custom-call(s32[4]{0:T(128)} %pad_add_fusion.1.place.refs_0_, bf16[384,256]{1,0:T(8,128)(2,1)} %bitcast.402, bf16[2,256,512]{2,1,0:T(8,128)(2,1)} %add_convert_fusion.refs_2_.refs_6_, f32[1,6144]{1,0:T(1,128)} %slice.278.refs_3_, bf16[1152,128]{1,0:T(8,128)(2,1)} %convert_element_type.506.refs_4_.refs_3_.refs_6_, ...), custom_call_target="tpu_custom_call" | custom-call | flops 1024 | bytes 1024 | tf_op jit(solution)/shard_map/block_forward/pallas_call | solution.py:248
  237.9 4.8 collective-permute-start.26
  246.0 3.7 collective-permute-start.28
  251.2 17.2 %block_forward.5.stream = f32[384,2048]{1,0:T(8,128)} custom-call(s32[4]{0:T(128)} %pad_add_fusion.1.place.refs_0_, f32[384,2048]{1,0:T(8,128)} %block_forward.4.refs_1_, f32[1,6144]{1,0:T(1,128)} %slice.279.refs_2_, bf16[1152,128]{1,0:T(8,128)(2,1)} %convert_element_type.506.refs_4_.refs_3_.refs_6_, bf16[2,4,2,144,512]{4,3,2,1,0:T(8,128)(2,1)} %pad_maximum_fusion.2.refs_4_, ...), custom_call_target="tpu_custom_call" | custom-call | flops 1024 | bytes 1024 | tf_op jit(solution)/shard_map/block_forward/pallas_call | solution.py:248
  268.4 6.6 %assemble.4 = (bf16[1,4,2,2,2,64,128]{6,5,4,3,2,1,0:T(8,128)(2,1)}, bf16[1,4,2,2,2,64,512]{6,5,4,3,2,1,0:T(8,128)(2,1)}, bf16[8,4,2,2,2,16,512]{6,5,4,3,2,1,0:T(8,128)(2,1)}) custom-call(s32[4]{0:T(128)} %pad_add_fusion.1.place.refs_0_, bf16[2,4,2,112,512]{4,3,2,1,0:T(8,128)(2,1)} %pad_maximum_fusion.4.refs_0_, ...), custom_call_target="tpu_custom_call" | custom-call | flops 1024 | bytes 1024 | tf_op jit(solution)/shard_map/assemble/pallas_call | solution.py:861
  275.1 7.2 %head_target.1.refs_5_ = f32[8,128]{1,0:T(8,128)} custom-call(f32[384,2048]{1,0:T(8,128)} %block_forward.5.stream, bf16[2048,128]{1,0:T(8,128)(2,1)} %bitcast.411, bf16[2048,512]{1,0:T(8,128)(2,1)} %bitcast.385, bf16[8,512,512]{2,1,0:T(8,128)(2,1)} %bitcast.376, s32[8,128]{1,0:T(8,128)} %pad.72.whole.refs_6_, f32[8,128]{1,0:T(8,128)} %select_maximum_fusion.real), custom_call_target="tpu_custom_call" | custom-call | flops 1024 | bytes 1024 | tf_op jit(solution)/shard_map/head_target/pallas_call | solution.py:573
  298.5 20.6 %block_forward.6 = (f32[384,2048]{1,0:T(8,128)}, f32[384,2048]{1,0:T(8,128)}, f32[384,512]{1,0:T(8,128)}, f32[384,512]{1,0:T(8,128)}, f32[384,2048]{1,0:T(8,128)...) custom-call(s32[4]{0:T(128)} %pad_add_fusion.1.place.refs_0_, ...), custom_call_target="tpu_custom_call" | custom-call | flops 1024 | bytes 1024 | tf_op jit(solution)/shard_map/block_forward/pallas_call | solution.py:248
  320.4 8.1 %collective-permute-done.38.refs_5_ = bf16[2,4,2,144,512]{4,3,2,1,0:T(8,128)(2,1)} collective-permute-done((bf16[2,4,2,144,512]{4,3,2,1,0:T(8,128)(2,1)}, bf16[2,4,2,144,512]{4,3,2,1,0:T(8,128)(2,1)}, u32[]{:S(2)}, u32[]{:S(2)}) %collective-permute-start.38) | collective-permute-done | bytes 2359328 | tf_op jit(solution)/shard_map/ppermute | solution.py:701
  336.8 18.7 %block_forward.7 = (f32[384,2048]{1,0:T(8,128)}, f32[384,512]{1,0:T(8,128)}, f32[384,512]{1,0:T(8,128)}, f32[384,2048]{1,0:T(8,128)}, f32[8,3072]{1,0:T(8,128)},...) custom-call(s32[4]{0:T(128)} %pad_add_fusion.1.place.refs_0_, ...), custom_call_target="tpu_custom_call" | custom-call | flops 1024 | bytes 1024 | tf_op jit(solution)/shard_map/block_forward/pallas_call | solution.py:248
  356.7 3.9 collective-permute-done.42.refs_2_
  362.1 6.6 assemble.5
  368.7 15.5 %head_loss.1 = (f32[1,1]{1,0:T(1,128)}, f32[384,2048]{1,0:T(8,128)}, bf16[2,2,4,2,112,512]{5,4,3,2,1,0:T(8,128)(2,1)}, bf16[2,4,2,112,512]{4,3,2,1,0:T(8,128)(2,...) custom-call(s32[4]{0:T(128)} %pad_add_fusion.1.place.refs_0_, ...), custom_call_target="tpu_custom_call" | custom-call | flops 1024 | bytes 1024 | tf_op jit(solution)/shard_map/head_loss/pallas_call | solution.py:414
  385.4 15.3 %back_out.1 = (f32[384,2048]{1,0:T(8,128)}, bf16[384,512]{1,0:T(8,128)(2,1)}, f32[1,5120]{1,0:T(1,128)}, bf16[2,2,4,2,32,512]{5,4,3,2,1,0:T(8,128)(2,1)}, bf16[2...) custom-call(s32[4]{0:T(128)} %pad_add_fusion.1.place.refs_0_, ...), custom_call_target="tpu_custom_call" | custom-call | flops 1024 | bytes 1024 | tf_op jit(solution)/shard_map/back_out/pallas_call | solution.py:414
  400.7 4.6 fusion
  407.1 12.3 %back_mid.2 = (bf16[384,512]{1,0:T(8,128)(2,1)}, f32[1,1024]{1,0:T(1,128)}, bf16[2,2,4,2,80,512]{5,4,3,2,1,0:T(8,128)(2,1)}, bf16[2,4,2,80,512]{4,3,2,1,0:T(8,12...) custom-call(s32[4]{0:T(128)} %pad_add_fusion.1.place.refs_0_, ...), custom_call_target="tpu_custom_call" | custom-call | flops 1024 | bytes 1024 | tf_op jit(solution)/shard_map/back_mid/pallas_call | solution.py:414
  419.5 9.4 %collective-permute-done.45 = bf16[2,4,2,112,512]{4,3,2,1,0:T(8,128)(2,1)} collective-permute-done((bf16[2,4,2,112,512]{4,3,2,1,0:T(8,128)(2,1)}, bf16[2,4,2,112,512]{4,3,2,1,0:T(8,128)(2,1)}, u32[]{:S(2)}, u32[]{:S(2)}) %collective-permute-start.45) | collective-permute-done | bytes 1835040 | tf_op jit(solution)/shard_map/ppermute | solution.py:701
  428.9 4.4 fusion.5
  436.8 19.7 %back_between.1 = (f32[384,2048]{1,0:T(8,128)}, bf16[384,512]{1,0:T(8,128)(2,1)}, f32[1,5120]{1,0:T(1,128)}, bf16[2,2,4,2,64,512]{5,4,3,2,1,0:T(8,128)(2,1)}, bf...) custom-call(s32[4]{0:T(128)} %pad_add_fusion.1.place.refs_0_, ...), custom_call_target="tpu_custom_call" | custom-call | flops 1024 | bytes 1024 | tf_op jit(solution)/shard_map/back_between/pallas_call | solution.py:414
  466.7 7.7 %collective-permute-done.50 = bf16[2,112,512]{2,1,0:T(8,128)(2,1)S(1)} collective-permute-done((bf16[2,112,512]{2,1,0:T(8,128)(2,1)S(1)}, bf16[2,112,512]{2,1,0:T(8,128)(2,1)S(1)}, u32[]{:S(2)}, u32[]{:S(2)}) %collective-permute-start.50) | collective-permute-done | bytes 229408 | tf_op jit(solution)/shard_map/ppermute | solution.py:701
  475.1 12.5 %back_mid.3 = (bf16[384,512]{1,0:T(8,128)(2,1)}, f32[1,1024]{1,0:T(1,128)}, bf16[2,2,4,2,80,512]{5,4,3,2,1,0:T(8,128)(2,1)}, bf16[2,4,2,80,512]{4,3,2,1,0:T(8,12...) custom-call(s32[4]{0:T(128)} %pad_add_fusion.1.place.refs_0_, ...), custom_call_target="tpu_custom_call" | custom-call | flops 1024 | bytes 1024 | tf_op jit(solution)/shard_map/back_mid/pallas_call | solution.py:414
  504.0 9.0 %back_first.1 = (bf16[2,2,4,2,64,512]{5,4,3,2,1,0:T(8,128)(2,1)}, bf16[2,4,2,64,512]{4,3,2,1,0:T(8,128)(2,1)}, bf16[4,2,64,512]{3,2,1,0:T(8,128)(2,1)}, bf16[4,2,64,512]{3,2,1,0:T(8,128)(2,1)}) custom-call(s32[4]{0:T(128)} %pad_add_fusion.1.place.refs_0_, bf16[384,512]{1,0:T(8,128)(2,1)} %get-tuple-element.698.refs_1_, ...), custom_call_target="tpu_custom_call" | custom-call | flops 1024 | bytes 1024 | tf_op jit(solution)/shard_map/back_first/pallas_call | solution.py:414
  517.3 4.1 concatenate.58
  535.4 5.1 collective-permute-done.64
  542.1 3.6 collective-permute-start.68
  551.0 5.3 collective-permute-done.69
  559.7 6.0 collective-permute-done.79
  570.8 4.9 collective-permute-start.74
  575.7 4.9 collective-permute-start.75
  594.3 5.9 collective-permute-done.82
  603.4 16.8 %directions.1 = (f32[8,128]{1,0:T(8,128)}, f32[1,115648]{1,0:T(1,128)}, f32[1,115648]{1,0:T(1,128)}, f32[1,115648]{1,0:T(1,128)}, f32[2,139456]{1,0:T(2,128)}, /*index=5*/f32[2,139456]{1,0:T(2,128)}, f32[2,139456]{1,0:T(2,128)}) custom-call(f32[64,512]{1,0:T(8,128)} %bitcast.404, f32[160,512]{1,0:T(8,128)} %bitcast.394, f32[128,512]{1,0:T(8,128)} %bitcast.399, ...), custom_call_target="tpu_custom_call" | custom-call | flops 1024 | bytes 1024 | tf_op jit(solution)/shard_map/directions/pallas_call | solution.py:1173
  629.5 3.5 collective-permute-start.89
  640.1 16.1 %update.1 = (f32[8,128]{1,0:T(8,128)}, f32[1,115648]{1,0:T(1,128)}, bf16[1,115648]{1,0:T(2,128)(2,1)}, f32[1,115648]{1,0:T(1,128)}, f32[2,139456]{1,0:T(2,128)},...) custom-call(f32[8,128]{1,0:T(8,128)} %copy-done.76, f32[1,115648]{1,0:T(1,128)} %bitcast.378, ...), custom_call_target="tpu_custom_call" | custom-call | flops 1024 | bytes 1024 | tf_op jit(solution)/shard_map/update/pallas_call | solution.py:1238
  (557 shorter events, 232.9 us)
Async XLA Ops:
  17.8 29.5 %collective-permute-start.1 = (bf16[688,512]{1,0:T(8,128)(2,1)}, bf16[688,512]{1,0:T(8,128)(2,1)S(1)}, u32[]{:S(2)}, u32[]{:S(2)}) collective-permute-start(bf16[688,512]{1,0:T(8,128)(2,1)} %dynamic-slice_dynamic-update-slice_fusion.3), channel_id=1, source_target_pairs={{0,1},{1,0},{2,3},{3,2},{4,5},{5,4},{6,7},{7,6},{8,9},{9,8},{10,11... | collective-permute-start | bytes 2113544 | tf_op jit(solution)/shard_map/ppermute | solution.py:701
  20.9 22.0 %collective-permute-start.3 = (bf16[2,144,512]{2,1,0:T(8,128)(2,1)S(1)}, bf16[2,144,512]{2,1,0:T(8,128)(2,1)S(1)}, u32[]{:S(2)}, u32[]{:S(2)}) collective-permute-start(bf16[2,144,512]{2,1,0:T(8,128)(2,1)S(1)} %pad_maximum_fusion.11.refs_0_), channel_id=1, source_target_pairs={{0,16},{1,17},{2,18},{3,19},{4,20},{5,21},{6,22},{7,23},{8,24},{9,... | collective-permute-start | bytes 884744 | tf_op jit(solution)/shard_map/ppermute | solution.py:701
  23.5 19.4 %collective-permute-start.4 = (bf16[2,144,512]{2,1,0:T(8,128)(2,1)S(1)}, bf16[2,144,512]{2,1,0:T(8,128)(2,1)S(1)}, u32[]{:S(2)}, u32[]{:S(2)}) collective-permute-start(bf16[2,144,512]{2,1,0:T(8,128)(2,1)S(1)} %pad_maximum_fusion.11.refs_0_), channel_id=1, source_target_pairs={{0,24},{1,25},{2,26},{3,27},{4,28},{5,29},{6,30},{7,31},{8,0},{9,1... | collective-permute-start | bytes 884744 | tf_op jit(solution)/shard_map/ppermute | solution.py:701
  49.4 34.2 %collective-permute-start.8 = (bf16[4,2,144,512]{3,2,1,0:T(8,128)(2,1)S(1)}, bf16[4,2,144,512]{3,2,1,0:T(8,128)(2,1)S(1)}, u32[]{:S(2)}, u32[]{:S(2)}) collective-permute-start(bf16[4,2,144,512]{3,2,1,0:T(8,128)(2,1)S(1)} %copy-done.8), channel_id=1, source_target_pairs={{0,2},{1,5},{2,0},{3,7},{4,6},{5,1},{6,4},{7,3},{8,10},{9,13},{10,... | collective-permute-start | bytes 3538952 | tf_op jit(solution)/shard_map/ppermute | solution.py:701
  51.0 16.6 %collective-permute-start.5 = (bf16[2,160,512]{2,1,0:T(8,128)(2,1)S(1)}, bf16[2,160,512]{2,1,0:T(8,128)(2,1)S(1)}, u32[]{:S(2)}, u32[]{:S(2)}) collective-permute-start(bf16[2,160,512]{2,1,0:T(8,128)(2,1)S(1)} %pad_maximum_fusion.8.refs_0_), channel_id=1, source_target_pairs={{0,8},{1,9},{2,10},{3,11},{4,12},{5,13},{6,14},{7,15},{8,16},{9,17... | collective-permute-start | bytes 983048 | tf_op jit(solution)/shard_map/ppermute | solution.py:701
  57.1 22.7 %collective-permute-start.6 = (bf16[2,160,512]{2,1,0:T(8,128)(2,1)S(1)}, bf16[2,160,512]{2,1,0:T(8,128)(2,1)S(1)}, u32[]{:S(2)}, u32[]{:S(2)}) collective-permute-start(bf16[2,160,512]{2,1,0:T(8,128)(2,1)S(1)} %pad_maximum_fusion.8.refs_0_), channel_id=1, source_target_pairs={{0,16},{1,17},{2,18},{3,19},{4,20},{5,21},{6,22},{7,23},{8,24},{9,... | collective-permute-start | bytes 983048 | tf_op jit(solution)/shard_map/ppermute | solution.py:701
  59.4 21.2 %collective-permute-start.7 = (bf16[2,160,512]{2,1,0:T(8,128)(2,1)S(1)}, bf16[2,160,512]{2,1,0:T(8,128)(2,1)}, u32[]{:S(2)}, u32[]{:S(2)}) collective-permute-start(bf16[2,160,512]{2,1,0:T(8,128)(2,1)S(1)} %pad_maximum_fusion.8.refs_0_), channel_id=1, source_target_pairs={{0,24},{1,25},{2,26},{3,27},{4,28},{5,29},{6,30},{7,31},{8,0},{9,1... | collective-permute-start | bytes 983048 | tf_op jit(solution)/shard_map/ppermute | solution.py:701
  87.7 43.2 %collective-permute-start.13 = (bf16[2,4,2,144,512]{4,3,2,1,0:T(8,128)(2,1)}, bf16[2,4,2,144,512]{4,3,2,1,0:T(8,128)(2,1)}, u32[]{:S(2)}, u32[]{:S(2)}) collective-permute-start(bf16[2,4,2,144,512]{4,3,2,1,0:T(8,128)(2,1)} %pad_maximum_fusion.2.refs_4_), channel_id=1, source_target_pairs={{0,4},{1,3},{2,6},{3,1},{4,0},{5,7},{6,2},{7,5},{8,12},{9,11},{10,... | collective-permute-start | bytes 7077896 | tf_op jit(solution)/shard_map/ppermute | solution.py:701
  88.2 31.8 %collective-permute-start.12 = (bf16[4,2,160,512]{3,2,1,0:T(8,128)(2,1)S(1)}, bf16[4,2,160,512]{3,2,1,0:T(8,128)(2,1)}, u32[]{:S(2)}, u32[]{:S(2)}) collective-permute-start(bf16[4,2,160,512]{3,2,1,0:T(8,128)(2,1)S(1)} %copy-done.5), channel_id=1, source_target_pairs={{0,2},{1,5},{2,0},{3,7},{4,6},{5,1},{6,4},{7,3},{8,10},{9,13},{10,... | collective-permute-start | bytes 3932168 | tf_op jit(solution)/shard_map/ppermute | solution.py:701
  89.7 17.1 %collective-permute-start.10 = (bf16[2,112,512]{2,1,0:T(8,128)(2,1)S(1)}, bf16[2,112,512]{2,1,0:T(8,128)(2,1)S(1)}, u32[]{:S(2)}, u32[]{:S(2)}) collective-permute-start(bf16[2,112,512]{2,1,0:T(8,128)(2,1)S(1)} %pad_maximum_fusion.16.refs_0_), channel_id=1, source_target_pairs={{0,16},{1,17},{2,18},{3,19},{4,20},{5,21},{6,22},{7,23},{8,24},{9,... | collective-permute-start | bytes 688136 | tf_op jit(solution)/shard_map/ppermute | solution.py:701
  130.9 41.5 %collective-permute-start.18 = (bf16[2,4,2,160,512]{4,3,2,1,0:T(8,128)(2,1)S(1)}, bf16[2,4,2,160,512]{4,3,2,1,0:T(8,128)(2,1)}, u32[]{:S(2)}, u32[]{:S(2)}) collective-permute-start(bf16[2,4,2,160,512]{4,3,2,1,0:T(8,128)(2,1)S(1)} %pad_maximum_fusion.refs_0_.refs_5_), channel_id=1, source_target_pairs={{0,4},{1,3},{2,6},{3,1},{4,0},{5,7},{6,2},{7,5},{8,12},{9,11},{10,... | collective-permute-start | bytes 7864328 | tf_op jit(solution)/shard_map/ppermute | solution.py:701
  131.9 37.3 %collective-permute-start.17 = (bf16[4,2,112,512]{3,2,1,0:T(8,128)(2,1)S(1)}, bf16[4,2,112,512]{3,2,1,0:T(8,128)(2,1)}, u32[]{:S(2)}, u32[]{:S(2)}) collective-permute-start(bf16[4,2,112,512]{3,2,1,0:T(8,128)(2,1)S(1)} %copy-done.10), channel_id=1, source_target_pairs={{0,2},{1,5},{2,0},{3,7},{4,6},{5,1},{6,4},{7,3},{8,10},{9,13},{10,... | collective-permute-start | bytes 2752520 | tf_op jit(solution)/shard_map/ppermute | solution.py:701
  135.8 16.7 %collective-permute-start.14 = (bf16[2,160,512]{2,1,0:T(8,128)(2,1)S(1)}, bf16[2,160,512]{2,1,0:T(8,128)(2,1)S(1)}, u32[]{:S(2)}, u32[]{:S(2)}) collective-permute-start(bf16[2,160,512]{2,1,0:T(8,128)(2,1)S(1)} %copy-done.20), channel_id=1, source_target_pairs={{0,8},{1,9},{2,10},{3,11},{4,12},{5,13},{6,14},{7,15},{8,16},{9,17... | collective-permute-start | bytes 983048 | tf_op jit(solution)/shard_map/ppermute | solution.py:701
  142.7 22.7 %collective-permute-start.15 = (bf16[2,160,512]{2,1,0:T(8,128)(2,1)S(1)}, bf16[2,160,512]{2,1,0:T(8,128)(2,1)S(1)}, u32[]{:S(2)}, u32[]{:S(2)}) collective-permute-start(bf16[2,160,512]{2,1,0:T(8,128)(2,1)S(1)} %copy-done.20), channel_id=1, source_target_pairs={{0,16},{1,17},{2,18},{3,19},{4,20},{5,21},{6,22},{7,23},{8,24},{9,... | collective-permute-start | bytes 983048 | tf_op jit(solution)/shard_map/ppermute | solution.py:701
  144.3 21.8 %collective-permute-start.16 = (bf16[2,160,512]{2,1,0:T(8,128)(2,1)S(1)}, bf16[2,160,512]{2,1,0:T(8,128)(2,1)}, u32[]{:S(2)}, u32[]{:S(2)}) collective-permute-start(bf16[2,160,512]{2,1,0:T(8,128)(2,1)S(1)} %copy-done.20), channel_id=1, source_target_pairs={{0,24},{1,25},{2,26},{3,27},{4,28},{5,29},{6,30},{7,31},{8,0},{9,1... | collective-permute-start | bytes 983048 | tf_op jit(solution)/shard_map/ppermute | solution.py:701
  172.4 18.6 %collective-permute-start.22 = (bf16[2,4,2,160,512]{4,3,2,1,0:T(8,128)(2,1)S(1)}, bf16[2,4,2,160,512]{4,3,2,1,0:T(8,128)(2,1)S(1)}, u32[]{:S(2)}, u32[]{:S(2)}) collective-permute-start(bf16[2,4,2,160,512]{4,3,2,1,0:T(8,128)(2,1)S(1)} %pad_maximum_fusion.refs_0_.refs_5_), channel_id=1, source_target_pairs={{0,1},{1,0},{2,3},{3,2},{4,5},{5,4},{6,7},{7,6},{8,9},{9,8},{10,11... | collective-permute-start | bytes 7864328 | tf_op jit(solution)/shard_map/ppermute | solution.py:701
  172.5 22.0 %collective-permute-start.23 = (bf16[2,4,2,160,512]{4,3,2,1,0:T(8,128)(2,1)}, bf16[2,4,2,160,512]{4,3,2,1,0:T(8,128)(2,1)}, u32[]{:S(2)}, u32[]{:S(2)}) collective-permute-start(bf16[2,4,2,160,512]{4,3,2,1,0:T(8,128)(2,1)} %collective-permute-done.18.refs_1_.refs_6_), channel_id=1, source_target_pairs={{0,1},{1,0},{2,3},{3,2},{4,5},{5,4},{6,7},{7,6},{8,9},{9,8},{10,11... | collective-permute-start | bytes 7864328 | tf_op jit(solution)/shard_map/ppermute | solution.py:701
  173.8 60.4 %collective-permute-start.25 = (bf16[2,4,2,112,512]{4,3,2,1,0:T(8,128)(2,1)}, bf16[2,4,2,112,512]{4,3,2,1,0:T(8,128)(2,1)}, u32[]{:S(2)}, u32[]{:S(2)}) collective-permute-start(bf16[2,4,2,112,512]{4,3,2,1,0:T(8,128)(2,1)} %pad_maximum_fusion.4.refs_0_), channel_id=1, source_target_pairs={{0,4},{1,3},{2,6},{3,1},{4,0},{5,7},{6,2},{7,5},{8,12},{9,11},{10,... | collective-permute-start | bytes 5505032 | tf_op jit(solution)/shard_map/ppermute | solution.py:701
  175.3 56.8 %collective-permute-start.24 = (bf16[4,2,160,512]{3,2,1,0:T(8,128)(2,1)}, bf16[4,2,160,512]{3,2,1,0:T(8,128)(2,1)}, u32[]{:S(2)}, u32[]{:S(2)}) collective-permute-start(bf16[4,2,160,512]{3,2,1,0:T(8,128)(2,1)} %stack_z.9), channel_id=1, source_target_pairs={{0,2},{1,5},{2,0},{3,7},{4,6},{5,1},{6,4},{7,3},{8,10},{9,13},{10,... | collective-permute-start | bytes 3932168 | tf_op jit(solution)/shard_map/ppermute | solution.py:701
  190.8 45.1 %collective-permute-start.29 = (bf16[2,4,2,144,512]{4,3,2,1,0:T(8,128)(2,1)}, bf16[2,4,2,144,512]{4,3,2,1,0:T(8,128)(2,1)}, u32[]{:S(2)}, u32[]{:S(2)}) collective-permute-start(bf16[2,4,2,144,512]{4,3,2,1,0:T(8,128)(2,1)} %pad_maximum_fusion.2.refs_4_), channel_id=1, source_target_pairs={{0,1},{1,0},{2,3},{3,2},{4,5},{5,4},{6,7},{7,6},{8,9},{9,8},{10,11... | collective-permute-start | bytes 7077896 | tf_op jit(solution)/shard_map/ppermute | solution.py:701
  192.4 17.1 %collective-permute-start.20 = (bf16[2,144,512]{2,1,0:T(8,128)(2,1)}, bf16[2,144,512]{2,1,0:T(8,128)(2,1)S(1)}, u32[]{:S(2)}, u32[]{:S(2)}) collective-permute-start(bf16[2,144,512]{2,1,0:T(8,128)(2,1)} %pad_maximum_fusion.12.refs_0_), channel_id=1, source_target_pairs={{0,16},{1,17},{2,18},{3,19},{4,20},{5,21},{6,22},{7,23},{8,24},{9,... | collective-permute-start | bytes 884744 | tf_op jit(solution)/shard_map/ppermute | solution.py:701
  194.5 33.9 %collective-permute-start.21 = (bf16[2,144,512]{2,1,0:T(8,128)(2,1)}, bf16[2,144,512]{2,1,0:T(8,128)(2,1)S(1)}, u32[]{:S(2)}, u32[]{:S(2)}) collective-permute-start(bf16[2,144,512]{2,1,0:T(8,128)(2,1)} %pad_maximum_fusion.12.refs_0_), channel_id=1, source_target_pairs={{0,24},{1,25},{2,26},{3,27},{4,28},{5,29},{6,30},{7,31},{8,0},{9,1... | collective-permute-start | bytes 884744 | tf_op jit(solution)/shard_map/ppermute | solution.py:701
  209.5 28.4 %collective-permute-start.30 = (bf16[2,4,2,144,512]{4,3,2,1,0:T(8,128)(2,1)}, bf16[2,4,2,144,512]{4,3,2,1,0:T(8,128)(2,1)}, u32[]{:S(2)}, u32[]{:S(2)}) collective-permute-start(bf16[2,4,2,144,512]{4,3,2,1,0:T(8,128)(2,1)} %collective-permute-done.13.refs_5_), channel_id=1, source_target_pairs={{0,1},{1,0},{2,3},{3,2},{4,5},{5,4},{6,7},{7,6},{8,9},{9,8},{10,11... | collective-permute-start | bytes 7077896 | tf_op jit(solution)/shard_map/ppermute | solution.py:701
  234.2 55.1 %collective-permute-start.34 = (bf16[2,4,2,160,512]{4,3,2,1,0:T(8,128)(2,1)S(1)}, bf16[2,4,2,160,512]{4,3,2,1,0:T(8,128)(2,1)}, u32[]{:S(2)}, u32[]{:S(2)}) collective-permute-start(bf16[2,4,2,160,512]{4,3,2,1,0:T(8,128)(2,1)S(1)} %pad_maximum_fusion.1.refs_5_), channel_id=1, source_target_pairs={{0,4},{1,3},{2,6},{3,1},{4,0},{5,7},{6,2},{7,5},{8,12},{9,11},{10,... | collective-permute-start | bytes 7864328 | tf_op jit(solution)/shard_map/ppermute | solution.py:701
  236.0 49.9 %collective-permute-start.33 = (bf16[4,2,144,512]{3,2,1,0:T(8,128)(2,1)}, bf16[4,2,144,512]{3,2,1,0:T(8,128)(2,1)}, u32[]{:S(2)}, u32[]{:S(2)}) collective-permute-start(bf16[4,2,144,512]{3,2,1,0:T(8,128)(2,1)} %stack_z.10), channel_id=1, source_target_pairs={{0,2},{1,5},{2,0},{3,7},{4,6},{5,1},{6,4},{7,3},{8,10},{9,13},{10,... | collective-permute-start | bytes 3538952 | tf_op jit(solution)/shard_map/ppermute | solution.py:701
  237.9 44.3 %collective-permute-start.26 = (bf16[2,112,512]{2,1,0:T(8,128)(2,1)S(1)}, bf16[2,112,512]{2,1,0:T(8,128)(2,1)S(1)}, u32[]{:S(2)}, u32[]{:S(2)}) collective-permute-start(bf16[2,112,512]{2,1,0:T(8,128)(2,1)S(1)} %pad_maximum_fusion.15.refs_0_), channel_id=1, source_target_pairs={{0,8},{1,9},{2,10},{3,11},{4,12},{5,13},{6,14},{7,15},{8,16},{9,17... | collective-permute-start | bytes 688136 | tf_op jit(solution)/shard_map/ppermute | solution.py:701
  242.8 39.5 %collective-permute-start.27 = (bf16[2,112,512]{2,1,0:T(8,128)(2,1)S(1)}, bf16[2,112,512]{2,1,0:T(8,128)(2,1)S(1)}, u32[]{:S(2)}, u32[]{:S(2)}) collective-permute-start(bf16[2,112,512]{2,1,0:T(8,128)(2,1)S(1)} %pad_maximum_fusion.15.refs_0_), channel_id=1, source_target_pairs={{0,16},{1,17},{2,18},{3,19},{4,20},{5,21},{6,22},{7,23},{8,24},{9,... | collective-permute-start | bytes 688136 | tf_op jit(solution)/shard_map/ppermute | solution.py:701
  246.0 36.2 %collective-permute-start.28 = (bf16[2,112,512]{2,1,0:T(8,128)(2,1)S(1)}, bf16[2,112,512]{2,1,0:T(8,128)(2,1)}, u32[]{:S(2)}, u32[]{:S(2)}) collective-permute-start(bf16[2,112,512]{2,1,0:T(8,128)(2,1)S(1)} %pad_maximum_fusion.15.refs_0_), channel_id=1, source_target_pairs={{0,24},{1,25},{2,26},{3,27},{4,28},{5,29},{6,30},{7,31},{8,0},{9,1... | collective-permute-start | bytes 688136 | tf_op jit(solution)/shard_map/ppermute | solution.py:701
  289.8 38.7 %collective-permute-start.38 = (bf16[2,4,2,144,512]{4,3,2,1,0:T(8,128)(2,1)}, bf16[2,4,2,144,512]{4,3,2,1,0:T(8,128)(2,1)}, u32[]{:S(2)}, u32[]{:S(2)}) collective-permute-start(bf16[2,4,2,144,512]{4,3,2,1,0:T(8,128)(2,1)} %pad_maximum_fusion.3.refs_4_), channel_id=1, source_target_pairs={{0,4},{1,3},{2,6},{3,1},{4,0},{5,7},{6,2},{7,5},{8,12},{9,11},{10,... | collective-permute-start | bytes 7077896 | tf_op jit(solution)/shard_map/ppermute | solution.py:701
  290.7 28.3 %collective-permute-start.35 = (bf16[4,2,112,512]{3,2,1,0:T(8,128)(2,1)S(1)}, bf16[4,2,112,512]{3,2,1,0:T(8,128)(2,1)}, u32[]{:S(2)}, u32[]{:S(2)}) collective-permute-start(bf16[4,2,112,512]{3,2,1,0:T(8,128)(2,1)S(1)} %copy-done.11), channel_id=1, source_target_pairs={{0,2},{1,5},{2,0},{3,7},{4,6},{5,1},{6,4},{7,3},{8,10},{9,13},{10,... | collective-permute-start | bytes 2752520 | tf_op jit(solution)/shard_map/ppermute | solution.py:701
  329.0 26.4 %collective-permute-start.39 = (bf16[2,4,2,112,512]{4,3,2,1,0:T(8,128)(2,1)S(1)}, bf16[2,4,2,112,512]{4,3,2,1,0:T(8,128)(2,1)S(1)}, u32[]{:S(2)}, u32[]{:S(2)}) collective-permute-start(bf16[2,4,2,112,512]{4,3,2,1,0:T(8,128)(2,1)S(1)} %pad_maximum_fusion.5.refs_0_), channel_id=1, source_target_pairs={{0,4},{1,3},{2,6},{3,1},{4,0},{5,7},{6,2},{7,5},{8,12},{9,11},{10,... | collective-permute-start | bytes 5505032 | tf_op jit(solution)/shard_map/ppermute | solution.py:701
  405.3 23.5 %collective-permute-start.45 = (bf16[2,4,2,112,512]{4,3,2,1,0:T(8,128)(2,1)}, bf16[2,4,2,112,512]{4,3,2,1,0:T(8,128)(2,1)}, u32[]{:S(2)}, u32[]{:S(2)}) collective-permute-start(bf16[2,4,2,112,512]{4,3,2,1,0:T(8,128)(2,1)} %fusion), channel_id=1, source_target_pairs={{0,4},{1,3},{2,6},{3,1},{4,0},{5,7},{6,2},{7,5},{8,12},{9,11},{10,... | collective-permute-start | bytes 5505032 | tf_op jit(solution)/shard_map/ppermute | solution.py:701
  428.9 27.6 %collective-permute-start.49 = (bf16[2,2,4,2,80,512]{5,4,3,2,1,0:T(8,128)(2,1)}, bf16[2,2,4,2,80,512]{5,4,3,2,1,0:T(8,128)(2,1)}, u32[]{:S(2)}, u32[]{:S(2)}) collective-permute-start(bf16[2,2,4,2,80,512]{5,4,3,2,1,0:T(8,128)(2,1)} %get-tuple-element.629), channel_id=1, source_target_pairs={{0,1},{1,0},{2,3},{3,2},{4,5},{5,4},{6,7},{7,6},{8,9},{9,8},{10,11... | collective-permute-start | bytes 7864328 | tf_op jit(solution)/shard_map/ppermute | solution.py:701
  433.3 23.2 %collective-permute-start.47 = (bf16[4,2,112,512]{3,2,1,0:T(8,128)(2,1)}, bf16[4,2,112,512]{3,2,1,0:T(8,128)(2,1)}, u32[]{:S(2)}, u32[]{:S(2)}) collective-permute-start(bf16[4,2,112,512]{3,2,1,0:T(8,128)(2,1)} %get-tuple-element.759), channel_id=1, source_target_pairs={{0,2},{1,5},{2,0},{3,7},{4,6},{5,1},{6,4},{7,3},{8,10},{9,13},{10,... | collective-permute-start | bytes 2752520 | tf_op jit(solution)/shard_map/ppermute | solution.py:701
  435.2 21.2 %collective-permute-start.48 = (bf16[2,4,2,32,512]{4,3,2,1,0:T(8,128)(2,1)}, bf16[2,4,2,32,512]{4,3,2,1,0:T(8,128)(2,1)S(1)}, u32[]{:S(2)}, u32[]{:S(2)}) collective-permute-start(bf16[2,4,2,32,512]{4,3,2,1,0:T(8,128)(2,1)} %fusion.13), channel_id=1, source_target_pairs={{0,4},{1,3},{2,6},{3,1},{4,0},{5,7},{6,2},{7,5},{8,12},{9,11},{10,... | collective-permute-start | bytes 1572872 | tf_op jit(solution)/shard_map/ppermute | solution.py:701
  456.5 32.4 %collective-permute-start.55 = (bf16[2,2,4,2,64,512]{5,4,3,2,1,0:T(8,128)(2,1)}, bf16[2,2,4,2,64,512]{5,4,3,2,1,0:T(8,128)(2,1)}, u32[]{:S(2)}, u32[]{:S(2)}) collective-permute-start(bf16[2,2,4,2,64,512]{5,4,3,2,1,0:T(8,128)(2,1)} %get-tuple-element.665), channel_id=1, source_target_pairs={{0,1},{1,0},{2,3},{3,2},{4,5},{5,4},{6,7},{7,6},{8,9},{9,8},{10,11... | collective-permute-start | bytes 6291464 | tf_op jit(solution)/shard_map/ppermute | solution.py:701
  460.0 28.8 %collective-permute-start.54 = (bf16[2,4,2,80,512]{4,3,2,1,0:T(8,128)(2,1)}, bf16[2,4,2,80,512]{4,3,2,1,0:T(8,128)(2,1)S(1)}, u32[]{:S(2)}, u32[]{:S(2)}) collective-permute-start(bf16[2,4,2,80,512]{4,3,2,1,0:T(8,128)(2,1)} %fusion.2), channel_id=1, source_target_pairs={{0,4},{1,3},{2,6},{3,1},{4,0},{5,7},{6,2},{7,5},{8,12},{9,11},{10,... | collective-permute-start | bytes 3932168 | tf_op jit(solution)/shard_map/ppermute | solution.py:701
  465.0 23.8 %collective-permute-start.53 = (bf16[4,2,32,512]{3,2,1,0:T(8,128)(2,1)}, bf16[4,2,32,512]{3,2,1,0:T(8,128)(2,1)S(1)}, u32[]{:S(2)}, u32[]{:S(2)}) collective-permute-start(bf16[4,2,32,512]{3,2,1,0:T(8,128)(2,1)} %get-tuple-element.766), channel_id=1, source_target_pairs={{0,2},{1,5},{2,0},{3,7},{4,6},{5,1},{6,4},{7,3},{8,10},{9,13},{10,... | collective-permute-start | bytes 786440 | tf_op jit(solution)/shard_map/ppermute | solution.py:701
  466.1 22.7 %collective-permute-start.51 = (bf16[2,112,512]{2,1,0:T(8,128)(2,1)}, bf16[2,112,512]{2,1,0:T(8,128)(2,1)}, u32[]{:S(2)}, u32[]{:S(2)}) collective-permute-start(bf16[2,112,512]{2,1,0:T(8,128)(2,1)} %get-tuple-element.764), channel_id=1, source_target_pairs={{0,16},{1,17},{2,18},{3,19},{4,20},{5,21},{6,22},{7,23},{8,24},{9,... | collective-permute-start | bytes 688136 | tf_op jit(solution)/shard_map/ppermute | solution.py:701
  490.0 31.4 %collective-permute-start.61 = (bf16[2,2,4,2,80,512]{5,4,3,2,1,0:T(8,128)(2,1)}, bf16[2,2,4,2,80,512]{5,4,3,2,1,0:T(8,128)(2,1)}, u32[]{:S(2)}, u32[]{:S(2)}) collective-permute-start(bf16[2,2,4,2,80,512]{5,4,3,2,1,0:T(8,128)(2,1)} %get-tuple-element.697), channel_id=1, source_target_pairs={{0,1},{1,0},{2,3},{3,2},{4,5},{5,4},{6,7},{7,6},{8,9},{9,8},{10,11... | collective-permute-start | bytes 7864328 | tf_op jit(solution)/shard_map/ppermute | solution.py:701
  492.0 21.0 %collective-permute-start.85 = (f32[112,512]{1,0:T(8,128)}, f32[112,512]{1,0:T(8,128)}, u32[]{:S(2)}, u32[]{:S(2)}) collective-permute-start(f32[112,512]{1,0:T(8,128)} %dynamic-slice_bitcast_fusion.1), channel_id=1, source_target_pairs={{0,1},{1,0},{2,3},{3,2},{4,5},{5,4},{6,7},{7,6},{8,9},{9,8},{10,11... | collective-permute-start | bytes 688136 | tf_op jit(solution)/shard_map/ppermute | solution.py:701
  496.3 25.1 %collective-permute-start.60 = (bf16[2,4,2,64,512]{4,3,2,1,0:T(8,128)(2,1)}, bf16[2,4,2,64,512]{4,3,2,1,0:T(8,128)(2,1)S(1)}, u32[]{:S(2)}, u32[]{:S(2)}) collective-permute-start(bf16[2,4,2,64,512]{4,3,2,1,0:T(8,128)(2,1)} %fusion.4), channel_id=1, source_target_pairs={{0,4},{1,3},{2,6},{3,1},{4,0},{5,7},{6,2},{7,5},{8,12},{9,11},{10,... | collective-permute-start | bytes 3145736 | tf_op jit(solution)/shard_map/ppermute | solution.py:701
  499.9 21.5 %collective-permute-start.59 = (bf16[4,2,80,512]{3,2,1,0:T(8,128)(2,1)}, bf16[4,2,80,512]{3,2,1,0:T(8,128)(2,1)}, u32[]{:S(2)}, u32[]{:S(2)}) collective-permute-start(bf16[4,2,80,512]{3,2,1,0:T(8,128)(2,1)} %get-tuple-element.761), channel_id=1, source_target_pairs={{0,2},{1,5},{2,0},{3,7},{4,6},{5,1},{6,4},{7,3},{8,10},{9,13},{10,... | collective-permute-start | bytes 1966088 | tf_op jit(solution)/shard_map/ppermute | solution.py:701
  521.4 25.7 %collective-permute-start.78 = (bf16[2,2,4,2,64,512]{5,4,3,2,1,0:T(8,128)(2,1)}, bf16[2,2,4,2,64,512]{5,4,3,2,1,0:T(8,128)(2,1)S(1)}, u32[]{:S(2)}, u32[]{:S(2)}) collective-permute-start(bf16[2,2,4,2,64,512]{5,4,3,2,1,0:T(8,128)(2,1)} %get-tuple-element.727), channel_id=1, source_target_pairs={{0,1},{1,0},{2,3},{3,2},{4,5},{5,4},{6,7},{7,6},{8,9},{9,8},{10,11... | collective-permute-start | bytes 6291464 | tf_op jit(solution)/shard_map/ppermute | solution.py:701
  522.9 17.8 %collective-permute-start.67 = (bf16[4,2,64,512]{3,2,1,0:T(8,128)(2,1)S(1)}, bf16[4,2,64,512]{3,2,1,0:T(8,128)(2,1)S(1)}, u32[]{:S(2)}, u32[]{:S(2)}) collective-permute-start(bf16[4,2,64,512]{3,2,1,0:T(8,128)(2,1)S(1)} %fusion.11), channel_id=1, source_target_pairs={{0,2},{1,5},{2,0},{3,7},{4,6},{5,1},{6,4},{7,3},{8,10},{9,13},{10,... | collective-permute-start | bytes 1572872 | tf_op jit(solution)/shard_map/ppermute | solution.py:701
  534.3 22.2 %collective-permute-start.72 = (bf16[2,4,2,80,512]{4,3,2,1,0:T(8,128)(2,1)S(1)}, bf16[2,4,2,80,512]{4,3,2,1,0:T(8,128)(2,1)S(1)}, u32[]{:S(2)}, u32[]{:S(2)}) collective-permute-start(bf16[2,4,2,80,512]{4,3,2,1,0:T(8,128)(2,1)S(1)} %fusion.1), channel_id=1, source_target_pairs={{0,4},{1,3},{2,6},{3,1},{4,0},{5,7},{6,2},{7,5},{8,12},{9,11},{10,... | collective-permute-start | bytes 3932168 | tf_op jit(solution)/shard_map/ppermute | solution.py:701
  548.5 17.2 %collective-permute-start.79 = (bf16[2,4,2,64,512]{4,3,2,1,0:T(8,128)(2,1)S(1)}, bf16[2,4,2,64,512]{4,3,2,1,0:T(8,128)(2,1)S(1)}, u32[]{:S(2)}, u32[]{:S(2)}) collective-permute-start(bf16[2,4,2,64,512]{4,3,2,1,0:T(8,128)(2,1)S(1)} %fusion.3), channel_id=1, source_target_pairs={{0,4},{1,3},{2,6},{3,1},{4,0},{5,7},{6,2},{7,5},{8,12},{9,11},{10,... | collective-permute-start | bytes 3145736 | tf_op jit(solution)/shard_map/ppermute | solution.py:701
  565.9 17.6 %collective-permute-start.80 = (bf16[4,2,64,512]{3,2,1,0:T(8,128)(2,1)S(1)}, bf16[4,2,64,512]{3,2,1,0:T(8,128)(2,1)S(1)}, u32[]{:S(2)}, u32[]{:S(2)}) collective-permute-start(bf16[4,2,64,512]{3,2,1,0:T(8,128)(2,1)S(1)} %fusion.9), channel_id=1, source_target_pairs={{0,2},{1,5},{2,0},{3,7},{4,6},{5,1},{6,4},{7,3},{8,10},{9,13},{10,... | collective-permute-start | bytes 1572872 | tf_op jit(solution)/shard_map/ppermute | solution.py:701
  (140 other events, 1332.0 us)

commit v5 on v4

--- a/solution.py
+++ b/solution.py
@@ -16,7 +16,7 @@
 TAPS = 9
 
 ROWS = 128
-LANES = 256
+LANES = 512
 VMEM_LIMIT = 60 * 1024 * 1024
 LIGHT = pl.CostEstimate(flops=1024, bytes_accessed=1024, transcendentals=0)
 
@@ -687,13 +687,13 @@
     ).astype(jnp.int32)
 
 
-def hop(array, axis_of_core, step=1):
+def hop(array, axis_of_core, step=1, swap=0):
     sizes = grid_sizes()
     pairs = []
     for place in itertools.product(*[range(size) for size in sizes]):
         axis = axis_of_core[place[3]]
         other = list(place)
-        other[axis] = (place[axis] + step) % sizes[axis]
+        other[axis] = place[axis] ^ swap if swap else (place[axis] + step) % sizes[axis]
         source, target = [
             ((z * sizes[1] + y) * sizes[2] + x) * sizes[3] + core for z, y, x, core in (place, other)
         ]
@@ -786,26 +786,6 @@
 def pack(parts, pieces):
     rows = jnp.concatenate([part.pack(piece) for part, piece in zip(parts, pieces)])
     return jnp.pad(rows, ((0, 2 * half_rows(parts) - rows.shape[0]), (0, 0)))
-
-
-def stack_kernel(size, place, *refs):
-    pairs = [
-        (refs[step], refs[size].at[lax.rem(place[0] - step + size, size)]) for step in range(size)
-    ]
-    copies(pairs, refs[size + 1])
-
-
-def stack_z(arrays, place):
-    size = len(arrays)
-    return pl.pallas_call(
-        functools.partial(stack_kernel, size),
-        out_shape=jax.ShapeDtypeStruct((size,) + arrays[0].shape, arrays[0].dtype),
-        in_specs=in_smem() + hbm(size),
-        out_specs=in_vmem(1)[0],
-        scratch_shapes=[pltpu.SemaphoreType.DMA((size,))],
-        cost_estimate=LIGHT,
-        name="stack_z",
-    )(place, *arrays)
 
 
 def assemble_pairs(parts, core, y, x, ins, outs):
@@ -875,9 +855,9 @@
     return array.reshape(array.shape[0], -1, array.shape[-1])
 
 
-def both_cores(own, other, core):
-    first = jnp.where(core == 0, own, other)
-    second = jnp.where(core == 0, other, own)
+def in_order(own, other, bit):
+    first = jnp.where(bit == 0, own, other)
+    second = jnp.where(bit == 0, other, own)
     return jnp.stack([first, second])
 
 
@@ -898,37 +878,47 @@
     held = []
     offset = 0
     for keep, half in zip(kept, halves):
-        held.append(both_cores(keep, got[offset : offset + half], core))
+        held.append(in_order(keep, got[offset : offset + half], core))
         offset += half
     return held
 
 
 def pipelined_gather(groups, pieces, place, state, arrived):
     count = len(groups)
-    depth = grid_sizes()[0]
+    low, high = (place[0] % 2, place[0] // 2)
     held = start_gather(groups[:1], pieces(None)[:1], place) + [None] * (count - 1)
+    held[0] = in_order(held[0], hop(held[0], ALONG_Z, swap=1), low)
     for tick in range(count + 3):
-        if tick == 1:
-            held[1:] = start_gather(groups[1:], pieces(early)[1:], place)
         near, far, last = [index if 0 <= index < count else None for index in range(tick - 1, tick - 4, -1)]
         live = [index for index in (tick, near, far, last) if index is not None and index < count]
+        if tick == 1:
+            live += range(2, count)
         items, state = together([held[index] for index in live], state)
         for index, item in zip(live, items):
             held[index] = item
+        if tick == 0:
+            held[1:] = start_gather(groups[1:], pieces(held[0])[1:], place)
         if last is not None:
-            held[last] = held[last] + [hop(item, ACROSS) for item in held[last]]
+            own, arrived_far, other = held[last]
+            held[last] = [own, arrived_far, other, hop(arrived_far, ACROSS)]
         if far is not None:
-            held[far] = [held[far], hop(held[far], FAR)]
+            held[far] = [held[far], hop(held[far], FAR), hop(held[far], ACROSS)]
         if near is not None:
             held[near] = [held[near], hop(held[near], NEAR)]
         if tick < count:
-            early = held[tick]
-            held[tick] = [held[tick]] + [hop(held[tick], ALONG_Z, step) for step in range(1, depth)]
+            held[tick] = [held[tick], hop(held[tick], ALONG_Z, swap=2)]
+        if tick < 2:
+            early = slice(1, 2) if tick == 0 else slice(2, count)
+            got = hop(jnp.concatenate(held[early], axis=1), ALONG_Z, swap=1)
+            ends = list(itertools.accumulate(half_rows(parts) for parts in groups[early]))
+            got = jnp.split(got, ends[:-1], axis=1)
+            held[early] = [in_order(item, other, low) for item, other in zip(held[early], got)]
         if last is not None:
             state = arrived(last, held[last], state)
         if tick < count:
-            items, state = together(held[tick], state)
-            held[tick] = stack_z(items, place)
+            (own, other), state = together(held[tick], state)
+            both = in_order(own, other, high)
+            held[tick] = both.reshape(-1, *both.shape[2:])
         if near is not None:
             items, state = together(held[near], state)
             held[near] = jnp.stack(items)
@@ -1008,7 +998,7 @@
     total = add_up(*items)
     keep = lax.dynamic_index_in_dim(total, core, 0, False)
     other = hop(lax.dynamic_index_in_dim(total, 1 - core, 0, False), ACROSS)
-    return both_cores(keep, other, core).reshape(-1, WIDTH)
+    return in_order(keep, other, core).reshape(-1, WIDTH)
 
 
 SCATTER_STAGES = 5
@@ -1049,7 +1039,7 @@
     return min(0.99, (1.0 + STEP) / (10.0 + STEP))
 
 
-SWEEP = 1024
+SWEEP = 8192
 
 
 def lamb_parts(grads, params, first, second):
@@ -1062,6 +1052,21 @@
     return (momentum, variance, direction)
 
 
+def stretches(cuts):
+    found = []
+    at = 0
+    for index, (start, size) in enumerate(cuts):
+        end = start + size
+        last = index == len(cuts) - 1
+        whole = end if last else end // ROWS * ROWS
+        found.append((at, whole - at, [index]))
+        at = whole
+        if end != whole:
+            found.append((whole, ROWS, [index, index + 1]))
+            at = whole + ROWS
+    return found
+
+
 def sweep(start, size, body, carry):
     steps = size // SWEEP
 
@@ -1069,7 +1074,7 @@
         return body(pl.ds(pl.multiple_of(start + index * SWEEP, ROWS), SWEEP), carry)
 
     if steps:
-        carry = lax.fori_loop(0, steps, step, carry, unroll=2)
+        carry = lax.fori_loop(0, steps, step, carry)
     return (carry, start + steps * SWEEP, size - steps * SWEEP)
 
 
@@ -1129,41 +1134,39 @@
         return (param * param, made[2] * made[2])
 
     found = []
-    width = top_ins[0].shape[1]
-
-    def top_step(lanes, carry):
-        size = lanes.size
-        squares = work(lanes, top_grad, top_ins, top_outs)
-        at = lanes.start + lax.broadcasted_iota(jnp.int32, (1, size), 1)
-        masks = [(at >= start) & (at < start + count) for start, count in top_cuts]
-        terms = [jnp.where(mask, value, 0.0) for mask in masks for value in squares]
-        if size != SWEEP:
-            return [row_sum(held) + row_sum(term) for held, term in zip(carry, terms)]
-        return [held + term for held, term in zip(carry, terms)]
-
-    zeros = [jnp.zeros((1, SWEEP), jnp.float32)] * (2 * len(top_cuts))
-    carry, start, rest = sweep(0, width, top_step, zeros)
-    carry = top_step(pl.ds(start, rest), carry) if rest else [row_sum(value) for value in carry]
-    found += [(index // 2, index % 2, value) for index, value in enumerate(carry)]
-
-    def block_step(lanes, carry):
-        return [held + term for held, term in zip(carry, work(lanes, block_grad, block_ins, block_outs))]
-
-    zeros = [jnp.zeros((BLOCKS, SWEEP), jnp.float32)] * 2
-    for index, (start, size) in enumerate(block_cuts):
-        carry, start, rest = sweep(start, size, block_step, zeros)
-        carry = [row_sum(value) for value in carry]
-        if rest:
-            terms = work(pl.ds(start, rest), block_grad, block_ins, block_outs)
-            carry = [held + row_sum(term) for held, term in zip(carry, terms)]
-        for block in range(BLOCKS):
-            lane = len(top_cuts) + block * len(block_cuts) + index
-            found += [(lane, row, value[block : block + 1]) for row, value in enumerate(carry)]
+
+    def run(cuts, grad, ins, outs, first_lane, height):
+        for start, size, segments in stretches(cuts):
+
+            def step(lanes, carry):
+                terms = work(lanes, grad, ins, outs)
+                return [held + term for held, term in zip(carry, terms)]
+
+            zeros = [jnp.zeros((height, SWEEP), jnp.float32)] * 2
+            carry, begin, rest = sweep(start, size, step, zeros)
+            sizes = [row_sum(value) for value in carry] if rest != size else None
+            if rest:
+                terms = work(pl.ds(begin, rest), grad, ins, outs)
+                at = begin + lax.broadcasted_iota(jnp.int32, terms[0].shape, 1)
+                if len(segments) > 1:
+                    edge = cuts[segments[1]][0]
+                    after = [row_sum(jnp.where(at >= edge, term, 0.0)) for term in terms]
+                    found.extend((first_lane, segments[1], *item) for item in enumerate(after))
+                    terms = [jnp.where(at < edge, term, 0.0) for term in terms]
+                more = [row_sum(term) for term in terms]
+                sizes = more if sizes is None else [held + term for held, term in zip(sizes, more)]
+            found.extend((first_lane, segments[0], *item) for item in enumerate(sizes))
+
+    run(top_cuts, top_grad, top_ins, top_outs, 0, 1)
+    run(block_cuts, block_grad, block_ins, block_outs, len(top_cuts), BLOCKS)
     rows = lax.broadcasted_iota(jnp.int32, sums.shape, 0)
     lanes = lax.broadcasted_iota(jnp.int32, sums.shape, 1)
     result = jnp.where((rows == 2) & (lanes == 0), loss[...], 0.0)
-    for lane, row, value in found:
-        result = jnp.where((rows == row) & (lanes == lane), value, result)
+    for first, segment, row, value in found:
+        for part in range(value.shape[0]):
+            lane = first + part * len(block_cuts) + segment
+            here = (rows == row) & (lanes == lane)
+            result = result + jnp.where(here, value[part : part + 1], 0.0)
     sums[...] = result
 
 
@@ -1203,32 +1206,26 @@
         half[:, lanes] = value.astype(jnp.bfloat16)
         averaged[:, lanes] = decay * average + (1.0 - decay) * value
 
-    def top_step(lanes, carry):
-        at = lanes.start + lax.broadcasted_iota(jnp.int32, (1, lanes.size), 1)
-        scale = jnp.broadcast_to(ratio[:, 3:4], at.shape)
-        for index in (2, 1, 0):
-            scale = jnp.where(at < top_cuts[index + 1][0], ratio[:, index : index + 1], scale)
-        work(lanes, top_ins, top_outs, scale)
-        return carry
-
-    _, start, rest = sweep(0, top_ins[0].shape[1], top_step, 0)
-    if rest:
-        top_step(pl.ds(start, rest), 0)
-    for index, (start, size) in enumerate(block_cuts):
-        scale = jnp.concatenate(
-            [
-                ratio[:, lane : lane + 1]
-                for lane in [4 + block * len(block_cuts) + index for block in range(BLOCKS)]
-            ]
-        )
-
-        def block_step(lanes, carry):
-            work(lanes, block_ins, block_outs, scale)
-            return carry
-
-        _, start, rest = sweep(start, size, block_step, 0)
-        if rest:
-            block_step(pl.ds(start, rest), 0)
+    def run(cuts, ins, outs, scales):
+        for start, size, segments in stretches(cuts):
+            scale = scales[segments[0]]
+
+            def step(lanes, carry):
+                work(lanes, ins, outs, scale)
+                return carry
+
+            _, begin, rest = sweep(start, size, step, 0)
+            if rest:
+                if len(segments) > 1:
+                    at = begin + lax.broadcasted_iota(jnp.int32, (1, rest), 1)
+                    scale = jnp.where(at < cuts[segments[1]][0], scale, scales[segments[1]])
+                work(pl.ds(begin, rest), ins, outs, scale)
+
+    lanes = [ratio[:, lane : lane + 1] for lane in range(len(top_cuts) + BLOCKS * len(block_cuts))]
+    run(top_cuts, top_ins, top_outs, lanes[: len(top_cuts)])
+    rest = lanes[len(top_cuts) :]
+    scales = [jnp.concatenate(rest[index :: len(block_cuts)]) for index in range(len(block_cuts))]
+    run(block_cuts, block_ins, block_outs, scales)
 
 
 def update(cuts, sums, top_ins, block_ins):

time: 670 us -> 628 us (0.937)
  waiting for transfers between devices: 175 us -> 225 us
  starting transfers between devices: 129 us -> 89.7 us
  Pallas kernels: 232 us -> 193 us
    ppermute x92 -> x83, waiting for transfers between devices: 175 us -> 225 us  [hop(): return lax.ppermute(array, AXES, pairs)]
    ppermute x92 -> x83, starting transfers between devices: 129 us -> 89.7 us  [hop(): return lax.ppermute(array, AXES, pairs)]
    pallas_call x6 -> x0, Pallas kernels: 17.8 us -> none  [stack_z(): pl.pallas_call(functools.partial(stack_kernel, size), out_shape=jax.Shape...]
    pallas_call x1, Pallas kernels: 16.1 us -> 7.49 us  [update(): pl.pallas_call(functools.partial(update_kernel, cuts), out_shape=[f32(8,...]
    unnamed x200 -> x122, local copies, waits for them, and re-layouts: 15.5 us -> 10.2 us
    another operation x26 -> x48, other arithmetic: 11.2 us -> 13.7 us  [the longest x44 13.7 us: in_order(): return jnp.stack([first, second])]
  transfers between devices with their start and end apart: 92 -> 83, of which waited for: 37 -> 36; matrix products, arithmetic and copies ran while one was open for 12% -> 14% of each run, Pallas kernels for 27% -> 24%
where the time goes in v5:
time: 628 us; the launch traced here: 624 us
  waiting for transfers between devices  225 us (36%)
  Pallas kernels  193 us (31%)
  starting transfers between devices  89.7 us (14%)
  other arithmetic  69 us (11%)
  local copies, waits for them, and re-layouts  45 us (7%)
    ppermute x83, waiting for transfers between devices, hop(): return lax.ppermute(array, AXES, pairs)  225 us
    ppermute x83, starting transfers between devices, hop(): return lax.ppermute(array, AXES, pairs)  89.7 us
    pallas_call x6, Pallas kernels, back_call(): pl.pallas_call(functools.partial(back_kernel, body, parts, tuned, counts)...  82.6 us
    pallas_call x4, Pallas kernels, block_forward(): pl.pallas_call(functools.partial(forward_kernel, count, keep, parts, skip...  69.2 us
    convert_element_type x12, other arithmetic, low_add(): return add_up(*terms).astype(jnp.bfloat16)  22.9 us
    pallas_call x3, Pallas kernels, assemble(): pl.pallas_call(functools.partial(assemble_kernel, parts, some), out_shape...  15.9 us
    another operation x44, other arithmetic, in_order(): return jnp.stack([first, second])  13.7 us
  transfers between devices with their start and end apart: 83, of which 36 were waited for; matrix products, arithmetic and copies ran while one was open for 14% of the time, Pallas kernels for 24%

profile of v5, /device:TPU:0, one launch (start us, length us, event | category | flops | bytes accessed | tf_op | source)
XLA Modules:
  0.0 624.3 jit_solution(18057201222085732390)
XLA Ops:
  6.4 3.0 collective-permute-start.1
  10.8 5.9 collective-permute-done.1
  30.9 20.2 %collective-permute-done.4 = bf16[2,2,144,512]{3,2,1,0:T(8,128)(2,1)S(1)} collective-permute-done((bf16[2,2,144,512]{3,2,1,0:T(8,128)(2,1)S(1)}, bf16[2,2,144,512]{3,2,1,0:T(8,128)(2,1)S(1)}, u32[]{:S(2)}, u32[]{:S(2)}) %collective-permute-start.4) | collective-permute-done | bytes 589856 | tf_op jit(solution)/shard_map/ppermute | solution.py:701
  52.4 7.9 %collective-permute-done.3 = bf16[2,160,512]{2,1,0:T(8,128)(2,1)S(1)} collective-permute-done((bf16[2,160,512]{2,1,0:T(8,128)(2,1)S(1)}, bf16[2,160,512]{2,1,0:T(8,128)(2,1)S(1)}, u32[]{:S(2)}, u32[]{:S(2)}) %collective-permute-start.3) | collective-permute-done | bytes 327712 | tf_op jit(solution)/shard_map/ppermute | solution.py:701
  60.4 3.1 collective-permute-start.6
  66.9 25.2 %collective-permute-done.6 = bf16[2,2,160,512]{3,2,1,0:T(8,128)(2,1)S(1)} collective-permute-done((bf16[2,2,160,512]{3,2,1,0:T(8,128)(2,1)S(1)}, bf16[2,2,160,512]{3,2,1,0:T(8,128)(2,1)S(1)}, u32[]{:S(2)}, u32[]{:S(2)}) %collective-permute-start.6) | collective-permute-done | bytes 655392 | tf_op jit(solution)/shard_map/ppermute | solution.py:701
  92.2 9.4 %collective-permute-done.5 = bf16[2,528,512]{2,1,0:T(8,128)(2,1)S(1)} collective-permute-done((bf16[2,528,512]{2,1,0:T(8,128)(2,1)S(1)}, bf16[2,528,512]{2,1,0:T(8,128)(2,1)S(1)}, u32[]{:S(2)}, u32[]{:S(2)}) %collective-permute-start.5) | collective-permute-done | bytes 1081376 | tf_op jit(solution)/shard_map/ppermute | solution.py:701
  106.8 21.4 %collective-permute-done.8 = bf16[2,2,112,512]{3,2,1,0:T(8,128)(2,1)S(1)} collective-permute-done((bf16[2,2,112,512]{3,2,1,0:T(8,128)(2,1)S(1)}, bf16[2,2,112,512]{3,2,1,0:T(8,128)(2,1)S(1)}, u32[]{:S(2)}, u32[]{:S(2)}) %collective-permute-start.8) | collective-permute-done | bytes 458784 | tf_op jit(solution)/shard_map/ppermute | solution.py:701
  128.4 7.7 %collective-permute-done.9 = bf16[4,2,160,512]{3,2,1,0:T(8,128)(2,1)S(1)} collective-permute-done((bf16[4,2,160,512]{3,2,1,0:T(8,128)(2,1)S(1)}, bf16[4,2,160,512]{3,2,1,0:T(8,128)(2,1)S(1)}, u32[]{:S(2)}, u32[]{:S(2)}) %collective-permute-start.9) | collective-permute-done | bytes 1310752 | tf_op jit(solution)/shard_map/ppermute | solution.py:701
  136.3 9.4 %collective-permute-done.10.refs_5_ = bf16[2,4,2,144,512]{4,3,2,1,0:T(8,128)(2,1)S(1)} collective-permute-done((bf16[2,4,2,144,512]{4,3,2,1,0:T(8,128)(2,1)S(1)}, bf16[2,4,2,144,512]{4,3,2,1,0:T(8,128)(2,1)S(1)}, u32[]{:S(2)}, u32[]{:S(2)}) %collective-permute-start.10) | collective-permute-done | bytes 2359328 | tf_op jit(solution)/shard_map/ppermute | solution.py:701
  151.3 29.5 %collective-permute-done.12 = bf16[2,2,160,512]{3,2,1,0:T(8,128)(2,1)S(1)} collective-permute-done((bf16[2,2,160,512]{3,2,1,0:T(8,128)(2,1)S(1)}, bf16[2,2,160,512]{3,2,1,0:T(8,128)(2,1)S(1)}, u32[]{:S(2)}, u32[]{:S(2)}) %collective-permute-start.12) | collective-permute-done | bytes 655392 | tf_op jit(solution)/shard_map/ppermute | solution.py:701
  183.6 3.7 collective-permute-done.14.refs_1_.refs_6_
  208.8 16.5 %block_forward.4.refs_1_ = f32[384,2048]{1,0:T(8,128)} custom-call(s32[4]{0:T(128)} %pad_add_fusion.1.place.refs_0_, bf16[384,256]{1,0:T(8,128)(2,1)} %bitcast.462, bf16[2,256,512]{2,1,0:T(8,128)(2,1)} %add_convert_fusion.refs_2_.refs_6_, f32[1,6144]{1,0:T(1,128)} %slice.278.refs_3_, bf16[1152,128]{1,0:T(8,128)(2,1)} %convert_element_type.506.refs_4_.refs_3_.refs_6_, ...), custom_call_target="tpu_custom_call" | custom-call | flops 1024 | bytes 1024 | tf_op jit(solution)/shard_map/block_forward/pallas_call | solution.py:248
  237.5 15.8 %block_forward.5.stream = f32[384,2048]{1,0:T(8,128)} custom-call(s32[4]{0:T(128)} %pad_add_fusion.1.place.refs_0_, f32[384,2048]{1,0:T(8,128)} %block_forward.4.refs_1_, f32[1,6144]{1,0:T(1,128)} %slice.279.refs_2_, bf16[1152,128]{1,0:T(8,128)(2,1)} %convert_element_type.506.refs_4_.refs_3_.refs_6_, bf16[2,4,2,144,512]{4,3,2,1,0:T(8,128)(2,1)} %copy-done.5, ...), custom_call_target="tpu_custom_call" | custom-call | flops 1024 | bytes 1024 | tf_op jit(solution)/shard_map/block_forward/pallas_call | solution.py:248
  253.4 6.6 %assemble.4 = (bf16[1,4,2,2,2,64,128]{6,5,4,3,2,1,0:T(8,128)(2,1)}, bf16[1,4,2,2,2,64,512]{6,5,4,3,2,1,0:T(8,128)(2,1)}, bf16[8,4,2,2,2,16,512]{6,5,4,3,2,1,0:T(8,128)(2,1)}) custom-call(s32[4]{0:T(128)} %pad_add_fusion.1.place.refs_0_, bf16[2,4,2,112,512]{4,3,2,1,0:T(8,128)(2,1)} %pad_maximum_fusion.4.refs_0_, ...), custom_call_target="tpu_custom_call" | custom-call | flops 1024 | bytes 1024 | tf_op jit(solution)/shard_map/assemble/pallas_call | solution.py:841
  260.1 6.9 %head_target.1.refs_5_ = f32[8,128]{1,0:T(8,128)} custom-call(f32[384,2048]{1,0:T(8,128)} %block_forward.5.stream, bf16[2048,128]{1,0:T(8,128)(2,1)} %bitcast.471, bf16[2048,512]{1,0:T(8,128)(2,1)} %bitcast.443, bf16[8,512,512]{2,1,0:T(8,128)(2,1)} %bitcast.432, s32[8,128]{1,0:T(8,128)} %pad.72.whole.refs_6_, f32[8,128]{1,0:T(8,128)} %select_maximum_fusion.real), custom_call_target="tpu_custom_call" | custom-call | flops 1024 | bytes 1024 | tf_op jit(solution)/shard_map/head_target/pallas_call | solution.py:573
  268.1 3.3 pad_maximum_fusion.3.refs_4_
  271.4 5.2 collective-permute-done.25.refs_6_
  283.3 19.4 %block_forward.6 = (f32[384,2048]{1,0:T(8,128)}, f32[384,2048]{1,0:T(8,128)}, f32[384,512]{1,0:T(8,128)}, f32[384,512]{1,0:T(8,128)}, f32[384,2048]{1,0:T(8,128)...) custom-call(s32[4]{0:T(128)} %pad_add_fusion.1.place.refs_0_, ...), custom_call_target="tpu_custom_call" | custom-call | flops 1024 | bytes 1024 | tf_op jit(solution)/shard_map/block_forward/pallas_call | solution.py:248
  304.1 11.6 %collective-permute-done.29.refs_5_ = bf16[2,4,2,144,512]{4,3,2,1,0:T(8,128)(2,1)} collective-permute-done((bf16[2,4,2,144,512]{4,3,2,1,0:T(8,128)(2,1)}, bf16[2,4,2,144,512]{4,3,2,1,0:T(8,128)(2,1)}, u32[]{:S(2)}, u32[]{:S(2)}) %collective-permute-start.29) | collective-permute-done | bytes 2359328 | tf_op jit(solution)/shard_map/ppermute | solution.py:701
  320.5 17.4 %block_forward.7 = (f32[384,2048]{1,0:T(8,128)}, f32[384,512]{1,0:T(8,128)}, f32[384,512]{1,0:T(8,128)}, f32[384,2048]{1,0:T(8,128)}, f32[8,3072]{1,0:T(8,128)},...) custom-call(s32[4]{0:T(128)} %pad_add_fusion.1.place.refs_0_, ...), custom_call_target="tpu_custom_call" | custom-call | flops 1024 | bytes 1024 | tf_op jit(solution)/shard_map/block_forward/pallas_call | solution.py:248
  339.6 3.1 collective-permute-done.34.refs_3_
  343.9 6.6 %assemble.5 = (bf16[1,4,2,2,2,64,128]{6,5,4,3,2,1,0:T(8,128)(2,1)}, bf16[1,4,2,2,2,64,512]{6,5,4,3,2,1,0:T(8,128)(2,1)}, bf16[8,4,2,2,2,16,512]{6,5,4,3,2,1,0:T(8,128)(2,1)}) custom-call(s32[4]{0:T(128)} %pad_add_fusion.1.place.refs_0_, bf16[2,4,2,112,512]{4,3,2,1,0:T(8,128)(2,1)} %copy-done.6, bf16[2,4,2,112,512]{4,3,2,1,0:T(8,128)(2,1)} %copy-done.15, ...), custom_call_target="tpu_custom_call" | custom-call | flops 1024 | bytes 1024 | tf_op jit(solution)/shard_map/assemble/pallas_call | solution.py:841
  350.6 15.5 %head_loss.1 = (f32[1,1]{1,0:T(1,128)}, f32[384,2048]{1,0:T(8,128)}, bf16[2,2,4,2,112,512]{5,4,3,2,1,0:T(8,128)(2,1)}, bf16[2,4,2,112,512]{4,3,2,1,0:T(8,128)(2,...) custom-call(s32[4]{0:T(128)} %pad_add_fusion.1.place.refs_0_, ...), custom_call_target="tpu_custom_call" | custom-call | flops 1024 | bytes 1024 | tf_op jit(solution)/shard_map/head_loss/pallas_call | solution.py:414
  366.9 14.7 %back_out.1 = (f32[384,2048]{1,0:T(8,128)}, bf16[384,512]{1,0:T(8,128)(2,1)}, f32[1,5120]{1,0:T(1,128)}, bf16[2,2,4,2,32,512]{5,4,3,2,1,0:T(8,128)(2,1)}, bf16[2...) custom-call(s32[4]{0:T(128)} %pad_add_fusion.1.place.refs_0_, ...), custom_call_target="tpu_custom_call" | custom-call | flops 1024 | bytes 1024 | tf_op jit(solution)/shard_map/back_out/pallas_call | solution.py:414
  381.6 4.7 fusion
  387.8 12.3 %back_mid.2 = (bf16[384,512]{1,0:T(8,128)(2,1)}, f32[1,1024]{1,0:T(1,128)}, bf16[2,2,4,2,80,512]{5,4,3,2,1,0:T(8,128)(2,1)}, bf16[2,4,2,80,512]{4,3,2,1,0:T(8,12...) custom-call(s32[4]{0:T(128)} %pad_add_fusion.1.place.refs_0_, ...), custom_call_target="tpu_custom_call" | custom-call | flops 1024 | bytes 1024 | tf_op jit(solution)/shard_map/back_mid/pallas_call | solution.py:414
  400.1 9.7 %collective-permute-done.36 = bf16[2,4,2,112,512]{4,3,2,1,0:T(8,128)(2,1)} collective-permute-done((bf16[2,4,2,112,512]{4,3,2,1,0:T(8,128)(2,1)}, bf16[2,4,2,112,512]{4,3,2,1,0:T(8,128)(2,1)}, u32[]{:S(2)}, u32[]{:S(2)}) %collective-permute-start.36) | collective-permute-done | bytes 1835040 | tf_op jit(solution)/shard_map/ppermute | solution.py:701
  409.8 4.4 fusion.5
  417.2 18.8 %back_between.1 = (f32[384,2048]{1,0:T(8,128)}, bf16[384,512]{1,0:T(8,128)(2,1)}, f32[1,5120]{1,0:T(1,128)}, bf16[2,2,4,2,64,512]{5,4,3,2,1,0:T(8,128)(2,1)}, bf...) custom-call(s32[4]{0:T(128)} %pad_add_fusion.1.place.refs_0_, ...), custom_call_target="tpu_custom_call" | custom-call | flops 1024 | bytes 1024 | tf_op jit(solution)/shard_map/back_between/pallas_call | solution.py:414
  447.1 5.5 collective-permute-done.41
  453.3 12.5 %back_mid.3 = (bf16[384,512]{1,0:T(8,128)(2,1)}, f32[1,1024]{1,0:T(1,128)}, bf16[2,2,4,2,80,512]{5,4,3,2,1,0:T(8,128)(2,1)}, bf16[2,4,2,80,512]{4,3,2,1,0:T(8,12...) custom-call(s32[4]{0:T(128)} %pad_add_fusion.1.place.refs_0_, ...), custom_call_target="tpu_custom_call" | custom-call | flops 1024 | bytes 1024 | tf_op jit(solution)/shard_map/back_mid/pallas_call | solution.py:414
  481.2 8.9 %back_first.1 = (bf16[2,2,4,2,64,512]{5,4,3,2,1,0:T(8,128)(2,1)}, bf16[2,4,2,64,512]{4,3,2,1,0:T(8,128)(2,1)}, bf16[4,2,64,512]{3,2,1,0:T(8,128)(2,1)}, bf16[4,2,64,512]{3,2,1,0:T(8,128)(2,1)}) custom-call(s32[4]{0:T(128)} %pad_add_fusion.1.place.refs_0_, bf16[384,512]{1,0:T(8,128)(2,1)} %get-tuple-element.694.refs_1_, ...), custom_call_target="tpu_custom_call" | custom-call | flops 1024 | bytes 1024 | tf_op jit(solution)/shard_map/back_first/pallas_call | solution.py:414
  494.4 4.1 concatenate.62
  513.1 5.5 collective-permute-done.55
  520.5 3.3 collective-permute-start.59
  529.2 5.3 collective-permute-done.60
  537.6 6.5 %collective-permute-done.70 = bf16[2,4,2,64,512]{4,3,2,1,0:T(8,128)(2,1)S(1)} collective-permute-done((bf16[2,4,2,64,512]{4,3,2,1,0:T(8,128)(2,1)S(1)}, bf16[2,4,2,64,512]{4,3,2,1,0:T(8,128)(2,1)S(1)}, u32[]{:S(2)}, u32[]{:S(2)}) %collective-permute-start.70) | collective-permute-done | bytes 1048608 | tf_op jit(solution)/shard_map/ppermute | solution.py:701
  549.1 3.8 collective-permute-start.65
  552.9 4.9 collective-permute-start.66
  561.1 3.2 collective-permute-start.73
  569.2 3.0 collective-permute-done.72
  572.1 6.3 %collective-permute-done.73 = bf16[2,64,512]{2,1,0:T(8,128)(2,1)S(1)} collective-permute-done((bf16[2,64,512]{2,1,0:T(8,128)(2,1)S(1)}, bf16[2,64,512]{2,1,0:T(8,128)(2,1)S(1)}, u32[]{:S(2)}, u32[]{:S(2)}) %collective-permute-start.73) | collective-permute-done | bytes 131104 | tf_op jit(solution)/shard_map/ppermute | solution.py:701
  581.3 10.9 %directions.1 = (f32[8,128]{1,0:T(8,128)}, f32[1,115648]{1,0:T(1,128)}, f32[1,115648]{1,0:T(1,128)}, f32[1,115648]{1,0:T(1,128)}, f32[2,139456]{1,0:T(2,128)}, /*index=5*/f32[2,139456]{1,0:T(2,128)}, f32[2,139456]{1,0:T(2,128)}) custom-call(f32[64,512]{1,0:T(8,128)} %bitcast.464, f32[160,512]{1,0:T(8,128)} %bitcast.453, f32[128,512]{1,0:T(8,128)} %bitcast.458, ...), custom_call_target="tpu_custom_call" | custom-call | flops 1024 | bytes 1024 | tf_op jit(solution)/shard_map/directions/pallas_call | solution.py:1176
  601.5 3.8 collective-permute-start.80
  605.3 2.9 collective-permute-start.81
  612.4 7.5 %update.1 = (f32[8,128]{1,0:T(8,128)}, f32[1,115648]{1,0:T(1,128)}, bf16[1,115648]{1,0:T(2,128)(2,1)}, f32[1,115648]{1,0:T(1,128)}, f32[2,139456]{1,0:T(2,128)},...) custom-call(f32[8,128]{1,0:T(8,128)} %copy-done.47, f32[1,115648]{1,0:T(1,128)} %bitcast.434, ...), custom_call_target="tpu_custom_call" | custom-call | flops 1024 | bytes 1024 | tf_op jit(solution)/shard_map/update/pallas_call | solution.py:1235
  621.1 3.0 reduce.12
  (480 shorter events, 181.7 us)
Async XLA Ops:
  22.6 28.5 %collective-permute-start.4 = (bf16[2,2,144,512]{3,2,1,0:T(8,128)(2,1)S(1)}, bf16[2,2,144,512]{3,2,1,0:T(8,128)(2,1)S(1)}, u32[]{:S(2)}, u32[]{:S(2)}) collective-permute-start(bf16[2,2,144,512]{3,2,1,0:T(8,128)(2,1)S(1)} %pad_maximum_fusion.15), channel_id=1, source_target_pairs={{0,16},{1,17},{2,18},{3,19},{4,20},{5,21},{6,22},{7,23},{8,24},{9,... | collective-permute-start | bytes 1769480 | tf_op jit(solution)/shard_map/ppermute | solution.py:701
  30.9 20.4 %collective-permute-start.2 = (bf16[688,512]{1,0:T(8,128)(2,1)}, bf16[688,512]{1,0:T(8,128)(2,1)S(1)}, u32[]{:S(2)}, u32[]{:S(2)}) collective-permute-start(bf16[688,512]{1,0:T(8,128)(2,1)} %dynamic-slice_dynamic-update-slice_fusion.3), channel_id=1, source_target_pairs={{0,1},{1,0},{2,3},{3,2},{4,5},{5,4},{6,7},{7,6},{8,9},{9,8},{10,11... | collective-permute-start | bytes 2113544 | tf_op jit(solution)/shard_map/ppermute | solution.py:701
  60.4 31.7 %collective-permute-start.6 = (bf16[2,2,160,512]{3,2,1,0:T(8,128)(2,1)S(1)}, bf16[2,2,160,512]{3,2,1,0:T(8,128)(2,1)S(1)}, u32[]{:S(2)}, u32[]{:S(2)}) collective-permute-start(bf16[2,2,160,512]{3,2,1,0:T(8,128)(2,1)S(1)} %pad_maximum_fusion.13), channel_id=1, source_target_pairs={{0,16},{1,17},{2,18},{3,19},{4,20},{5,21},{6,22},{7,23},{8,24},{9,... | collective-permute-start | bytes 1966088 | tf_op jit(solution)/shard_map/ppermute | solution.py:701
  63.6 38.1 %collective-permute-start.5 = (bf16[2,528,512]{2,1,0:T(8,128)(2,1)S(1)}, bf16[2,528,512]{2,1,0:T(8,128)(2,1)S(1)}, u32[]{:S(2)}, u32[]{:S(2)}) collective-permute-start(bf16[2,528,512]{2,1,0:T(8,128)(2,1)S(1)} %pad_maximum_fusion.10), channel_id=1, source_target_pairs={{0,8},{1,9},{2,10},{3,11},{4,12},{5,13},{6,14},{7,15},{8,0},{9,1},... | collective-permute-start | bytes 3244040 | tf_op jit(solution)/shard_map/ppermute | solution.py:701
  65.4 37.1 %collective-permute-start.7 = (bf16[4,2,144,512]{3,2,1,0:T(8,128)(2,1)S(1)}, bf16[4,2,144,512]{3,2,1,0:T(8,128)(2,1)S(1)}, u32[]{:S(2)}, u32[]{:S(2)}) collective-permute-start(bf16[4,2,144,512]{3,2,1,0:T(8,128)(2,1)S(1)} %bitcast.429), channel_id=1, source_target_pairs={{0,2},{1,5},{2,0},{3,7},{4,6},{5,1},{6,4},{7,3},{8,10},{9,13},{10,... | collective-permute-start | bytes 3538952 | tf_op jit(solution)/shard_map/ppermute | solution.py:701
  102.7 43.0 %collective-permute-start.10 = (bf16[2,4,2,144,512]{4,3,2,1,0:T(8,128)(2,1)S(1)}, bf16[2,4,2,144,512]{4,3,2,1,0:T(8,128)(2,1)S(1)}, u32[]{:S(2)}, u32[]{:S(2)}) collective-permute-start(bf16[2,4,2,144,512]{4,3,2,1,0:T(8,128)(2,1)S(1)} %pad_maximum_fusion.2.refs_4_), channel_id=1, source_target_pairs={{0,4},{1,3},{2,6},{3,1},{4,0},{5,7},{6,2},{7,5},{8,12},{9,11},{10,... | collective-permute-start | bytes 7077896 | tf_op jit(solution)/shard_map/ppermute | solution.py:701
  104.3 41.4 %collective-permute-start.11 = (bf16[2,4,2,144,512]{4,3,2,1,0:T(8,128)(2,1)S(1)}, bf16[2,4,2,144,512]{4,3,2,1,0:T(8,128)(2,1)S(1)}, u32[]{:S(2)}, u32[]{:S(2)}) collective-permute-start(bf16[2,4,2,144,512]{4,3,2,1,0:T(8,128)(2,1)S(1)} %pad_maximum_fusion.2.refs_4_), channel_id=1, source_target_pairs={{0,1},{1,0},{2,3},{3,2},{4,5},{5,4},{6,7},{7,6},{8,9},{9,8},{10,11... | collective-permute-start | bytes 7077896 | tf_op jit(solution)/shard_map/ppermute | solution.py:701
  104.3 31.7 %collective-permute-start.9 = (bf16[4,2,160,512]{3,2,1,0:T(8,128)(2,1)S(1)}, bf16[4,2,160,512]{3,2,1,0:T(8,128)(2,1)S(1)}, u32[]{:S(2)}, u32[]{:S(2)}) collective-permute-start(bf16[4,2,160,512]{3,2,1,0:T(8,128)(2,1)S(1)} %bitcast.425), channel_id=1, source_target_pairs={{0,2},{1,5},{2,0},{3,7},{4,6},{5,1},{6,4},{7,3},{8,10},{9,13},{10,... | collective-permute-start | bytes 3932168 | tf_op jit(solution)/shard_map/ppermute | solution.py:701
  105.8 22.4 %collective-permute-start.8 = (bf16[2,2,112,512]{3,2,1,0:T(8,128)(2,1)S(1)}, bf16[2,2,112,512]{3,2,1,0:T(8,128)(2,1)S(1)}, u32[]{:S(2)}, u32[]{:S(2)}) collective-permute-start(bf16[2,2,112,512]{3,2,1,0:T(8,128)(2,1)S(1)} %pad_maximum_fusion.18), channel_id=1, source_target_pairs={{0,16},{1,17},{2,18},{3,19},{4,20},{5,21},{6,22},{7,23},{8,24},{9,... | collective-permute-start | bytes 1376264 | tf_op jit(solution)/shard_map/ppermute | solution.py:701
  145.7 41.6 %collective-permute-start.14 = (bf16[2,4,2,160,512]{4,3,2,1,0:T(8,128)(2,1)S(1)}, bf16[2,4,2,160,512]{4,3,2,1,0:T(8,128)(2,1)}, u32[]{:S(2)}, u32[]{:S(2)}) collective-permute-start(bf16[2,4,2,160,512]{4,3,2,1,0:T(8,128)(2,1)S(1)} %pad_maximum_fusion.refs_0_.refs_5_), channel_id=1, source_target_pairs={{0,4},{1,3},{2,6},{3,1},{4,0},{5,7},{6,2},{7,5},{8,12},{9,11},{10,... | collective-permute-start | bytes 7864328 | tf_op jit(solution)/shard_map/ppermute | solution.py:701
  147.3 40.1 %collective-permute-start.15 = (bf16[2,4,2,160,512]{4,3,2,1,0:T(8,128)(2,1)S(1)}, bf16[2,4,2,160,512]{4,3,2,1,0:T(8,128)(2,1)S(1)}, u32[]{:S(2)}, u32[]{:S(2)}) collective-permute-start(bf16[2,4,2,160,512]{4,3,2,1,0:T(8,128)(2,1)S(1)} %pad_maximum_fusion.refs_0_.refs_5_), channel_id=1, source_target_pairs={{0,1},{1,0},{2,3},{3,2},{4,5},{5,4},{6,7},{7,6},{8,9},{9,8},{10,11... | collective-permute-start | bytes 7864328 | tf_op jit(solution)/shard_map/ppermute | solution.py:701
  148.8 32.1 %collective-permute-start.12 = (bf16[2,2,160,512]{3,2,1,0:T(8,128)(2,1)S(1)}, bf16[2,2,160,512]{3,2,1,0:T(8,128)(2,1)S(1)}, u32[]{:S(2)}, u32[]{:S(2)}) collective-permute-start(bf16[2,2,160,512]{3,2,1,0:T(8,128)(2,1)S(1)} %pad_maximum_fusion.14), channel_id=1, source_target_pairs={{0,16},{1,17},{2,18},{3,19},{4,20},{5,21},{6,22},{7,23},{8,24},{9,... | collective-permute-start | bytes 1966088 | tf_op jit(solution)/shard_map/ppermute | solution.py:701
  149.6 32.6 %collective-permute-start.13 = (bf16[4,2,112,512]{3,2,1,0:T(8,128)(2,1)S(1)}, bf16[4,2,112,512]{3,2,1,0:T(8,128)(2,1)S(1)}, u32[]{:S(2)}, u32[]{:S(2)}) collective-permute-start(bf16[4,2,112,512]{3,2,1,0:T(8,128)(2,1)S(1)} %bitcast.435), channel_id=1, source_target_pairs={{0,2},{1,5},{2,0},{3,7},{4,6},{5,1},{6,4},{7,3},{8,10},{9,13},{10,... | collective-permute-start | bytes 2752520 | tf_op jit(solution)/shard_map/ppermute | solution.py:701
  193.2 39.0 %collective-permute-start.19 = (bf16[2,4,2,112,512]{4,3,2,1,0:T(8,128)(2,1)}, bf16[2,4,2,112,512]{4,3,2,1,0:T(8,128)(2,1)}, u32[]{:S(2)}, u32[]{:S(2)}) collective-permute-start(bf16[2,4,2,112,512]{4,3,2,1,0:T(8,128)(2,1)} %pad_maximum_fusion.4.refs_0_), channel_id=1, source_target_pairs={{0,4},{1,3},{2,6},{3,1},{4,0},{5,7},{6,2},{7,5},{8,12},{9,11},{10,... | collective-permute-start | bytes 5505032 | tf_op jit(solution)/shard_map/ppermute | solution.py:701
  194.7 37.4 %collective-permute-start.20 = (bf16[2,4,2,112,512]{4,3,2,1,0:T(8,128)(2,1)}, bf16[2,4,2,112,512]{4,3,2,1,0:T(8,128)(2,1)}, u32[]{:S(2)}, u32[]{:S(2)}) collective-permute-start(bf16[2,4,2,112,512]{4,3,2,1,0:T(8,128)(2,1)} %pad_maximum_fusion.4.refs_0_), channel_id=1, source_target_pairs={{0,1},{1,0},{2,3},{3,2},{4,5},{5,4},{6,7},{7,6},{8,9},{9,8},{10,11... | collective-permute-start | bytes 5505032 | tf_op jit(solution)/shard_map/ppermute | solution.py:701
  194.9 32.9 %collective-permute-start.18 = (bf16[4,2,160,512]{3,2,1,0:T(8,128)(2,1)}, bf16[4,2,160,512]{3,2,1,0:T(8,128)(2,1)}, u32[]{:S(2)}, u32[]{:S(2)}) collective-permute-start(bf16[4,2,160,512]{3,2,1,0:T(8,128)(2,1)} %bitcast.65), channel_id=1, source_target_pairs={{0,2},{1,5},{2,0},{3,7},{4,6},{5,1},{6,4},{7,3},{8,10},{9,13},{10,... | collective-permute-start | bytes 3932168 | tf_op jit(solution)/shard_map/ppermute | solution.py:701
  198.9 28.9 %collective-permute-start.16 = (bf16[2,2,144,512]{3,2,1,0:T(8,128)(2,1)S(1)}, bf16[2,2,144,512]{3,2,1,0:T(8,128)(2,1)}, u32[]{:S(2)}, u32[]{:S(2)}) collective-permute-start(bf16[2,2,144,512]{3,2,1,0:T(8,128)(2,1)S(1)} %pad_maximum_fusion.16), channel_id=1, source_target_pairs={{0,16},{1,17},{2,18},{3,19},{4,20},{5,21},{6,22},{7,23},{8,24},{9,... | collective-permute-start | bytes 1769480 | tf_op jit(solution)/shard_map/ppermute | solution.py:701
  203.0 32.0 %collective-permute-start.22 = (bf16[2,4,2,144,512]{4,3,2,1,0:T(8,128)(2,1)}, bf16[2,4,2,144,512]{4,3,2,1,0:T(8,128)(2,1)}, u32[]{:S(2)}, u32[]{:S(2)}) collective-permute-start(bf16[2,4,2,144,512]{4,3,2,1,0:T(8,128)(2,1)} %copy-done.12), channel_id=1, source_target_pairs={{0,1},{1,0},{2,3},{3,2},{4,5},{5,4},{6,7},{7,6},{8,9},{9,8},{10,11... | collective-permute-start | bytes 7077896 | tf_op jit(solution)/shard_map/ppermute | solution.py:701
  232.2 44.5 %collective-permute-start.25 = (bf16[2,4,2,160,512]{4,3,2,1,0:T(8,128)(2,1)S(1)}, bf16[2,4,2,160,512]{4,3,2,1,0:T(8,128)(2,1)}, u32[]{:S(2)}, u32[]{:S(2)}) collective-permute-start(bf16[2,4,2,160,512]{4,3,2,1,0:T(8,128)(2,1)S(1)} %pad_maximum_fusion.1.refs_5_), channel_id=1, source_target_pairs={{0,4},{1,3},{2,6},{3,1},{4,0},{5,7},{6,2},{7,5},{8,12},{9,11},{10,... | collective-permute-start | bytes 7864328 | tf_op jit(solution)/shard_map/ppermute | solution.py:701
  233.1 43.6 %collective-permute-start.26 = (bf16[2,4,2,160,512]{4,3,2,1,0:T(8,128)(2,1)S(1)}, bf16[2,4,2,160,512]{4,3,2,1,0:T(8,128)(2,1)}, u32[]{:S(2)}, u32[]{:S(2)}) collective-permute-start(bf16[2,4,2,160,512]{4,3,2,1,0:T(8,128)(2,1)S(1)} %pad_maximum_fusion.1.refs_5_), channel_id=1, source_target_pairs={{0,1},{1,0},{2,3},{3,2},{4,5},{5,4},{6,7},{7,6},{8,9},{9,8},{10,11... | collective-permute-start | bytes 7864328 | tf_op jit(solution)/shard_map/ppermute | solution.py:701
  233.1 20.3 %collective-permute-start.23 = (bf16[2,4,2,112,512]{4,3,2,1,0:T(8,128)(2,1)}, bf16[2,4,2,112,512]{4,3,2,1,0:T(8,128)(2,1)}, u32[]{:S(2)}, u32[]{:S(2)}) collective-permute-start(bf16[2,4,2,112,512]{4,3,2,1,0:T(8,128)(2,1)} %collective-permute-done.19.refs_1_), channel_id=1, source_target_pairs={{0,1},{1,0},{2,3},{3,2},{4,5},{5,4},{6,7},{7,6},{8,9},{9,8},{10,11... | collective-permute-start | bytes 5505032 | tf_op jit(solution)/shard_map/ppermute | solution.py:701
  233.6 33.4 %collective-permute-start.24 = (bf16[4,2,144,512]{3,2,1,0:T(8,128)(2,1)}, bf16[4,2,144,512]{3,2,1,0:T(8,128)(2,1)}, u32[]{:S(2)}, u32[]{:S(2)}) collective-permute-start(bf16[4,2,144,512]{3,2,1,0:T(8,128)(2,1)} %bitcast.72), channel_id=1, source_target_pairs={{0,2},{1,5},{2,0},{3,7},{4,6},{5,1},{6,4},{7,3},{8,10},{9,13},{10,... | collective-permute-start | bytes 3538952 | tf_op jit(solution)/shard_map/ppermute | solution.py:701
  235.1 31.9 %collective-permute-start.21 = (bf16[2,2,112,512]{3,2,1,0:T(8,128)(2,1)S(1)}, bf16[2,2,112,512]{3,2,1,0:T(8,128)(2,1)}, u32[]{:S(2)}, u32[]{:S(2)}) collective-permute-start(bf16[2,2,112,512]{3,2,1,0:T(8,128)(2,1)S(1)} %copy-done.14), channel_id=1, source_target_pairs={{0,16},{1,17},{2,18},{3,19},{4,20},{5,21},{6,22},{7,23},{8,24},{9,... | collective-permute-start | bytes 1376264 | tf_op jit(solution)/shard_map/ppermute | solution.py:701
  276.7 39.0 %collective-permute-start.29 = (bf16[2,4,2,144,512]{4,3,2,1,0:T(8,128)(2,1)}, bf16[2,4,2,144,512]{4,3,2,1,0:T(8,128)(2,1)}, u32[]{:S(2)}, u32[]{:S(2)}) collective-permute-start(bf16[2,4,2,144,512]{4,3,2,1,0:T(8,128)(2,1)} %pad_maximum_fusion.3.refs_4_), channel_id=1, source_target_pairs={{0,4},{1,3},{2,6},{3,1},{4,0},{5,7},{6,2},{7,5},{8,12},{9,11},{10,... | collective-permute-start | bytes 7077896 | tf_op jit(solution)/shard_map/ppermute | solution.py:701
  277.5 38.2 %collective-permute-start.30 = (bf16[2,4,2,144,512]{4,3,2,1,0:T(8,128)(2,1)}, bf16[2,4,2,144,512]{4,3,2,1,0:T(8,128)(2,1)}, u32[]{:S(2)}, u32[]{:S(2)}) collective-permute-start(bf16[2,4,2,144,512]{4,3,2,1,0:T(8,128)(2,1)} %pad_maximum_fusion.3.refs_4_), channel_id=1, source_target_pairs={{0,1},{1,0},{2,3},{3,2},{4,5},{5,4},{6,7},{7,6},{8,9},{9,8},{10,11... | collective-permute-start | bytes 7077896 | tf_op jit(solution)/shard_map/ppermute | solution.py:701
  277.7 25.0 %collective-permute-start.27 = (bf16[4,2,112,512]{3,2,1,0:T(8,128)(2,1)S(1)}, bf16[4,2,112,512]{3,2,1,0:T(8,128)(2,1)}, u32[]{:S(2)}, u32[]{:S(2)}) collective-permute-start(bf16[4,2,112,512]{3,2,1,0:T(8,128)(2,1)S(1)} %bitcast.437), channel_id=1, source_target_pairs={{0,2},{1,5},{2,0},{3,7},{4,6},{5,1},{6,4},{7,3},{8,10},{9,13},{10,... | collective-permute-start | bytes 2752520 | tf_op jit(solution)/shard_map/ppermute | solution.py:701
  315.7 23.2 %collective-permute-start.31 = (bf16[2,4,2,112,512]{4,3,2,1,0:T(8,128)(2,1)S(1)}, bf16[2,4,2,112,512]{4,3,2,1,0:T(8,128)(2,1)S(1)}, u32[]{:S(2)}, u32[]{:S(2)}) collective-permute-start(bf16[2,4,2,112,512]{4,3,2,1,0:T(8,128)(2,1)S(1)} %pad_maximum_fusion.5.refs_0_), channel_id=1, source_target_pairs={{0,4},{1,3},{2,6},{3,1},{4,0},{5,7},{6,2},{7,5},{8,12},{9,11},{10,... | collective-permute-start | bytes 5505032 | tf_op jit(solution)/shard_map/ppermute | solution.py:701
  316.5 22.4 %collective-permute-start.32 = (bf16[2,4,2,112,512]{4,3,2,1,0:T(8,128)(2,1)S(1)}, bf16[2,4,2,112,512]{4,3,2,1,0:T(8,128)(2,1)}, u32[]{:S(2)}, u32[]{:S(2)}) collective-permute-start(bf16[2,4,2,112,512]{4,3,2,1,0:T(8,128)(2,1)S(1)} %pad_maximum_fusion.5.refs_0_), channel_id=1, source_target_pairs={{0,1},{1,0},{2,3},{3,2},{4,5},{5,4},{6,7},{7,6},{8,9},{9,8},{10,11... | collective-permute-start | bytes 5505032 | tf_op jit(solution)/shard_map/ppermute | solution.py:701
  366.1 15.5 %collective-permute-start.35 = (bf16[2,2,4,2,112,512]{5,4,3,2,1,0:T(8,128)(2,1)}, bf16[2,2,4,2,112,512]{5,4,3,2,1,0:T(8,128)(2,1)S(1)}, u32[]{:S(2)}, u32[]{:S(2)}) collective-permute-start(bf16[2,2,4,2,112,512]{5,4,3,2,1,0:T(8,128)(2,1)} %get-tuple-element.562), channel_id=1, source_target_pairs={{0,1},{1,0},{2,3},{3,2},{4,5},{5,4},{6,7},{7,6},{8,9},{9,8},{10,11... | collective-permute-start | bytes 11010056 | tf_op jit(solution)/shard_map/ppermute | solution.py:701
  386.3 23.5 %collective-permute-start.36 = (bf16[2,4,2,112,512]{4,3,2,1,0:T(8,128)(2,1)}, bf16[2,4,2,112,512]{4,3,2,1,0:T(8,128)(2,1)}, u32[]{:S(2)}, u32[]{:S(2)}) collective-permute-start(bf16[2,4,2,112,512]{4,3,2,1,0:T(8,128)(2,1)} %fusion), channel_id=1, source_target_pairs={{0,4},{1,3},{2,6},{3,1},{4,0},{5,7},{6,2},{7,5},{8,12},{9,11},{10,... | collective-permute-start | bytes 5505032 | tf_op jit(solution)/shard_map/ppermute | solution.py:701
  409.8 26.2 %collective-permute-start.40 = (bf16[2,2,4,2,80,512]{5,4,3,2,1,0:T(8,128)(2,1)}, bf16[2,2,4,2,80,512]{5,4,3,2,1,0:T(8,128)(2,1)}, u32[]{:S(2)}, u32[]{:S(2)}) collective-permute-start(bf16[2,2,4,2,80,512]{5,4,3,2,1,0:T(8,128)(2,1)} %get-tuple-element.625), channel_id=1, source_target_pairs={{0,1},{1,0},{2,3},{3,2},{4,5},{5,4},{6,7},{7,6},{8,9},{9,8},{10,11... | collective-permute-start | bytes 7864328 | tf_op jit(solution)/shard_map/ppermute | solution.py:701
  414.2 21.8 %collective-permute-start.38 = (bf16[4,2,112,512]{3,2,1,0:T(8,128)(2,1)}, bf16[4,2,112,512]{3,2,1,0:T(8,128)(2,1)}, u32[]{:S(2)}, u32[]{:S(2)}) collective-permute-start(bf16[4,2,112,512]{3,2,1,0:T(8,128)(2,1)} %get-tuple-element.755), channel_id=1, source_target_pairs={{0,2},{1,5},{2,0},{3,7},{4,6},{5,1},{6,4},{7,3},{8,10},{9,13},{10,... | collective-permute-start | bytes 2752520 | tf_op jit(solution)/shard_map/ppermute | solution.py:701
  415.1 20.9 %collective-permute-start.39 = (bf16[2,4,2,32,512]{4,3,2,1,0:T(8,128)(2,1)S(1)}, bf16[2,4,2,32,512]{4,3,2,1,0:T(8,128)(2,1)}, u32[]{:S(2)}, u32[]{:S(2)}) collective-permute-start(bf16[2,4,2,32,512]{4,3,2,1,0:T(8,128)(2,1)S(1)} %fusion.13), channel_id=1, source_target_pairs={{0,4},{1,3},{2,6},{3,1},{4,0},{5,7},{6,2},{7,5},{8,12},{9,11},{10,... | collective-permute-start | bytes 1572872 | tf_op jit(solution)/shard_map/ppermute | solution.py:701
  436.0 31.0 %collective-permute-start.46 = (bf16[2,2,4,2,64,512]{5,4,3,2,1,0:T(8,128)(2,1)}, bf16[2,2,4,2,64,512]{5,4,3,2,1,0:T(8,128)(2,1)}, u32[]{:S(2)}, u32[]{:S(2)}) collective-permute-start(bf16[2,2,4,2,64,512]{5,4,3,2,1,0:T(8,128)(2,1)} %get-tuple-element.661), channel_id=1, source_target_pairs={{0,1},{1,0},{2,3},{3,2},{4,5},{5,4},{6,7},{7,6},{8,9},{9,8},{10,11... | collective-permute-start | bytes 6291464 | tf_op jit(solution)/shard_map/ppermute | solution.py:701
  438.9 28.1 %collective-permute-start.45 = (bf16[2,4,2,80,512]{4,3,2,1,0:T(8,128)(2,1)}, bf16[2,4,2,80,512]{4,3,2,1,0:T(8,128)(2,1)S(1)}, u32[]{:S(2)}, u32[]{:S(2)}) collective-permute-start(bf16[2,4,2,80,512]{4,3,2,1,0:T(8,128)(2,1)} %fusion.2), channel_id=1, source_target_pairs={{0,4},{1,3},{2,6},{3,1},{4,0},{5,7},{6,2},{7,5},{8,12},{9,11},{10,... | collective-permute-start | bytes 3932168 | tf_op jit(solution)/shard_map/ppermute | solution.py:701
  444.3 22.7 %collective-permute-start.44 = (bf16[4,2,32,512]{3,2,1,0:T(8,128)(2,1)S(1)}, bf16[4,2,32,512]{3,2,1,0:T(8,128)(2,1)S(1)}, u32[]{:S(2)}, u32[]{:S(2)}) collective-permute-start(bf16[4,2,32,512]{3,2,1,0:T(8,128)(2,1)S(1)} %get-tuple-element.762), channel_id=1, source_target_pairs={{0,2},{1,5},{2,0},{3,7},{4,6},{5,1},{6,4},{7,3},{8,10},{9,13},{10,... | collective-permute-start | bytes 786440 | tf_op jit(solution)/shard_map/ppermute | solution.py:701
  445.1 21.9 %collective-permute-start.42 = (bf16[2,112,512]{2,1,0:T(8,128)(2,1)}, bf16[2,112,512]{2,1,0:T(8,128)(2,1)}, u32[]{:S(2)}, u32[]{:S(2)}) collective-permute-start(bf16[2,112,512]{2,1,0:T(8,128)(2,1)} %get-tuple-element.760), channel_id=1, source_target_pairs={{0,16},{1,17},{2,18},{3,19},{4,20},{5,21},{6,22},{7,23},{8,24},{9,... | collective-permute-start | bytes 688136 | tf_op jit(solution)/shard_map/ppermute | solution.py:701
  468.1 30.4 %collective-permute-start.52 = (bf16[2,2,4,2,80,512]{5,4,3,2,1,0:T(8,128)(2,1)}, bf16[2,2,4,2,80,512]{5,4,3,2,1,0:T(8,128)(2,1)}, u32[]{:S(2)}, u32[]{:S(2)}) collective-permute-start(bf16[2,2,4,2,80,512]{5,4,3,2,1,0:T(8,128)(2,1)} %get-tuple-element.693), channel_id=1, source_target_pairs={{0,1},{1,0},{2,3},{3,2},{4,5},{5,4},{6,7},{7,6},{8,9},{9,8},{10,11... | collective-permute-start | bytes 7864328 | tf_op jit(solution)/shard_map/ppermute | solution.py:701
  470.1 20.0 %collective-permute-start.76 = (f32[112,512]{1,0:T(8,128)}, f32[112,512]{1,0:T(8,128)}, u32[]{:S(2)}, u32[]{:S(2)}) collective-permute-start(f32[112,512]{1,0:T(8,128)} %dynamic-slice_bitcast_fusion.1), channel_id=1, source_target_pairs={{0,1},{1,0},{2,3},{3,2},{4,5},{5,4},{6,7},{7,6},{8,9},{9,8},{10,11... | collective-permute-start | bytes 688136 | tf_op jit(solution)/shard_map/ppermute | solution.py:701
  473.5 25.1 %collective-permute-start.51 = (bf16[2,4,2,64,512]{4,3,2,1,0:T(8,128)(2,1)S(1)}, bf16[2,4,2,64,512]{4,3,2,1,0:T(8,128)(2,1)}, u32[]{:S(2)}, u32[]{:S(2)}) collective-permute-start(bf16[2,4,2,64,512]{4,3,2,1,0:T(8,128)(2,1)S(1)} %fusion.4), channel_id=1, source_target_pairs={{0,4},{1,3},{2,6},{3,1},{4,0},{5,7},{6,2},{7,5},{8,12},{9,11},{10,... | collective-permute-start | bytes 3145736 | tf_op jit(solution)/shard_map/ppermute | solution.py:701
  477.7 20.8 %collective-permute-start.50 = (bf16[4,2,80,512]{3,2,1,0:T(8,128)(2,1)}, bf16[4,2,80,512]{3,2,1,0:T(8,128)(2,1)}, u32[]{:S(2)}, u32[]{:S(2)}) collective-permute-start(bf16[4,2,80,512]{3,2,1,0:T(8,128)(2,1)} %get-tuple-element.757), channel_id=1, source_target_pairs={{0,2},{1,5},{2,0},{3,7},{4,6},{5,1},{6,4},{7,3},{8,10},{9,13},{10,... | collective-permute-start | bytes 1966088 | tf_op jit(solution)/shard_map/ppermute | solution.py:701
  499.2 26.1 %collective-permute-start.69 = (bf16[2,2,4,2,64,512]{5,4,3,2,1,0:T(8,128)(2,1)}, bf16[2,2,4,2,64,512]{5,4,3,2,1,0:T(8,128)(2,1)S(1)}, u32[]{:S(2)}, u32[]{:S(2)}) collective-permute-start(bf16[2,2,4,2,64,512]{5,4,3,2,1,0:T(8,128)(2,1)} %get-tuple-element.723), channel_id=1, source_target_pairs={{0,1},{1,0},{2,3},{3,2},{4,5},{5,4},{6,7},{7,6},{8,9},{9,8},{10,11... | collective-permute-start | bytes 6291464 | tf_op jit(solution)/shard_map/ppermute | solution.py:701
  500.8 18.1 %collective-permute-start.58 = (bf16[4,2,64,512]{3,2,1,0:T(8,128)(2,1)S(1)}, bf16[4,2,64,512]{3,2,1,0:T(8,128)(2,1)S(1)}, u32[]{:S(2)}, u32[]{:S(2)}) collective-permute-start(bf16[4,2,64,512]{3,2,1,0:T(8,128)(2,1)S(1)} %fusion.11), channel_id=1, source_target_pairs={{0,2},{1,5},{2,0},{3,7},{4,6},{5,1},{6,4},{7,3},{8,10},{9,13},{10,... | collective-permute-start | bytes 1572872 | tf_op jit(solution)/shard_map/ppermute | solution.py:701
  512.5 22.1 %collective-permute-start.63 = (bf16[2,4,2,80,512]{4,3,2,1,0:T(8,128)(2,1)S(1)}, bf16[2,4,2,80,512]{4,3,2,1,0:T(8,128)(2,1)S(1)}, u32[]{:S(2)}, u32[]{:S(2)}) collective-permute-start(bf16[2,4,2,80,512]{4,3,2,1,0:T(8,128)(2,1)S(1)} %fusion.1), channel_id=1, source_target_pairs={{0,4},{1,3},{2,6},{3,1},{4,0},{5,7},{6,2},{7,5},{8,12},{9,11},{10,... | collective-permute-start | bytes 3932168 | tf_op jit(solution)/shard_map/ppermute | solution.py:701
  526.8 17.3 %collective-permute-start.70 = (bf16[2,4,2,64,512]{4,3,2,1,0:T(8,128)(2,1)S(1)}, bf16[2,4,2,64,512]{4,3,2,1,0:T(8,128)(2,1)S(1)}, u32[]{:S(2)}, u32[]{:S(2)}) collective-permute-start(bf16[2,4,2,64,512]{4,3,2,1,0:T(8,128)(2,1)S(1)} %fusion.3), channel_id=1, source_target_pairs={{0,4},{1,3},{2,6},{3,1},{4,0},{5,7},{6,2},{7,5},{8,12},{9,11},{10,... | collective-permute-start | bytes 3145736 | tf_op jit(solution)/shard_map/ppermute | solution.py:701
  544.3 16.4 %collective-permute-start.71 = (bf16[4,2,64,512]{3,2,1,0:T(8,128)(2,1)S(1)}, bf16[4,2,64,512]{3,2,1,0:T(8,128)(2,1)S(1)}, u32[]{:S(2)}, u32[]{:S(2)}) collective-permute-start(bf16[4,2,64,512]{3,2,1,0:T(8,128)(2,1)S(1)} %fusion.9), channel_id=1, source_target_pairs={{0,2},{1,5},{2,0},{3,7},{4,6},{5,1},{6,4},{7,3},{8,10},{9,13},{10,... | collective-permute-start | bytes 1572872 | tf_op jit(solution)/shard_map/ppermute | solution.py:701
  552.9 16.1 %collective-permute-start.66 = (bf16[2,80,512]{2,1,0:T(8,128)(2,1)S(1)}, bf16[2,80,512]{2,1,0:T(8,128)(2,1)S(1)}, u32[]{:S(2)}, u32[]{:S(2)}) collective-permute-start(bf16[2,80,512]{2,1,0:T(8,128)(2,1)S(1)} %get-tuple-element.770), channel_id=1, source_target_pairs={{0,16},{1,17},{2,18},{3,19},{4,20},{5,21},{6,22},{7,23},{8,24},{9,... | collective-permute-start | bytes 491528 | tf_op jit(solution)/shard_map/ppermute | solution.py:701
  561.1 17.4 %collective-permute-start.73 = (bf16[2,64,512]{2,1,0:T(8,128)(2,1)S(1)}, bf16[2,64,512]{2,1,0:T(8,128)(2,1)S(1)}, u32[]{:S(2)}, u32[]{:S(2)}) collective-permute-start(bf16[2,64,512]{2,1,0:T(8,128)(2,1)S(1)} %get-tuple-element.790), channel_id=1, source_target_pairs={{0,16},{1,17},{2,18},{3,19},{4,20},{5,21},{6,22},{7,23},{8,24},{9,... | collective-permute-start | bytes 393224 | tf_op jit(solution)/shard_map/ppermute | solution.py:701
  (93 other events, 812.7 us)

commit v6 on v5

--- a/solution.py
+++ b/solution.py
@@ -426,14 +426,16 @@
     return (list(outs[: len(out_shape)]), list(outs[len(out_shape) :]))
 
 
-def back_out(grad, stream, hid_two, hid_three, rstd, w_out, gains, parts, tuned, place):
+def back_out(grad, stream, hid_two, hid_three, rstd, w_out, gains, dpool, parts, tuned, place):
     rows = stream.shape[0]
 
     def body(ins, outs, made, scratch, done):
-        back_out_body(rows // ROWS, *ins, *outs, scratch, made[0])
+        made[1][...] = ins[7][...]
+        done(1)
+        back_out_body(rows // ROWS, *ins[:7], *outs, scratch, made[0])
         done(0)
 
-    ins = [grad, stream, hid_two, hid_three, rstd, w_out, gains]
+    ins = [grad, stream, hid_two, hid_three, rstd, w_out, gains, dpool]
     out_shape = [f32(rows, D), bf16(rows, BOT), f32(1, 2 * BOT + 2 * D)]
     return back_call("back_out", body, ins, out_shape, out_scratch(rows), parts, tuned, place)
 
@@ -508,10 +510,26 @@
     ).astype(jnp.bfloat16)
 
 
-def head_forward(count, stream, pool, proj, heads, games, pool_t, pooled):
+def merge(value):
+    return value.reshape(-1, value.shape[-1])
+
+
+def fetch_ends(parts, tuned, place, sources, weights, sems):
+    first = len(parts) - 3
+    fetch(parts, tuned, place, sources, dict(enumerate(weights, first)), sems)
+
+    def arrived(index):
+        weight = weights[index]
+        pltpu.make_async_copy(weight, weight, sems.at[first + index]).wait()
+        return weight
+
+    return arrived
+
+
+def head_forward(count, stream, arrived, games, pool_t, pooled):
+    pool = merge(arrived(0)[...]).astype(jnp.float32)
     for part in range(D // ROWS):
-        lanes = pl.ds(part * ROWS, ROWS)
-        pool_t[:, lanes] = pool[lanes, :].astype(jnp.float32).T
+        pool_t[:, pl.ds(part * ROWS, ROWS)] = pool[part * ROWS : (part + 1) * ROWS].T
     pooled[...] = jnp.zeros_like(pooled)
 
     def weigh(frame, rows, lanes):
@@ -519,11 +537,12 @@
         pooled[frame, lanes] = jnp.sum(value * pool_t[:, lanes], axis=0, keepdims=True)
 
     each_chunk(count, D, weigh)
-    before = dot(pooled[...].astype(jnp.bfloat16), proj[...])
+    before = dot(pooled[...].astype(jnp.bfloat16), merge(arrived(1)[...]))
     hidden = silu(before).astype(jnp.bfloat16)
+    heads = arrived(2)
     scores = None
     for game in range(GAMES):
-        pair = [dot(hidden, heads[2 * game + half]) for half in range(2)]
+        pair = [dot(hidden, merge(heads[2 * game + half])) for half in range(2)]
         term = jnp.where(games == game, jnp.concatenate(pair, axis=1), 0.0)
         scores = term if scores is None else scores + term
     return ([pick_atoms(scores, action) for action in range(ACTIONS)], before, hidden)
@@ -547,10 +566,10 @@
     return jnp.sum(value, axis=1, keepdims=True)
 
 
-def target_kernel(count, stream, pool, proj, heads, whole, real, out, pool_t, pooled):
-    logits, _, _ = head_forward(
-        count, stream, pool, proj, heads, whole[:, 0:1], pool_t, pooled
-    )
+def target_kernel(count, parts, tuned, place, stream, whole, real, *refs):
+    sources, (out, *weights, sems, pool_t, pooled) = (refs[:-7], refs[-7:])
+    arrived = fetch_ends(parts, tuned, place, sources, weights, sems)
+    logits, _, _ = head_forward(count, stream, arrived, whole[:, 0:1], pool_t, pooled)
     chosen = None
     for action in range(ACTIONS):
         term = jnp.where(whole[:, 2:3] == action, logits[action], 0.0)
@@ -568,27 +587,33 @@
     out[...] = jnp.where(inside, total, 0.0)
 
 
-def head_target(stream, pool, proj, heads, whole, real):
+def ends_scratch(parts, buffers, tuned):
+    scratch = [pltpu.VMEM(shape, jnp.bfloat16) for shape in weight_shapes(parts, buffers, tuned)[-3:]]
+    scratch += [pltpu.SemaphoreType.DMA((len(parts),))]
+    return scratch + [pltpu.VMEM((ROWS, D), jnp.float32), pltpu.VMEM((8, D), jnp.float32)]
+
+
+def head_target(stream, whole, real, parts, buffers, tuned, place):
     count = stream.shape[0] // ROWS
     return pl.pallas_call(
-        functools.partial(target_kernel, count),
+        functools.partial(target_kernel, count, parts, tuned),
         out_shape=f32(8, ROWS),
-        in_specs=in_vmem(6),
+        in_specs=in_smem() + in_vmem(3) + hbm(len(buffers)),
         out_specs=in_vmem(1)[0],
-        scratch_shapes=[pltpu.VMEM((ROWS, D), jnp.float32), pltpu.VMEM((8, D), jnp.float32)],
+        scratch_shapes=ends_scratch(parts, buffers, tuned),
         compiler_params=pltpu.CompilerParams(vmem_limit_bytes=VMEM_LIMIT),
         cost_estimate=LIGHT,
         name="head_target",
-    )(stream, pool, proj, heads, whole, real)
-
-
-def loss_body(count, frames_all, ins, outs, made, scratch, done):
-    stream, pool, proj, heads, target, whole, legal = ins
-    loss, dstream = outs
-    dheads, dproj, dpool = made
-    pool_t, pooled, dpooled = scratch
+    )(place, stream, whole, real, *buffers)
+
+
+def loss_kernel(count, frames_all, parts, tuned, place, stream, target, whole, legal, *refs):
+    sources, refs = (refs[:-11], refs[-11:])
+    loss, dstream, dpool, acts, *weights, sems, pool_t, pooled, dpooled = refs
+    arrived = fetch_ends(parts, tuned, place, sources, weights, sems)
+    _, proj, heads = weights
     games, taken = (whole[:, 0:1], whole[:, 1:2])
-    logits, before, hidden = head_forward(count, stream, pool, proj, heads, games, pool_t, pooled)
+    logits, before, hidden = head_forward(count, stream, arrived, games, pool_t, pooled)
     atoms = support_lanes()
     inside = atom_lanes() < ATOMS
     logps, probs, values = ([], [], [])
@@ -626,18 +651,21 @@
     losses = cross + CQL_WEIGHT * (jnp.log(mass) + largest - taken_value)
     loss[...] = jnp.sum(jnp.where(real, losses, 0.0), axis=0, keepdims=True)
     dhidden = None
+    spread = spread.astype(jnp.bfloat16)
     for game in range(GAMES):
         mine = jnp.where(games == game, spread, 0.0).astype(jnp.bfloat16)
         for half in range(2):
             part = mine[:, half * WIDTH : (half + 1) * WIDTH]
-            dheads[2 * game + half] = dot_rows(hidden, part).astype(jnp.bfloat16)
-            term = dot_lanes(part, heads[2 * game + half])
+            term = dot_lanes(part, merge(heads[2 * game + half]))
             dhidden = term if dhidden is None else dhidden + term
-    done(0)
     dbefore = (silu_slope(before) * dhidden).astype(jnp.bfloat16)
-    dproj[0] = dot_rows(pooled[...].astype(jnp.bfloat16), dbefore).astype(jnp.bfloat16)
-    done(1)
-    dpooled[...] = dot_lanes(dbefore, proj[...]).astype(jnp.bfloat16).astype(jnp.float32)
+    pieces = [hidden, dbefore]
+    pieces += [pooled[:, part * WIDTH : (part + 1) * WIDTH] for part in range(D // WIDTH)]
+    lanes = lax.broadcasted_iota(jnp.int32, (8, WIDTH), 1)
+    marked = jnp.where(lanes == WIDTH - 1, games.astype(jnp.float32), spread[:, WIDTH:].astype(jnp.float32))
+    pieces += [spread[:, :WIDTH], marked]
+    acts[...] = jnp.concatenate([piece.astype(jnp.float32) for piece in pieces]).astype(jnp.bfloat16)
+    dpooled[...] = dot_lanes(dbefore, merge(proj[...])).astype(jnp.bfloat16).astype(jnp.float32)
 
     def push(frame, rows, lanes):
         dstream[rows, lanes] = dpooled[frame, lanes] * pool_t[:, lanes]
@@ -655,19 +683,72 @@
         return carry
 
     lax.fori_loop(0, D // ROWS, gather_pool, 0)
-    done(2)
-
-
-def head_loss(stream, pool, proj, heads, target, whole, legal, frames_all, parts, tuned, place):
+
+
+def head_loss(stream, target, whole, legal, frames_all, parts, buffers, tuned, place):
     rows = stream.shape[0]
-    scratch = [
-        pltpu.VMEM((ROWS, D), jnp.float32),
-        pltpu.VMEM((8, D), jnp.float32),
-        pltpu.VMEM((8, D), jnp.float32),
-    ]
-    ins = [stream, pool, proj, heads, target, whole, legal]
-    body = functools.partial(loss_body, rows // ROWS, frames_all)
-    return back_call("head_loss", body, ins, [f32(1, 1), f32(rows, D)], scratch, parts, tuned, place)
+    return pl.pallas_call(
+        functools.partial(loss_kernel, rows // ROWS, frames_all, parts, tuned),
+        out_shape=[f32(1, 1), f32(rows, D), bf16(1, D, ROWS), bf16(ACTS, WIDTH)],
+        in_specs=in_smem() + in_vmem(4) + hbm(len(buffers)),
+        out_specs=in_vmem(4),
+        scratch_shapes=ends_scratch(parts, buffers, tuned) + [pltpu.VMEM((8, D), jnp.float32)],
+        compiler_params=pltpu.CompilerParams(vmem_limit_bytes=VMEM_LIMIT),
+        cost_estimate=LIGHT,
+        name="head_loss",
+    )(place, stream, target, whole, legal, *buffers)
+
+
+ACTS = 64
+
+
+def own_heads_kernel(parts, tuned, place, *refs):
+    sources, (heads, proj, acts, sems) = (refs[:-4], refs[-4:])
+    fetch(parts, tuned, place, sources, {0: acts}, sems)
+    pltpu.make_async_copy(acts, acts, sems.at[0]).wait()
+    value = acts[...].reshape(-1, ACTS, WIDTH).astype(jnp.float32)
+    pieces = [value[:, first : first + 8].reshape(-1, WIDTH) for first in range(0, ACTS, 8)]
+    pieces = [piece.astype(jnp.bfloat16) for piece in pieces]
+    hidden, dbefore, scores = (pieces[0], pieces[1], pieces[-2:])
+    games = scores[1][:, WIDTH - 1 :].astype(jnp.float32)
+    lanes = lax.broadcasted_iota(jnp.int32, scores[1].shape, 1)
+    scores[1] = jnp.where(lanes < WIDTH - 1, scores[1].astype(jnp.float32), 0.0).astype(jnp.bfloat16)
+    row = lax.broadcasted_iota(jnp.int32, (WIDTH, ROWS), 0)
+    lane = lax.broadcasted_iota(jnp.int32, (WIDTH, ROWS), 1)
+
+    def own(items, count):
+        total = None
+        for block, item in enumerate(items):
+            wanted = (row + block * WIDTH == place[4] * count + lane) & (lane < count)
+            term = dot(item, jnp.where(wanted, 1.0, 0.0).astype(jnp.bfloat16))
+            total = term if total is None else total + term
+        return total.astype(jnp.bfloat16)
+
+    count = heads.shape[1]
+    mine = own([hidden], count)
+    for game in range(GAMES):
+        for half in range(2):
+            chosen = jnp.where(games == game, scores[half].astype(jnp.float32), 0.0)
+            heads[2 * game + half] = dot_rows(mine, chosen.astype(jnp.bfloat16))[:count]
+    count = proj.shape[1]
+    proj[0] = dot_rows(own(pieces[2:-2], count), dbefore)[:count]
+
+
+def own_heads(buffers, heads, proj, tuned, place):
+    parts = [Part(1, ACTS, WIDTH)]
+    return pl.pallas_call(
+        functools.partial(own_heads_kernel, parts, tuned),
+        out_shape=[f32(part.blocks, part.rows, part.lanes) for part in (heads, proj)],
+        in_specs=in_smem() + hbm(len(buffers)),
+        out_specs=in_vmem(2),
+        scratch_shapes=[
+            pltpu.VMEM(weight_shapes(parts, buffers, tuned)[0], jnp.bfloat16),
+            pltpu.SemaphoreType.DMA((1,)),
+        ],
+        compiler_params=pltpu.CompilerParams(vmem_limit_bytes=VMEM_LIMIT),
+        cost_estimate=LIGHT,
+        name="own_heads",
+    )(place, *buffers)
 
 
 WIDTH = 512
@@ -682,22 +763,36 @@
 def spot():
     sizes = grid_sizes()
     wide, narrow = (lax.axis_index("wide"), lax.axis_index("narrow"))
-    return jnp.stack(
-        [wide // sizes[1], wide % sizes[1], narrow // sizes[3], narrow % sizes[3]]
-    ).astype(jnp.int32)
+    place = [wide // sizes[1], wide % sizes[1], narrow // sizes[3], narrow % sizes[3]]
+    return jnp.stack(place + [wide * lax.axis_size("narrow") + narrow]).astype(jnp.int32)
 
 
 def hop(array, axis_of_core, step=1, swap=0):
+    sizes = grid_sizes()
+
+    def target(place):
+        axis = axis_of_core[place[3]]
+        other = list(place)
+        other[axis] = place[axis] ^ swap if swap else (place[axis] + step) % sizes[axis]
+        return other
+
+    return send(array, target)
+
+
+def flip(array, *bits):
+    return send(array, lambda place: [value ^ bit for value, bit in zip(place, bits)])
+
+
+def send(array, target):
     sizes = grid_sizes()
     pairs = []
     for place in itertools.product(*[range(size) for size in sizes]):
-        axis = axis_of_core[place[3]]
-        other = list(place)
-        other[axis] = place[axis] ^ swap if swap else (place[axis] + step) % sizes[axis]
-        source, target = [
-            ((z * sizes[1] + y) * sizes[2] + x) * sizes[3] + core for z, y, x, core in (place, other)
-        ]
-        pairs.append((source, target))
+        pairs.append(
+            tuple(
+                ((z * sizes[1] + y) * sizes[2] + x) * sizes[3] + core
+                for z, y, x, core in (place, target(place))
+            )
+        )
     return lax.ppermute(array, AXES, pairs)
 
 
@@ -977,47 +1072,87 @@
     return add_up(*terms).astype(jnp.bfloat16)
 
 
-def scatter_stage(stage, parts, items, place):
+def scatter_stages(place, direct):
     depth = grid_sizes()[0]
     z, core = (place[0], place[3])
-    if stage == 0:
+    low, high = (z % 2, z // 2)
+
+    def across(items):
         to_core, *rest = items
         return rest + [hop(to_core, ACROSS)]
-    if stage == 1:
+
+    def far(items):
         to_far, to_near, own, from_core = items
         return [to_near, own, from_core, hop(low_add(to_far, from_core[1]), FAR)]
-    if stage == 2:
+
+    def near(items):
         to_near, own, from_core, from_far = items
         from_near = hop(low_add(to_near, from_core[0, 1], from_far[1]), NEAR)
         return [add_up(own, from_core[0, 0], from_far[0]), from_near]
-    if stage == 3:
+
+    def pick(array, at):
+        return lax.dynamic_index_in_dim(array, at, 0, False)
+
+    def along(items):
         summed = lax.optimization_barrier(add_up(*items))
-        sent = [lax.dynamic_index_in_dim(summed, lax.rem(z + step, depth), 0, False) for step in range(1, depth)]
-        along = [hop(item.astype(jnp.bfloat16), ALONG_Z, step + 1) for step, item in enumerate(sent)]
-        return [lax.dynamic_index_in_dim(summed, z, 0, False)] + along
-    total = add_up(*items)
-    keep = lax.dynamic_index_in_dim(total, core, 0, False)
-    other = hop(lax.dynamic_index_in_dim(total, 1 - core, 0, False), ACROSS)
-    return in_order(keep, other, core).reshape(-1, WIDTH)
-
-
-SCATTER_STAGES = 5
-
-
-def pipelined_scatter(groups, place, state, steps):
-    count = len(groups)
-    held = [None] * count
-    for tick in range(count + SCATTER_STAGES):
-        live = [index for index in range(tick - SCATTER_STAGES, tick) if 0 <= index < count]
-        if tick <= count:
-            items, state = together([held[index] for index in live], state)
-            for index, item in zip(live, items):
-                held[index] = item
-        for index in live:
-            held[index] = scatter_stage(tick - 1 - index, groups[index], held[index], place)
+        sent = [pick(summed, lax.rem(z + step, depth)) for step in range(1, depth)]
+        got = [hop(item.astype(jnp.bfloat16), ALONG_Z, step + 1) for step, item in enumerate(sent)]
+        return [pick(summed, z)] + got
+
+    def pairs(items):
+        summed = lax.optimization_barrier(add_up(*items))
+        summed = summed.reshape(2, 2, *summed.shape[1:])
+        return [pick(summed, high), hop(pick(summed, 1 - high).astype(jnp.bfloat16), ALONG_Z, swap=2)]
+
+    def neighbours(items):
+        summed = add_up(*items)
+        return [pick(summed, low), hop(pick(summed, 1 - low).astype(jnp.bfloat16), ALONG_Z, swap=1)]
+
+    def finish(items):
+        total = add_up(*items)
+        other = hop(pick(total, 1 - core), ACROSS)
+        return in_order(pick(total, core), other, core).reshape(-1, WIDTH)
+
+    return [across, far, near] + ([along] if direct else [pairs, neighbours]) + [finish]
+
+
+def share_stages(part, place):
+    low, high = (place[0] % 2, place[0] // 2)
+
+    def along(item):
+        one, two, three = [hop(item, ALONG_Z, swap=bits) for bits in (1, 2, 3)]
+        both = in_order(in_order(item, one, low), in_order(two, three, low), high)
+        return both.reshape(-1, *both.shape[2:])
+
+    return [
+        lambda item: start_gather([[part]], [[item]], place)[0],
+        along,
+        lambda item: jnp.stack([item, hop(item, NEAR)]),
+        lambda item: [item, hop(item, FAR), hop(item, ACROSS)],
+        lambda items: items + [hop(items[1], ACROSS)],
+    ]
+
+
+def pipelined_scatter(count, place, state, steps, shared):
+    held, todo = ([], [])
+    part, piece, more = shared
+    share = share_stages(part, place)
+    for tick in range(count + 5):
+        live = [index for index in range(len(held)) if todo[index]]
+        items, state, piece = together([held[index] for index in live], state, piece)
+        for index, item in zip(live, items):
+            held[index] = item
+            for _ in range(2 if index == tick - 1 else 1):
+                held[index] = todo[index].pop(0)(held[index])
+        if share:
+            piece = share.pop(0)(piece)
+        elif more:
+            piece = more.pop(0)(piece, held)
         if tick < count:
-            held[tick], state = steps[tick](state)
-    return (held, state)
+            dealt, state = steps[tick](state)
+            held.append(dealt)
+            todo.append(scatter_stages(place, tick >= count - 2))
+    return (held, piece, state)
 
 
 CQL_WEIGHT = 0.05
@@ -1192,7 +1327,7 @@
     top_cuts, block_cuts = cuts
     top_ins, block_ins, refs = (refs[:3], refs[3:6], refs[6:])
     norms, *refs = refs
-    top_outs, block_outs = (refs[:3], refs[3:])
+    top_outs, block_outs = (refs[:2], refs[2:])
     norm = jnp.sqrt(sums[...])
     norms[...] = norm
     ratio = LEARNING_RATE * (norm[0:1] / (norm[1:2] + 1e-06))
@@ -1200,11 +1335,12 @@
 
     def work(lanes, ins, outs, scale):
         param, direction, average = [ref[:, lanes] for ref in ins]
-        updated, half, averaged = outs
+        updated, averaged, *half = outs
         value = param - scale * direction
         updated[:, lanes] = value
-        half[:, lanes] = value.astype(jnp.bfloat16)
         averaged[:, lanes] = decay * average + (1.0 - decay) * value
+        for ref in half:
+            ref[:, lanes] = value.astype(jnp.bfloat16)
 
     def run(cuts, ins, outs, scales):
         for start, size, segments in stretches(cuts):
@@ -1229,14 +1365,13 @@
 
 
 def update(cuts, sums, top_ins, block_ins):
-    shapes = []
-    for array in (top_ins[0], block_ins[0]):
-        shapes += [f32(*array.shape), bf16(*array.shape), f32(*array.shape)]
+    shapes = [f32(*array.shape) for array in [top_ins[0]] * 2 + [block_ins[0]] * 2]
+    shapes.append(bf16(*block_ins[0].shape))
     return pl.pallas_call(
         functools.partial(update_kernel, cuts),
         out_shape=[f32(8, ROWS)] + shapes,
         in_specs=in_vmem(7),
-        out_specs=in_vmem(7),
+        out_specs=in_vmem(6),
         compiler_params=pltpu.CompilerParams(vmem_limit_bytes=VMEM_LIMIT),
         cost_estimate=LIGHT,
         name="update",
@@ -1306,10 +1441,9 @@
 def total(array):
     if lax.axis_size("wide") != 8 or lax.axis_size("narrow") != 4:
         return lax.psum(array, AXES)
-    array = array + hop(array, ACROSS)
-    array = array + hop(array, (2, 2))
-    array = array + hop(array, (1, 1))
-    one, two, three = [hop(array, ALONG_Z, step) for step in (1, 2, 3)]
+    array = array + flip(array, 0, 0, 0, 1)
+    array = (array + flip(array, 0, 0, 1, 0)) + (flip(array, 0, 1, 0, 0) + flip(array, 0, 1, 1, 0))
+    one, two, three = [flip(array, bits, 0, 0, 0) for bits in (1, 2, 3)]
     return (array + two) + (one + three)
 
 
@@ -1385,9 +1519,6 @@
     def block_weight(index, name):
         return merged(full["online", name, index]).reshape(-1, BOT)
 
-    def top_weights(net):
-        return (full[net, "pool"][0], full[net, "proj"][0], full[net, "heads"])
-
     def hold(net, index, group, buffers, state):
         full["held", index] = (group, buffers)
         return state
@@ -1398,15 +1529,20 @@
         gains = gains.transpose(1, 0, 2).reshape(2 * BLOCKS, -1).astype(jnp.float32)
         return run_block("target", 0, group, buffers, state | {"gains": gains})
 
-    def keep_ends(net, group, buffers, state):
-        arrays = assemble(group_parts(group), buffers, place) if tuned else buffers
-        full.update(zip(keys[group], arrays))
-        if net == "target":
-            for index in range(1, BLOCKS):
-                state = run_block(net, index, *full["held", index], state)
-            stream = state.pop("stream")
-            state |= {"target": head_target(stream, *top_weights(net), whole, real)}
-        return state
+    def target_ends(group, buffers, state):
+        for index in range(1, BLOCKS):
+            state = run_block("target", index, *full["held", index], state)
+        target = head_target(
+            state.pop("stream"), whole, real, group_parts(group), buffers, tuned, place
+        )
+        return state | {"target": target}
+
+    def online_ends(group, buffers, state):
+        loss, dstream, dpool, acts = head_loss(
+            state.pop("stream"), state.pop("target"), whole, legal, frames_all,
+            group_parts(group), buffers, tuned, place,
+        )
+        return state | {"loss": loss, "grad": dstream, "pool": dpool, "acts": acts}
 
     def run_block(net, index, group, buffers, state):
         keep = net == "online"
@@ -1439,11 +1575,11 @@
     for index in range(1, BLOCKS):
         add_group(block_keys("target", index), hold, "target", index)
     add_group([("gains",), ("target", "patch")] + block_keys("target", 0), read_gains)
-    add_group([("target", name) for name in ends], keep_ends, "target")
+    add_group([("target", name) for name in ends], target_ends)
     for index in range(BLOCKS):
         start = [] if index else [("online", "patch")]
         add_group(start + block_keys("online", index), run_block, "online", index)
-    add_group([("online", name) for name in ends], keep_ends, "online")
+    add_group([("online", name) for name in ends], online_ends)
 
     def group_parts(group):
         return [part_of(key) for key in keys[group]]
@@ -1462,13 +1598,6 @@
     keys = []
     steps = []
 
-    def loss_step(group, state):
-        (loss, dstream), dealt = head_loss(
-            state.pop("stream"), *top_weights("online"), state.pop("target"), whole, legal, frames_all,
-            group, tuned, place,
-        )
-        return (dealt, state | {"loss": loss, "grad": dstream})
-
     def out_inputs(index, state):
         stream, hid_one, hid_two, hid_three, rstd = state["kept%d" % index]
         gain = state["gains"][BLOCKS + index : BLOCKS + index + 1]
@@ -1476,7 +1605,7 @@
 
     def out_step(index, group, state):
         (dres, low, late), dealt = back_out(
-            state["grad"], *out_inputs(index, state), group, tuned, place
+            state.pop("grad"), *out_inputs(index, state), state.pop("pool"), group, tuned, place
         )
         return (dealt, state | {"grad": dres, "low": low, "late%d" % index: late})
 
@@ -1517,22 +1646,31 @@
             lambda state: run(*names, [parts[key[0]] for key in group], dict(state))
         )
 
-    add_step([("heads",), ("proj",), ("pool",)], loss_step)
-    add_step([("w_out", BLOCKS - 1)], out_step, BLOCKS - 1)
+    loss_part, acts = (state.pop("loss"), state.pop("acts"))
+    add_step([("w_out", BLOCKS - 1), ("pool",)], out_step, BLOCKS - 1)
     for index in reversed(range(BLOCKS)):
         add_step([("w_mid", index)], mid_step, index)
         if index:
             add_step([("w_in", index), ("w_out", index - 1)], between_step, index)
     add_step([("w_in", 0), ("patch",), ("gains",)], first_step)
+    def read_heads(buffers, rows):
+        return own_heads(buffers, parts["heads"], parts["proj"], tuned, place)
+
+    def read_late(pair, rows):
+        pool = parts["pool"]
+        first = parts["w_out"].travel
+        return flat_late(pool.unpack(rows[0][first : first + pool.travel]), pair[1], pair[0])[None]
+
     groups = [[parts[key[0]] for key in group] for group in keys]
     if tuned:
-        mine, state = pipelined_scatter(groups, place, state, steps)
+        shared = (Part(1, ACTS, WIDTH), acts[None], [read_heads, read_late])
+        mine, late, state = pipelined_scatter(len(groups), place, state, steps, shared)
     else:
         mine = []
         for group, step in zip(groups, steps):
             arrays, state = step(state)
             mine.append(pack(group, [plain_scatter(array) for array in arrays]))
-    loss_part = state["loss"]
+        late = read_late(read_heads([plain_gather(acts[None])], mine), mine)
     at = {}
     moves = []
     for number, group in enumerate(keys):
@@ -1548,15 +1686,10 @@
                 steps.append((None, patch_rows(count, first)))
             first += count
         moves.append(steps)
-    late = []
-    for name in ("pool", "proj", "heads"):
-        number, first = at[name,]
-        late.append(parts[name].unpack(mine[number][first : first + parts[name].travel]))
-    late = flat_late(*late)[None]
     cuts = (top_cuts, block_cuts)
     tops = [array[None] for array in (params_top, first_top, second_top, average_top)]
     sums, *made = directions(
-        cuts, mine[1:], moves[1:], (at["gains",][0] - 1, at["gains",][1]), late, loss_part,
+        cuts, mine, moves, at["gains",], late, loss_part,
         tops[:3], [params_blocks, first_blocks, second_blocks],
     )
     momentum_top, variance_top, direction_top, momentum_blocks, variance_blocks, direction_blocks = made
@@ -1565,7 +1698,7 @@
         cuts, sums, [tops[0], direction_top, tops[3]],
         [params_blocks, direction_blocks, average_blocks],
     )
-    updated_top, half_top, averaged_top, updated_blocks, half_blocks, averaged_blocks = made
+    updated_top, averaged_top, updated_blocks, averaged_blocks, half_blocks = made
     loss_total = sums[2, 0]
     matrix_norms = norms[:2, : len(top_cuts) + BLOCKS * len(block_cuts)]
     number, first = at["gains",]
@@ -1574,7 +1707,7 @@
         loss_total,
         matrix_norms,
         updated_top[0],
-        half_top[0],
+        updated_top[0].astype(jnp.bfloat16),
         momentum_top[0],
         variance_top[0],
         averaged_top[0],

time: 628 us -> 610 us (0.971)
  Pallas kernels: 193 us -> 180 us
  starting transfers between devices: 89.7 us -> 77.3 us
    pallas_call x1 -> x3, Pallas kernels: 6.89 us -> 22.9 us  [the longest x1 12.1 us: head_loss(): pl.pallas_call(functools.partial(loss_kernel, rows // ROWS, frames_all, p...]
    pallas_call x6 -> x5, Pallas kernels: 82.6 us -> 67.4 us  [back_call(): pl.pallas_call(functools.partial(back_kernel, body, parts, tuned, counts)...]
    pallas_call x3 -> x1, Pallas kernels: 15.9 us -> 2.61 us  [assemble(): pl.pallas_call(functools.partial(assemble_kernel, parts, some), out_shape...]
    ppermute x83 -> x82, starting transfers between devices: 89.7 us -> 77.3 us  [send(): return lax.ppermute(array, AXES, pairs)]
    ppermute x83 -> x82, waiting for transfers between devices: 225 us -> 228 us  [send(): return lax.ppermute(array, AXES, pairs)]
    another operation x44 -> x47, other arithmetic: 13.7 us -> 12.2 us  [in_order(): return jnp.stack([first, second])]
    convert_element_type x12 -> x10, other arithmetic: 22.9 us -> 23.3 us  [low_add(): return add_up(*terms).astype(jnp.bfloat16)]
  transfers between devices with their start and end apart: 83 -> 82, of which waited for: 36 -> 34; matrix products, arithmetic and copies ran while one was open for 14% -> 14% of each run, Pallas kernels for 24% -> 25%
where the time goes in v6:
time: 610 us; the launch traced here: 606 us
  waiting for transfers between devices  228 us (37%)
  Pallas kernels  180 us (30%)
  starting transfers between devices  77.3 us (13%)
  other arithmetic  69.3 us (11%)
  local copies, waits for them, and re-layouts  49.3 us (8%)
    ppermute x82, waiting for transfers between devices, send(): return lax.ppermute(array, AXES, pairs)  228 us
    ppermute x82, starting transfers between devices, send(): return lax.ppermute(array, AXES, pairs)  77.3 us
    pallas_call x4, Pallas kernels, block_forward(): pl.pallas_call(functools.partial(forward_kernel, count, keep, parts, skip...  69.2 us
    pallas_call x5, Pallas kernels, back_call(): pl.pallas_call(functools.partial(back_kernel, body, parts, tuned, counts)...  67.4 us
    convert_element_type x10, other arithmetic, low_add(): return add_up(*terms).astype(jnp.bfloat16)  23.3 us
    another operation x47, other arithmetic, in_order(): return jnp.stack([first, second])  12.2 us
  transfers between devices with their start and end apart: 82, of which 34 were waited for; matrix products, arithmetic and copies ran while one was open for 14% of the time, Pallas kernels for 25%

profile of v6, /device:TPU:0, one launch (start us, length us, event | category | flops | bytes accessed | tf_op | source)
XLA Modules:
  0.0 606.2 jit_solution(10660996937372275965)
XLA Ops:
  6.3 3.0 collective-permute-start.1
  10.7 5.9 collective-permute-done.1
  22.5 2.8 collective-permute-start.4
  30.8 20.2 %collective-permute-done.4 = bf16[2,2,144,512]{3,2,1,0:T(8,128)(2,1)S(1)} collective-permute-done((bf16[2,2,144,512]{3,2,1,0:T(8,128)(2,1)S(1)}, bf16[2,2,144,512]{3,2,1,0:T(8,128)(2,1)S(1)}, u32[]{:S(2)}, u32[]{:S(2)}) %collective-permute-start.4) | collective-permute-done | bytes 589856 | tf_op jit(solution)/shard_map/ppermute | solution.py:796
  52.3 7.9 %collective-permute-done.3 = bf16[2,160,512]{2,1,0:T(8,128)(2,1)S(1)} collective-permute-done((bf16[2,160,512]{2,1,0:T(8,128)(2,1)S(1)}, bf16[2,160,512]{2,1,0:T(8,128)(2,1)S(1)}, u32[]{:S(2)}, u32[]{:S(2)}) %collective-permute-start.3) | collective-permute-done | bytes 327712 | tf_op jit(solution)/shard_map/ppermute | solution.py:796
  60.3 3.1 collective-permute-start.6
  66.8 25.2 %collective-permute-done.6 = bf16[2,2,160,512]{3,2,1,0:T(8,128)(2,1)S(1)} collective-permute-done((bf16[2,2,160,512]{3,2,1,0:T(8,128)(2,1)S(1)}, bf16[2,2,160,512]{3,2,1,0:T(8,128)(2,1)S(1)}, u32[]{:S(2)}, u32[]{:S(2)}) %collective-permute-start.6) | collective-permute-done | bytes 655392 | tf_op jit(solution)/shard_map/ppermute | solution.py:796
  92.2 9.4 %collective-permute-done.5 = bf16[2,528,512]{2,1,0:T(8,128)(2,1)S(1)} collective-permute-done((bf16[2,528,512]{2,1,0:T(8,128)(2,1)S(1)}, bf16[2,528,512]{2,1,0:T(8,128)(2,1)S(1)}, u32[]{:S(2)}, u32[]{:S(2)}) %collective-permute-start.5) | collective-permute-done | bytes 1081376 | tf_op jit(solution)/shard_map/ppermute | solution.py:796
  106.7 21.4 %collective-permute-done.8 = bf16[2,2,112,512]{3,2,1,0:T(8,128)(2,1)S(1)} collective-permute-done((bf16[2,2,112,512]{3,2,1,0:T(8,128)(2,1)S(1)}, bf16[2,2,112,512]{3,2,1,0:T(8,128)(2,1)S(1)}, u32[]{:S(2)}, u32[]{:S(2)}) %collective-permute-start.8) | collective-permute-done | bytes 458784 | tf_op jit(solution)/shard_map/ppermute | solution.py:796
  128.3 7.7 %collective-permute-done.9 = bf16[4,2,160,512]{3,2,1,0:T(8,128)(2,1)S(1)} collective-permute-done((bf16[4,2,160,512]{3,2,1,0:T(8,128)(2,1)S(1)}, bf16[4,2,160,512]{3,2,1,0:T(8,128)(2,1)S(1)}, u32[]{:S(2)}, u32[]{:S(2)}) %collective-permute-start.9) | collective-permute-done | bytes 1310752 | tf_op jit(solution)/shard_map/ppermute | solution.py:796
  136.2 9.4 %collective-permute-done.10.refs_5_ = bf16[2,4,2,144,512]{4,3,2,1,0:T(8,128)(2,1)S(1)} collective-permute-done((bf16[2,4,2,144,512]{4,3,2,1,0:T(8,128)(2,1)S(1)}, bf16[2,4,2,144,512]{4,3,2,1,0:T(8,128)(2,1)S(1)}, u32[]{:S(2)}, u32[]{:S(2)}) %collective-permute-start.10) | collective-permute-done | bytes 2359328 | tf_op jit(solution)/shard_map/ppermute | solution.py:796
  150.6 29.5 %collective-permute-done.12 = bf16[2,2,160,512]{3,2,1,0:T(8,128)(2,1)S(1)} collective-permute-done((bf16[2,2,160,512]{3,2,1,0:T(8,128)(2,1)S(1)}, bf16[2,2,160,512]{3,2,1,0:T(8,128)(2,1)S(1)}, u32[]{:S(2)}, u32[]{:S(2)}) %collective-permute-start.12) | collective-permute-done | bytes 655392 | tf_op jit(solution)/shard_map/ppermute | solution.py:796
  183.0 4.3 collective-permute-done.14.refs_1_.refs_6_
  207.4 2.6 assemble.1
  211.7 16.5 %block_forward.4.refs_1_ = f32[384,2048]{1,0:T(8,128)} custom-call(s32[5]{0:T(128)} %stack.339.place.refs_0_, bf16[384,256]{1,0:T(8,128)(2,1)} %bitcast.433, bf16[2,256,512]{2,1,0:T(8,128)(2,1)} %add_convert_fusion.refs_2_.refs_6_, f32[1,6144]{1,0:T(1,128)} %slice.257.refs_3_, bf16[1152,128]{1,0:T(8,128)(2,1)} %convert_element_type.407.refs_4_.refs_3_.refs_6_, ...), custom_call_target="tpu_custom_call" | custom-call | flops 1024 | bytes 1024 | tf_op jit(solution)/shard_map/block_forward/pallas_call | solution.py:248
  239.3 15.8 %block_forward.5.stream = f32[384,2048]{1,0:T(8,128)} custom-call(s32[5]{0:T(128)} %stack.339.place.refs_0_, f32[384,2048]{1,0:T(8,128)} %block_forward.4.refs_1_, f32[1,6144]{1,0:T(1,128)} %slice.258.refs_2_, bf16[1152,128]{1,0:T(8,128)(2,1)} %convert_element_type.407.refs_4_.refs_3_.refs_6_, bf16[2,4,2,144,512]{4,3,2,1,0:T(8,128)(2,1)} %copy-done.5, ...), custom_call_target="tpu_custom_call" | custom-call | flops 1024 | bytes 1024 | tf_op jit(solution)/shard_map/block_forward/pallas_call | solution.py:248
  255.1 6.7 %head_target.1.target = f32[8,128]{1,0:T(8,128)} custom-call(s32[5]{0:T(128)} %stack.339.place.refs_0_, f32[384,2048]{1,0:T(8,128)} %block_forward.5.stream, s32[8,128]{1,0:T(8,128)} %pad.72.whole, f32[8,128]{1,0:T(8,128)} %select_maximum_fusion.real, bf16[2,4,2,112,512]{4,3,2,1,0:T(8,128)(2,1)} %pad_maximum_fusion.4.refs_0_, ...), custom_call_target="tpu_custom_call" | custom-call | flops 1024 | bytes 1024 | tf_op jit(solution)/shard_map/head_target/pallas_call | solution.py:598
  264.2 3.2 pad_maximum_fusion.3.refs_4_
  267.4 9.7 %collective-permute-done.25.refs_6_ = bf16[2,4,2,160,512]{4,3,2,1,0:T(8,128)(2,1)} collective-permute-done((bf16[2,4,2,160,512]{4,3,2,1,0:T(8,128)(2,1)S(1)}, bf16[2,4,2,160,512]{4,3,2,1,0:T(8,128)(2,1)}, u32[]{:S(2)}, u32[]{:S(2)}) %collective-permute-start.25) | collective-permute-done | bytes 2621472 | tf_op jit(solution)/shard_map/ppermute | solution.py:796
  283.8 19.4 %block_forward.6 = (f32[384,2048]{1,0:T(8,128)}, f32[384,2048]{1,0:T(8,128)}, f32[384,512]{1,0:T(8,128)}, f32[384,512]{1,0:T(8,128)}, f32[384,2048]{1,0:T(8,128)...) custom-call(s32[5]{0:T(128)} %stack.339.place.refs_0_, ...), custom_call_target="tpu_custom_call" | custom-call | flops 1024 | bytes 1024 | tf_op jit(solution)/shard_map/block_forward/pallas_call | solution.py:248
  304.5 11.5 %collective-permute-done.29.refs_5_ = bf16[2,4,2,144,512]{4,3,2,1,0:T(8,128)(2,1)} collective-permute-done((bf16[2,4,2,144,512]{4,3,2,1,0:T(8,128)(2,1)}, bf16[2,4,2,144,512]{4,3,2,1,0:T(8,128)(2,1)}, u32[]{:S(2)}, u32[]{:S(2)}) %collective-permute-start.29) | collective-permute-done | bytes 2359328 | tf_op jit(solution)/shard_map/ppermute | solution.py:796
  320.9 17.5 %block_forward.7 = (f32[384,2048]{1,0:T(8,128)}, f32[384,512]{1,0:T(8,128)}, f32[384,512]{1,0:T(8,128)}, f32[384,2048]{1,0:T(8,128)}, f32[8,3072]{1,0:T(8,128)},...) custom-call(s32[5]{0:T(128)} %stack.339.place.refs_0_, ...), custom_call_target="tpu_custom_call" | custom-call | flops 1024 | bytes 1024 | tf_op jit(solution)/shard_map/block_forward/pallas_call | solution.py:248
  339.9 3.2 collective-permute-done.34.refs_3_
  343.2 12.1 %head_loss.1 = (f32[1,1]{1,0:T(1,128)}, f32[384,2048]{1,0:T(8,128)}, bf16[1,2048,128]{2,1,0:T(8,128)(2,1)}, bf16[64,512]{1,0:T(8,128)(2,1)}) custom-call(s32[5]{0:T(128)} %stack.339.place.refs_0_, f32[384,2048]{1,0:T(8,128)} %get-tuple-element.508.stream, f32[8,128]{1,0:T(8,128)} %head_target.1.target, s32[8,128]{1,0:T(8,128)} %pad.72.whole, ...), custom_call_target="tpu_custom_call" | custom-call | flops 1024 | bytes 1024 | tf_op jit(solution)/shard_map/head_loss/pallas_call | solution.py:690
  356.9 14.9 %back_out.1 = (f32[384,2048]{1,0:T(8,128)}, bf16[384,512]{1,0:T(8,128)(2,1)}, f32[1,5120]{1,0:T(1,128)}, bf16[2,2,4,2,48,512]{5,4,3,2,1,0:T(8,128)(2,1)}, bf16[2...) custom-call(s32[5]{0:T(128)} %stack.339.place.refs_0_, ...), custom_call_target="tpu_custom_call" | custom-call | flops 1024 | bytes 1024 | tf_op jit(solution)/shard_map/back_out/pallas_call | solution.py:414
  372.3 3.3 collective-permute-done.36
  382.7 12.2 %back_mid.2 = (bf16[384,512]{1,0:T(8,128)(2,1)}, f32[1,1024]{1,0:T(1,128)}, bf16[2,2,4,2,80,512]{5,4,3,2,1,0:T(8,128)(2,1)}, bf16[2,4,2,80,512]{4,3,2,1,0:T(8,12...) custom-call(s32[5]{0:T(128)} %stack.339.place.refs_0_, ...), custom_call_target="tpu_custom_call" | custom-call | flops 1024 | bytes 1024 | tf_op jit(solution)/shard_map/back_mid/pallas_call | solution.py:414
  395.2 5.1 collective-permute-done.42
  407.3 19.1 %back_between.1 = (f32[384,2048]{1,0:T(8,128)}, bf16[384,512]{1,0:T(8,128)(2,1)}, f32[1,5120]{1,0:T(1,128)}, bf16[2,2,4,2,64,512]{5,4,3,2,1,0:T(8,128)(2,1)}, bf...) custom-call(s32[5]{0:T(128)} %stack.339.place.refs_0_, ...), custom_call_target="tpu_custom_call" | custom-call | flops 1024 | bytes 1024 | tf_op jit(solution)/shard_map/back_between/pallas_call | solution.py:414
  427.4 4.4 collective-permute-done.47
  434.6 2.9 fusion.6
  442.2 12.3 %back_mid.3 = (bf16[384,512]{1,0:T(8,128)(2,1)}, f32[1,1024]{1,0:T(1,128)}, bf16[2,2,4,2,80,512]{5,4,3,2,1,0:T(8,128)(2,1)}, bf16[2,4,2,80,512]{4,3,2,1,0:T(8,12...) custom-call(s32[5]{0:T(128)} %stack.339.place.refs_0_, ...), custom_call_target="tpu_custom_call" | custom-call | flops 1024 | bytes 1024 | tf_op jit(solution)/shard_map/back_mid/pallas_call | solution.py:414
  454.5 6.7 %collective-permute-done.49.refs_1_ = bf16[2,4,2,32,512]{4,3,2,1,0:T(8,128)(2,1)} collective-permute-done((bf16[2,4,2,32,512]{4,3,2,1,0:T(8,128)(2,1)}, bf16[2,4,2,32,512]{4,3,2,1,0:T(8,128)(2,1)}, u32[]{:S(2)}, u32[]{:S(2)}) %collective-permute-start.49) | collective-permute-done | bytes 524320 | tf_op jit(solution)/shard_map/ppermute | solution.py:796
  463.2 3.4 collective-permute-done.54
  466.6 3.2 fusion
  480.6 8.9 %back_first.1 = (bf16[2,2,4,2,64,512]{5,4,3,2,1,0:T(8,128)(2,1)}, bf16[2,4,2,64,512]{4,3,2,1,0:T(8,128)(2,1)}, bf16[4,2,64,512]{3,2,1,0:T(8,128)(2,1)}, bf16[4,2,64,512]{3,2,1,0:T(8,128)(2,1)}) custom-call(s32[5]{0:T(128)} %stack.339.place.refs_0_, bf16[384,512]{1,0:T(8,128)(2,1)} %get-tuple-element.645.refs_1_, ...), custom_call_target="tpu_custom_call" | custom-call | flops 1024 | bytes 1024 | tf_op jit(solution)/shard_map/back_first/pallas_call | solution.py:414
  491.1 3.5 collective-permute-done.52
  494.8 3.4 fusion.5
  503.2 2.7 collective-permute-start.58
  509.5 4.0 own_heads.1
  515.6 7.9 %collective-permute-done.62 = bf16[2,4,2,64,512]{4,3,2,1,0:T(8,128)(2,1)} collective-permute-done((bf16[2,4,2,64,512]{4,3,2,1,0:T(8,128)(2,1)}, bf16[2,4,2,64,512]{4,3,2,1,0:T(8,128)(2,1)}, u32[]{:S(2)}, u32[]{:S(2)}) %collective-permute-start.62) | collective-permute-done | bytes 1048608 | tf_op jit(solution)/shard_map/ppermute | solution.py:796
  523.6 2.9 fusion.7
  536.2 4.8 concatenate.90
  543.4 6.5 %collective-permute-done.64 = bf16[2,64,512]{2,1,0:T(8,128)(2,1)S(1)} collective-permute-done((bf16[2,64,512]{2,1,0:T(8,128)(2,1)}, bf16[2,64,512]{2,1,0:T(8,128)(2,1)S(1)}, u32[]{:S(2)}, u32[]{:S(2)}) %collective-permute-start.64) | collective-permute-done | bytes 131104 | tf_op jit(solution)/shard_map/ppermute | solution.py:796
  551.6 3.0 collective-permute-start.72
  558.5 4.9 collective-permute-done.72
  565.9 10.9 %directions.1 = (f32[8,128]{1,0:T(8,128)}, f32[1,115648]{1,0:T(1,128)}, f32[1,115648]{1,0:T(1,128)}, f32[1,115648]{1,0:T(1,128)}, f32[2,139456]{1,0:T(2,128)}, /*index=5*/f32[2,139456]{1,0:T(2,128)}, f32[2,139456]{1,0:T(2,128)}) custom-call(f32[96,512]{1,0:T(8,128)} %bitcast.431, f32[160,512]{1,0:T(8,128)} %bitcast.420, f32[128,512]{1,0:T(8,128)} %bitcast.426, ...), custom_call_target="tpu_custom_call" | custom-call | flops 1024 | bytes 1024 | tf_op jit(solution)/shard_map/directions/pallas_call | solution.py:1311
  596.0 7.1 %update.1 = (f32[8,128]{1,0:T(8,128)}, f32[1,115648]{1,0:T(1,128)}, f32[1,115648]{1,0:T(1,128)}, f32[2,139456]{1,0:T(2,128)}, f32[2,139456]{1,0:T(2,128)}, /*index=5*/bf16[2,139456]{1,0:T(2,128)(2,1)}) custom-call(f32[8,128]{1,0:T(8,128)} %copy-done.51, f32[1,115648]{1,0:T(1,128)} %bitcast.401, f32[1,115648]{1,0:T(1,128)} %get-tuple-element.709.refs_1_, ...), custom_call_target="tpu_custom_call" | custom-call | flops 1024 | bytes 1024 | tf_op jit(solution)/shard_map/update/pallas_call | solution.py:1370
  (490 shorter events, 177.2 us)
Async XLA Ops:
  22.5 28.5 %collective-permute-start.4 = (bf16[2,2,144,512]{3,2,1,0:T(8,128)(2,1)S(1)}, bf16[2,2,144,512]{3,2,1,0:T(8,128)(2,1)S(1)}, u32[]{:S(2)}, u32[]{:S(2)}) collective-permute-start(bf16[2,2,144,512]{3,2,1,0:T(8,128)(2,1)S(1)} %pad_maximum_fusion.15), channel_id=1, source_target_pairs={{0,16},{1,17},{2,18},{3,19},{4,20},{5,21},{6,22},{7,23},{8,24},{9,... | collective-permute-start | bytes 1769480 | tf_op jit(solution)/shard_map/ppermute | solution.py:796
  30.8 20.4 %collective-permute-start.2 = (bf16[688,512]{1,0:T(8,128)(2,1)}, bf16[688,512]{1,0:T(8,128)(2,1)S(1)}, u32[]{:S(2)}, u32[]{:S(2)}) collective-permute-start(bf16[688,512]{1,0:T(8,128)(2,1)} %dynamic-slice_dynamic-update-slice_fusion.3), channel_id=1, source_target_pairs={{0,1},{1,0},{2,3},{3,2},{4,5},{5,4},{6,7},{7,6},{8,9},{9,8},{10,11... | collective-permute-start | bytes 2113544 | tf_op jit(solution)/shard_map/ppermute | solution.py:796
  60.3 31.7 %collective-permute-start.6 = (bf16[2,2,160,512]{3,2,1,0:T(8,128)(2,1)S(1)}, bf16[2,2,160,512]{3,2,1,0:T(8,128)(2,1)S(1)}, u32[]{:S(2)}, u32[]{:S(2)}) collective-permute-start(bf16[2,2,160,512]{3,2,1,0:T(8,128)(2,1)S(1)} %pad_maximum_fusion.13), channel_id=1, source_target_pairs={{0,16},{1,17},{2,18},{3,19},{4,20},{5,21},{6,22},{7,23},{8,24},{9,... | collective-permute-start | bytes 1966088 | tf_op jit(solution)/shard_map/ppermute | solution.py:796
  63.5 38.1 %collective-permute-start.5 = (bf16[2,528,512]{2,1,0:T(8,128)(2,1)S(1)}, bf16[2,528,512]{2,1,0:T(8,128)(2,1)S(1)}, u32[]{:S(2)}, u32[]{:S(2)}) collective-permute-start(bf16[2,528,512]{2,1,0:T(8,128)(2,1)S(1)} %pad_maximum_fusion.10), channel_id=1, source_target_pairs={{0,8},{1,9},{2,10},{3,11},{4,12},{5,13},{6,14},{7,15},{8,0},{9,1},... | collective-permute-start | bytes 3244040 | tf_op jit(solution)/shard_map/ppermute | solution.py:796
  65.3 37.1 %collective-permute-start.7 = (bf16[4,2,144,512]{3,2,1,0:T(8,128)(2,1)S(1)}, bf16[4,2,144,512]{3,2,1,0:T(8,128)(2,1)S(1)}, u32[]{:S(2)}, u32[]{:S(2)}) collective-permute-start(bf16[4,2,144,512]{3,2,1,0:T(8,128)(2,1)S(1)} %bitcast.398), channel_id=1, source_target_pairs={{0,2},{1,5},{2,0},{3,7},{4,6},{5,1},{6,4},{7,3},{8,10},{9,13},{10,... | collective-permute-start | bytes 3538952 | tf_op jit(solution)/shard_map/ppermute | solution.py:796
  102.7 43.0 %collective-permute-start.10 = (bf16[2,4,2,144,512]{4,3,2,1,0:T(8,128)(2,1)S(1)}, bf16[2,4,2,144,512]{4,3,2,1,0:T(8,128)(2,1)S(1)}, u32[]{:S(2)}, u32[]{:S(2)}) collective-permute-start(bf16[2,4,2,144,512]{4,3,2,1,0:T(8,128)(2,1)S(1)} %pad_maximum_fusion.2.refs_4_), channel_id=1, source_target_pairs={{0,4},{1,3},{2,6},{3,1},{4,0},{5,7},{6,2},{7,5},{8,12},{9,11},{10,... | collective-permute-start | bytes 7077896 | tf_op jit(solution)/shard_map/ppermute | solution.py:796
  104.3 41.4 %collective-permute-start.11 = (bf16[2,4,2,144,512]{4,3,2,1,0:T(8,128)(2,1)S(1)}, bf16[2,4,2,144,512]{4,3,2,1,0:T(8,128)(2,1)S(1)}, u32[]{:S(2)}, u32[]{:S(2)}) collective-permute-start(bf16[2,4,2,144,512]{4,3,2,1,0:T(8,128)(2,1)S(1)} %pad_maximum_fusion.2.refs_4_), channel_id=1, source_target_pairs={{0,1},{1,0},{2,3},{3,2},{4,5},{5,4},{6,7},{7,6},{8,9},{9,8},{10,11... | collective-permute-start | bytes 7077896 | tf_op jit(solution)/shard_map/ppermute | solution.py:796
  104.3 31.7 %collective-permute-start.9 = (bf16[4,2,160,512]{3,2,1,0:T(8,128)(2,1)S(1)}, bf16[4,2,160,512]{3,2,1,0:T(8,128)(2,1)S(1)}, u32[]{:S(2)}, u32[]{:S(2)}) collective-permute-start(bf16[4,2,160,512]{3,2,1,0:T(8,128)(2,1)S(1)} %bitcast.394), channel_id=1, source_target_pairs={{0,2},{1,5},{2,0},{3,7},{4,6},{5,1},{6,4},{7,3},{8,10},{9,13},{10,... | collective-permute-start | bytes 3932168 | tf_op jit(solution)/shard_map/ppermute | solution.py:796
  105.8 22.4 %collective-permute-start.8 = (bf16[2,2,112,512]{3,2,1,0:T(8,128)(2,1)S(1)}, bf16[2,2,112,512]{3,2,1,0:T(8,128)(2,1)S(1)}, u32[]{:S(2)}, u32[]{:S(2)}) collective-permute-start(bf16[2,2,112,512]{3,2,1,0:T(8,128)(2,1)S(1)} %pad_maximum_fusion.19), channel_id=1, source_target_pairs={{0,16},{1,17},{2,18},{3,19},{4,20},{5,21},{6,22},{7,23},{8,24},{9,... | collective-permute-start | bytes 1376264 | tf_op jit(solution)/shard_map/ppermute | solution.py:796
  145.6 41.6 %collective-permute-start.14 = (bf16[2,4,2,160,512]{4,3,2,1,0:T(8,128)(2,1)S(1)}, bf16[2,4,2,160,512]{4,3,2,1,0:T(8,128)(2,1)}, u32[]{:S(2)}, u32[]{:S(2)}) collective-permute-start(bf16[2,4,2,160,512]{4,3,2,1,0:T(8,128)(2,1)S(1)} %pad_maximum_fusion.refs_0_.refs_5_), channel_id=1, source_target_pairs={{0,4},{1,3},{2,6},{3,1},{4,0},{5,7},{6,2},{7,5},{8,12},{9,11},{10,... | collective-permute-start | bytes 7864328 | tf_op jit(solution)/shard_map/ppermute | solution.py:796
  147.2 40.1 %collective-permute-start.15 = (bf16[2,4,2,160,512]{4,3,2,1,0:T(8,128)(2,1)S(1)}, bf16[2,4,2,160,512]{4,3,2,1,0:T(8,128)(2,1)S(1)}, u32[]{:S(2)}, u32[]{:S(2)}) collective-permute-start(bf16[2,4,2,160,512]{4,3,2,1,0:T(8,128)(2,1)S(1)} %pad_maximum_fusion.refs_0_.refs_5_), channel_id=1, source_target_pairs={{0,1},{1,0},{2,3},{3,2},{4,5},{5,4},{6,7},{7,6},{8,9},{9,8},{10,11... | collective-permute-start | bytes 7864328 | tf_op jit(solution)/shard_map/ppermute | solution.py:796
  148.0 32.1 %collective-permute-start.12 = (bf16[2,2,160,512]{3,2,1,0:T(8,128)(2,1)S(1)}, bf16[2,2,160,512]{3,2,1,0:T(8,128)(2,1)S(1)}, u32[]{:S(2)}, u32[]{:S(2)}) collective-permute-start(bf16[2,2,160,512]{3,2,1,0:T(8,128)(2,1)S(1)} %pad_maximum_fusion.14), channel_id=1, source_target_pairs={{0,16},{1,17},{2,18},{3,19},{4,20},{5,21},{6,22},{7,23},{8,24},{9,... | collective-permute-start | bytes 1966088 | tf_op jit(solution)/shard_map/ppermute | solution.py:796
  148.9 32.6 %collective-permute-start.13 = (bf16[4,2,112,512]{3,2,1,0:T(8,128)(2,1)S(1)}, bf16[4,2,112,512]{3,2,1,0:T(8,128)(2,1)S(1)}, u32[]{:S(2)}, u32[]{:S(2)}) collective-permute-start(bf16[4,2,112,512]{3,2,1,0:T(8,128)(2,1)S(1)} %bitcast.404), channel_id=1, source_target_pairs={{0,2},{1,5},{2,0},{3,7},{4,6},{5,1},{6,4},{7,3},{8,10},{9,13},{10,... | collective-permute-start | bytes 2752520 | tf_op jit(solution)/shard_map/ppermute | solution.py:796
  188.8 17.1 %collective-permute-start.17 = (bf16[2,4,2,160,512]{4,3,2,1,0:T(8,128)(2,1)}, bf16[2,4,2,160,512]{4,3,2,1,0:T(8,128)(2,1)S(1)}, u32[]{:S(2)}, u32[]{:S(2)}) collective-permute-start(bf16[2,4,2,160,512]{4,3,2,1,0:T(8,128)(2,1)} %collective-permute-done.14.refs_1_.refs_6_), channel_id=1, source_target_pairs={{0,1},{1,0},{2,3},{3,2},{4,5},{5,4},{6,7},{7,6},{8,9},{9,8},{10,11... | collective-permute-start | bytes 7864328 | tf_op jit(solution)/shard_map/ppermute | solution.py:796
  193.1 35.2 %collective-permute-start.18 = (bf16[4,2,160,512]{3,2,1,0:T(8,128)(2,1)}, bf16[4,2,160,512]{3,2,1,0:T(8,128)(2,1)}, u32[]{:S(2)}, u32[]{:S(2)}) collective-permute-start(bf16[4,2,160,512]{3,2,1,0:T(8,128)(2,1)} %bitcast.66), channel_id=1, source_target_pairs={{0,2},{1,5},{2,0},{3,7},{4,6},{5,1},{6,4},{7,3},{8,10},{9,13},{10,... | collective-permute-start | bytes 3932168 | tf_op jit(solution)/shard_map/ppermute | solution.py:796
  195.3 37.4 %collective-permute-start.19 = (bf16[2,4,2,112,512]{4,3,2,1,0:T(8,128)(2,1)}, bf16[2,4,2,112,512]{4,3,2,1,0:T(8,128)(2,1)}, u32[]{:S(2)}, u32[]{:S(2)}) collective-permute-start(bf16[2,4,2,112,512]{4,3,2,1,0:T(8,128)(2,1)} %pad_maximum_fusion.4.refs_0_), channel_id=1, source_target_pairs={{0,4},{1,3},{2,6},{3,1},{4,0},{5,7},{6,2},{7,5},{8,12},{9,11},{10,... | collective-permute-start | bytes 5505032 | tf_op jit(solution)/shard_map/ppermute | solution.py:796
  196.8 35.9 %collective-permute-start.20 = (bf16[2,4,2,112,512]{4,3,2,1,0:T(8,128)(2,1)}, bf16[2,4,2,112,512]{4,3,2,1,0:T(8,128)(2,1)}, u32[]{:S(2)}, u32[]{:S(2)}) collective-permute-start(bf16[2,4,2,112,512]{4,3,2,1,0:T(8,128)(2,1)} %pad_maximum_fusion.4.refs_0_), channel_id=1, source_target_pairs={{0,1},{1,0},{2,3},{3,2},{4,5},{5,4},{6,7},{7,6},{8,9},{9,8},{10,11... | collective-permute-start | bytes 5505032 | tf_op jit(solution)/shard_map/ppermute | solution.py:796
  198.4 29.9 %collective-permute-start.16 = (bf16[2,2,144,512]{3,2,1,0:T(8,128)(2,1)S(1)}, bf16[2,2,144,512]{3,2,1,0:T(8,128)(2,1)}, u32[]{:S(2)}, u32[]{:S(2)}) collective-permute-start(bf16[2,2,144,512]{3,2,1,0:T(8,128)(2,1)S(1)} %pad_maximum_fusion.16), channel_id=1, source_target_pairs={{0,16},{1,17},{2,18},{3,19},{4,20},{5,21},{6,22},{7,23},{8,24},{9,... | collective-permute-start | bytes 1769480 | tf_op jit(solution)/shard_map/ppermute | solution.py:796
  205.9 28.9 %collective-permute-start.22 = (bf16[2,4,2,144,512]{4,3,2,1,0:T(8,128)(2,1)}, bf16[2,4,2,144,512]{4,3,2,1,0:T(8,128)(2,1)}, u32[]{:S(2)}, u32[]{:S(2)}) collective-permute-start(bf16[2,4,2,144,512]{4,3,2,1,0:T(8,128)(2,1)} %copy-done.16), channel_id=1, source_target_pairs={{0,1},{1,0},{2,3},{3,2},{4,5},{5,4},{6,7},{7,6},{8,9},{9,8},{10,11... | collective-permute-start | bytes 7077896 | tf_op jit(solution)/shard_map/ppermute | solution.py:796
  232.7 44.5 %collective-permute-start.25 = (bf16[2,4,2,160,512]{4,3,2,1,0:T(8,128)(2,1)S(1)}, bf16[2,4,2,160,512]{4,3,2,1,0:T(8,128)(2,1)}, u32[]{:S(2)}, u32[]{:S(2)}) collective-permute-start(bf16[2,4,2,160,512]{4,3,2,1,0:T(8,128)(2,1)S(1)} %pad_maximum_fusion.1.refs_5_), channel_id=1, source_target_pairs={{0,4},{1,3},{2,6},{3,1},{4,0},{5,7},{6,2},{7,5},{8,12},{9,11},{10,... | collective-permute-start | bytes 7864328 | tf_op jit(solution)/shard_map/ppermute | solution.py:796
  233.3 43.9 %collective-permute-start.26 = (bf16[2,4,2,160,512]{4,3,2,1,0:T(8,128)(2,1)S(1)}, bf16[2,4,2,160,512]{4,3,2,1,0:T(8,128)(2,1)}, u32[]{:S(2)}, u32[]{:S(2)}) collective-permute-start(bf16[2,4,2,160,512]{4,3,2,1,0:T(8,128)(2,1)S(1)} %pad_maximum_fusion.1.refs_5_), channel_id=1, source_target_pairs={{0,1},{1,0},{2,3},{3,2},{4,5},{5,4},{6,7},{7,6},{8,9},{9,8},{10,11... | collective-permute-start | bytes 7864328 | tf_op jit(solution)/shard_map/ppermute | solution.py:796
  233.3 21.8 %collective-permute-start.23 = (bf16[2,4,2,112,512]{4,3,2,1,0:T(8,128)(2,1)}, bf16[2,4,2,112,512]{4,3,2,1,0:T(8,128)(2,1)}, u32[]{:S(2)}, u32[]{:S(2)}) collective-permute-start(bf16[2,4,2,112,512]{4,3,2,1,0:T(8,128)(2,1)} %collective-permute-done.19.refs_1_), channel_id=1, source_target_pairs={{0,1},{1,0},{2,3},{3,2},{4,5},{5,4},{6,7},{7,6},{8,9},{9,8},{10,11... | collective-permute-start | bytes 5505032 | tf_op jit(solution)/shard_map/ppermute | solution.py:796
  233.8 29.2 %collective-permute-start.24 = (bf16[4,2,144,512]{3,2,1,0:T(8,128)(2,1)}, bf16[4,2,144,512]{3,2,1,0:T(8,128)(2,1)}, u32[]{:S(2)}, u32[]{:S(2)}) collective-permute-start(bf16[4,2,144,512]{3,2,1,0:T(8,128)(2,1)} %bitcast.73), channel_id=1, source_target_pairs={{0,2},{1,5},{2,0},{3,7},{4,6},{5,1},{6,4},{7,3},{8,10},{9,13},{10,... | collective-permute-start | bytes 3538952 | tf_op jit(solution)/shard_map/ppermute | solution.py:796
  234.8 27.1 %collective-permute-start.21 = (bf16[2,2,112,512]{3,2,1,0:T(8,128)(2,1)S(1)}, bf16[2,2,112,512]{3,2,1,0:T(8,128)(2,1)}, u32[]{:S(2)}, u32[]{:S(2)}) collective-permute-start(bf16[2,2,112,512]{3,2,1,0:T(8,128)(2,1)S(1)} %copy-done.21), channel_id=1, source_target_pairs={{0,16},{1,17},{2,18},{3,19},{4,20},{5,21},{6,22},{7,23},{8,24},{9,... | collective-permute-start | bytes 1376264 | tf_op jit(solution)/shard_map/ppermute | solution.py:796
  277.2 38.8 %collective-permute-start.29 = (bf16[2,4,2,144,512]{4,3,2,1,0:T(8,128)(2,1)}, bf16[2,4,2,144,512]{4,3,2,1,0:T(8,128)(2,1)}, u32[]{:S(2)}, u32[]{:S(2)}) collective-permute-start(bf16[2,4,2,144,512]{4,3,2,1,0:T(8,128)(2,1)} %pad_maximum_fusion.3.refs_4_), channel_id=1, source_target_pairs={{0,4},{1,3},{2,6},{3,1},{4,0},{5,7},{6,2},{7,5},{8,12},{9,11},{10,... | collective-permute-start | bytes 7077896 | tf_op jit(solution)/shard_map/ppermute | solution.py:796
  277.7 38.3 %collective-permute-start.30 = (bf16[2,4,2,144,512]{4,3,2,1,0:T(8,128)(2,1)}, bf16[2,4,2,144,512]{4,3,2,1,0:T(8,128)(2,1)}, u32[]{:S(2)}, u32[]{:S(2)}) collective-permute-start(bf16[2,4,2,144,512]{4,3,2,1,0:T(8,128)(2,1)} %pad_maximum_fusion.3.refs_4_), channel_id=1, source_target_pairs={{0,1},{1,0},{2,3},{3,2},{4,5},{5,4},{6,7},{7,6},{8,9},{9,8},{10,11... | collective-permute-start | bytes 7077896 | tf_op jit(solution)/shard_map/ppermute | solution.py:796
  278.0 25.2 %collective-permute-start.27 = (bf16[4,2,112,512]{3,2,1,0:T(8,128)(2,1)S(1)}, bf16[4,2,112,512]{3,2,1,0:T(8,128)(2,1)}, u32[]{:S(2)}, u32[]{:S(2)}) collective-permute-start(bf16[4,2,112,512]{3,2,1,0:T(8,128)(2,1)S(1)} %bitcast.406), channel_id=1, source_target_pairs={{0,2},{1,5},{2,0},{3,7},{4,6},{5,1},{6,4},{7,3},{8,10},{9,13},{10,... | collective-permute-start | bytes 2752520 | tf_op jit(solution)/shard_map/ppermute | solution.py:796
  316.0 23.2 %collective-permute-start.31 = (bf16[2,4,2,112,512]{4,3,2,1,0:T(8,128)(2,1)S(1)}, bf16[2,4,2,112,512]{4,3,2,1,0:T(8,128)(2,1)S(1)}, u32[]{:S(2)}, u32[]{:S(2)}) collective-permute-start(bf16[2,4,2,112,512]{4,3,2,1,0:T(8,128)(2,1)S(1)} %pad_maximum_fusion.5.refs_0_), channel_id=1, source_target_pairs={{0,4},{1,3},{2,6},{3,1},{4,0},{5,7},{6,2},{7,5},{8,12},{9,11},{10,... | collective-permute-start | bytes 5505032 | tf_op jit(solution)/shard_map/ppermute | solution.py:796
  316.7 22.6 %collective-permute-start.32 = (bf16[2,4,2,112,512]{4,3,2,1,0:T(8,128)(2,1)S(1)}, bf16[2,4,2,112,512]{4,3,2,1,0:T(8,128)(2,1)}, u32[]{:S(2)}, u32[]{:S(2)}) collective-permute-start(bf16[2,4,2,112,512]{4,3,2,1,0:T(8,128)(2,1)S(1)} %pad_maximum_fusion.5.refs_0_), channel_id=1, source_target_pairs={{0,1},{1,0},{2,3},{3,2},{4,5},{5,4},{6,7},{7,6},{8,9},{9,8},{10,11... | collective-permute-start | bytes 5505032 | tf_op jit(solution)/shard_map/ppermute | solution.py:796
  356.1 15.7 %collective-permute-start.35 = (bf16[32,512]{1,0:T(8,128)(2,1)S(1)}, bf16[32,512]{1,0:T(8,128)(2,1)S(1)}, u32[]{:S(2)}, u32[]{:S(2)}) collective-permute-start(bf16[32,512]{1,0:T(8,128)(2,1)S(1)} %dynamic-slice_bitcast_fusion.13), channel_id=1, source_target_pairs={{0,1},{1,0},{2,3},{3,2},{4,5},{5,4},{6,7},{7,6},{8,9},{9,8},{10,11... | collective-permute-start | bytes 98312 | tf_op jit(solution)/shard_map/ppermute | solution.py:796
  376.9 18.1 %collective-permute-start.37 = (bf16[2,4,2,48,512]{4,3,2,1,0:T(8,128)(2,1)S(1)}, bf16[2,4,2,48,512]{4,3,2,1,0:T(8,128)(2,1)S(1)}, u32[]{:S(2)}, u32[]{:S(2)}) collective-permute-start(bf16[2,4,2,48,512]{4,3,2,1,0:T(8,128)(2,1)S(1)} %fusion.4), channel_id=1, source_target_pairs={{0,4},{1,3},{2,6},{3,1},{4,0},{5,7},{6,2},{7,5},{8,12},{9,11},{10,... | collective-permute-start | bytes 2359304 | tf_op jit(solution)/shard_map/ppermute | solution.py:796
  377.6 17.3 %collective-permute-start.38 = (bf16[2,32,512]{2,1,0:T(8,128)(2,1)S(1)}, bf16[2,32,512]{2,1,0:T(8,128)(2,1)S(1)}, u32[]{:S(2)}, u32[]{:S(2)}) collective-permute-start(bf16[2,32,512]{2,1,0:T(8,128)(2,1)S(1)} %pad_maximum_fusion.34), channel_id=1, source_target_pairs={{0,8},{1,9},{2,10},{3,11},{4,12},{5,13},{6,14},{7,15},{8,0},{9,1},... | collective-permute-start | bytes 196616 | tf_op jit(solution)/shard_map/ppermute | solution.py:796
  379.5 15.4 %collective-permute-start.39 = (bf16[2,32,512]{2,1,0:T(8,128)(2,1)S(1)}, bf16[2,32,512]{2,1,0:T(8,128)(2,1)S(1)}, u32[]{:S(2)}, u32[]{:S(2)}) collective-permute-start(bf16[2,32,512]{2,1,0:T(8,128)(2,1)S(1)} %pad_maximum_fusion.34), channel_id=1, source_target_pairs={{0,16},{1,17},{2,18},{3,19},{4,20},{5,21},{6,22},{7,23},{8,24},{9,... | collective-permute-start | bytes 196616 | tf_op jit(solution)/shard_map/ppermute | solution.py:796
  402.2 25.1 %collective-permute-start.43 = (bf16[2,4,2,80,512]{4,3,2,1,0:T(8,128)(2,1)}, bf16[2,4,2,80,512]{4,3,2,1,0:T(8,128)(2,1)}, u32[]{:S(2)}, u32[]{:S(2)}) collective-permute-start(bf16[2,4,2,80,512]{4,3,2,1,0:T(8,128)(2,1)} %fusion.1), channel_id=1, source_target_pairs={{0,4},{1,3},{2,6},{3,1},{4,0},{5,7},{6,2},{7,5},{8,12},{9,11},{10,... | collective-permute-start | bytes 3932168 | tf_op jit(solution)/shard_map/ppermute | solution.py:796
  404.6 22.7 %collective-permute-start.41 = (bf16[4,2,48,512]{3,2,1,0:T(8,128)(2,1)}, bf16[4,2,48,512]{3,2,1,0:T(8,128)(2,1)S(1)}, u32[]{:S(2)}, u32[]{:S(2)}) collective-permute-start(bf16[4,2,48,512]{3,2,1,0:T(8,128)(2,1)} %get-tuple-element.739), channel_id=1, source_target_pairs={{0,2},{1,5},{2,0},{3,7},{4,6},{5,1},{6,4},{7,3},{8,10},{9,13},{10,... | collective-permute-start | bytes 1179656 | tf_op jit(solution)/shard_map/ppermute | solution.py:796
  405.3 21.1 %collective-permute-start.44 = (bf16[4,2,32,512]{3,2,1,0:T(8,128)(2,1)S(1)}, bf16[4,2,32,512]{3,2,1,0:T(8,128)(2,1)S(1)}, u32[]{:S(2)}, u32[]{:S(2)}) collective-permute-start(bf16[4,2,32,512]{3,2,1,0:T(8,128)(2,1)S(1)} %bitcast.428), channel_id=1, source_target_pairs={{0,2},{1,5},{2,0},{3,7},{4,6},{5,1},{6,4},{7,3},{8,10},{9,13},{10,... | collective-permute-start | bytes 786440 | tf_op jit(solution)/shard_map/ppermute | solution.py:796
  433.5 27.8 %collective-permute-start.48 = (bf16[2,4,2,64,512]{4,3,2,1,0:T(8,128)(2,1)}, bf16[2,4,2,64,512]{4,3,2,1,0:T(8,128)(2,1)}, u32[]{:S(2)}, u32[]{:S(2)}) collective-permute-start(bf16[2,4,2,64,512]{4,3,2,1,0:T(8,128)(2,1)} %fusion.3), channel_id=1, source_target_pairs={{0,4},{1,3},{2,6},{3,1},{4,0},{5,7},{6,2},{7,5},{8,12},{9,11},{10,... | collective-permute-start | bytes 3145736 | tf_op jit(solution)/shard_map/ppermute | solution.py:796
  437.5 23.8 %collective-permute-start.46 = (bf16[4,2,80,512]{3,2,1,0:T(8,128)(2,1)}, bf16[4,2,80,512]{3,2,1,0:T(8,128)(2,1)}, u32[]{:S(2)}, u32[]{:S(2)}) collective-permute-start(bf16[4,2,80,512]{3,2,1,0:T(8,128)(2,1)} %get-tuple-element.733), channel_id=1, source_target_pairs={{0,2},{1,5},{2,0},{3,7},{4,6},{5,1},{6,4},{7,3},{8,10},{9,13},{10,... | collective-permute-start | bytes 1966088 | tf_op jit(solution)/shard_map/ppermute | solution.py:796
  438.2 23.1 %collective-permute-start.49 = (bf16[2,4,2,32,512]{4,3,2,1,0:T(8,128)(2,1)}, bf16[2,4,2,32,512]{4,3,2,1,0:T(8,128)(2,1)}, u32[]{:S(2)}, u32[]{:S(2)}) collective-permute-start(bf16[2,4,2,32,512]{4,3,2,1,0:T(8,128)(2,1)} %pad_maximum_fusion.17.refs_0_), channel_id=1, source_target_pairs={{0,4},{1,3},{2,6},{3,1},{4,0},{5,7},{6,2},{7,5},{8,12},{9,11},{10,... | collective-permute-start | bytes 1572872 | tf_op jit(solution)/shard_map/ppermute | solution.py:796
  439.1 22.1 %collective-permute-start.50 = (bf16[2,4,2,32,512]{4,3,2,1,0:T(8,128)(2,1)}, bf16[2,4,2,32,512]{4,3,2,1,0:T(8,128)(2,1)}, u32[]{:S(2)}, u32[]{:S(2)}) collective-permute-start(bf16[2,4,2,32,512]{4,3,2,1,0:T(8,128)(2,1)} %pad_maximum_fusion.17.refs_0_), channel_id=1, source_target_pairs={{0,1},{1,0},{2,3},{3,2},{4,5},{5,4},{6,7},{7,6},{8,9},{9,8},{10,11... | collective-permute-start | bytes 1572872 | tf_op jit(solution)/shard_map/ppermute | solution.py:796
  469.8 24.9 %collective-permute-start.55 = (bf16[2,4,2,80,512]{4,3,2,1,0:T(8,128)(2,1)}, bf16[2,4,2,80,512]{4,3,2,1,0:T(8,128)(2,1)}, u32[]{:S(2)}, u32[]{:S(2)}) collective-permute-start(bf16[2,4,2,80,512]{4,3,2,1,0:T(8,128)(2,1)} %fusion), channel_id=1, source_target_pairs={{0,4},{1,3},{2,6},{3,1},{4,0},{5,7},{6,2},{7,5},{8,12},{9,11},{10,... | collective-permute-start | bytes 3932168 | tf_op jit(solution)/shard_map/ppermute | solution.py:796
  473.3 21.3 %collective-permute-start.53 = (bf16[4,2,64,512]{3,2,1,0:T(8,128)(2,1)}, bf16[4,2,64,512]{3,2,1,0:T(8,128)(2,1)}, u32[]{:S(2)}, u32[]{:S(2)}) collective-permute-start(bf16[4,2,64,512]{3,2,1,0:T(8,128)(2,1)} %get-tuple-element.737), channel_id=1, source_target_pairs={{0,2},{1,5},{2,0},{3,7},{4,6},{5,1},{6,4},{7,3},{8,10},{9,13},{10,... | collective-permute-start | bytes 1572872 | tf_op jit(solution)/shard_map/ppermute | solution.py:796
  477.2 17.4 %collective-permute-start.52 = (bf16[2,2,80,512]{3,2,1,0:T(8,128)(2,1)}, bf16[2,2,80,512]{3,2,1,0:T(8,128)(2,1)}, u32[]{:S(2)}, u32[]{:S(2)}) collective-permute-start(bf16[2,2,80,512]{3,2,1,0:T(8,128)(2,1)} %fusion.26), channel_id=1, source_target_pairs={{0,16},{1,17},{2,18},{3,19},{4,20},{5,21},{6,22},{7,23},{8,24},{9,... | collective-permute-start | bytes 983048 | tf_op jit(solution)/shard_map/ppermute | solution.py:796
  478.4 16.2 %collective-permute-start.56 = (bf16[2,4,2,32,512]{4,3,2,1,0:T(8,128)(2,1)}, bf16[2,4,2,32,512]{4,3,2,1,0:T(8,128)(2,1)}, u32[]{:S(2)}, u32[]{:S(2)}) collective-permute-start(bf16[2,4,2,32,512]{4,3,2,1,0:T(8,128)(2,1)} %collective-permute-done.49.refs_1_), channel_id=1, source_target_pairs={{0,1},{1,0},{2,3},{3,2},{4,5},{5,4},{6,7},{7,6},{8,9},{9,8},{10,11... | collective-permute-start | bytes 1572872 | tf_op jit(solution)/shard_map/ppermute | solution.py:796
  498.2 17.4 %collective-permute-start.60 = (bf16[4,2,80,512]{3,2,1,0:T(8,128)(2,1)}, bf16[4,2,80,512]{3,2,1,0:T(8,128)(2,1)}, u32[]{:S(2)}, u32[]{:S(2)}) collective-permute-start(bf16[4,2,80,512]{3,2,1,0:T(8,128)(2,1)} %get-tuple-element.731), channel_id=1, source_target_pairs={{0,2},{1,5},{2,0},{3,7},{4,6},{5,1},{6,4},{7,3},{8,10},{9,13},{10,... | collective-permute-start | bytes 1966088 | tf_op jit(solution)/shard_map/ppermute | solution.py:796
  526.5 23.5 %collective-permute-start.68 = (bf16[4,2,64,512]{3,2,1,0:T(8,128)(2,1)}, bf16[4,2,64,512]{3,2,1,0:T(8,128)(2,1)S(1)}, u32[]{:S(2)}, u32[]{:S(2)}) collective-permute-start(bf16[4,2,64,512]{3,2,1,0:T(8,128)(2,1)} %get-tuple-element.735), channel_id=1, source_target_pairs={{0,2},{1,5},{2,0},{3,7},{4,6},{5,1},{6,4},{7,3},{8,10},{9,13},{10,... | collective-permute-start | bytes 1572872 | tf_op jit(solution)/shard_map/ppermute | solution.py:796
  532.3 17.7 %collective-permute-start.65 = (bf16[2,80,512]{2,1,0:T(8,128)(2,1)}, bf16[2,80,512]{2,1,0:T(8,128)(2,1)S(1)}, u32[]{:S(2)}, u32[]{:S(2)}) collective-permute-start(bf16[2,80,512]{2,1,0:T(8,128)(2,1)} %get-tuple-element.747), channel_id=1, source_target_pairs={{0,8},{1,9},{2,10},{3,11},{4,12},{5,13},{6,14},{7,15},{8,16},{9,17... | collective-permute-start | bytes 491528 | tf_op jit(solution)/shard_map/ppermute | solution.py:796
  532.4 17.6 %collective-permute-start.66 = (bf16[2,80,512]{2,1,0:T(8,128)(2,1)}, bf16[2,80,512]{2,1,0:T(8,128)(2,1)S(1)}, u32[]{:S(2)}, u32[]{:S(2)}) collective-permute-start(bf16[2,80,512]{2,1,0:T(8,128)(2,1)} %get-tuple-element.746), channel_id=1, source_target_pairs={{0,16},{1,17},{2,18},{3,19},{4,20},{5,21},{6,22},{7,23},{8,24},{9,... | collective-permute-start | bytes 491528 | tf_op jit(solution)/shard_map/ppermute | solution.py:796
  (95 other events, 860.2 us)

commit v7 on v6

--- a/solution.py
+++ b/solution.py
@@ -17,7 +17,7 @@
 
 ROWS = 128
 LANES = 512
-VMEM_LIMIT = 60 * 1024 * 1024
+VMEM_LIMIT = 44 * 1024 * 1024
 LIGHT = pl.CostEstimate(flops=1024, bytes_accessed=1024, transcendentals=0)
 
 
@@ -981,18 +981,18 @@
 def pipelined_gather(groups, pieces, place, state, arrived):
     count = len(groups)
     low, high = (place[0] % 2, place[0] // 2)
-    held = start_gather(groups[:1], pieces(None)[:1], place) + [None] * (count - 1)
-    held[0] = in_order(held[0], hop(held[0], ALONG_Z, swap=1), low)
+    held = start_gather(groups[:1], pieces(None)[:1], place)
     for tick in range(count + 3):
         near, far, last = [index if 0 <= index < count else None for index in range(tick - 1, tick - 4, -1)]
         live = [index for index in (tick, near, far, last) if index is not None and index < count]
-        if tick == 1:
-            live += range(2, count)
+        if tick in (1, 2):
+            live += range(tick + 1, count)
         items, state = together([held[index] for index in live], state)
         for index, item in zip(live, items):
             held[index] = item
         if tick == 0:
-            held[1:] = start_gather(groups[1:], pieces(held[0])[1:], place)
+            held += start_gather(groups[1:2], pieces(held[0])[1:2], place)
+            held += start_gather(groups[2:], pieces(held[1])[2:], place)
         if last is not None:
             own, arrived_far, other = held[last]
             held[last] = [own, arrived_far, other, hop(arrived_far, ACROSS)]
@@ -1000,10 +1000,12 @@
             held[far] = [held[far], hop(held[far], FAR), hop(held[far], ACROSS)]
         if near is not None:
             held[near] = [held[near], hop(held[near], NEAR)]
-        if tick < count:
+        if tick == 0:
+            held[0] = [held[0]] + [hop(held[0], ALONG_Z, swap=bits) for bits in (1, 2, 3)]
+        elif tick < count:
             held[tick] = [held[tick], hop(held[tick], ALONG_Z, swap=2)]
-        if tick < 2:
-            early = slice(1, 2) if tick == 0 else slice(2, count)
+        if tick < 3:
+            early = slice(tick + 1, tick + 2 if tick < 2 else count)
             got = hop(jnp.concatenate(held[early], axis=1), ALONG_Z, swap=1)
             ends = list(itertools.accumulate(half_rows(parts) for parts in groups[early]))
             got = jnp.split(got, ends[:-1], axis=1)
@@ -1011,8 +1013,10 @@
         if last is not None:
             state = arrived(last, held[last], state)
         if tick < count:
-            (own, other), state = together(held[tick], state)
-            both = in_order(own, other, high)
+            items, state = together(held[tick], state)
+            if tick == 0:
+                items = [in_order(*items[:2], low), in_order(*items[2:], low)]
+            both = in_order(*items, high)
             held[tick] = both.reshape(-1, *both.shape[2:])
         if near is not None:
             items, state = together(held[near], state)
@@ -1088,7 +1092,7 @@
     def near(items):
         to_near, own, from_core, from_far = items
         from_near = hop(low_add(to_near, from_core[0, 1], from_far[1]), NEAR)
-        return [add_up(own, from_core[0, 0], from_far[0]), from_near]
+        return [own, from_core[0, 0], from_far[0], from_near]
 
     def pick(array, at):
         return lax.dynamic_index_in_dim(array, at, 0, False)

time: 610 us -> 570 us (0.934)
  local copies, waits for them, and re-layouts: 49.3 us -> 80.6 us
  waiting for transfers between devices: 228 us -> 203 us
  Pallas kernels: 180 us -> 156 us
  other arithmetic: 69.3 us -> 48.1 us
    unnamed x127 -> x241, local copies, waits for them, and re-layouts: 8.32 us -> 36.8 us
    ppermute x82 -> x85, waiting for transfers between devices: 228 us -> 203 us  [send(): return lax.ppermute(array, AXES, pairs)]
    squeeze x0 -> x10, local copies, waits for them, and re-layouts: none -> 14.6 us  [near(): return [own, from_core[0, 0], from_far[0], from_near]]
    pallas_call x5, Pallas kernels: 67.4 us -> 56.8 us  [back_call(): pl.pallas_call(functools.partial(back_kernel, body, parts, tuned, counts)...]
    convert_element_type x10, other arithmetic: 23.3 us -> 14.4 us  [low_add(): return add_up(*terms).astype(jnp.bfloat16)]
    ppermute x82 -> x85, starting transfers between devices: 77.3 us -> 73.3 us  [send(): return lax.ppermute(array, AXES, pairs)]
    another operation x47 -> x48, other arithmetic: 12.2 us -> 11.9 us  [in_order(): return jnp.stack([first, second])]
  transfers between devices with their start and end apart: 82 -> 85, of which waited for: 34 -> 35; matrix products, arithmetic and copies ran while one was open for 14% -> 13% of each run, Pallas kernels for 25% -> 23%
where the time goes in v7:
time: 570 us; the launch traced here: 565 us
  waiting for transfers between devices  203 us (36%)
  Pallas kernels  156 us (27%)
  local copies, waits for them, and re-layouts  80.6 us (14%)
  starting transfers between devices  73.3 us (13%)
  other arithmetic  48.1 us (8%)
    ppermute x85, waiting for transfers between devices, send(): return lax.ppermute(array, AXES, pairs)  203 us
    ppermute x85, starting transfers between devices, send(): return lax.ppermute(array, AXES, pairs)  73.3 us
    pallas_call x4, Pallas kernels, block_forward(): pl.pallas_call(functools.partial(forward_kernel, count, keep, parts, skip...  66.3 us
    pallas_call x5, Pallas kernels, back_call(): pl.pallas_call(functools.partial(back_kernel, body, parts, tuned, counts)...  56.8 us
    unnamed x241, local copies, waits for them, and re-layouts  36.8 us
    squeeze x10, local copies, waits for them, and re-layouts, near(): return [own, from_core[0, 0], from_far[0], from_near]  14.6 us
    convert_element_type x10, other arithmetic, low_add(): return add_up(*terms).astype(jnp.bfloat16)  14.4 us
    another operation x48, other arithmetic, in_order(): return jnp.stack([first, second])  11.9 us
  transfers between devices with their start and end apart: 85, of which 35 were waited for; matrix products, arithmetic and copies ran while one was open for 13% of the time, Pallas kernels for 23%

profile of v7, /device:TPU:0, one launch (start us, length us, event | category | flops | bytes accessed | tf_op | source)
XLA Modules:
  0.0 565.3 jit_solution(12170667265011666433)
XLA Ops:
  9.5 3.0 collective-permute-start.3
  12.5 2.6 collective-permute-start.4
  22.1 3.9 collective-permute-done.3
  26.0 10.0 %collective-permute-done.4 = bf16[2,144,512]{2,1,0:T(8,128)(2,1)S(1)} collective-permute-done((bf16[2,144,512]{2,1,0:T(8,128)(2,1)S(1)}, bf16[2,144,512]{2,1,0:T(8,128)(2,1)S(1)}, u32[]{:S(2)}, u32[]{:S(2)}) %collective-permute-start.4) | collective-permute-done | bytes 294944 | tf_op jit(solution)/shard_map/ppermute | solution.py:796
  37.3 2.2 collective-permute-done.2
  41.8 4.6 collective-permute-start.8
  46.4 17.9 %collective-permute-done.7 = bf16[2,112,512]{2,1,0:T(8,128)(2,1)S(1)} collective-permute-done((bf16[2,112,512]{2,1,0:T(8,128)(2,1)S(1)}, bf16[2,112,512]{2,1,0:T(8,128)(2,1)S(1)}, u32[]{:S(2)}, u32[]{:S(2)}) %collective-permute-start.7) | collective-permute-done | bytes 229408 | tf_op jit(solution)/shard_map/ppermute | solution.py:796
  64.4 9.7 %collective-permute-done.8 = bf16[2,2,160,512]{3,2,1,0:T(8,128)(2,1)S(1)} collective-permute-done((bf16[2,2,160,512]{3,2,1,0:T(8,128)(2,1)S(1)}, bf16[2,2,160,512]{3,2,1,0:T(8,128)(2,1)S(1)}, u32[]{:S(2)}, u32[]{:S(2)}) %collective-permute-start.8) | collective-permute-done | bytes 655392 | tf_op jit(solution)/shard_map/ppermute | solution.py:796
  76.7 2.6 collective-permute-start.10
  79.3 18.9 %collective-permute-done.11 = bf16[2,2,112,512]{3,2,1,0:T(8,128)(2,1)S(1)} collective-permute-done((bf16[2,2,112,512]{3,2,1,0:T(8,128)(2,1)S(1)}, bf16[2,2,112,512]{3,2,1,0:T(8,128)(2,1)S(1)}, u32[]{:S(2)}, u32[]{:S(2)}) %collective-permute-start.11) | collective-permute-done | bytes 458784 | tf_op jit(solution)/shard_map/ppermute | solution.py:796
  98.4 9.7 %collective-permute-done.10 = bf16[2,416,512]{2,1,0:T(8,128)(2,1)S(1)} collective-permute-done((bf16[2,416,512]{2,1,0:T(8,128)(2,1)S(1)}, bf16[2,416,512]{2,1,0:T(8,128)(2,1)S(1)}, u32[]{:S(2)}, u32[]{:S(2)}) %collective-permute-start.10) | collective-permute-done | bytes 852000 | tf_op jit(solution)/shard_map/ppermute | solution.py:796
  108.5 9.0 %collective-permute-done.13.refs_5_ = bf16[2,4,2,144,512]{4,3,2,1,0:T(8,128)(2,1)S(1)} collective-permute-done((bf16[2,4,2,144,512]{4,3,2,1,0:T(8,128)(2,1)S(1)}, bf16[2,4,2,144,512]{4,3,2,1,0:T(8,128)(2,1)S(1)}, u32[]{:S(2)}, u32[]{:S(2)}) %collective-permute-start.13) | collective-permute-done | bytes 2359328 | tf_op jit(solution)/shard_map/ppermute | solution.py:796
  121.1 28.8 %collective-permute-done.15 = bf16[2,2,160,512]{3,2,1,0:T(8,128)(2,1)S(1)} collective-permute-done((bf16[2,2,160,512]{3,2,1,0:T(8,128)(2,1)S(1)}, bf16[2,2,160,512]{3,2,1,0:T(8,128)(2,1)S(1)}, u32[]{:S(2)}, u32[]{:S(2)}) %collective-permute-start.15) | collective-permute-done | bytes 655392 | tf_op jit(solution)/shard_map/ppermute | solution.py:796
  152.8 6.4 %collective-permute-done.17.refs_1_.refs_6_ = bf16[2,4,2,160,512]{4,3,2,1,0:T(8,128)(2,1)} collective-permute-done((bf16[2,4,2,160,512]{4,3,2,1,0:T(8,128)(2,1)S(1)}, bf16[2,4,2,160,512]{4,3,2,1,0:T(8,128)(2,1)}, u32[]{:S(2)}, u32[]{:S(2)}) %collective-permute-start.17) | collective-permute-done | bytes 2621472 | tf_op jit(solution)/shard_map/ppermute | solution.py:796
  172.0 15.8 %block_forward.4.refs_1_ = f32[384,2048]{1,0:T(8,128)} custom-call(s32[5]{0:T(128)S(1)} %stack.344.place.refs_0_, bf16[384,256]{1,0:T(8,128)(2,1)S(1)} %bitcast.401, bf16[2,256,512]{2,1,0:T(8,128)(2,1)S(1)} %add_convert_fusion.refs_2_.refs_6_, f32[1,6144]{1,0:T(1,128)S(1)} %slice.253.refs_3_, ...), custom_call_target="tpu_custom_call" | custom-call | flops 1024 | bytes 1024 | tf_op jit(solution)/shard_map/block_forward/pallas_call | solution.py:248
  189.4 3.7 collective-permute-done.19
  207.6 15.5 %block_forward.5.stream = f32[384,2048]{1,0:T(8,128)} custom-call(s32[5]{0:T(128)S(1)} %stack.344.place.refs_0_, f32[384,2048]{1,0:T(8,128)} %block_forward.4.refs_1_, f32[1,6144]{1,0:T(1,128)S(1)} %slice.254.refs_2_, bf16[1152,128]{1,0:T(8,128)(2,1)S(1)} %convert_element_type.381.refs_4_.refs_3_.refs_6_, bf16[2,4,2,144,512]{4,3,2,1,0:T(8,128)(2,1)S(1)} %copy-done.6, ...), custom_call_target="tpu_custom_call" | custom-call | flops 1024 | bytes 1024 | tf_op jit(solution)/shard_map/block_forward/pallas_call | solution.py:248
  223.2 6.1 %head_target.1.target = f32[8,128]{1,0:T(8,128)S(1)} custom-call(s32[5]{0:T(128)S(1)} %stack.344.place.refs_0_, f32[384,2048]{1,0:T(8,128)} %block_forward.5.stream, s32[8,128]{1,0:T(8,128)S(1)} %pad.72.whole, f32[8,128]{1,0:T(8,128)S(1)} %select_maximum_fusion.real, bf16[2,4,2,112,512]{4,3,2,1,0:T(8,128)(2,1)} %pad_maximum_fusion.4.refs_0_, ...), custom_call_target="tpu_custom_call" | custom-call | flops 1024 | bytes 1024 | tf_op jit(solution)/shard_map/head_target/pallas_call | solution.py:598
  232.6 10.4 %collective-permute-done.28.refs_6_ = bf16[2,4,2,160,512]{4,3,2,1,0:T(8,128)(2,1)} collective-permute-done((bf16[2,4,2,160,512]{4,3,2,1,0:T(8,128)(2,1)S(1)}, bf16[2,4,2,160,512]{4,3,2,1,0:T(8,128)(2,1)}, u32[]{:S(2)}, u32[]{:S(2)}) %collective-permute-start.28) | collective-permute-done | bytes 2621472 | tf_op jit(solution)/shard_map/ppermute | solution.py:796
  245.3 2.8 collective-permute-done.31.refs_8_
  249.7 18.1 %block_forward.6 = (f32[384,2048]{1,0:T(8,128)}, f32[384,2048]{1,0:T(8,128)}, f32[384,512]{1,0:T(8,128)S(1)}, f32[384,512]{1,0:T(8,128)S(1)}, f32[384,2048]{1,0:...) custom-call(s32[5]{0:T(128)S(1)} %stack.344.place.refs_0_, ...), custom_call_target="tpu_custom_call" | custom-call | flops 1024 | bytes 1024 | tf_op jit(solution)/shard_map/block_forward/pallas_call | solution.py:248
  271.2 10.5 %collective-permute-done.32.refs_5_ = bf16[2,4,2,144,512]{4,3,2,1,0:T(8,128)(2,1)S(1)} collective-permute-done((bf16[2,4,2,144,512]{4,3,2,1,0:T(8,128)(2,1)S(1)}, bf16[2,4,2,144,512]{4,3,2,1,0:T(8,128)(2,1)S(1)}, u32[]{:S(2)}, u32[]{:S(2)}) %collective-permute-start.32) | collective-permute-done | bytes 2359328 | tf_op jit(solution)/shard_map/ppermute | solution.py:796
  283.5 2.8 collective-permute-done.36.refs_7_
  287.7 16.9 %block_forward.7 = (f32[384,2048]{1,0:T(8,128)}, f32[384,512]{1,0:T(8,128)S(1)}, f32[384,512]{1,0:T(8,128)S(1)}, f32[384,2048]{1,0:T(8,128)}, f32[8,3072]{1,0:T(...) custom-call(s32[5]{0:T(128)S(1)} %stack.344.place.refs_0_, ...), custom_call_target="tpu_custom_call" | custom-call | flops 1024 | bytes 1024 | tf_op jit(solution)/shard_map/block_forward/pallas_call | solution.py:248
  310.6 3.7 collective-permute-done.37.refs_3_
  315.8 11.1 %head_loss.1 = (f32[1,1]{1,0:T(1,128)}, f32[384,2048]{1,0:T(8,128)}, bf16[1,2048,128]{2,1,0:T(8,128)(2,1)S(1)}, bf16[64,512]{1,0:T(8,128)(2,1)S(1)}) custom-call(s32[5]{0:T(128)S(1)} %stack.344.place.refs_0_, f32[384,2048]{1,0:T(8,128)} %get-tuple-element.532.stream, f32[8,128]{1,0:T(8,128)S(1)} %head_target.1.target, s32[8,128]{1,0:T(8,128)S(1)} %pad.72.whole, ...), custom_call_target="tpu_custom_call" | custom-call | flops 1024 | bytes 1024 | tf_op jit(solution)/shard_map/head_loss/pallas_call | solution.py:690
  334.3 11.4 %back_out.1 = (f32[384,2048]{1,0:T(8,128)S(1)}, bf16[384,512]{1,0:T(8,128)(2,1)S(1)}, f32[1,5120]{1,0:T(1,128)S(1)}, bf16[2,2,4,2,48,512]{5,4,3,2,1,0:T(8,128)(2...) custom-call(s32[5]{0:T(128)S(1)} %stack.344.place.refs_0_, ...), custom_call_target="tpu_custom_call" | custom-call | flops 1024 | bytes 1024 | tf_op jit(solution)/shard_map/back_out/pallas_call | solution.py:414
  347.7 3.3 collective-permute-done.39
  352.0 2.4 collective-permute-start.42
  356.4 9.4 %back_mid.2 = (bf16[384,512]{1,0:T(8,128)(2,1)S(1)}, f32[1,1024]{1,0:T(1,128)S(1)}, bf16[2,2,4,2,80,512]{5,4,3,2,1,0:T(8,128)(2,1)S(1)}, bf16[2,4,2,80,512]{4,3,...) custom-call(s32[5]{0:T(128)S(1)} %stack.344.place.refs_0_, ...), custom_call_target="tpu_custom_call" | custom-call | flops 1024 | bytes 1024 | tf_op jit(solution)/shard_map/back_mid/pallas_call | solution.py:414
  366.0 4.9 collective-permute-done.45
  375.2 17.3 %back_between.1 = (f32[384,2048]{1,0:T(8,128)}, bf16[384,512]{1,0:T(8,128)(2,1)S(1)}, f32[1,5120]{1,0:T(1,128)S(1)}, bf16[2,2,4,2,64,512]{5,4,3,2,1,0:T(8,128)(2...) custom-call(s32[5]{0:T(128)S(1)} %stack.344.place.refs_0_, ...), custom_call_target="tpu_custom_call" | custom-call | flops 1024 | bytes 1024 | tf_op jit(solution)/shard_map/back_between/pallas_call | solution.py:414
  397.6 3.0 collective-permute-done.50
  408.3 10.5 %back_mid.3 = (bf16[384,512]{1,0:T(8,128)(2,1)S(1)}, f32[1,1024]{1,0:T(1,128)S(1)}, bf16[2,2,4,2,80,512]{5,4,3,2,1,0:T(8,128)(2,1)}, bf16[2,4,2,80,512]{4,3,2,1,...) custom-call(s32[5]{0:T(128)S(1)} %stack.344.place.refs_0_, ...), custom_call_target="tpu_custom_call" | custom-call | flops 1024 | bytes 1024 | tf_op jit(solution)/shard_map/back_mid/pallas_call | solution.py:414
  418.9 2.3 slice_bitcast_fusion.7
  434.0 2.6 collective-permute-start.55
  437.9 8.2 %back_first.1 = (bf16[2,2,4,2,64,512]{5,4,3,2,1,0:T(8,128)(2,1)}, bf16[2,4,2,64,512]{4,3,2,1,0:T(8,128)(2,1)S(1)}, bf16[4,2,64,512]{3,2,1,0:T(8,128)(2,1)S(1)}, bf16[4,2,64,512]{3,2,1,0:T(8,128)(2,1)S(1)}) custom-call(s32[5]{0:T(128)S(1)} %stack.344.place.refs_0_, bf16[384,512]{1,0:T(8,128)(2,1)S(1)} %copy-done.62, ...), custom_call_target="tpu_custom_call" | custom-call | flops 1024 | bytes 1024 | tf_op jit(solution)/shard_map/back_first/pallas_call | solution.py:414
  449.0 2.6 collective-permute-done.55
  453.8 2.5 fusion.5
  466.5 2.5 fusion.2
  473.7 10.3 %collective-permute-done.65 = bf16[2,4,2,64,512]{4,3,2,1,0:T(8,128)(2,1)S(1)} collective-permute-done((bf16[2,4,2,64,512]{4,3,2,1,0:T(8,128)(2,1)}, bf16[2,4,2,64,512]{4,3,2,1,0:T(8,128)(2,1)S(1)}, u32[]{:S(2)}, u32[]{:S(2)}) %collective-permute-start.65) | collective-permute-done | bytes 1048608 | tf_op jit(solution)/shard_map/ppermute | solution.py:796
  498.8 2.4 collective-permute-start.69
  507.3 9.0 %collective-permute-done.67 = bf16[2,64,512]{2,1,0:T(8,128)(2,1)S(1)} collective-permute-done((bf16[2,64,512]{2,1,0:T(8,128)(2,1)S(1)}, bf16[2,64,512]{2,1,0:T(8,128)(2,1)S(1)}, u32[]{:S(2)}, u32[]{:S(2)}) %collective-permute-start.67) | collective-permute-done | bytes 131104 | tf_op jit(solution)/shard_map/ppermute | solution.py:796
  526.1 4.7 collective-permute-done.75
  533.1 7.7 %directions.1 = (f32[8,128]{1,0:T(8,128)S(1)}, f32[1,115648]{1,0:T(1,128)}, f32[1,115648]{1,0:T(1,128)}, f32[1,115648]{1,0:T(1,128)S(1)}, f32[2,139456]{1,0:T(2,...) custom-call(f32[96,512]{1,0:T(8,128)S(1)} %bitcast.400, f32[160,512]{1,0:T(8,128)S(1)} %bitcast.394, ...), custom_call_target="tpu_custom_call" | custom-call | flops 1024 | bytes 1024 | tf_op jit(solution)/shard_map/directions/pallas_call | solution.py:1315
  548.4 2.2 collective-permute-start.82
  554.5 2.7 collective-permute-done.84
  557.8 4.7 update.1
  (626 shorter events, 187.8 us)
Async XLA Ops:
  9.5 16.5 %collective-permute-start.3 = (bf16[2,144,512]{2,1,0:T(8,128)(2,1)S(1)}, bf16[2,144,512]{2,1,0:T(8,128)(2,1)S(1)}, u32[]{:S(2)}, u32[]{:S(2)}) collective-permute-start(bf16[2,144,512]{2,1,0:T(8,128)(2,1)S(1)} %pad_maximum_fusion.26), channel_id=1, source_target_pairs={{0,8},{1,9},{2,10},{3,11},{4,12},{5,13},{6,14},{7,15},{8,0},{9,1},... | collective-permute-start | bytes 884744 | tf_op jit(solution)/shard_map/ppermute | solution.py:796
  12.5 23.5 %collective-permute-start.4 = (bf16[2,144,512]{2,1,0:T(8,128)(2,1)S(1)}, bf16[2,144,512]{2,1,0:T(8,128)(2,1)S(1)}, u32[]{:S(2)}, u32[]{:S(2)}) collective-permute-start(bf16[2,144,512]{2,1,0:T(8,128)(2,1)S(1)} %pad_maximum_fusion.26), channel_id=1, source_target_pairs={{0,16},{1,17},{2,18},{3,19},{4,20},{5,21},{6,22},{7,23},{8,24},{9,... | collective-permute-start | bytes 884744 | tf_op jit(solution)/shard_map/ppermute | solution.py:796
  15.1 20.9 %collective-permute-start.5 = (bf16[2,144,512]{2,1,0:T(8,128)(2,1)S(1)}, bf16[2,144,512]{2,1,0:T(8,128)(2,1)}, u32[]{:S(2)}, u32[]{:S(2)}) collective-permute-start(bf16[2,144,512]{2,1,0:T(8,128)(2,1)S(1)} %pad_maximum_fusion.26), channel_id=1, source_target_pairs={{0,24},{1,25},{2,26},{3,27},{4,28},{5,29},{6,30},{7,31},{8,16},{9,... | collective-permute-start | bytes 884744 | tf_op jit(solution)/shard_map/ppermute | solution.py:796
  19.2 20.3 %collective-permute-start.2 = (bf16[2,160,512]{2,1,0:T(8,128)(2,1)S(1)}, bf16[2,160,512]{2,1,0:T(8,128)(2,1)S(1)}, u32[]{:S(2)}, u32[]{:S(2)}) collective-permute-start(bf16[2,160,512]{2,1,0:T(8,128)(2,1)S(1)} %pad_maximum_fusion.22), channel_id=1, source_target_pairs={{0,8},{1,9},{2,10},{3,11},{4,12},{5,13},{6,14},{7,15},{8,0},{9,1},... | collective-permute-start | bytes 983048 | tf_op jit(solution)/shard_map/ppermute | solution.py:796
  22.1 17.6 %collective-permute-start.6 = (bf16[528,512]{1,0:T(8,128)(2,1)S(1)}, bf16[528,512]{1,0:T(8,128)(2,1)S(1)}, u32[]{:S(2)}, u32[]{:S(2)}) collective-permute-start(bf16[528,512]{1,0:T(8,128)(2,1)S(1)} %pad_maximum_fusion.18), channel_id=1, source_target_pairs={{0,1},{1,0},{2,3},{3,2},{4,5},{5,4},{6,7},{7,6},{8,9},{9,8},{10,11... | collective-permute-start | bytes 1622024 | tf_op jit(solution)/shard_map/ppermute | solution.py:796
  40.1 34.3 %collective-permute-start.9 = (bf16[4,2,144,512]{3,2,1,0:T(8,128)(2,1)S(1)}, bf16[4,2,144,512]{3,2,1,0:T(8,128)(2,1)S(1)}, u32[]{:S(2)}, u32[]{:S(2)}) collective-permute-start(bf16[4,2,144,512]{3,2,1,0:T(8,128)(2,1)S(1)} %bitcast.414), channel_id=1, source_target_pairs={{0,2},{1,5},{2,0},{3,7},{4,6},{5,1},{6,4},{7,3},{8,10},{9,13},{10,... | collective-permute-start | bytes 3538952 | tf_op jit(solution)/shard_map/ppermute | solution.py:796
  41.8 32.3 %collective-permute-start.8 = (bf16[2,2,160,512]{3,2,1,0:T(8,128)(2,1)S(1)}, bf16[2,2,160,512]{3,2,1,0:T(8,128)(2,1)S(1)}, u32[]{:S(2)}, u32[]{:S(2)}) collective-permute-start(bf16[2,2,160,512]{3,2,1,0:T(8,128)(2,1)S(1)} %pad_maximum_fusion.13), channel_id=1, source_target_pairs={{0,16},{1,17},{2,18},{3,19},{4,20},{5,21},{6,22},{7,23},{8,24},{9,... | collective-permute-start | bytes 1966088 | tf_op jit(solution)/shard_map/ppermute | solution.py:796
  46.4 17.9 %collective-permute-start.7 = (bf16[2,112,512]{2,1,0:T(8,128)(2,1)S(1)}, bf16[2,112,512]{2,1,0:T(8,128)(2,1)S(1)}, u32[]{:S(2)}, u32[]{:S(2)}) collective-permute-start(bf16[2,112,512]{2,1,0:T(8,128)(2,1)S(1)} %pad_maximum_fusion.31), channel_id=1, source_target_pairs={{0,8},{1,9},{2,10},{3,11},{4,12},{5,13},{6,14},{7,15},{8,0},{9,1},... | collective-permute-start | bytes 688136 | tf_op jit(solution)/shard_map/ppermute | solution.py:796
  74.6 43.0 %collective-permute-start.13 = (bf16[2,4,2,144,512]{4,3,2,1,0:T(8,128)(2,1)S(1)}, bf16[2,4,2,144,512]{4,3,2,1,0:T(8,128)(2,1)S(1)}, u32[]{:S(2)}, u32[]{:S(2)}) collective-permute-start(bf16[2,4,2,144,512]{4,3,2,1,0:T(8,128)(2,1)S(1)} %pad_maximum_fusion.2.refs_4_), channel_id=1, source_target_pairs={{0,4},{1,3},{2,6},{3,1},{4,0},{5,7},{6,2},{7,5},{8,12},{9,11},{10,... | collective-permute-start | bytes 7077896 | tf_op jit(solution)/shard_map/ppermute | solution.py:796
  75.2 42.4 %collective-permute-start.14 = (bf16[2,4,2,144,512]{4,3,2,1,0:T(8,128)(2,1)S(1)}, bf16[2,4,2,144,512]{4,3,2,1,0:T(8,128)(2,1)S(1)}, u32[]{:S(2)}, u32[]{:S(2)}) collective-permute-start(bf16[2,4,2,144,512]{4,3,2,1,0:T(8,128)(2,1)S(1)} %pad_maximum_fusion.2.refs_4_), channel_id=1, source_target_pairs={{0,1},{1,0},{2,3},{3,2},{4,5},{5,4},{6,7},{7,6},{8,9},{9,8},{10,11... | collective-permute-start | bytes 7077896 | tf_op jit(solution)/shard_map/ppermute | solution.py:796
  75.2 23.1 %collective-permute-start.11 = (bf16[2,2,112,512]{3,2,1,0:T(8,128)(2,1)S(1)}, bf16[2,2,112,512]{3,2,1,0:T(8,128)(2,1)S(1)}, u32[]{:S(2)}, u32[]{:S(2)}) collective-permute-start(bf16[2,2,112,512]{3,2,1,0:T(8,128)(2,1)S(1)} %pad_maximum_fusion.20), channel_id=1, source_target_pairs={{0,16},{1,17},{2,18},{3,19},{4,20},{5,21},{6,22},{7,23},{8,24},{9,... | collective-permute-start | bytes 1376264 | tf_op jit(solution)/shard_map/ppermute | solution.py:796
  75.2 33.1 %collective-permute-start.12 = (bf16[4,2,160,512]{3,2,1,0:T(8,128)(2,1)S(1)}, bf16[4,2,160,512]{3,2,1,0:T(8,128)(2,1)S(1)}, u32[]{:S(2)}, u32[]{:S(2)}) collective-permute-start(bf16[4,2,160,512]{3,2,1,0:T(8,128)(2,1)S(1)} %bitcast.410), channel_id=1, source_target_pairs={{0,2},{1,5},{2,0},{3,7},{4,6},{5,1},{6,4},{7,3},{8,10},{9,13},{10,... | collective-permute-start | bytes 3932168 | tf_op jit(solution)/shard_map/ppermute | solution.py:796
  76.7 31.4 %collective-permute-start.10 = (bf16[2,416,512]{2,1,0:T(8,128)(2,1)S(1)}, bf16[2,416,512]{2,1,0:T(8,128)(2,1)S(1)}, u32[]{:S(2)}, u32[]{:S(2)}) collective-permute-start(bf16[2,416,512]{2,1,0:T(8,128)(2,1)S(1)} %pad_maximum_fusion.12), channel_id=1, source_target_pairs={{0,8},{1,9},{2,10},{3,11},{4,12},{5,13},{6,14},{7,15},{8,0},{9,1},... | collective-permute-start | bytes 2555912 | tf_op jit(solution)/shard_map/ppermute | solution.py:796
  117.6 41.6 %collective-permute-start.17 = (bf16[2,4,2,160,512]{4,3,2,1,0:T(8,128)(2,1)S(1)}, bf16[2,4,2,160,512]{4,3,2,1,0:T(8,128)(2,1)}, u32[]{:S(2)}, u32[]{:S(2)}) collective-permute-start(bf16[2,4,2,160,512]{4,3,2,1,0:T(8,128)(2,1)S(1)} %pad_maximum_fusion.refs_0_.refs_5_), channel_id=1, source_target_pairs={{0,4},{1,3},{2,6},{3,1},{4,0},{5,7},{6,2},{7,5},{8,12},{9,11},{10,... | collective-permute-start | bytes 7864328 | tf_op jit(solution)/shard_map/ppermute | solution.py:796
  118.1 41.1 %collective-permute-start.18 = (bf16[2,4,2,160,512]{4,3,2,1,0:T(8,128)(2,1)S(1)}, bf16[2,4,2,160,512]{4,3,2,1,0:T(8,128)(2,1)S(1)}, u32[]{:S(2)}, u32[]{:S(2)}) collective-permute-start(bf16[2,4,2,160,512]{4,3,2,1,0:T(8,128)(2,1)S(1)} %pad_maximum_fusion.refs_0_.refs_5_), channel_id=1, source_target_pairs={{0,1},{1,0},{2,3},{3,2},{4,5},{5,4},{6,7},{7,6},{8,9},{9,8},{10,11... | collective-permute-start | bytes 7864328 | tf_op jit(solution)/shard_map/ppermute | solution.py:796
  118.5 31.5 %collective-permute-start.15 = (bf16[2,2,160,512]{3,2,1,0:T(8,128)(2,1)S(1)}, bf16[2,2,160,512]{3,2,1,0:T(8,128)(2,1)S(1)}, u32[]{:S(2)}, u32[]{:S(2)}) collective-permute-start(bf16[2,2,160,512]{3,2,1,0:T(8,128)(2,1)S(1)} %pad_maximum_fusion.14), channel_id=1, source_target_pairs={{0,16},{1,17},{2,18},{3,19},{4,20},{5,21},{6,22},{7,23},{8,24},{9,... | collective-permute-start | bytes 1966088 | tf_op jit(solution)/shard_map/ppermute | solution.py:796
  118.6 32.7 %collective-permute-start.16 = (bf16[4,2,112,512]{3,2,1,0:T(8,128)(2,1)S(1)}, bf16[4,2,112,512]{3,2,1,0:T(8,128)(2,1)S(1)}, u32[]{:S(2)}, u32[]{:S(2)}) collective-permute-start(bf16[4,2,112,512]{3,2,1,0:T(8,128)(2,1)S(1)} %bitcast.418), channel_id=1, source_target_pairs={{0,2},{1,5},{2,0},{3,7},{4,6},{5,1},{6,4},{7,3},{8,10},{9,13},{10,... | collective-permute-start | bytes 2752520 | tf_op jit(solution)/shard_map/ppermute | solution.py:796
  161.4 32.0 %collective-permute-start.21 = (bf16[4,2,160,512]{3,2,1,0:T(8,128)(2,1)}, bf16[4,2,160,512]{3,2,1,0:T(8,128)(2,1)}, u32[]{:S(2)}, u32[]{:S(2)}) collective-permute-start(bf16[4,2,160,512]{3,2,1,0:T(8,128)(2,1)} %bitcast.66), channel_id=1, source_target_pairs={{0,2},{1,5},{2,0},{3,7},{4,6},{5,1},{6,4},{7,3},{8,10},{9,13},{10,... | collective-permute-start | bytes 3932168 | tf_op jit(solution)/shard_map/ppermute | solution.py:796
  163.1 35.5 %collective-permute-start.22 = (bf16[2,4,2,112,512]{4,3,2,1,0:T(8,128)(2,1)}, bf16[2,4,2,112,512]{4,3,2,1,0:T(8,128)(2,1)}, u32[]{:S(2)}, u32[]{:S(2)}) collective-permute-start(bf16[2,4,2,112,512]{4,3,2,1,0:T(8,128)(2,1)} %pad_maximum_fusion.4.refs_0_), channel_id=1, source_target_pairs={{0,4},{1,3},{2,6},{3,1},{4,0},{5,7},{6,2},{7,5},{8,12},{9,11},{10,... | collective-permute-start | bytes 5505032 | tf_op jit(solution)/shard_map/ppermute | solution.py:796
  163.7 34.9 %collective-permute-start.23 = (bf16[2,4,2,112,512]{4,3,2,1,0:T(8,128)(2,1)}, bf16[2,4,2,112,512]{4,3,2,1,0:T(8,128)(2,1)}, u32[]{:S(2)}, u32[]{:S(2)}) collective-permute-start(bf16[2,4,2,112,512]{4,3,2,1,0:T(8,128)(2,1)} %pad_maximum_fusion.4.refs_0_), channel_id=1, source_target_pairs={{0,1},{1,0},{2,3},{3,2},{4,5},{5,4},{6,7},{7,6},{8,9},{9,8},{10,11... | collective-permute-start | bytes 5505032 | tf_op jit(solution)/shard_map/ppermute | solution.py:796
  164.2 29.0 %collective-permute-start.19 = (bf16[2,2,144,512]{3,2,1,0:T(8,128)(2,1)}, bf16[2,2,144,512]{3,2,1,0:T(8,128)(2,1)}, u32[]{:S(2)}, u32[]{:S(2)}) collective-permute-start(bf16[2,2,144,512]{3,2,1,0:T(8,128)(2,1)} %pad_maximum_fusion.17), channel_id=1, source_target_pairs={{0,16},{1,17},{2,18},{3,19},{4,20},{5,21},{6,22},{7,23},{8,24},{9,... | collective-permute-start | bytes 1769480 | tf_op jit(solution)/shard_map/ppermute | solution.py:796
  166.4 34.7 %collective-permute-start.25 = (bf16[2,4,2,144,512]{4,3,2,1,0:T(8,128)(2,1)}, bf16[2,4,2,144,512]{4,3,2,1,0:T(8,128)(2,1)}, u32[]{:S(2)}, u32[]{:S(2)}) collective-permute-start(bf16[2,4,2,144,512]{4,3,2,1,0:T(8,128)(2,1)} %copy-done.10), channel_id=1, source_target_pairs={{0,1},{1,0},{2,3},{3,2},{4,5},{5,4},{6,7},{7,6},{8,9},{9,8},{10,11... | collective-permute-start | bytes 7077896 | tf_op jit(solution)/shard_map/ppermute | solution.py:796
  198.6 44.4 %collective-permute-start.28 = (bf16[2,4,2,160,512]{4,3,2,1,0:T(8,128)(2,1)S(1)}, bf16[2,4,2,160,512]{4,3,2,1,0:T(8,128)(2,1)}, u32[]{:S(2)}, u32[]{:S(2)}) collective-permute-start(bf16[2,4,2,160,512]{4,3,2,1,0:T(8,128)(2,1)S(1)} %pad_maximum_fusion.1.refs_5_), channel_id=1, source_target_pairs={{0,4},{1,3},{2,6},{3,1},{4,0},{5,7},{6,2},{7,5},{8,12},{9,11},{10,... | collective-permute-start | bytes 7864328 | tf_op jit(solution)/shard_map/ppermute | solution.py:796
  199.3 43.8 %collective-permute-start.29 = (bf16[2,4,2,160,512]{4,3,2,1,0:T(8,128)(2,1)S(1)}, bf16[2,4,2,160,512]{4,3,2,1,0:T(8,128)(2,1)}, u32[]{:S(2)}, u32[]{:S(2)}) collective-permute-start(bf16[2,4,2,160,512]{4,3,2,1,0:T(8,128)(2,1)S(1)} %pad_maximum_fusion.1.refs_5_), channel_id=1, source_target_pairs={{0,1},{1,0},{2,3},{3,2},{4,5},{5,4},{6,7},{7,6},{8,9},{9,8},{10,11... | collective-permute-start | bytes 7864328 | tf_op jit(solution)/shard_map/ppermute | solution.py:796
  200.0 23.1 %collective-permute-start.26 = (bf16[2,4,2,112,512]{4,3,2,1,0:T(8,128)(2,1)}, bf16[2,4,2,112,512]{4,3,2,1,0:T(8,128)(2,1)}, u32[]{:S(2)}, u32[]{:S(2)}) collective-permute-start(bf16[2,4,2,112,512]{4,3,2,1,0:T(8,128)(2,1)} %collective-permute-done.22.refs_1_), channel_id=1, source_target_pairs={{0,1},{1,0},{2,3},{3,2},{4,5},{5,4},{6,7},{7,6},{8,9},{9,8},{10,11... | collective-permute-start | bytes 5505032 | tf_op jit(solution)/shard_map/ppermute | solution.py:796
  200.1 29.3 %collective-permute-start.27 = (bf16[4,2,144,512]{3,2,1,0:T(8,128)(2,1)}, bf16[4,2,144,512]{3,2,1,0:T(8,128)(2,1)}, u32[]{:S(2)}, u32[]{:S(2)}) collective-permute-start(bf16[4,2,144,512]{3,2,1,0:T(8,128)(2,1)} %bitcast.73), channel_id=1, source_target_pairs={{0,2},{1,5},{2,0},{3,7},{4,6},{5,1},{6,4},{7,3},{8,10},{9,13},{10,... | collective-permute-start | bytes 3538952 | tf_op jit(solution)/shard_map/ppermute | solution.py:796
  201.1 28.2 %collective-permute-start.24 = (bf16[2,2,112,512]{3,2,1,0:T(8,128)(2,1)}, bf16[2,2,112,512]{3,2,1,0:T(8,128)(2,1)}, u32[]{:S(2)}, u32[]{:S(2)}) collective-permute-start(bf16[2,2,112,512]{3,2,1,0:T(8,128)(2,1)} %pad_maximum_fusion.21), channel_id=1, source_target_pairs={{0,16},{1,17},{2,18},{3,19},{4,20},{5,21},{6,22},{7,23},{8,24},{9,... | collective-permute-start | bytes 1376264 | tf_op jit(solution)/shard_map/ppermute | solution.py:796
  243.0 38.7 %collective-permute-start.32 = (bf16[2,4,2,144,512]{4,3,2,1,0:T(8,128)(2,1)S(1)}, bf16[2,4,2,144,512]{4,3,2,1,0:T(8,128)(2,1)S(1)}, u32[]{:S(2)}, u32[]{:S(2)}) collective-permute-start(bf16[2,4,2,144,512]{4,3,2,1,0:T(8,128)(2,1)S(1)} %pad_maximum_fusion.3.refs_4_), channel_id=1, source_target_pairs={{0,4},{1,3},{2,6},{3,1},{4,0},{5,7},{6,2},{7,5},{8,12},{9,11},{10,... | collective-permute-start | bytes 7077896 | tf_op jit(solution)/shard_map/ppermute | solution.py:796
  243.7 38.0 %collective-permute-start.33 = (bf16[2,4,2,144,512]{4,3,2,1,0:T(8,128)(2,1)S(1)}, bf16[2,4,2,144,512]{4,3,2,1,0:T(8,128)(2,1)S(1)}, u32[]{:S(2)}, u32[]{:S(2)}) collective-permute-start(bf16[2,4,2,144,512]{4,3,2,1,0:T(8,128)(2,1)S(1)} %pad_maximum_fusion.3.refs_4_), channel_id=1, source_target_pairs={{0,1},{1,0},{2,3},{3,2},{4,5},{5,4},{6,7},{7,6},{8,9},{9,8},{10,11... | collective-permute-start | bytes 7077896 | tf_op jit(solution)/shard_map/ppermute | solution.py:796
  244.7 24.4 %collective-permute-start.30 = (bf16[4,2,112,512]{3,2,1,0:T(8,128)(2,1)S(1)}, bf16[4,2,112,512]{3,2,1,0:T(8,128)(2,1)}, u32[]{:S(2)}, u32[]{:S(2)}) collective-permute-start(bf16[4,2,112,512]{3,2,1,0:T(8,128)(2,1)S(1)} %bitcast.420), channel_id=1, source_target_pairs={{0,2},{1,5},{2,0},{3,7},{4,6},{5,1},{6,4},{7,3},{8,10},{9,13},{10,... | collective-permute-start | bytes 2752520 | tf_op jit(solution)/shard_map/ppermute | solution.py:796
  281.8 27.0 %collective-permute-start.34 = (bf16[2,4,2,112,512]{4,3,2,1,0:T(8,128)(2,1)S(1)}, bf16[2,4,2,112,512]{4,3,2,1,0:T(8,128)(2,1)}, u32[]{:S(2)}, u32[]{:S(2)}) collective-permute-start(bf16[2,4,2,112,512]{4,3,2,1,0:T(8,128)(2,1)S(1)} %pad_maximum_fusion.5.refs_0_), channel_id=1, source_target_pairs={{0,4},{1,3},{2,6},{3,1},{4,0},{5,7},{6,2},{7,5},{8,12},{9,11},{10,... | collective-permute-start | bytes 5505032 | tf_op jit(solution)/shard_map/ppermute | solution.py:796
  282.5 26.3 %collective-permute-start.35 = (bf16[2,4,2,112,512]{4,3,2,1,0:T(8,128)(2,1)S(1)}, bf16[2,4,2,112,512]{4,3,2,1,0:T(8,128)(2,1)S(1)}, u32[]{:S(2)}, u32[]{:S(2)}) collective-permute-start(bf16[2,4,2,112,512]{4,3,2,1,0:T(8,128)(2,1)S(1)} %pad_maximum_fusion.5.refs_0_), channel_id=1, source_target_pairs={{0,1},{1,0},{2,3},{3,2},{4,5},{5,4},{6,7},{7,6},{8,9},{9,8},{10,11... | collective-permute-start | bytes 5505032 | tf_op jit(solution)/shard_map/ppermute | solution.py:796
  328.4 19.1 %collective-permute-start.38 = (bf16[32,512]{1,0:T(8,128)(2,1)S(1)}, bf16[32,512]{1,0:T(8,128)(2,1)S(1)}, u32[]{:S(2)}, u32[]{:S(2)}) collective-permute-start(bf16[32,512]{1,0:T(8,128)(2,1)S(1)} %dynamic-slice_bitcast_fusion.13), channel_id=1, source_target_pairs={{0,1},{1,0},{2,3},{3,2},{4,5},{5,4},{6,7},{7,6},{8,9},{9,8},{10,11... | collective-permute-start | bytes 98312 | tf_op jit(solution)/shard_map/ppermute | solution.py:796
  371.4 24.8 %collective-permute-start.46 = (bf16[2,4,2,80,512]{4,3,2,1,0:T(8,128)(2,1)S(1)}, bf16[2,4,2,80,512]{4,3,2,1,0:T(8,128)(2,1)}, u32[]{:S(2)}, u32[]{:S(2)}) collective-permute-start(bf16[2,4,2,80,512]{4,3,2,1,0:T(8,128)(2,1)S(1)} %fusion.1), channel_id=1, source_target_pairs={{0,4},{1,3},{2,6},{3,1},{4,0},{5,7},{6,2},{7,5},{8,12},{9,11},{10,... | collective-permute-start | bytes 3932168 | tf_op jit(solution)/shard_map/ppermute | solution.py:796
  372.8 22.0 %collective-permute-start.47 = (bf16[4,2,32,512]{3,2,1,0:T(8,128)(2,1)S(1)}, bf16[4,2,32,512]{3,2,1,0:T(8,128)(2,1)S(1)}, u32[]{:S(2)}, u32[]{:S(2)}) collective-permute-start(bf16[4,2,32,512]{3,2,1,0:T(8,128)(2,1)S(1)} %bitcast.429), channel_id=1, source_target_pairs={{0,2},{1,5},{2,0},{3,7},{4,6},{5,1},{6,4},{7,3},{8,10},{9,13},{10,... | collective-permute-start | bytes 786440 | tf_op jit(solution)/shard_map/ppermute | solution.py:796
  374.4 20.6 %collective-permute-start.44 = (bf16[4,2,48,512]{3,2,1,0:T(8,128)(2,1)S(1)}, bf16[4,2,48,512]{3,2,1,0:T(8,128)(2,1)S(1)}, u32[]{:S(2)}, u32[]{:S(2)}) collective-permute-start(bf16[4,2,48,512]{3,2,1,0:T(8,128)(2,1)S(1)} %fusion.9), channel_id=1, source_target_pairs={{0,2},{1,5},{2,0},{3,7},{4,6},{5,1},{6,4},{7,3},{8,10},{9,13},{10,... | collective-permute-start | bytes 1179656 | tf_op jit(solution)/shard_map/ppermute | solution.py:796
  396.2 27.0 %collective-permute-start.52 = (bf16[2,4,2,32,512]{4,3,2,1,0:T(8,128)(2,1)S(1)}, bf16[2,4,2,32,512]{4,3,2,1,0:T(8,128)(2,1)S(1)}, u32[]{:S(2)}, u32[]{:S(2)}) collective-permute-start(bf16[2,4,2,32,512]{4,3,2,1,0:T(8,128)(2,1)S(1)} %pad_maximum_fusion.19.refs_0_), channel_id=1, source_target_pairs={{0,4},{1,3},{2,6},{3,1},{4,0},{5,7},{6,2},{7,5},{8,12},{9,11},{10,... | collective-permute-start | bytes 1572872 | tf_op jit(solution)/shard_map/ppermute | solution.py:796
  397.6 25.6 %collective-permute-start.53 = (bf16[2,4,2,32,512]{4,3,2,1,0:T(8,128)(2,1)S(1)}, bf16[2,4,2,32,512]{4,3,2,1,0:T(8,128)(2,1)S(1)}, u32[]{:S(2)}, u32[]{:S(2)}) collective-permute-start(bf16[2,4,2,32,512]{4,3,2,1,0:T(8,128)(2,1)S(1)} %pad_maximum_fusion.19.refs_0_), channel_id=1, source_target_pairs={{0,1},{1,0},{2,3},{3,2},{4,5},{5,4},{6,7},{7,6},{8,9},{9,8},{10,11... | collective-permute-start | bytes 1572872 | tf_op jit(solution)/shard_map/ppermute | solution.py:796
  402.2 21.9 %collective-permute-start.51 = (bf16[2,4,2,64,512]{4,3,2,1,0:T(8,128)(2,1)S(1)}, bf16[2,4,2,64,512]{4,3,2,1,0:T(8,128)(2,1)S(1)}, u32[]{:S(2)}, u32[]{:S(2)}) collective-permute-start(bf16[2,4,2,64,512]{4,3,2,1,0:T(8,128)(2,1)S(1)} %fusion.3), channel_id=1, source_target_pairs={{0,4},{1,3},{2,6},{3,1},{4,0},{5,7},{6,2},{7,5},{8,12},{9,11},{10,... | collective-permute-start | bytes 3145736 | tf_op jit(solution)/shard_map/ppermute | solution.py:796
  405.3 18.8 %collective-permute-start.49 = (bf16[4,2,80,512]{3,2,1,0:T(8,128)(2,1)S(1)}, bf16[4,2,80,512]{3,2,1,0:T(8,128)(2,1)S(1)}, u32[]{:S(2)}, u32[]{:S(2)}) collective-permute-start(bf16[4,2,80,512]{3,2,1,0:T(8,128)(2,1)S(1)} %fusion.6), channel_id=1, source_target_pairs={{0,2},{1,5},{2,0},{3,7},{4,6},{5,1},{6,4},{7,3},{8,10},{9,13},{10,... | collective-permute-start | bytes 1966088 | tf_op jit(solution)/shard_map/ppermute | solution.py:796
  406.5 16.6 %collective-permute-start.48 = (bf16[2,2,48,512]{3,2,1,0:T(8,128)(2,1)S(1)}, bf16[2,2,48,512]{3,2,1,0:T(8,128)(2,1)S(1)}, u32[]{:S(2)}, u32[]{:S(2)}) collective-permute-start(bf16[2,2,48,512]{3,2,1,0:T(8,128)(2,1)S(1)} %fusion.39), channel_id=1, source_target_pairs={{0,16},{1,17},{2,18},{3,19},{4,20},{5,21},{6,22},{7,23},{8,24},{9,... | collective-permute-start | bytes 589832 | tf_op jit(solution)/shard_map/ppermute | solution.py:796
  427.3 24.4 %collective-permute-start.56 = (bf16[4,2,64,512]{3,2,1,0:T(8,128)(2,1)S(1)}, bf16[4,2,64,512]{3,2,1,0:T(8,128)(2,1)S(1)}, u32[]{:S(2)}, u32[]{:S(2)}) collective-permute-start(bf16[4,2,64,512]{3,2,1,0:T(8,128)(2,1)S(1)} %fusion.8), channel_id=1, source_target_pairs={{0,2},{1,5},{2,0},{3,7},{4,6},{5,1},{6,4},{7,3},{8,10},{9,13},{10,... | collective-permute-start | bytes 1572872 | tf_op jit(solution)/shard_map/ppermute | solution.py:796
  432.3 20.4 %collective-permute-start.58 = (bf16[2,4,2,80,512]{4,3,2,1,0:T(8,128)(2,1)S(1)}, bf16[2,4,2,80,512]{4,3,2,1,0:T(8,128)(2,1)S(1)}, u32[]{:S(2)}, u32[]{:S(2)}) collective-permute-start(bf16[2,4,2,80,512]{4,3,2,1,0:T(8,128)(2,1)S(1)} %fusion), channel_id=1, source_target_pairs={{0,4},{1,3},{2,6},{3,1},{4,0},{5,7},{6,2},{7,5},{8,12},{9,11},{10,... | collective-permute-start | bytes 3932168 | tf_op jit(solution)/shard_map/ppermute | solution.py:796
  434.0 17.6 %collective-permute-start.55 = (bf16[2,2,80,512]{3,2,1,0:T(8,128)(2,1)S(1)}, bf16[2,2,80,512]{3,2,1,0:T(8,128)(2,1)S(1)}, u32[]{:S(2)}, u32[]{:S(2)}) collective-permute-start(bf16[2,2,80,512]{3,2,1,0:T(8,128)(2,1)S(1)} %fusion.26), channel_id=1, source_target_pairs={{0,16},{1,17},{2,18},{3,19},{4,20},{5,21},{6,22},{7,23},{8,24},{9,... | collective-permute-start | bytes 983048 | tf_op jit(solution)/shard_map/ppermute | solution.py:796
  456.3 17.4 %collective-permute-start.63 = (bf16[4,2,80,512]{3,2,1,0:T(8,128)(2,1)}, bf16[4,2,80,512]{3,2,1,0:T(8,128)(2,1)}, u32[]{:S(2)}, u32[]{:S(2)}) collective-permute-start(bf16[4,2,80,512]{3,2,1,0:T(8,128)(2,1)} %fusion.5), channel_id=1, source_target_pairs={{0,2},{1,5},{2,0},{3,7},{4,6},{5,1},{6,4},{7,3},{8,10},{9,13},{10,... | collective-permute-start | bytes 1966088 | tf_op jit(solution)/shard_map/ppermute | solution.py:796
  491.1 25.3 %collective-permute-start.71 = (bf16[4,2,64,512]{3,2,1,0:T(8,128)(2,1)}, bf16[4,2,64,512]{3,2,1,0:T(8,128)(2,1)}, u32[]{:S(2)}, u32[]{:S(2)}) collective-permute-start(bf16[4,2,64,512]{3,2,1,0:T(8,128)(2,1)} %fusion.7), channel_id=1, source_target_pairs={{0,2},{1,5},{2,0},{3,7},{4,6},{5,1},{6,4},{7,3},{8,10},{9,13},{10,... | collective-permute-start | bytes 1572872 | tf_op jit(solution)/shard_map/ppermute | solution.py:796
  498.7 17.7 %collective-permute-start.68 = (bf16[2,80,512]{2,1,0:T(8,128)(2,1)}, bf16[2,80,512]{2,1,0:T(8,128)(2,1)S(1)}, u32[]{:S(2)}, u32[]{:S(2)}) collective-permute-start(bf16[2,80,512]{2,1,0:T(8,128)(2,1)} %get-tuple-element.767), channel_id=1, source_target_pairs={{0,8},{1,9},{2,10},{3,11},{4,12},{5,13},{6,14},{7,15},{8,16},{9,17... | collective-permute-start | bytes 491528 | tf_op jit(solution)/shard_map/ppermute | solution.py:796
  498.8 17.6 %collective-permute-start.69 = (bf16[2,80,512]{2,1,0:T(8,128)(2,1)}, bf16[2,80,512]{2,1,0:T(8,128)(2,1)S(1)}, u32[]{:S(2)}, u32[]{:S(2)}) collective-permute-start(bf16[2,80,512]{2,1,0:T(8,128)(2,1)} %get-tuple-element.766), channel_id=1, source_target_pairs={{0,16},{1,17},{2,18},{3,19},{4,20},{5,21},{6,22},{7,23},{8,24},{9,... | collective-permute-start | bytes 491528 | tf_op jit(solution)/shard_map/ppermute | solution.py:796
  (156 other events, 979.1 us)

commit v8 on v7

--- a/solution.py
+++ b/solution.py
@@ -426,26 +426,27 @@
     return (list(outs[: len(out_shape)]), list(outs[len(out_shape) :]))
 
 
-def back_out(grad, stream, hid_two, hid_three, rstd, w_out, gains, dpool, parts, tuned, place):
+def back_out(grad, stream, hid_two, hid_three, rstd, w_out, gains, parts, tuned, place):
     rows = stream.shape[0]
 
     def body(ins, outs, made, scratch, done):
-        made[1][...] = ins[7][...]
-        done(1)
-        back_out_body(rows // ROWS, *ins[:7], *outs, scratch, made[0])
+        back_out_body(rows // ROWS, *ins, *outs, scratch, made[0])
         done(0)
 
-    ins = [grad, stream, hid_two, hid_three, rstd, w_out, gains, dpool]
+    ins = [grad, stream, hid_two, hid_three, rstd, w_out, gains]
     out_shape = [f32(rows, D), bf16(rows, BOT), f32(1, 2 * BOT + 2 * D)]
     return back_call("back_out", body, ins, out_shape, out_scratch(rows), parts, tuned, place)
 
 
-def back_mid(grad, hid_one, rstd, w_mid, gains, shift, parts, tuned, place):
+def back_mid(grad, hid_one, rstd, w_mid, gains, shift, more, parts, tuned, place):
     rows = grad.shape[0]
     stats = stat_rows(rows // ROWS)
 
     def body(ins, outs, made, scratch, done):
-        back_mid_body(rows // ROWS, *ins, *outs, scratch, made[0])
+        for index in range(1, len(made)):
+            made[index][...] = ins[5 + index][...]
+            done(index)
+        back_mid_body(rows // ROWS, *ins[:6], *outs, scratch, made[0])
         done(0)
 
     scratch = [
@@ -455,7 +456,7 @@
         pltpu.VMEM((stats, BOT), jnp.float32),
         pltpu.VMEM((stats, BOT), jnp.float32),
     ]
-    ins = [grad, hid_one, rstd, w_mid, gains, shift]
+    ins = [grad, hid_one, rstd, w_mid, gains, shift, *more]
     out_shape = [bf16(rows, BOT), f32(1, 2 * BOT)]
     return back_call("back_mid", body, ins, out_shape, scratch, parts, tuned, place)
 
@@ -515,7 +516,7 @@
 
 
 def fetch_ends(parts, tuned, place, sources, weights, sems):
-    first = len(parts) - 3
+    first = len(parts) - 2
     fetch(parts, tuned, place, sources, dict(enumerate(weights, first)), sems)
 
     def arrived(index):
@@ -526,10 +527,10 @@
     return arrived
 
 
-def head_forward(count, stream, arrived, games, pool_t, pooled):
-    pool = merge(arrived(0)[...]).astype(jnp.float32)
+def head_forward(count, stream, pool, arrived, games, pool_t, pooled):
     for part in range(D // ROWS):
-        pool_t[:, pl.ds(part * ROWS, ROWS)] = pool[part * ROWS : (part + 1) * ROWS].T
+        lanes = pl.ds(part * ROWS, ROWS)
+        pool_t[:, lanes] = pool[lanes, :].astype(jnp.float32).T
     pooled[...] = jnp.zeros_like(pooled)
 
     def weigh(frame, rows, lanes):
@@ -537,9 +538,9 @@
         pooled[frame, lanes] = jnp.sum(value * pool_t[:, lanes], axis=0, keepdims=True)
 
     each_chunk(count, D, weigh)
-    before = dot(pooled[...].astype(jnp.bfloat16), merge(arrived(1)[...]))
+    before = dot(pooled[...].astype(jnp.bfloat16), merge(arrived(0)[...]))
     hidden = silu(before).astype(jnp.bfloat16)
-    heads = arrived(2)
+    heads = arrived(1)
     scores = None
     for game in range(GAMES):
         pair = [dot(hidden, merge(heads[2 * game + half])) for half in range(2)]
@@ -566,10 +567,10 @@
     return jnp.sum(value, axis=1, keepdims=True)
 
 
-def target_kernel(count, parts, tuned, place, stream, whole, real, *refs):
-    sources, (out, *weights, sems, pool_t, pooled) = (refs[:-7], refs[-7:])
+def target_kernel(count, parts, tuned, place, stream, pool, whole, real, *refs):
+    sources, (out, *weights, sems, pool_t, pooled) = (refs[:-6], refs[-6:])
     arrived = fetch_ends(parts, tuned, place, sources, weights, sems)
-    logits, _, _ = head_forward(count, stream, arrived, whole[:, 0:1], pool_t, pooled)
+    logits, _, _ = head_forward(count, stream, pool, arrived, whole[:, 0:1], pool_t, pooled)
     chosen = None
     for action in range(ACTIONS):
         term = jnp.where(whole[:, 2:3] == action, logits[action], 0.0)
@@ -588,32 +589,32 @@
 
 
 def ends_scratch(parts, buffers, tuned):
-    scratch = [pltpu.VMEM(shape, jnp.bfloat16) for shape in weight_shapes(parts, buffers, tuned)[-3:]]
+    scratch = [pltpu.VMEM(shape, jnp.bfloat16) for shape in weight_shapes(parts, buffers, tuned)[-2:]]
     scratch += [pltpu.SemaphoreType.DMA((len(parts),))]
     return scratch + [pltpu.VMEM((ROWS, D), jnp.float32), pltpu.VMEM((8, D), jnp.float32)]
 
 
-def head_target(stream, whole, real, parts, buffers, tuned, place):
+def head_target(stream, pool, whole, real, parts, buffers, tuned, place):
     count = stream.shape[0] // ROWS
     return pl.pallas_call(
         functools.partial(target_kernel, count, parts, tuned),
         out_shape=f32(8, ROWS),
-        in_specs=in_smem() + in_vmem(3) + hbm(len(buffers)),
+        in_specs=in_smem() + in_vmem(4) + hbm(len(buffers)),
         out_specs=in_vmem(1)[0],
         scratch_shapes=ends_scratch(parts, buffers, tuned),
         compiler_params=pltpu.CompilerParams(vmem_limit_bytes=VMEM_LIMIT),
         cost_estimate=LIGHT,
         name="head_target",
-    )(place, stream, whole, real, *buffers)
-
-
-def loss_kernel(count, frames_all, parts, tuned, place, stream, target, whole, legal, *refs):
-    sources, refs = (refs[:-11], refs[-11:])
+    )(place, stream, pool, whole, real, *buffers)
+
+
+def loss_kernel(count, frames_all, parts, tuned, place, stream, pool, target, whole, legal, *refs):
+    sources, refs = (refs[:-10], refs[-10:])
     loss, dstream, dpool, acts, *weights, sems, pool_t, pooled, dpooled = refs
     arrived = fetch_ends(parts, tuned, place, sources, weights, sems)
-    _, proj, heads = weights
+    proj, heads = weights
     games, taken = (whole[:, 0:1], whole[:, 1:2])
-    logits, before, hidden = head_forward(count, stream, arrived, games, pool_t, pooled)
+    logits, before, hidden = head_forward(count, stream, pool, arrived, games, pool_t, pooled)
     atoms = support_lanes()
     inside = atom_lanes() < ATOMS
     logps, probs, values = ([], [], [])
@@ -685,18 +686,18 @@
     lax.fori_loop(0, D // ROWS, gather_pool, 0)
 
 
-def head_loss(stream, target, whole, legal, frames_all, parts, buffers, tuned, place):
+def head_loss(stream, pool, target, whole, legal, frames_all, parts, buffers, tuned, place):
     rows = stream.shape[0]
     return pl.pallas_call(
         functools.partial(loss_kernel, rows // ROWS, frames_all, parts, tuned),
         out_shape=[f32(1, 1), f32(rows, D), bf16(1, D, ROWS), bf16(ACTS, WIDTH)],
-        in_specs=in_smem() + in_vmem(4) + hbm(len(buffers)),
+        in_specs=in_smem() + in_vmem(5) + hbm(len(buffers)),
         out_specs=in_vmem(4),
         scratch_shapes=ends_scratch(parts, buffers, tuned) + [pltpu.VMEM((8, D), jnp.float32)],
         compiler_params=pltpu.CompilerParams(vmem_limit_bytes=VMEM_LIMIT),
         cost_estimate=LIGHT,
         name="head_loss",
-    )(place, stream, target, whole, legal, *buffers)
+    )(place, stream, pool, target, whole, legal, *buffers)
 
 
 ACTS = 64
@@ -1523,13 +1524,17 @@
     def block_weight(index, name):
         return merged(full["online", name, index]).reshape(-1, BOT)
 
-    def hold(net, index, group, buffers, state):
+    def lead(group, buffers):
+        return assemble(group_parts(group), buffers, place, [0])[0] if tuned else buffers[0]
+
+    def hold(index, group, buffers, state):
         full["held", index] = (group, buffers)
-        return state
+        if index > 1:
+            return state
+        return state | {"target_pool": lead(group, buffers)[0]}
 
     def read_gains(group, buffers, state):
-        gains = assemble(group_parts(group), buffers, place, [0])[0] if tuned else buffers[0]
-        gains = gains.reshape(devices, TILE, WIDTH)[:, : 2 * BLOCKS, :gain_width]
+        gains = lead(group, buffers).reshape(devices, TILE, WIDTH)[:, : 2 * BLOCKS, :gain_width]
         gains = gains.transpose(1, 0, 2).reshape(2 * BLOCKS, -1).astype(jnp.float32)
         return run_block("target", 0, group, buffers, state | {"gains": gains})
 
@@ -1537,13 +1542,14 @@
         for index in range(1, BLOCKS):
             state = run_block("target", index, *full["held", index], state)
         target = head_target(
-            state.pop("stream"), whole, real, group_parts(group), buffers, tuned, place
+            state.pop("stream"), state.pop("target_pool"), whole, real,
+            group_parts(group), buffers, tuned, place,
         )
         return state | {"target": target}
 
     def online_ends(group, buffers, state):
         loss, dstream, dpool, acts = head_loss(
-            state.pop("stream"), state.pop("target"), whole, legal, frames_all,
+            state.pop("stream"), state.pop("online_pool"), state.pop("target"), whole, legal, frames_all,
             group_parts(group), buffers, tuned, place,
         )
         return state | {"loss": loss, "grad": dstream, "pool": dpool, "acts": acts}
@@ -1555,7 +1561,7 @@
         stream = [state["pixels" if keep else "following"], spread]
         if index:
             stream = [state["stream"]]
-        skip = 1 if keys[group][0] == ("gains",) else 0
+        skip = 1 if keys[group][0][-1] in ("gains", "pool") else 0
         out, *kept = block_forward(
             stream, gain, shift, group_parts(group), skip, buffers, place, keep, tuned
         )
@@ -1564,10 +1570,12 @@
             start = kept.pop(0) if index == 0 else stream[0]
             full.update(zip([(net, name, index) for name in block_names], kept[-3:]))
             state |= {"kept%d" % index: [start, *kept[:-3]]}
+            if index == 0:
+                state |= {"online_pool": lead(group, buffers)[0]}
         return state
 
     keys, then = ([], [])
-    ends = ("pool", "proj", "heads")
+    ends = ("proj", "heads")
 
     def add_group(group, run, *names):
         keys.append(group)
@@ -1577,11 +1585,12 @@
         return [(net, name, index) for name in block_names]
 
     for index in range(1, BLOCKS):
-        add_group(block_keys("target", index), hold, "target", index)
+        start = [("target", "pool")] if index == 1 else []
+        add_group(start + block_keys("target", index), hold, index)
     add_group([("gains",), ("target", "patch")] + block_keys("target", 0), read_gains)
     add_group([("target", name) for name in ends], target_ends)
     for index in range(BLOCKS):
-        start = [] if index else [("online", "patch")]
+        start = [] if index else [("online", "pool"), ("online", "patch")]
         add_group(start + block_keys("online", index), run_block, "online", index)
     add_group([("online", name) for name in ends], online_ends)
 
@@ -1609,15 +1618,17 @@
 
     def out_step(index, group, state):
         (dres, low, late), dealt = back_out(
-            state.pop("grad"), *out_inputs(index, state), state.pop("pool"), group, tuned, place
+            state.pop("grad"), *out_inputs(index, state), group, tuned, place
         )
         return (dealt, state | {"grad": dres, "low": low, "late%d" % index: late})
 
     def mid_step(index, group, state):
         stream, hid_one, hid_two, hid_three, rstd = state["kept%d" % index]
         gain = state["gains"][BLOCKS + index : BLOCKS + index + 1]
+        more = [state.pop("pool")] if len(group) > 1 else []
         (low, early), dealt = back_mid(
-            state["low"], hid_one, rstd, block_weight(index, "w_mid"), gain, shift, group, tuned, place
+            state["low"], hid_one, rstd, block_weight(index, "w_mid"), gain, shift, more,
+            group, tuned, place,
         )
         return (dealt, state | {"low": low, "early%d" % index: early})
 
@@ -1651,9 +1662,10 @@
         )
 
     loss_part, acts = (state.pop("loss"), state.pop("acts"))
-    add_step([("w_out", BLOCKS - 1), ("pool",)], out_step, BLOCKS - 1)
+    add_step([("w_out", BLOCKS - 1)], out_step, BLOCKS - 1)
     for index in reversed(range(BLOCKS)):
-        add_step([("w_mid", index)], mid_step, index)
+        more = [("pool",)] if index == BLOCKS - 1 else []
+        add_step([("w_mid", index)] + more, mid_step, index)
         if index:
             add_step([("w_in", index), ("w_out", index - 1)], between_step, index)
     add_step([("w_in", 0), ("patch",), ("gains",)], first_step)
@@ -1662,8 +1674,8 @@
 
     def read_late(pair, rows):
         pool = parts["pool"]
-        first = parts["w_out"].travel
-        return flat_late(pool.unpack(rows[0][first : first + pool.travel]), pair[1], pair[0])[None]
+        first = parts["w_mid"].travel
+        return flat_late(pool.unpack(rows[1][first : first + pool.travel]), pair[1], pair[0])[None]
 
     groups = [[parts[key[0]] for key in group] for group in keys]
     if tuned:

time: 570 us -> 558 us (0.979)
  waiting for transfers between devices: 203 us -> 191 us
    ppermute x85, waiting for transfers between devices: 203 us -> 191 us  [send(): return lax.ppermute(array, AXES, pairs)]
    unnamed x241 -> x261, local copies, waits for them, and re-layouts: 36.8 us -> 41.7 us
  transfers between devices with their start and end apart: 85 -> 85, of which waited for: 35 -> 37; matrix products, arithmetic and copies ran while one was open for 13% -> 13% of each run, Pallas kernels for 23% -> 24%
where the time goes in v8:
time: 558 us; the launch traced here: 553 us
  waiting for transfers between devices  191 us (34%)
  Pallas kernels  158 us (28%)
  local copies, waits for them, and re-layouts  80 us (14%)
  starting transfers between devices  72.4 us (13%)
  other arithmetic  48 us (9%)
    ppermute x85, waiting for transfers between devices, send(): return lax.ppermute(array, AXES, pairs)  191 us
    ppermute x85, starting transfers between devices, send(): return lax.ppermute(array, AXES, pairs)  72.4 us
    pallas_call x4, Pallas kernels, block_forward(): pl.pallas_call(functools.partial(forward_kernel, count, keep, parts, skip...  66.4 us
    pallas_call x5, Pallas kernels, back_call(): pl.pallas_call(functools.partial(back_kernel, body, parts, tuned, counts)...  57 us
    unnamed x261, local copies, waits for them, and re-layouts  41.7 us
    another operation x48, other arithmetic, in_order(): return jnp.stack([first, second])  14.7 us
    convert_element_type x10, other arithmetic, low_add(): return add_up(*terms).astype(jnp.bfloat16)  12.1 us
  transfers between devices with their start and end apart: 85, of which 37 were waited for; matrix products, arithmetic and copies ran while one was open for 13% of the time, Pallas kernels for 24%

profile of v8, /device:TPU:0, one launch (start us, length us, event | category | flops | bytes accessed | tf_op | source)
XLA Modules:
  0.0 552.9 jit_solution(8514150502370162170)
XLA Ops:
  9.8 3.0 collective-permute-start.3
  12.8 2.6 collective-permute-start.4
  22.4 3.9 collective-permute-done.3
  26.4 9.9 %collective-permute-done.4 = bf16[2,144,512]{2,1,0:T(8,128)(2,1)} collective-permute-done((bf16[2,144,512]{2,1,0:T(8,128)(2,1)S(1)}, bf16[2,144,512]{2,1,0:T(8,128)(2,1)}, u32[]{:S(2)}, u32[]{:S(2)}) %collective-permute-start.4) | collective-permute-done | bytes 294944 | tf_op jit(solution)/shard_map/ppermute | solution.py:797
  42.1 4.7 collective-permute-start.8
  46.8 17.2 %collective-permute-done.7 = bf16[2,96,512]{2,1,0:T(8,128)(2,1)S(1)} collective-permute-done((bf16[2,96,512]{2,1,0:T(8,128)(2,1)S(1)}, bf16[2,96,512]{2,1,0:T(8,128)(2,1)S(1)}, u32[]{:S(2)}, u32[]{:S(2)}) %collective-permute-start.7) | collective-permute-done | bytes 196640 | tf_op jit(solution)/shard_map/ppermute | solution.py:797
  64.1 10.4 %collective-permute-done.8 = bf16[2,2,160,512]{3,2,1,0:T(8,128)(2,1)S(1)} collective-permute-done((bf16[2,2,160,512]{3,2,1,0:T(8,128)(2,1)S(1)}, bf16[2,2,160,512]{3,2,1,0:T(8,128)(2,1)S(1)}, u32[]{:S(2)}, u32[]{:S(2)}) %collective-permute-start.8) | collective-permute-done | bytes 655392 | tf_op jit(solution)/shard_map/ppermute | solution.py:797
  77.2 2.3 collective-permute-start.11
  79.6 24.3 %collective-permute-done.11 = bf16[2,2,96,512]{3,2,1,0:T(8,128)(2,1)S(1)} collective-permute-done((bf16[2,2,96,512]{3,2,1,0:T(8,128)(2,1)S(1)}, bf16[2,2,96,512]{3,2,1,0:T(8,128)(2,1)S(1)}, u32[]{:S(2)}, u32[]{:S(2)}) %collective-permute-start.11) | collective-permute-done | bytes 393248 | tf_op jit(solution)/shard_map/ppermute | solution.py:797
  107.5 10.5 %collective-permute-done.13.refs_1_.refs_5_ = bf16[2,4,2,144,512]{4,3,2,1,0:T(8,128)(2,1)} collective-permute-done((bf16[2,4,2,144,512]{4,3,2,1,0:T(8,128)(2,1)S(1)}, bf16[2,4,2,144,512]{4,3,2,1,0:T(8,128)(2,1)}, u32[]{:S(2)}, u32[]{:S(2)}) %collective-permute-start.13) | collective-permute-done | bytes 2359328 | tf_op jit(solution)/shard_map/ppermute | solution.py:797
  128.8 25.0 %collective-permute-done.15 = bf16[2,2,160,512]{3,2,1,0:T(8,128)(2,1)} collective-permute-done((bf16[2,2,160,512]{3,2,1,0:T(8,128)(2,1)}, bf16[2,2,160,512]{3,2,1,0:T(8,128)(2,1)}, u32[]{:S(2)}, u32[]{:S(2)}) %collective-permute-start.15) | collective-permute-done | bytes 655392 | tf_op jit(solution)/shard_map/ppermute | solution.py:797
  156.3 2.4 pad_maximum_fusion.4.refs_0_
  169.9 15.8 %block_forward.4.refs_1_ = f32[384,2048]{1,0:T(8,128)} custom-call(s32[5]{0:T(128)S(1)} %stack.344.place.refs_0_, bf16[384,256]{1,0:T(8,128)(2,1)S(1)} %bitcast.403, bf16[2,256,512]{2,1,0:T(8,128)(2,1)S(1)} %add_convert_fusion.refs_2_.refs_6_, f32[1,6144]{1,0:T(1,128)S(1)} %slice.253.refs_3_, ...), custom_call_target="tpu_custom_call" | custom-call | flops 1024 | bytes 1024 | tf_op jit(solution)/shard_map/block_forward/pallas_call | solution.py:248
  187.4 4.6 collective-permute-done.20
  204.0 15.6 %block_forward.5.stream = f32[384,2048]{1,0:T(8,128)} custom-call(s32[5]{0:T(128)S(1)} %stack.344.place.refs_0_, f32[384,2048]{1,0:T(8,128)} %block_forward.4.refs_1_, f32[1,6144]{1,0:T(1,128)S(1)} %slice.254.refs_2_, bf16[1152,128]{1,0:T(8,128)(2,1)S(1)} %convert_element_type.375.refs_4_.refs_3_.refs_6_, bf16[2,4,2,144,512]{4,3,2,1,0:T(8,128)(2,1)S(1)} %copy-done.2, ...), custom_call_target="tpu_custom_call" | custom-call | flops 1024 | bytes 1024 | tf_op jit(solution)/shard_map/block_forward/pallas_call | solution.py:248
  221.6 4.5 head_target.1.target
  230.8 10.7 %collective-permute-done.28.refs_6_.refs_1_ = bf16[2,4,2,160,512]{4,3,2,1,0:T(8,128)(2,1)} collective-permute-done((bf16[2,4,2,160,512]{4,3,2,1,0:T(8,128)(2,1)S(1)}, bf16[2,4,2,160,512]{4,3,2,1,0:T(8,128)(2,1)}, u32[]{:S(2)}, u32[]{:S(2)}) %collective-permute-start.28) | collective-permute-done | bytes 2621472 | tf_op jit(solution)/shard_map/ppermute | solution.py:797
  243.8 2.8 collective-permute-done.31.refs_8_.refs_3_
  250.6 18.0 %block_forward.6 = (f32[384,2048]{1,0:T(8,128)}, f32[384,2048]{1,0:T(8,128)}, f32[384,512]{1,0:T(8,128)S(1)}, f32[384,512]{1,0:T(8,128)S(1)}, f32[384,2048]{1,0:...) custom-call(s32[5]{0:T(128)S(1)} %stack.344.place.refs_0_, ...), custom_call_target="tpu_custom_call" | custom-call | flops 1024 | bytes 1024 | tf_op jit(solution)/shard_map/block_forward/pallas_call | solution.py:248
  272.7 6.1 %collective-permute-done.32.refs_5_ = bf16[2,4,2,144,512]{4,3,2,1,0:T(8,128)(2,1)S(1)} collective-permute-done((bf16[2,4,2,144,512]{4,3,2,1,0:T(8,128)(2,1)S(1)}, bf16[2,4,2,144,512]{4,3,2,1,0:T(8,128)(2,1)S(1)}, u32[]{:S(2)}, u32[]{:S(2)}) %collective-permute-start.32) | collective-permute-done | bytes 2359328 | tf_op jit(solution)/shard_map/ppermute | solution.py:797
  280.4 2.9 collective-permute-done.36.refs_7_
  284.7 16.9 %block_forward.7 = (f32[384,2048]{1,0:T(8,128)}, f32[384,512]{1,0:T(8,128)S(1)}, f32[384,512]{1,0:T(8,128)S(1)}, f32[384,2048]{1,0:T(8,128)}, f32[8,3072]{1,0:T(...) custom-call(s32[5]{0:T(128)S(1)} %stack.344.place.refs_0_, ...), custom_call_target="tpu_custom_call" | custom-call | flops 1024 | bytes 1024 | tf_op jit(solution)/shard_map/block_forward/pallas_call | solution.py:248
  307.7 3.4 collective-permute-done.37.refs_3_
  312.5 10.9 %head_loss.1 = (f32[1,1]{1,0:T(1,128)}, f32[384,2048]{1,0:T(8,128)}, bf16[1,2048,128]{2,1,0:T(8,128)(2,1)S(1)}, bf16[64,512]{1,0:T(8,128)(2,1)S(1)}) custom-call(s32[5]{0:T(128)S(1)} %stack.344.place.refs_0_, f32[384,2048]{1,0:T(8,128)} %get-tuple-element.550.stream, bf16[2048,128]{1,0:T(8,128)(2,1)S(1)} %bitcast.393, f32[8,128]{1,0:T(8,128)S(1)} %head_target.1.target, ...), custom_call_target="tpu_custom_call" | custom-call | flops 1024 | bytes 1024 | tf_op jit(solution)/shard_map/head_loss/pallas_call | solution.py:691
  328.2 11.3 %back_out.1 = (f32[384,2048]{1,0:T(8,128)S(1)}, bf16[384,512]{1,0:T(8,128)(2,1)S(1)}, f32[1,5120]{1,0:T(1,128)S(1)}, bf16[2,2,4,2,32,512]{5,4,3,2,1,0:T(8,128)(2...) custom-call(s32[5]{0:T(128)S(1)} %stack.344.place.refs_0_, ...), custom_call_target="tpu_custom_call" | custom-call | flops 1024 | bytes 1024 | tf_op jit(solution)/shard_map/back_out/pallas_call | solution.py:414
  341.4 2.3 collective-permute-start.42
  345.9 9.7 %back_mid.2 = (bf16[384,512]{1,0:T(8,128)(2,1)S(1)}, f32[1,1024]{1,0:T(1,128)S(1)}, bf16[2,2,4,2,80,512]{5,4,3,2,1,0:T(8,128)(2,1)S(1)}, bf16[2,4,2,80,512]{4,3,...) custom-call(s32[5]{0:T(128)S(1)} %stack.344.place.refs_0_, ...), custom_call_target="tpu_custom_call" | custom-call | flops 1024 | bytes 1024 | tf_op jit(solution)/shard_map/back_mid/pallas_call | solution.py:414
  357.0 8.1 %collective-permute-done.40 = bf16[2,4,2,32,512]{4,3,2,1,0:T(8,128)(2,1)S(1)} collective-permute-done((bf16[2,4,2,32,512]{4,3,2,1,0:T(8,128)(2,1)S(1)}, bf16[2,4,2,32,512]{4,3,2,1,0:T(8,128)(2,1)S(1)}, u32[]{:S(2)}, u32[]{:S(2)}) %collective-permute-start.40) | collective-permute-done | bytes 524320 | tf_op jit(solution)/shard_map/ppermute | solution.py:797
  365.0 4.9 collective-permute-done.45
  375.4 17.3 %back_between.1 = (f32[384,2048]{1,0:T(8,128)}, bf16[384,512]{1,0:T(8,128)(2,1)S(1)}, f32[1,5120]{1,0:T(1,128)S(1)}, bf16[2,2,4,2,64,512]{5,4,3,2,1,0:T(8,128)(2...) custom-call(s32[5]{0:T(128)S(1)} %stack.344.place.refs_0_, ...), custom_call_target="tpu_custom_call" | custom-call | flops 1024 | bytes 1024 | tf_op jit(solution)/shard_map/back_between/pallas_call | solution.py:414
  397.1 3.4 collective-permute-done.50
  410.2 10.5 %back_mid.3 = (bf16[384,512]{1,0:T(8,128)(2,1)S(1)}, f32[1,1024]{1,0:T(1,128)S(1)}, bf16[2,2,4,2,80,512]{5,4,3,2,1,0:T(8,128)(2,1)}, bf16[2,4,2,80,512]{4,3,2,1,...) custom-call(s32[5]{0:T(128)S(1)} %stack.344.place.refs_0_, ...), custom_call_target="tpu_custom_call" | custom-call | flops 1024 | bytes 1024 | tf_op jit(solution)/shard_map/back_mid/pallas_call | solution.py:414
  433.6 2.9 collective-permute-start.55
  437.9 8.2 %back_first.1 = (bf16[2,2,4,2,64,512]{5,4,3,2,1,0:T(8,128)(2,1)}, bf16[2,4,2,64,512]{4,3,2,1,0:T(8,128)(2,1)S(1)}, bf16[4,2,64,512]{3,2,1,0:T(8,128)(2,1)S(1)}, bf16[4,2,64,512]{3,2,1,0:T(8,128)(2,1)S(1)}) custom-call(s32[5]{0:T(128)S(1)} %stack.344.place.refs_0_, bf16[384,512]{1,0:T(8,128)(2,1)S(1)} %copy-done.65, ...), custom_call_target="tpu_custom_call" | custom-call | flops 1024 | bytes 1024 | tf_op jit(solution)/shard_map/back_first/pallas_call | solution.py:414
  456.7 2.5 collective-permute-start.62
  465.4 2.6 collective-permute-done.61
  468.0 3.2 collective-permute-done.62
  471.2 5.1 collective-permute-done.65
  488.6 2.9 collective-permute-start.70
  492.7 4.2 concatenate.118
  497.0 6.7 %collective-permute-done.67 = bf16[2,64,512]{2,1,0:T(8,128)(2,1)} collective-permute-done((bf16[2,64,512]{2,1,0:T(8,128)(2,1)}, bf16[2,64,512]{2,1,0:T(8,128)(2,1)}, u32[]{:S(2)}, u32[]{:S(2)}) %collective-permute-start.67) | collective-permute-done | bytes 131104 | tf_op jit(solution)/shard_map/ppermute | solution.py:797
  513.4 4.7 collective-permute-done.75
  520.3 7.7 %directions.1 = (f32[8,128]{1,0:T(8,128)S(1)}, f32[1,115648]{1,0:T(1,128)}, f32[1,115648]{1,0:T(1,128)}, f32[1,115648]{1,0:T(1,128)S(1)}, f32[2,139456]{1,0:T(2,...) custom-call(f32[64,512]{1,0:T(8,128)S(1)} %bitcast.405, f32[160,512]{1,0:T(8,128)S(1)} %bitcast.398, ...), custom_call_target="tpu_custom_call" | custom-call | flops 1024 | bytes 1024 | tf_op jit(solution)/shard_map/directions/pallas_call | solution.py:1316
  533.3 2.9 collective-permute-done.81
  536.2 2.3 collective-permute-start.82
  539.5 2.2 collective-permute-start.84
  542.4 2.6 collective-permute-done.84
  545.5 4.7 update.1
  (645 shorter events, 187.5 us)
Async XLA Ops:
  9.8 16.6 %collective-permute-start.3 = (bf16[2,144,512]{2,1,0:T(8,128)(2,1)S(1)}, bf16[2,144,512]{2,1,0:T(8,128)(2,1)}, u32[]{:S(2)}, u32[]{:S(2)}) collective-permute-start(bf16[2,144,512]{2,1,0:T(8,128)(2,1)S(1)} %pad_maximum_fusion.27), channel_id=1, source_target_pairs={{0,8},{1,9},{2,10},{3,11},{4,12},{5,13},{6,14},{7,15},{8,0},{9,1},... | collective-permute-start | bytes 884744 | tf_op jit(solution)/shard_map/ppermute | solution.py:797
  12.8 23.6 %collective-permute-start.4 = (bf16[2,144,512]{2,1,0:T(8,128)(2,1)S(1)}, bf16[2,144,512]{2,1,0:T(8,128)(2,1)}, u32[]{:S(2)}, u32[]{:S(2)}) collective-permute-start(bf16[2,144,512]{2,1,0:T(8,128)(2,1)S(1)} %pad_maximum_fusion.27), channel_id=1, source_target_pairs={{0,16},{1,17},{2,18},{3,19},{4,20},{5,21},{6,22},{7,23},{8,24},{9,... | collective-permute-start | bytes 884744 | tf_op jit(solution)/shard_map/ppermute | solution.py:797
  15.3 21.0 %collective-permute-start.5 = (bf16[2,144,512]{2,1,0:T(8,128)(2,1)S(1)}, bf16[2,144,512]{2,1,0:T(8,128)(2,1)}, u32[]{:S(2)}, u32[]{:S(2)}) collective-permute-start(bf16[2,144,512]{2,1,0:T(8,128)(2,1)S(1)} %pad_maximum_fusion.27), channel_id=1, source_target_pairs={{0,24},{1,25},{2,26},{3,27},{4,28},{5,29},{6,30},{7,31},{8,16},{9,... | collective-permute-start | bytes 884744 | tf_op jit(solution)/shard_map/ppermute | solution.py:797
  18.9 20.8 %collective-permute-start.2 = (bf16[2,160,512]{2,1,0:T(8,128)(2,1)S(1)}, bf16[2,160,512]{2,1,0:T(8,128)(2,1)S(1)}, u32[]{:S(2)}, u32[]{:S(2)}) collective-permute-start(bf16[2,160,512]{2,1,0:T(8,128)(2,1)S(1)} %pad_maximum_fusion.22), channel_id=1, source_target_pairs={{0,8},{1,9},{2,10},{3,11},{4,12},{5,13},{6,14},{7,15},{8,0},{9,1},... | collective-permute-start | bytes 983048 | tf_op jit(solution)/shard_map/ppermute | solution.py:797
  22.4 17.5 %collective-permute-start.6 = (bf16[496,512]{1,0:T(8,128)(2,1)S(1)}, bf16[496,512]{1,0:T(8,128)(2,1)S(1)}, u32[]{:S(2)}, u32[]{:S(2)}) collective-permute-start(bf16[496,512]{1,0:T(8,128)(2,1)S(1)} %pad_maximum_fusion.19), channel_id=1, source_target_pairs={{0,1},{1,0},{2,3},{3,2},{4,5},{5,4},{6,7},{7,6},{8,9},{9,8},{10,11... | collective-permute-start | bytes 1523720 | tf_op jit(solution)/shard_map/ppermute | solution.py:797
  40.3 34.4 %collective-permute-start.9 = (bf16[4,2,144,512]{3,2,1,0:T(8,128)(2,1)S(1)}, bf16[4,2,144,512]{3,2,1,0:T(8,128)(2,1)S(1)}, u32[]{:S(2)}, u32[]{:S(2)}) collective-permute-start(bf16[4,2,144,512]{3,2,1,0:T(8,128)(2,1)S(1)} %bitcast.417), channel_id=1, source_target_pairs={{0,2},{1,5},{2,0},{3,7},{4,6},{5,1},{6,4},{7,3},{8,10},{9,13},{10,... | collective-permute-start | bytes 3538952 | tf_op jit(solution)/shard_map/ppermute | solution.py:797
  42.1 32.5 %collective-permute-start.8 = (bf16[2,2,160,512]{3,2,1,0:T(8,128)(2,1)S(1)}, bf16[2,2,160,512]{3,2,1,0:T(8,128)(2,1)S(1)}, u32[]{:S(2)}, u32[]{:S(2)}) collective-permute-start(bf16[2,2,160,512]{3,2,1,0:T(8,128)(2,1)S(1)} %pad_maximum_fusion.13), channel_id=1, source_target_pairs={{0,16},{1,17},{2,18},{3,19},{4,20},{5,21},{6,22},{7,23},{8,24},{9,... | collective-permute-start | bytes 1966088 | tf_op jit(solution)/shard_map/ppermute | solution.py:797
  46.8 17.2 %collective-permute-start.7 = (bf16[2,96,512]{2,1,0:T(8,128)(2,1)S(1)}, bf16[2,96,512]{2,1,0:T(8,128)(2,1)S(1)}, u32[]{:S(2)}, u32[]{:S(2)}) collective-permute-start(bf16[2,96,512]{2,1,0:T(8,128)(2,1)S(1)} %pad_maximum_fusion.32), channel_id=1, source_target_pairs={{0,8},{1,9},{2,10},{3,11},{4,12},{5,13},{6,14},{7,15},{8,0},{9,1},... | collective-permute-start | bytes 589832 | tf_op jit(solution)/shard_map/ppermute | solution.py:797
  75.0 43.1 %collective-permute-start.13 = (bf16[2,4,2,144,512]{4,3,2,1,0:T(8,128)(2,1)S(1)}, bf16[2,4,2,144,512]{4,3,2,1,0:T(8,128)(2,1)}, u32[]{:S(2)}, u32[]{:S(2)}) collective-permute-start(bf16[2,4,2,144,512]{4,3,2,1,0:T(8,128)(2,1)S(1)} %pad_maximum_fusion.2.refs_0_.refs_4_), channel_id=1, source_target_pairs={{0,4},{1,3},{2,6},{3,1},{4,0},{5,7},{6,2},{7,5},{8,12},{9,11},{10,... | collective-permute-start | bytes 7077896 | tf_op jit(solution)/shard_map/ppermute | solution.py:797
  75.6 42.5 %collective-permute-start.14 = (bf16[2,4,2,144,512]{4,3,2,1,0:T(8,128)(2,1)S(1)}, bf16[2,4,2,144,512]{4,3,2,1,0:T(8,128)(2,1)S(1)}, u32[]{:S(2)}, u32[]{:S(2)}) collective-permute-start(bf16[2,4,2,144,512]{4,3,2,1,0:T(8,128)(2,1)S(1)} %pad_maximum_fusion.2.refs_0_.refs_4_), channel_id=1, source_target_pairs={{0,1},{1,0},{2,3},{3,2},{4,5},{5,4},{6,7},{7,6},{8,9},{9,8},{10,11... | collective-permute-start | bytes 7077896 | tf_op jit(solution)/shard_map/ppermute | solution.py:797
  75.6 31.7 %collective-permute-start.12 = (bf16[4,2,160,512]{3,2,1,0:T(8,128)(2,1)S(1)}, bf16[4,2,160,512]{3,2,1,0:T(8,128)(2,1)S(1)}, u32[]{:S(2)}, u32[]{:S(2)}) collective-permute-start(bf16[4,2,160,512]{3,2,1,0:T(8,128)(2,1)S(1)} %bitcast.413), channel_id=1, source_target_pairs={{0,2},{1,5},{2,0},{3,7},{4,6},{5,1},{6,4},{7,3},{8,10},{9,13},{10,... | collective-permute-start | bytes 3932168 | tf_op jit(solution)/shard_map/ppermute | solution.py:797
  77.1 28.9 %collective-permute-start.10 = (bf16[2,400,512]{2,1,0:T(8,128)(2,1)S(1)}, bf16[2,400,512]{2,1,0:T(8,128)(2,1)S(1)}, u32[]{:S(2)}, u32[]{:S(2)}) collective-permute-start(bf16[2,400,512]{2,1,0:T(8,128)(2,1)S(1)} %pad_maximum_fusion.10), channel_id=1, source_target_pairs={{0,8},{1,9},{2,10},{3,11},{4,12},{5,13},{6,14},{7,15},{8,0},{9,1},... | collective-permute-start | bytes 2457608 | tf_op jit(solution)/shard_map/ppermute | solution.py:797
  77.2 26.6 %collective-permute-start.11 = (bf16[2,2,96,512]{3,2,1,0:T(8,128)(2,1)S(1)}, bf16[2,2,96,512]{3,2,1,0:T(8,128)(2,1)S(1)}, u32[]{:S(2)}, u32[]{:S(2)}) collective-permute-start(bf16[2,2,96,512]{3,2,1,0:T(8,128)(2,1)S(1)} %pad_maximum_fusion.20), channel_id=1, source_target_pairs={{0,16},{1,17},{2,18},{3,19},{4,20},{5,21},{6,22},{7,23},{8,24},{9,... | collective-permute-start | bytes 1179656 | tf_op jit(solution)/shard_map/ppermute | solution.py:797
  119.5 40.2 %collective-permute-start.18 = (bf16[2,4,2,160,512]{4,3,2,1,0:T(8,128)(2,1)S(1)}, bf16[2,4,2,160,512]{4,3,2,1,0:T(8,128)(2,1)}, u32[]{:S(2)}, u32[]{:S(2)}) collective-permute-start(bf16[2,4,2,160,512]{4,3,2,1,0:T(8,128)(2,1)S(1)} %pad_maximum_fusion.refs_0_.refs_5_), channel_id=1, source_target_pairs={{0,4},{1,3},{2,6},{3,1},{4,0},{5,7},{6,2},{7,5},{8,12},{9,11},{10,... | collective-permute-start | bytes 7864328 | tf_op jit(solution)/shard_map/ppermute | solution.py:797
  120.0 39.7 %collective-permute-start.19 = (bf16[2,4,2,160,512]{4,3,2,1,0:T(8,128)(2,1)S(1)}, bf16[2,4,2,160,512]{4,3,2,1,0:T(8,128)(2,1)}, u32[]{:S(2)}, u32[]{:S(2)}) collective-permute-start(bf16[2,4,2,160,512]{4,3,2,1,0:T(8,128)(2,1)S(1)} %pad_maximum_fusion.refs_0_.refs_5_), channel_id=1, source_target_pairs={{0,1},{1,0},{2,3},{3,2},{4,5},{5,4},{6,7},{7,6},{8,9},{9,8},{10,11... | collective-permute-start | bytes 7864328 | tf_op jit(solution)/shard_map/ppermute | solution.py:797
  122.1 31.7 %collective-permute-start.17 = (bf16[4,2,96,512]{3,2,1,0:T(8,128)(2,1)S(1)}, bf16[4,2,96,512]{3,2,1,0:T(8,128)(2,1)}, u32[]{:S(2)}, u32[]{:S(2)}) collective-permute-start(bf16[4,2,96,512]{3,2,1,0:T(8,128)(2,1)S(1)} %bitcast.423), channel_id=1, source_target_pairs={{0,2},{1,5},{2,0},{3,7},{4,6},{5,1},{6,4},{7,3},{8,10},{9,13},{10,... | collective-permute-start | bytes 2359304 | tf_op jit(solution)/shard_map/ppermute | solution.py:797
  122.7 31.1 %collective-permute-start.15 = (bf16[2,2,160,512]{3,2,1,0:T(8,128)(2,1)}, bf16[2,2,160,512]{3,2,1,0:T(8,128)(2,1)}, u32[]{:S(2)}, u32[]{:S(2)}) collective-permute-start(bf16[2,2,160,512]{3,2,1,0:T(8,128)(2,1)} %pad_maximum_fusion.14), channel_id=1, source_target_pairs={{0,16},{1,17},{2,18},{3,19},{4,20},{5,21},{6,22},{7,23},{8,24},{9,... | collective-permute-start | bytes 1966088 | tf_op jit(solution)/shard_map/ppermute | solution.py:797
  160.5 32.0 %collective-permute-start.22 = (bf16[4,2,160,512]{3,2,1,0:T(8,128)(2,1)}, bf16[4,2,160,512]{3,2,1,0:T(8,128)(2,1)}, u32[]{:S(2)}, u32[]{:S(2)}) collective-permute-start(bf16[4,2,160,512]{3,2,1,0:T(8,128)(2,1)} %bitcast.67), channel_id=1, source_target_pairs={{0,2},{1,5},{2,0},{3,7},{4,6},{5,1},{6,4},{7,3},{8,10},{9,13},{10,... | collective-permute-start | bytes 3932168 | tf_op jit(solution)/shard_map/ppermute | solution.py:797
  162.2 34.9 %collective-permute-start.23 = (bf16[2,4,2,96,512]{4,3,2,1,0:T(8,128)(2,1)}, bf16[2,4,2,96,512]{4,3,2,1,0:T(8,128)(2,1)}, u32[]{:S(2)}, u32[]{:S(2)}) collective-permute-start(bf16[2,4,2,96,512]{4,3,2,1,0:T(8,128)(2,1)} %pad_maximum_fusion.4.refs_0_), channel_id=1, source_target_pairs={{0,4},{1,3},{2,6},{3,1},{4,0},{5,7},{6,2},{7,5},{8,12},{9,11},{10,... | collective-permute-start | bytes 4718600 | tf_op jit(solution)/shard_map/ppermute | solution.py:797
  162.7 34.3 %collective-permute-start.24 = (bf16[2,4,2,96,512]{4,3,2,1,0:T(8,128)(2,1)}, bf16[2,4,2,96,512]{4,3,2,1,0:T(8,128)(2,1)}, u32[]{:S(2)}, u32[]{:S(2)}) collective-permute-start(bf16[2,4,2,96,512]{4,3,2,1,0:T(8,128)(2,1)} %pad_maximum_fusion.4.refs_0_), channel_id=1, source_target_pairs={{0,1},{1,0},{2,3},{3,2},{4,5},{5,4},{6,7},{7,6},{8,9},{9,8},{10,11... | collective-permute-start | bytes 4718600 | tf_op jit(solution)/shard_map/ppermute | solution.py:797
  163.1 28.8 %collective-permute-start.20 = (bf16[2,2,144,512]{3,2,1,0:T(8,128)(2,1)}, bf16[2,2,144,512]{3,2,1,0:T(8,128)(2,1)}, u32[]{:S(2)}, u32[]{:S(2)}) collective-permute-start(bf16[2,2,144,512]{3,2,1,0:T(8,128)(2,1)} %pad_maximum_fusion.17), channel_id=1, source_target_pairs={{0,16},{1,17},{2,18},{3,19},{4,20},{5,21},{6,22},{7,23},{8,24},{9,... | collective-permute-start | bytes 1769480 | tf_op jit(solution)/shard_map/ppermute | solution.py:797
  197.0 44.5 %collective-permute-start.28 = (bf16[2,4,2,160,512]{4,3,2,1,0:T(8,128)(2,1)S(1)}, bf16[2,4,2,160,512]{4,3,2,1,0:T(8,128)(2,1)}, u32[]{:S(2)}, u32[]{:S(2)}) collective-permute-start(bf16[2,4,2,160,512]{4,3,2,1,0:T(8,128)(2,1)S(1)} %pad_maximum_fusion.1.refs_5_.refs_0_), channel_id=1, source_target_pairs={{0,4},{1,3},{2,6},{3,1},{4,0},{5,7},{6,2},{7,5},{8,12},{9,11},{10,... | collective-permute-start | bytes 7864328 | tf_op jit(solution)/shard_map/ppermute | solution.py:797
  198.1 43.5 %collective-permute-start.29 = (bf16[2,4,2,160,512]{4,3,2,1,0:T(8,128)(2,1)S(1)}, bf16[2,4,2,160,512]{4,3,2,1,0:T(8,128)(2,1)}, u32[]{:S(2)}, u32[]{:S(2)}) collective-permute-start(bf16[2,4,2,160,512]{4,3,2,1,0:T(8,128)(2,1)S(1)} %pad_maximum_fusion.1.refs_5_.refs_0_), channel_id=1, source_target_pairs={{0,1},{1,0},{2,3},{3,2},{4,5},{5,4},{6,7},{7,6},{8,9},{9,8},{10,11... | collective-permute-start | bytes 7864328 | tf_op jit(solution)/shard_map/ppermute | solution.py:797
  198.1 21.6 %collective-permute-start.26 = (bf16[2,4,2,96,512]{4,3,2,1,0:T(8,128)(2,1)}, bf16[2,4,2,96,512]{4,3,2,1,0:T(8,128)(2,1)}, u32[]{:S(2)}, u32[]{:S(2)}) collective-permute-start(bf16[2,4,2,96,512]{4,3,2,1,0:T(8,128)(2,1)} %collective-permute-done.23.refs_1_), channel_id=1, source_target_pairs={{0,1},{1,0},{2,3},{3,2},{4,5},{5,4},{6,7},{7,6},{8,9},{9,8},{10,11... | collective-permute-start | bytes 4718600 | tf_op jit(solution)/shard_map/ppermute | solution.py:797
  198.6 29.2 %collective-permute-start.27 = (bf16[4,2,144,512]{3,2,1,0:T(8,128)(2,1)}, bf16[4,2,144,512]{3,2,1,0:T(8,128)(2,1)}, u32[]{:S(2)}, u32[]{:S(2)}) collective-permute-start(bf16[4,2,144,512]{3,2,1,0:T(8,128)(2,1)} %bitcast.74), channel_id=1, source_target_pairs={{0,2},{1,5},{2,0},{3,7},{4,6},{5,1},{6,4},{7,3},{8,10},{9,13},{10,... | collective-permute-start | bytes 3538952 | tf_op jit(solution)/shard_map/ppermute | solution.py:797
  199.4 26.7 %collective-permute-start.25 = (bf16[2,2,96,512]{3,2,1,0:T(8,128)(2,1)}, bf16[2,2,96,512]{3,2,1,0:T(8,128)(2,1)}, u32[]{:S(2)}, u32[]{:S(2)}) collective-permute-start(bf16[2,2,96,512]{3,2,1,0:T(8,128)(2,1)} %pad_maximum_fusion.21), channel_id=1, source_target_pairs={{0,16},{1,17},{2,18},{3,19},{4,20},{5,21},{6,22},{7,23},{8,24},{9,... | collective-permute-start | bytes 1179656 | tf_op jit(solution)/shard_map/ppermute | solution.py:797
  241.5 37.3 %collective-permute-start.32 = (bf16[2,4,2,144,512]{4,3,2,1,0:T(8,128)(2,1)S(1)}, bf16[2,4,2,144,512]{4,3,2,1,0:T(8,128)(2,1)S(1)}, u32[]{:S(2)}, u32[]{:S(2)}) collective-permute-start(bf16[2,4,2,144,512]{4,3,2,1,0:T(8,128)(2,1)S(1)} %pad_maximum_fusion.3.refs_4_), channel_id=1, source_target_pairs={{0,4},{1,3},{2,6},{3,1},{4,0},{5,7},{6,2},{7,5},{8,12},{9,11},{10,... | collective-permute-start | bytes 7077896 | tf_op jit(solution)/shard_map/ppermute | solution.py:797
  242.5 36.3 %collective-permute-start.33 = (bf16[2,4,2,144,512]{4,3,2,1,0:T(8,128)(2,1)S(1)}, bf16[2,4,2,144,512]{4,3,2,1,0:T(8,128)(2,1)}, u32[]{:S(2)}, u32[]{:S(2)}) collective-permute-start(bf16[2,4,2,144,512]{4,3,2,1,0:T(8,128)(2,1)S(1)} %pad_maximum_fusion.3.refs_4_), channel_id=1, source_target_pairs={{0,1},{1,0},{2,3},{3,2},{4,5},{5,4},{6,7},{7,6},{8,9},{9,8},{10,11... | collective-permute-start | bytes 7077896 | tf_op jit(solution)/shard_map/ppermute | solution.py:797
  243.2 27.6 %collective-permute-start.30 = (bf16[4,2,96,512]{3,2,1,0:T(8,128)(2,1)S(1)}, bf16[4,2,96,512]{3,2,1,0:T(8,128)(2,1)}, u32[]{:S(2)}, u32[]{:S(2)}) collective-permute-start(bf16[4,2,96,512]{3,2,1,0:T(8,128)(2,1)S(1)} %bitcast.425), channel_id=1, source_target_pairs={{0,2},{1,5},{2,0},{3,7},{4,6},{5,1},{6,4},{7,3},{8,10},{9,13},{10,... | collective-permute-start | bytes 2359304 | tf_op jit(solution)/shard_map/ppermute | solution.py:797
  278.8 27.3 %collective-permute-start.34 = (bf16[2,4,2,96,512]{4,3,2,1,0:T(8,128)(2,1)S(1)}, bf16[2,4,2,96,512]{4,3,2,1,0:T(8,128)(2,1)}, u32[]{:S(2)}, u32[]{:S(2)}) collective-permute-start(bf16[2,4,2,96,512]{4,3,2,1,0:T(8,128)(2,1)S(1)} %pad_maximum_fusion.5.refs_0_), channel_id=1, source_target_pairs={{0,4},{1,3},{2,6},{3,1},{4,0},{5,7},{6,2},{7,5},{8,12},{9,11},{10,... | collective-permute-start | bytes 4718600 | tf_op jit(solution)/shard_map/ppermute | solution.py:797
  279.8 26.3 %collective-permute-start.35 = (bf16[2,4,2,96,512]{4,3,2,1,0:T(8,128)(2,1)S(1)}, bf16[2,4,2,96,512]{4,3,2,1,0:T(8,128)(2,1)S(1)}, u32[]{:S(2)}, u32[]{:S(2)}) collective-permute-start(bf16[2,4,2,96,512]{4,3,2,1,0:T(8,128)(2,1)S(1)} %pad_maximum_fusion.5.refs_0_), channel_id=1, source_target_pairs={{0,1},{1,0},{2,3},{3,2},{4,5},{5,4},{6,7},{7,6},{8,9},{9,8},{10,11... | collective-permute-start | bytes 4718600 | tf_op jit(solution)/shard_map/ppermute | solution.py:797
  324.2 17.0 %collective-permute-start.38 = (bf16[32,512]{1,0:T(8,128)(2,1)S(1)}, bf16[32,512]{1,0:T(8,128)(2,1)S(1)}, u32[]{:S(2)}, u32[]{:S(2)}) collective-permute-start(bf16[32,512]{1,0:T(8,128)(2,1)S(1)} %dynamic-slice_bitcast_fusion.13), channel_id=1, source_target_pairs={{0,1},{1,0},{2,3},{3,2},{4,5},{5,4},{6,7},{7,6},{8,9},{9,8},{10,11... | collective-permute-start | bytes 98312 | tf_op jit(solution)/shard_map/ppermute | solution.py:797
  341.4 15.4 %collective-permute-start.42 = (bf16[2,32,512]{2,1,0:T(8,128)(2,1)S(1)}, bf16[2,32,512]{2,1,0:T(8,128)(2,1)S(1)}, u32[]{:S(2)}, u32[]{:S(2)}) collective-permute-start(bf16[2,32,512]{2,1,0:T(8,128)(2,1)S(1)} %pad_maximum_fusion.37), channel_id=1, source_target_pairs={{0,16},{1,17},{2,18},{3,19},{4,20},{5,21},{6,22},{7,23},{8,24},{9,... | collective-permute-start | bytes 196616 | tf_op jit(solution)/shard_map/ppermute | solution.py:797
  371.5 23.8 %collective-permute-start.46 = (bf16[2,4,2,80,512]{4,3,2,1,0:T(8,128)(2,1)S(1)}, bf16[2,4,2,80,512]{4,3,2,1,0:T(8,128)(2,1)}, u32[]{:S(2)}, u32[]{:S(2)}) collective-permute-start(bf16[2,4,2,80,512]{4,3,2,1,0:T(8,128)(2,1)S(1)} %fusion.1), channel_id=1, source_target_pairs={{0,4},{1,3},{2,6},{3,1},{4,0},{5,7},{6,2},{7,5},{8,12},{9,11},{10,... | collective-permute-start | bytes 3932168 | tf_op jit(solution)/shard_map/ppermute | solution.py:797
  372.5 22.6 %collective-permute-start.47 = (bf16[4,2,32,512]{3,2,1,0:T(8,128)(2,1)S(1)}, bf16[4,2,32,512]{3,2,1,0:T(8,128)(2,1)S(1)}, u32[]{:S(2)}, u32[]{:S(2)}) collective-permute-start(bf16[4,2,32,512]{3,2,1,0:T(8,128)(2,1)S(1)} %bitcast.436), channel_id=1, source_target_pairs={{0,2},{1,5},{2,0},{3,7},{4,6},{5,1},{6,4},{7,3},{8,10},{9,13},{10,... | collective-permute-start | bytes 786440 | tf_op jit(solution)/shard_map/ppermute | solution.py:797
  373.9 21.4 %collective-permute-start.44 = (bf16[4,2,32,512]{3,2,1,0:T(8,128)(2,1)S(1)}, bf16[4,2,32,512]{3,2,1,0:T(8,128)(2,1)S(1)}, u32[]{:S(2)}, u32[]{:S(2)}) collective-permute-start(bf16[4,2,32,512]{3,2,1,0:T(8,128)(2,1)S(1)} %fusion.12), channel_id=1, source_target_pairs={{0,2},{1,5},{2,0},{3,7},{4,6},{5,1},{6,4},{7,3},{8,10},{9,13},{10,... | collective-permute-start | bytes 786440 | tf_op jit(solution)/shard_map/ppermute | solution.py:797
  396.0 27.1 %collective-permute-start.52 = (bf16[2,4,2,32,512]{4,3,2,1,0:T(8,128)(2,1)S(1)}, bf16[2,4,2,32,512]{4,3,2,1,0:T(8,128)(2,1)S(1)}, u32[]{:S(2)}, u32[]{:S(2)}) collective-permute-start(bf16[2,4,2,32,512]{4,3,2,1,0:T(8,128)(2,1)S(1)} %pad_maximum_fusion.18.refs_0_), channel_id=1, source_target_pairs={{0,4},{1,3},{2,6},{3,1},{4,0},{5,7},{6,2},{7,5},{8,12},{9,11},{10,... | collective-permute-start | bytes 1572872 | tf_op jit(solution)/shard_map/ppermute | solution.py:797
  397.1 26.0 %collective-permute-start.53 = (bf16[2,4,2,32,512]{4,3,2,1,0:T(8,128)(2,1)S(1)}, bf16[2,4,2,32,512]{4,3,2,1,0:T(8,128)(2,1)S(1)}, u32[]{:S(2)}, u32[]{:S(2)}) collective-permute-start(bf16[2,4,2,32,512]{4,3,2,1,0:T(8,128)(2,1)S(1)} %pad_maximum_fusion.18.refs_0_), channel_id=1, source_target_pairs={{0,1},{1,0},{2,3},{3,2},{4,5},{5,4},{6,7},{7,6},{8,9},{9,8},{10,11... | collective-permute-start | bytes 1572872 | tf_op jit(solution)/shard_map/ppermute | solution.py:797
  402.1 22.7 %collective-permute-start.51 = (bf16[2,4,2,64,512]{4,3,2,1,0:T(8,128)(2,1)S(1)}, bf16[2,4,2,64,512]{4,3,2,1,0:T(8,128)(2,1)S(1)}, u32[]{:S(2)}, u32[]{:S(2)}) collective-permute-start(bf16[2,4,2,64,512]{4,3,2,1,0:T(8,128)(2,1)S(1)} %fusion.3), channel_id=1, source_target_pairs={{0,4},{1,3},{2,6},{3,1},{4,0},{5,7},{6,2},{7,5},{8,12},{9,11},{10,... | collective-permute-start | bytes 3145736 | tf_op jit(solution)/shard_map/ppermute | solution.py:797
  404.6 20.1 %collective-permute-start.49 = (bf16[4,2,80,512]{3,2,1,0:T(8,128)(2,1)S(1)}, bf16[4,2,80,512]{3,2,1,0:T(8,128)(2,1)S(1)}, u32[]{:S(2)}, u32[]{:S(2)}) collective-permute-start(bf16[4,2,80,512]{3,2,1,0:T(8,128)(2,1)S(1)} %fusion.5), channel_id=1, source_target_pairs={{0,2},{1,5},{2,0},{3,7},{4,6},{5,1},{6,4},{7,3},{8,10},{9,13},{10,... | collective-permute-start | bytes 1966088 | tf_op jit(solution)/shard_map/ppermute | solution.py:797
  406.2 16.9 %collective-permute-start.48 = (bf16[2,2,32,512]{3,2,1,0:T(8,128)(2,1)S(1)}, bf16[2,2,32,512]{3,2,1,0:T(8,128)(2,1)S(1)}, u32[]{:S(2)}, u32[]{:S(2)}) collective-permute-start(bf16[2,2,32,512]{3,2,1,0:T(8,128)(2,1)S(1)} %fusion.25), channel_id=1, source_target_pairs={{0,16},{1,17},{2,18},{3,19},{4,20},{5,21},{6,22},{7,23},{8,24},{9,... | collective-permute-start | bytes 393224 | tf_op jit(solution)/shard_map/ppermute | solution.py:797
  429.2 22.6 %collective-permute-start.56 = (bf16[4,2,64,512]{3,2,1,0:T(8,128)(2,1)S(1)}, bf16[4,2,64,512]{3,2,1,0:T(8,128)(2,1)S(1)}, u32[]{:S(2)}, u32[]{:S(2)}) collective-permute-start(bf16[4,2,64,512]{3,2,1,0:T(8,128)(2,1)S(1)} %fusion.7), channel_id=1, source_target_pairs={{0,2},{1,5},{2,0},{3,7},{4,6},{5,1},{6,4},{7,3},{8,10},{9,13},{10,... | collective-permute-start | bytes 1572872 | tf_op jit(solution)/shard_map/ppermute | solution.py:797
  432.9 19.1 %collective-permute-start.58 = (bf16[2,4,2,80,512]{4,3,2,1,0:T(8,128)(2,1)S(1)}, bf16[2,4,2,80,512]{4,3,2,1,0:T(8,128)(2,1)S(1)}, u32[]{:S(2)}, u32[]{:S(2)}) collective-permute-start(bf16[2,4,2,80,512]{4,3,2,1,0:T(8,128)(2,1)S(1)} %fusion), channel_id=1, source_target_pairs={{0,4},{1,3},{2,6},{3,1},{4,0},{5,7},{6,2},{7,5},{8,12},{9,11},{10,... | collective-permute-start | bytes 3932168 | tf_op jit(solution)/shard_map/ppermute | solution.py:797
  433.6 18.2 %collective-permute-start.55 = (bf16[2,2,80,512]{3,2,1,0:T(8,128)(2,1)S(1)}, bf16[2,2,80,512]{3,2,1,0:T(8,128)(2,1)S(1)}, u32[]{:S(2)}, u32[]{:S(2)}) collective-permute-start(bf16[2,2,80,512]{3,2,1,0:T(8,128)(2,1)S(1)} %fusion.13), channel_id=1, source_target_pairs={{0,16},{1,17},{2,18},{3,19},{4,20},{5,21},{6,22},{7,23},{8,24},{9,... | collective-permute-start | bytes 983048 | tf_op jit(solution)/shard_map/ppermute | solution.py:797
  455.1 16.1 %collective-permute-start.63 = (bf16[4,2,80,512]{3,2,1,0:T(8,128)(2,1)S(1)}, bf16[4,2,80,512]{3,2,1,0:T(8,128)(2,1)S(1)}, u32[]{:S(2)}, u32[]{:S(2)}) collective-permute-start(bf16[4,2,80,512]{3,2,1,0:T(8,128)(2,1)S(1)} %fusion.4), channel_id=1, source_target_pairs={{0,2},{1,5},{2,0},{3,7},{4,6},{5,1},{6,4},{7,3},{8,10},{9,13},{10,... | collective-permute-start | bytes 1966088 | tf_op jit(solution)/shard_map/ppermute | solution.py:797
  483.8 19.8 %collective-permute-start.71 = (bf16[4,2,64,512]{3,2,1,0:T(8,128)(2,1)}, bf16[4,2,64,512]{3,2,1,0:T(8,128)(2,1)}, u32[]{:S(2)}, u32[]{:S(2)}) collective-permute-start(bf16[4,2,64,512]{3,2,1,0:T(8,128)(2,1)} %fusion.6), channel_id=1, source_target_pairs={{0,2},{1,5},{2,0},{3,7},{4,6},{5,1},{6,4},{7,3},{8,10},{9,13},{10,... | collective-permute-start | bytes 1572872 | tf_op jit(solution)/shard_map/ppermute | solution.py:797
  486.1 17.5 %collective-permute-start.68 = (bf16[2,80,512]{2,1,0:T(8,128)(2,1)}, bf16[2,80,512]{2,1,0:T(8,128)(2,1)}, u32[]{:S(2)}, u32[]{:S(2)}) collective-permute-start(bf16[2,80,512]{2,1,0:T(8,128)(2,1)} %get-tuple-element.787), channel_id=1, source_target_pairs={{0,8},{1,9},{2,10},{3,11},{4,12},{5,13},{6,14},{7,15},{8,16},{9,17... | collective-permute-start | bytes 491528 | tf_op jit(solution)/shard_map/ppermute | solution.py:797
  487.9 15.7 %collective-permute-start.69 = (bf16[2,80,512]{2,1,0:T(8,128)(2,1)}, bf16[2,80,512]{2,1,0:T(8,128)(2,1)}, u32[]{:S(2)}, u32[]{:S(2)}) collective-permute-start(bf16[2,80,512]{2,1,0:T(8,128)(2,1)} %get-tuple-element.786), channel_id=1, source_target_pairs={{0,16},{1,17},{2,18},{3,19},{4,20},{5,21},{6,22},{7,23},{8,24},{9,... | collective-permute-start | bytes 491528 | tf_op jit(solution)/shard_map/ppermute | solution.py:797
  (164 other events, 951.3 us)

commit v9 on v8

--- a/solution.py
+++ b/solution.py
@@ -1093,19 +1093,23 @@
     def near(items):
         to_near, own, from_core, from_far = items
         from_near = hop(low_add(to_near, from_core[0, 1], from_far[1]), NEAR)
-        return [own, from_core[0, 0], from_far[0], from_near]
+        return [own, from_core, from_far, from_near]
 
     def pick(array, at):
         return lax.dynamic_index_in_dim(array, at, 0, False)
 
+    def gathered(items):
+        own, from_core, from_far, from_near = items
+        return lax.optimization_barrier(add_up(own, from_core[0, 0], from_far[0], from_near))
+
     def along(items):
-        summed = lax.optimization_barrier(add_up(*items))
+        summed = gathered(items)
         sent = [pick(summed, lax.rem(z + step, depth)) for step in range(1, depth)]
         got = [hop(item.astype(jnp.bfloat16), ALONG_Z, step + 1) for step, item in enumerate(sent)]
         return [pick(summed, z)] + got
 
     def pairs(items):
-        summed = lax.optimization_barrier(add_up(*items))
+        summed = gathered(items)
         summed = summed.reshape(2, 2, *summed.shape[1:])
         return [pick(summed, high), hop(pick(summed, 1 - high).astype(jnp.bfloat16), ALONG_Z, swap=2)]
 
@@ -1124,14 +1128,14 @@
 def share_stages(part, place):
     low, high = (place[0] % 2, place[0] // 2)
 
-    def along(item):
-        one, two, three = [hop(item, ALONG_Z, swap=bits) for bits in (1, 2, 3)]
-        both = in_order(in_order(item, one, low), in_order(two, three, low), high)
+    def pairs(item):
+        both = in_order(item, hop(item, ALONG_Z, swap=2), high)
         return both.reshape(-1, *both.shape[2:])
 
     return [
         lambda item: start_gather([[part]], [[item]], place)[0],
-        along,
+        lambda item: in_order(item, hop(item, ALONG_Z, swap=1), low),
+        pairs,
         lambda item: jnp.stack([item, hop(item, NEAR)]),
         lambda item: [item, hop(item, FAR), hop(item, ACROSS)],
         lambda items: items + [hop(items[1], ACROSS)],
@@ -1156,7 +1160,7 @@
         if tick < count:
             dealt, state = steps[tick](state)
             held.append(dealt)
-            todo.append(scatter_stages(place, tick >= count - 2))
+            todo.append(scatter_stages(place, tick >= count - 3))
     return (held, piece, state)
 
 

time: 558 us -> 552 us (0.989)
  local copies, waits for them, and re-layouts: 80 us -> 66.5 us
  other arithmetic: 48 us -> 58.8 us
    squeeze x10 -> x0, local copies, waits for them, and re-layouts: 9.44 us -> none  [near(): return [own, from_core[0, 0], from_far[0], from_near]]
    add x13 -> x12, other arithmetic: 4.75 us -> 12.3 us  [add_up(): total = total + term.astype(jnp.float32)]
    unnamed x261 -> x223, local copies, waits for them, and re-layouts: 41.7 us -> 37.7 us
    another operation x48 -> x49, other arithmetic: 14.7 us -> 15.6 us  [in_order(): return jnp.stack([first, second])]
  transfers between devices with their start and end apart: 85 -> 85, of which waited for: 37 -> 40; matrix products, arithmetic and copies ran while one was open for 13% -> 13% of each run, Pallas kernels for 24% -> 25%
where the time goes in v9:
time: 552 us; the launch traced here: 547 us
  waiting for transfers between devices  190 us (34%)
  Pallas kernels  158 us (29%)
  starting transfers between devices  69.4 us (13%)
  local copies, waits for them, and re-layouts  66.5 us (12%)
  other arithmetic  58.8 us (11%)
    ppermute x85, waiting for transfers between devices, send(): return lax.ppermute(array, AXES, pairs)  190 us
    ppermute x85, starting transfers between devices, send(): return lax.ppermute(array, AXES, pairs)  69.4 us
    pallas_call x4, Pallas kernels, block_forward(): pl.pallas_call(functools.partial(forward_kernel, count, keep, parts, skip...  66.4 us
    pallas_call x5, Pallas kernels, back_call(): pl.pallas_call(functools.partial(back_kernel, body, parts, tuned, counts)...  56.3 us
    unnamed x223, local copies, waits for them, and re-layouts  37.7 us
    another operation x49, other arithmetic, in_order(): return jnp.stack([first, second])  15.6 us
    convert_element_type x10, other arithmetic, low_add(): return add_up(*terms).astype(jnp.bfloat16)  14.5 us
    add x12, other arithmetic, add_up(): total = total + term.astype(jnp.float32)  12.3 us
  transfers between devices with their start and end apart: 85, of which 40 were waited for; matrix products, arithmetic and copies ran while one was open for 13% of the time, Pallas kernels for 25%

profile of v9, /device:TPU:0, one launch (start us, length us, event | category | flops | bytes accessed | tf_op | source)
XLA Modules:
  0.0 546.8 jit_solution(8850740699105619159)
XLA Ops:
  9.8 3.0 collective-permute-start.3
  12.8 2.6 collective-permute-start.4
  22.4 3.9 collective-permute-done.3
  26.4 9.9 %collective-permute-done.4 = bf16[2,144,512]{2,1,0:T(8,128)(2,1)} collective-permute-done((bf16[2,144,512]{2,1,0:T(8,128)(2,1)S(1)}, bf16[2,144,512]{2,1,0:T(8,128)(2,1)}, u32[]{:S(2)}, u32[]{:S(2)}) %collective-permute-start.4) | collective-permute-done | bytes 294944 | tf_op jit(solution)/shard_map/ppermute | solution.py:797
  42.1 4.7 collective-permute-start.8
  46.8 17.2 %collective-permute-done.7 = bf16[2,96,512]{2,1,0:T(8,128)(2,1)S(1)} collective-permute-done((bf16[2,96,512]{2,1,0:T(8,128)(2,1)S(1)}, bf16[2,96,512]{2,1,0:T(8,128)(2,1)S(1)}, u32[]{:S(2)}, u32[]{:S(2)}) %collective-permute-start.7) | collective-permute-done | bytes 196640 | tf_op jit(solution)/shard_map/ppermute | solution.py:797
  64.1 10.4 %collective-permute-done.8 = bf16[2,2,160,512]{3,2,1,0:T(8,128)(2,1)S(1)} collective-permute-done((bf16[2,2,160,512]{3,2,1,0:T(8,128)(2,1)S(1)}, bf16[2,2,160,512]{3,2,1,0:T(8,128)(2,1)S(1)}, u32[]{:S(2)}, u32[]{:S(2)}) %collective-permute-start.8) | collective-permute-done | bytes 655392 | tf_op jit(solution)/shard_map/ppermute | solution.py:797
  79.6 24.3 %collective-permute-done.11 = bf16[2,2,96,512]{3,2,1,0:T(8,128)(2,1)S(1)} collective-permute-done((bf16[2,2,96,512]{3,2,1,0:T(8,128)(2,1)S(1)}, bf16[2,2,96,512]{3,2,1,0:T(8,128)(2,1)S(1)}, u32[]{:S(2)}, u32[]{:S(2)}) %collective-permute-start.11) | collective-permute-done | bytes 393248 | tf_op jit(solution)/shard_map/ppermute | solution.py:797
  107.5 10.5 %collective-permute-done.13.refs_1_.refs_5_ = bf16[2,4,2,144,512]{4,3,2,1,0:T(8,128)(2,1)} collective-permute-done((bf16[2,4,2,144,512]{4,3,2,1,0:T(8,128)(2,1)S(1)}, bf16[2,4,2,144,512]{4,3,2,1,0:T(8,128)(2,1)}, u32[]{:S(2)}, u32[]{:S(2)}) %collective-permute-start.13) | collective-permute-done | bytes 2359328 | tf_op jit(solution)/shard_map/ppermute | solution.py:797
  128.8 25.0 %collective-permute-done.15 = bf16[2,2,160,512]{3,2,1,0:T(8,128)(2,1)} collective-permute-done((bf16[2,2,160,512]{3,2,1,0:T(8,128)(2,1)}, bf16[2,2,160,512]{3,2,1,0:T(8,128)(2,1)}, u32[]{:S(2)}, u32[]{:S(2)}) %collective-permute-start.15) | collective-permute-done | bytes 655392 | tf_op jit(solution)/shard_map/ppermute | solution.py:797
  156.4 2.5 pad_maximum_fusion.4.refs_0_
  170.0 15.8 %block_forward.4.refs_1_ = f32[384,2048]{1,0:T(8,128)} custom-call(s32[5]{0:T(128)S(1)} %stack.339.place.refs_0_, bf16[384,256]{1,0:T(8,128)(2,1)S(1)} %bitcast.412, bf16[2,256,512]{2,1,0:T(8,128)(2,1)S(1)} %add_convert_fusion.refs_2_.refs_6_, f32[1,6144]{1,0:T(1,128)S(1)} %slice.253.refs_3_, ...), custom_call_target="tpu_custom_call" | custom-call | flops 1024 | bytes 1024 | tf_op jit(solution)/shard_map/block_forward/pallas_call | solution.py:248
  187.4 4.5 collective-permute-done.20
  204.0 15.6 %block_forward.5.stream = f32[384,2048]{1,0:T(8,128)} custom-call(s32[5]{0:T(128)S(1)} %stack.339.place.refs_0_, f32[384,2048]{1,0:T(8,128)} %block_forward.4.refs_1_, f32[1,6144]{1,0:T(1,128)S(1)} %slice.254.refs_2_, bf16[1152,128]{1,0:T(8,128)(2,1)S(1)} %convert_element_type.414.refs_4_.refs_3_.refs_6_, bf16[2,4,2,144,512]{4,3,2,1,0:T(8,128)(2,1)S(1)} %copy-done.2, ...), custom_call_target="tpu_custom_call" | custom-call | flops 1024 | bytes 1024 | tf_op jit(solution)/shard_map/block_forward/pallas_call | solution.py:248
  221.6 4.5 head_target.1.target
  230.8 10.7 %collective-permute-done.28.refs_6_.refs_1_ = bf16[2,4,2,160,512]{4,3,2,1,0:T(8,128)(2,1)} collective-permute-done((bf16[2,4,2,160,512]{4,3,2,1,0:T(8,128)(2,1)S(1)}, bf16[2,4,2,160,512]{4,3,2,1,0:T(8,128)(2,1)}, u32[]{:S(2)}, u32[]{:S(2)}) %collective-permute-start.28) | collective-permute-done | bytes 2621472 | tf_op jit(solution)/shard_map/ppermute | solution.py:797
  243.8 2.8 collective-permute-done.31.refs_8_.refs_3_
  250.6 18.0 %block_forward.6 = (f32[384,2048]{1,0:T(8,128)}, f32[384,2048]{1,0:T(8,128)}, f32[384,512]{1,0:T(8,128)S(1)}, f32[384,512]{1,0:T(8,128)S(1)}, f32[384,2048]{1,0:...) custom-call(s32[5]{0:T(128)S(1)} %stack.339.place.refs_0_, ...), custom_call_target="tpu_custom_call" | custom-call | flops 1024 | bytes 1024 | tf_op jit(solution)/shard_map/block_forward/pallas_call | solution.py:248
  272.7 6.1 %collective-permute-done.32.refs_5_ = bf16[2,4,2,144,512]{4,3,2,1,0:T(8,128)(2,1)S(1)} collective-permute-done((bf16[2,4,2,144,512]{4,3,2,1,0:T(8,128)(2,1)S(1)}, bf16[2,4,2,144,512]{4,3,2,1,0:T(8,128)(2,1)S(1)}, u32[]{:S(2)}, u32[]{:S(2)}) %collective-permute-start.32) | collective-permute-done | bytes 2359328 | tf_op jit(solution)/shard_map/ppermute | solution.py:797
  280.4 2.9 collective-permute-done.36.refs_7_
  284.7 17.0 %block_forward.7 = (f32[384,2048]{1,0:T(8,128)}, f32[384,512]{1,0:T(8,128)S(1)}, f32[384,512]{1,0:T(8,128)S(1)}, f32[384,2048]{1,0:T(8,128)}, f32[8,3072]{1,0:T(...) custom-call(s32[5]{0:T(128)S(1)} %stack.339.place.refs_0_, ...), custom_call_target="tpu_custom_call" | custom-call | flops 1024 | bytes 1024 | tf_op jit(solution)/shard_map/block_forward/pallas_call | solution.py:248
  308.4 3.4 collective-permute-done.37.refs_3_
  313.2 10.9 %head_loss.1 = (f32[1,1]{1,0:T(1,128)}, f32[384,2048]{1,0:T(8,128)}, bf16[1,2048,128]{2,1,0:T(8,128)(2,1)S(1)}, bf16[64,512]{1,0:T(8,128)(2,1)S(1)}) custom-call(s32[5]{0:T(128)S(1)} %stack.339.place.refs_0_, f32[384,2048]{1,0:T(8,128)} %get-tuple-element.550.stream, bf16[2048,128]{1,0:T(8,128)(2,1)S(1)} %bitcast.402, f32[8,128]{1,0:T(8,128)S(1)} %head_target.1.target, ...), custom_call_target="tpu_custom_call" | custom-call | flops 1024 | bytes 1024 | tf_op jit(solution)/shard_map/head_loss/pallas_call | solution.py:691
  329.7 11.2 %back_out.1 = (f32[384,2048]{1,0:T(8,128)S(1)}, bf16[384,512]{1,0:T(8,128)(2,1)S(1)}, f32[1,5120]{1,0:T(1,128)S(1)}, bf16[2,2,4,2,32,512]{5,4,3,2,1,0:T(8,128)(2...) custom-call(s32[5]{0:T(128)S(1)} %stack.339.place.refs_0_, ...), custom_call_target="tpu_custom_call" | custom-call | flops 1024 | bytes 1024 | tf_op jit(solution)/shard_map/back_out/pallas_call | solution.py:414
  342.8 2.5 collective-permute-done.39
  346.6 9.8 %back_mid.2 = (bf16[384,512]{1,0:T(8,128)(2,1)S(1)}, f32[1,1024]{1,0:T(1,128)S(1)}, bf16[2,2,4,2,80,512]{5,4,3,2,1,0:T(8,128)(2,1)S(1)}, bf16[2,4,2,80,512]{4,3,...) custom-call(s32[5]{0:T(128)S(1)} %stack.339.place.refs_0_, ...), custom_call_target="tpu_custom_call" | custom-call | flops 1024 | bytes 1024 | tf_op jit(solution)/shard_map/back_mid/pallas_call | solution.py:414
  356.8 4.7 collective-permute-done.43
  366.9 16.5 %back_between.1 = (f32[384,2048]{1,0:T(8,128)}, bf16[384,512]{1,0:T(8,128)(2,1)S(1)}, f32[1,5120]{1,0:T(1,128)S(1)}, bf16[2,2,4,2,64,512]{5,4,3,2,1,0:T(8,128)(2...) custom-call(s32[5]{0:T(128)S(1)} %stack.339.place.refs_0_, ...), custom_call_target="tpu_custom_call" | custom-call | flops 1024 | bytes 1024 | tf_op jit(solution)/shard_map/back_between/pallas_call | solution.py:414
  384.5 4.1 collective-permute-done.48
  397.7 10.6 %back_mid.3 = (bf16[384,512]{1,0:T(8,128)(2,1)S(1)}, f32[1,1024]{1,0:T(1,128)S(1)}, bf16[2,2,4,2,80,512]{5,4,3,2,1,0:T(8,128)(2,1)}, bf16[2,4,2,80,512]{4,3,2,1,...) custom-call(s32[5]{0:T(128)S(1)} %stack.339.place.refs_0_, ...), custom_call_target="tpu_custom_call" | custom-call | flops 1024 | bytes 1024 | tf_op jit(solution)/shard_map/back_mid/pallas_call | solution.py:414
  410.7 3.6 collective-permute-done.50
  417.5 2.4 fusion.11
  423.1 3.3 fusion
  429.9 3.1 collective-permute-done.51
  435.0 8.2 %back_first.1 = (bf16[2,2,4,2,64,512]{5,4,3,2,1,0:T(8,128)(2,1)}, bf16[2,4,2,64,512]{4,3,2,1,0:T(8,128)(2,1)S(1)}, bf16[4,2,64,512]{3,2,1,0:T(8,128)(2,1)S(1)}, bf16[4,2,64,512]{3,2,1,0:T(8,128)(2,1)S(1)}) custom-call(s32[5]{0:T(128)S(1)} %stack.339.place.refs_0_, bf16[384,512]{1,0:T(8,128)(2,1)S(1)} %copy-done.59, ...), custom_call_target="tpu_custom_call" | custom-call | flops 1024 | bytes 1024 | tf_op jit(solution)/shard_map/back_first/pallas_call | solution.py:414
  444.1 5.7 %collective-permute-done.52 = bf16[2,2,80,512]{3,2,1,0:T(8,128)(2,1)} collective-permute-done((bf16[2,2,80,512]{3,2,1,0:T(8,128)(2,1)}, bf16[2,2,80,512]{3,2,1,0:T(8,128)(2,1)}, u32[]{:S(2)}, u32[]{:S(2)}) %collective-permute-start.52) | collective-permute-done | bytes 327712 | tf_op jit(solution)/shard_map/ppermute | solution.py:797
  454.5 2.6 collective-permute-start.61
  462.8 4.7 collective-permute-done.61
  469.3 3.5 collective-permute-done.59
  473.6 2.4 fusion.9
  483.8 3.0 own_heads.1
  489.2 5.2 collective-permute-done.70
  497.6 3.4 collective-permute-start.74
  506.5 4.0 concatenate.90
  513.6 7.7 %directions.1 = (f32[8,128]{1,0:T(8,128)S(1)}, f32[1,115648]{1,0:T(1,128)}, f32[1,115648]{1,0:T(1,128)}, f32[1,115648]{1,0:T(1,128)S(1)}, f32[2,139456]{1,0:T(2,...) custom-call(f32[64,512]{1,0:T(8,128)S(1)} %bitcast.414, f32[160,512]{1,0:T(8,128)S(1)} %bitcast.407, ...), custom_call_target="tpu_custom_call" | custom-call | flops 1024 | bytes 1024 | tf_op jit(solution)/shard_map/directions/pallas_call | solution.py:1320
  530.8 2.7 collective-permute-start.83
  535.1 3.8 collective-permute-done.84
  539.5 4.7 update.1
  (594 shorter events, 183.5 us)
Async XLA Ops:
  9.8 16.6 %collective-permute-start.3 = (bf16[2,144,512]{2,1,0:T(8,128)(2,1)S(1)}, bf16[2,144,512]{2,1,0:T(8,128)(2,1)}, u32[]{:S(2)}, u32[]{:S(2)}) collective-permute-start(bf16[2,144,512]{2,1,0:T(8,128)(2,1)S(1)} %pad_maximum_fusion.27), channel_id=1, source_target_pairs={{0,8},{1,9},{2,10},{3,11},{4,12},{5,13},{6,14},{7,15},{8,0},{9,1},... | collective-permute-start | bytes 884744 | tf_op jit(solution)/shard_map/ppermute | solution.py:797
  12.8 23.6 %collective-permute-start.4 = (bf16[2,144,512]{2,1,0:T(8,128)(2,1)S(1)}, bf16[2,144,512]{2,1,0:T(8,128)(2,1)}, u32[]{:S(2)}, u32[]{:S(2)}) collective-permute-start(bf16[2,144,512]{2,1,0:T(8,128)(2,1)S(1)} %pad_maximum_fusion.27), channel_id=1, source_target_pairs={{0,16},{1,17},{2,18},{3,19},{4,20},{5,21},{6,22},{7,23},{8,24},{9,... | collective-permute-start | bytes 884744 | tf_op jit(solution)/shard_map/ppermute | solution.py:797
  15.3 21.0 %collective-permute-start.5 = (bf16[2,144,512]{2,1,0:T(8,128)(2,1)S(1)}, bf16[2,144,512]{2,1,0:T(8,128)(2,1)}, u32[]{:S(2)}, u32[]{:S(2)}) collective-permute-start(bf16[2,144,512]{2,1,0:T(8,128)(2,1)S(1)} %pad_maximum_fusion.27), channel_id=1, source_target_pairs={{0,24},{1,25},{2,26},{3,27},{4,28},{5,29},{6,30},{7,31},{8,16},{9,... | collective-permute-start | bytes 884744 | tf_op jit(solution)/shard_map/ppermute | solution.py:797
  18.9 20.8 %collective-permute-start.2 = (bf16[2,160,512]{2,1,0:T(8,128)(2,1)S(1)}, bf16[2,160,512]{2,1,0:T(8,128)(2,1)S(1)}, u32[]{:S(2)}, u32[]{:S(2)}) collective-permute-start(bf16[2,160,512]{2,1,0:T(8,128)(2,1)S(1)} %pad_maximum_fusion.22), channel_id=1, source_target_pairs={{0,8},{1,9},{2,10},{3,11},{4,12},{5,13},{6,14},{7,15},{8,0},{9,1},... | collective-permute-start | bytes 983048 | tf_op jit(solution)/shard_map/ppermute | solution.py:797
  22.4 17.5 %collective-permute-start.6 = (bf16[496,512]{1,0:T(8,128)(2,1)S(1)}, bf16[496,512]{1,0:T(8,128)(2,1)S(1)}, u32[]{:S(2)}, u32[]{:S(2)}) collective-permute-start(bf16[496,512]{1,0:T(8,128)(2,1)S(1)} %pad_maximum_fusion.19), channel_id=1, source_target_pairs={{0,1},{1,0},{2,3},{3,2},{4,5},{5,4},{6,7},{7,6},{8,9},{9,8},{10,11... | collective-permute-start | bytes 1523720 | tf_op jit(solution)/shard_map/ppermute | solution.py:797
  40.3 34.4 %collective-permute-start.9 = (bf16[4,2,144,512]{3,2,1,0:T(8,128)(2,1)S(1)}, bf16[4,2,144,512]{3,2,1,0:T(8,128)(2,1)S(1)}, u32[]{:S(2)}, u32[]{:S(2)}) collective-permute-start(bf16[4,2,144,512]{3,2,1,0:T(8,128)(2,1)S(1)} %bitcast.426), channel_id=1, source_target_pairs={{0,2},{1,5},{2,0},{3,7},{4,6},{5,1},{6,4},{7,3},{8,10},{9,13},{10,... | collective-permute-start | bytes 3538952 | tf_op jit(solution)/shard_map/ppermute | solution.py:797
  42.1 32.5 %collective-permute-start.8 = (bf16[2,2,160,512]{3,2,1,0:T(8,128)(2,1)S(1)}, bf16[2,2,160,512]{3,2,1,0:T(8,128)(2,1)S(1)}, u32[]{:S(2)}, u32[]{:S(2)}) collective-permute-start(bf16[2,2,160,512]{3,2,1,0:T(8,128)(2,1)S(1)} %pad_maximum_fusion.13), channel_id=1, source_target_pairs={{0,16},{1,17},{2,18},{3,19},{4,20},{5,21},{6,22},{7,23},{8,24},{9,... | collective-permute-start | bytes 1966088 | tf_op jit(solution)/shard_map/ppermute | solution.py:797
  46.8 17.2 %collective-permute-start.7 = (bf16[2,96,512]{2,1,0:T(8,128)(2,1)S(1)}, bf16[2,96,512]{2,1,0:T(8,128)(2,1)S(1)}, u32[]{:S(2)}, u32[]{:S(2)}) collective-permute-start(bf16[2,96,512]{2,1,0:T(8,128)(2,1)S(1)} %pad_maximum_fusion.32), channel_id=1, source_target_pairs={{0,8},{1,9},{2,10},{3,11},{4,12},{5,13},{6,14},{7,15},{8,0},{9,1},... | collective-permute-start | bytes 589832 | tf_op jit(solution)/shard_map/ppermute | solution.py:797
  75.0 43.1 %collective-permute-start.13 = (bf16[2,4,2,144,512]{4,3,2,1,0:T(8,128)(2,1)S(1)}, bf16[2,4,2,144,512]{4,3,2,1,0:T(8,128)(2,1)}, u32[]{:S(2)}, u32[]{:S(2)}) collective-permute-start(bf16[2,4,2,144,512]{4,3,2,1,0:T(8,128)(2,1)S(1)} %pad_maximum_fusion.2.refs_0_.refs_4_), channel_id=1, source_target_pairs={{0,4},{1,3},{2,6},{3,1},{4,0},{5,7},{6,2},{7,5},{8,12},{9,11},{10,... | collective-permute-start | bytes 7077896 | tf_op jit(solution)/shard_map/ppermute | solution.py:797
  75.6 42.5 %collective-permute-start.14 = (bf16[2,4,2,144,512]{4,3,2,1,0:T(8,128)(2,1)S(1)}, bf16[2,4,2,144,512]{4,3,2,1,0:T(8,128)(2,1)S(1)}, u32[]{:S(2)}, u32[]{:S(2)}) collective-permute-start(bf16[2,4,2,144,512]{4,3,2,1,0:T(8,128)(2,1)S(1)} %pad_maximum_fusion.2.refs_0_.refs_4_), channel_id=1, source_target_pairs={{0,1},{1,0},{2,3},{3,2},{4,5},{5,4},{6,7},{7,6},{8,9},{9,8},{10,11... | collective-permute-start | bytes 7077896 | tf_op jit(solution)/shard_map/ppermute | solution.py:797
  75.6 31.7 %collective-permute-start.12 = (bf16[4,2,160,512]{3,2,1,0:T(8,128)(2,1)S(1)}, bf16[4,2,160,512]{3,2,1,0:T(8,128)(2,1)S(1)}, u32[]{:S(2)}, u32[]{:S(2)}) collective-permute-start(bf16[4,2,160,512]{3,2,1,0:T(8,128)(2,1)S(1)} %bitcast.422), channel_id=1, source_target_pairs={{0,2},{1,5},{2,0},{3,7},{4,6},{5,1},{6,4},{7,3},{8,10},{9,13},{10,... | collective-permute-start | bytes 3932168 | tf_op jit(solution)/shard_map/ppermute | solution.py:797
  77.1 28.9 %collective-permute-start.10 = (bf16[2,400,512]{2,1,0:T(8,128)(2,1)S(1)}, bf16[2,400,512]{2,1,0:T(8,128)(2,1)S(1)}, u32[]{:S(2)}, u32[]{:S(2)}) collective-permute-start(bf16[2,400,512]{2,1,0:T(8,128)(2,1)S(1)} %pad_maximum_fusion.10), channel_id=1, source_target_pairs={{0,8},{1,9},{2,10},{3,11},{4,12},{5,13},{6,14},{7,15},{8,0},{9,1},... | collective-permute-start | bytes 2457608 | tf_op jit(solution)/shard_map/ppermute | solution.py:797
  77.2 26.6 %collective-permute-start.11 = (bf16[2,2,96,512]{3,2,1,0:T(8,128)(2,1)S(1)}, bf16[2,2,96,512]{3,2,1,0:T(8,128)(2,1)S(1)}, u32[]{:S(2)}, u32[]{:S(2)}) collective-permute-start(bf16[2,2,96,512]{3,2,1,0:T(8,128)(2,1)S(1)} %pad_maximum_fusion.20), channel_id=1, source_target_pairs={{0,16},{1,17},{2,18},{3,19},{4,20},{5,21},{6,22},{7,23},{8,24},{9,... | collective-permute-start | bytes 1179656 | tf_op jit(solution)/shard_map/ppermute | solution.py:797
  119.5 40.2 %collective-permute-start.18 = (bf16[2,4,2,160,512]{4,3,2,1,0:T(8,128)(2,1)S(1)}, bf16[2,4,2,160,512]{4,3,2,1,0:T(8,128)(2,1)}, u32[]{:S(2)}, u32[]{:S(2)}) collective-permute-start(bf16[2,4,2,160,512]{4,3,2,1,0:T(8,128)(2,1)S(1)} %pad_maximum_fusion.refs_0_.refs_5_), channel_id=1, source_target_pairs={{0,4},{1,3},{2,6},{3,1},{4,0},{5,7},{6,2},{7,5},{8,12},{9,11},{10,... | collective-permute-start | bytes 7864328 | tf_op jit(solution)/shard_map/ppermute | solution.py:797
  120.1 39.7 %collective-permute-start.19 = (bf16[2,4,2,160,512]{4,3,2,1,0:T(8,128)(2,1)S(1)}, bf16[2,4,2,160,512]{4,3,2,1,0:T(8,128)(2,1)}, u32[]{:S(2)}, u32[]{:S(2)}) collective-permute-start(bf16[2,4,2,160,512]{4,3,2,1,0:T(8,128)(2,1)S(1)} %pad_maximum_fusion.refs_0_.refs_5_), channel_id=1, source_target_pairs={{0,1},{1,0},{2,3},{3,2},{4,5},{5,4},{6,7},{7,6},{8,9},{9,8},{10,11... | collective-permute-start | bytes 7864328 | tf_op jit(solution)/shard_map/ppermute | solution.py:797
  122.1 31.7 %collective-permute-start.17 = (bf16[4,2,96,512]{3,2,1,0:T(8,128)(2,1)S(1)}, bf16[4,2,96,512]{3,2,1,0:T(8,128)(2,1)}, u32[]{:S(2)}, u32[]{:S(2)}) collective-permute-start(bf16[4,2,96,512]{3,2,1,0:T(8,128)(2,1)S(1)} %bitcast.430), channel_id=1, source_target_pairs={{0,2},{1,5},{2,0},{3,7},{4,6},{5,1},{6,4},{7,3},{8,10},{9,13},{10,... | collective-permute-start | bytes 2359304 | tf_op jit(solution)/shard_map/ppermute | solution.py:797
  122.7 31.1 %collective-permute-start.15 = (bf16[2,2,160,512]{3,2,1,0:T(8,128)(2,1)}, bf16[2,2,160,512]{3,2,1,0:T(8,128)(2,1)}, u32[]{:S(2)}, u32[]{:S(2)}) collective-permute-start(bf16[2,2,160,512]{3,2,1,0:T(8,128)(2,1)} %pad_maximum_fusion.14), channel_id=1, source_target_pairs={{0,16},{1,17},{2,18},{3,19},{4,20},{5,21},{6,22},{7,23},{8,24},{9,... | collective-permute-start | bytes 1966088 | tf_op jit(solution)/shard_map/ppermute | solution.py:797
  160.5 32.0 %collective-permute-start.22 = (bf16[4,2,160,512]{3,2,1,0:T(8,128)(2,1)}, bf16[4,2,160,512]{3,2,1,0:T(8,128)(2,1)}, u32[]{:S(2)}, u32[]{:S(2)}) collective-permute-start(bf16[4,2,160,512]{3,2,1,0:T(8,128)(2,1)} %bitcast.67), channel_id=1, source_target_pairs={{0,2},{1,5},{2,0},{3,7},{4,6},{5,1},{6,4},{7,3},{8,10},{9,13},{10,... | collective-permute-start | bytes 3932168 | tf_op jit(solution)/shard_map/ppermute | solution.py:797
  162.2 34.9 %collective-permute-start.23 = (bf16[2,4,2,96,512]{4,3,2,1,0:T(8,128)(2,1)}, bf16[2,4,2,96,512]{4,3,2,1,0:T(8,128)(2,1)}, u32[]{:S(2)}, u32[]{:S(2)}) collective-permute-start(bf16[2,4,2,96,512]{4,3,2,1,0:T(8,128)(2,1)} %pad_maximum_fusion.4.refs_0_), channel_id=1, source_target_pairs={{0,4},{1,3},{2,6},{3,1},{4,0},{5,7},{6,2},{7,5},{8,12},{9,11},{10,... | collective-permute-start | bytes 4718600 | tf_op jit(solution)/shard_map/ppermute | solution.py:797
  162.7 34.3 %collective-permute-start.24 = (bf16[2,4,2,96,512]{4,3,2,1,0:T(8,128)(2,1)}, bf16[2,4,2,96,512]{4,3,2,1,0:T(8,128)(2,1)}, u32[]{:S(2)}, u32[]{:S(2)}) collective-permute-start(bf16[2,4,2,96,512]{4,3,2,1,0:T(8,128)(2,1)} %pad_maximum_fusion.4.refs_0_), channel_id=1, source_target_pairs={{0,1},{1,0},{2,3},{3,2},{4,5},{5,4},{6,7},{7,6},{8,9},{9,8},{10,11... | collective-permute-start | bytes 4718600 | tf_op jit(solution)/shard_map/ppermute | solution.py:797
  163.1 28.8 %collective-permute-start.20 = (bf16[2,2,144,512]{3,2,1,0:T(8,128)(2,1)}, bf16[2,2,144,512]{3,2,1,0:T(8,128)(2,1)}, u32[]{:S(2)}, u32[]{:S(2)}) collective-permute-start(bf16[2,2,144,512]{3,2,1,0:T(8,128)(2,1)} %pad_maximum_fusion.17), channel_id=1, source_target_pairs={{0,16},{1,17},{2,18},{3,19},{4,20},{5,21},{6,22},{7,23},{8,24},{9,... | collective-permute-start | bytes 1769480 | tf_op jit(solution)/shard_map/ppermute | solution.py:797
  197.0 44.5 %collective-permute-start.28 = (bf16[2,4,2,160,512]{4,3,2,1,0:T(8,128)(2,1)S(1)}, bf16[2,4,2,160,512]{4,3,2,1,0:T(8,128)(2,1)}, u32[]{:S(2)}, u32[]{:S(2)}) collective-permute-start(bf16[2,4,2,160,512]{4,3,2,1,0:T(8,128)(2,1)S(1)} %pad_maximum_fusion.1.refs_5_.refs_0_), channel_id=1, source_target_pairs={{0,4},{1,3},{2,6},{3,1},{4,0},{5,7},{6,2},{7,5},{8,12},{9,11},{10,... | collective-permute-start | bytes 7864328 | tf_op jit(solution)/shard_map/ppermute | solution.py:797
  198.0 43.5 %collective-permute-start.29 = (bf16[2,4,2,160,512]{4,3,2,1,0:T(8,128)(2,1)S(1)}, bf16[2,4,2,160,512]{4,3,2,1,0:T(8,128)(2,1)}, u32[]{:S(2)}, u32[]{:S(2)}) collective-permute-start(bf16[2,4,2,160,512]{4,3,2,1,0:T(8,128)(2,1)S(1)} %pad_maximum_fusion.1.refs_5_.refs_0_), channel_id=1, source_target_pairs={{0,1},{1,0},{2,3},{3,2},{4,5},{5,4},{6,7},{7,6},{8,9},{9,8},{10,11... | collective-permute-start | bytes 7864328 | tf_op jit(solution)/shard_map/ppermute | solution.py:797
  198.0 21.6 %collective-permute-start.26 = (bf16[2,4,2,96,512]{4,3,2,1,0:T(8,128)(2,1)}, bf16[2,4,2,96,512]{4,3,2,1,0:T(8,128)(2,1)}, u32[]{:S(2)}, u32[]{:S(2)}) collective-permute-start(bf16[2,4,2,96,512]{4,3,2,1,0:T(8,128)(2,1)} %collective-permute-done.23.refs_1_), channel_id=1, source_target_pairs={{0,1},{1,0},{2,3},{3,2},{4,5},{5,4},{6,7},{7,6},{8,9},{9,8},{10,11... | collective-permute-start | bytes 4718600 | tf_op jit(solution)/shard_map/ppermute | solution.py:797
  198.6 29.2 %collective-permute-start.27 = (bf16[4,2,144,512]{3,2,1,0:T(8,128)(2,1)}, bf16[4,2,144,512]{3,2,1,0:T(8,128)(2,1)}, u32[]{:S(2)}, u32[]{:S(2)}) collective-permute-start(bf16[4,2,144,512]{3,2,1,0:T(8,128)(2,1)} %bitcast.74), channel_id=1, source_target_pairs={{0,2},{1,5},{2,0},{3,7},{4,6},{5,1},{6,4},{7,3},{8,10},{9,13},{10,... | collective-permute-start | bytes 3538952 | tf_op jit(solution)/shard_map/ppermute | solution.py:797
  199.4 26.8 %collective-permute-start.25 = (bf16[2,2,96,512]{3,2,1,0:T(8,128)(2,1)}, bf16[2,2,96,512]{3,2,1,0:T(8,128)(2,1)}, u32[]{:S(2)}, u32[]{:S(2)}) collective-permute-start(bf16[2,2,96,512]{3,2,1,0:T(8,128)(2,1)} %pad_maximum_fusion.21), channel_id=1, source_target_pairs={{0,16},{1,17},{2,18},{3,19},{4,20},{5,21},{6,22},{7,23},{8,24},{9,... | collective-permute-start | bytes 1179656 | tf_op jit(solution)/shard_map/ppermute | solution.py:797
  241.5 37.3 %collective-permute-start.32 = (bf16[2,4,2,144,512]{4,3,2,1,0:T(8,128)(2,1)S(1)}, bf16[2,4,2,144,512]{4,3,2,1,0:T(8,128)(2,1)S(1)}, u32[]{:S(2)}, u32[]{:S(2)}) collective-permute-start(bf16[2,4,2,144,512]{4,3,2,1,0:T(8,128)(2,1)S(1)} %pad_maximum_fusion.3.refs_4_), channel_id=1, source_target_pairs={{0,4},{1,3},{2,6},{3,1},{4,0},{5,7},{6,2},{7,5},{8,12},{9,11},{10,... | collective-permute-start | bytes 7077896 | tf_op jit(solution)/shard_map/ppermute | solution.py:797
  242.5 36.3 %collective-permute-start.33 = (bf16[2,4,2,144,512]{4,3,2,1,0:T(8,128)(2,1)S(1)}, bf16[2,4,2,144,512]{4,3,2,1,0:T(8,128)(2,1)}, u32[]{:S(2)}, u32[]{:S(2)}) collective-permute-start(bf16[2,4,2,144,512]{4,3,2,1,0:T(8,128)(2,1)S(1)} %pad_maximum_fusion.3.refs_4_), channel_id=1, source_target_pairs={{0,1},{1,0},{2,3},{3,2},{4,5},{5,4},{6,7},{7,6},{8,9},{9,8},{10,11... | collective-permute-start | bytes 7077896 | tf_op jit(solution)/shard_map/ppermute | solution.py:797
  243.2 27.6 %collective-permute-start.30 = (bf16[4,2,96,512]{3,2,1,0:T(8,128)(2,1)S(1)}, bf16[4,2,96,512]{3,2,1,0:T(8,128)(2,1)}, u32[]{:S(2)}, u32[]{:S(2)}) collective-permute-start(bf16[4,2,96,512]{3,2,1,0:T(8,128)(2,1)S(1)} %bitcast.432), channel_id=1, source_target_pairs={{0,2},{1,5},{2,0},{3,7},{4,6},{5,1},{6,4},{7,3},{8,10},{9,13},{10,... | collective-permute-start | bytes 2359304 | tf_op jit(solution)/shard_map/ppermute | solution.py:797
  278.8 27.9 %collective-permute-start.34 = (bf16[2,4,2,96,512]{4,3,2,1,0:T(8,128)(2,1)S(1)}, bf16[2,4,2,96,512]{4,3,2,1,0:T(8,128)(2,1)}, u32[]{:S(2)}, u32[]{:S(2)}) collective-permute-start(bf16[2,4,2,96,512]{4,3,2,1,0:T(8,128)(2,1)S(1)} %pad_maximum_fusion.5.refs_0_), channel_id=1, source_target_pairs={{0,4},{1,3},{2,6},{3,1},{4,0},{5,7},{6,2},{7,5},{8,12},{9,11},{10,... | collective-permute-start | bytes 4718600 | tf_op jit(solution)/shard_map/ppermute | solution.py:797
  279.8 26.9 %collective-permute-start.35 = (bf16[2,4,2,96,512]{4,3,2,1,0:T(8,128)(2,1)S(1)}, bf16[2,4,2,96,512]{4,3,2,1,0:T(8,128)(2,1)S(1)}, u32[]{:S(2)}, u32[]{:S(2)}) collective-permute-start(bf16[2,4,2,96,512]{4,3,2,1,0:T(8,128)(2,1)S(1)} %pad_maximum_fusion.5.refs_0_), channel_id=1, source_target_pairs={{0,1},{1,0},{2,3},{3,2},{4,5},{5,4},{6,7},{7,6},{8,9},{9,8},{10,11... | collective-permute-start | bytes 4718600 | tf_op jit(solution)/shard_map/ppermute | solution.py:797
  324.7 17.8 %collective-permute-start.38 = (bf16[32,512]{1,0:T(8,128)(2,1)S(1)}, bf16[32,512]{1,0:T(8,128)(2,1)S(1)}, u32[]{:S(2)}, u32[]{:S(2)}) collective-permute-start(bf16[32,512]{1,0:T(8,128)(2,1)S(1)} %dynamic-slice_bitcast_fusion.12), channel_id=1, source_target_pairs={{0,1},{1,0},{2,3},{3,2},{4,5},{5,4},{6,7},{7,6},{8,9},{9,8},{10,11... | collective-permute-start | bytes 98312 | tf_op jit(solution)/shard_map/ppermute | solution.py:797
  361.9 22.5 %collective-permute-start.44 = (bf16[2,4,2,80,512]{4,3,2,1,0:T(8,128)(2,1)S(1)}, bf16[2,4,2,80,512]{4,3,2,1,0:T(8,128)(2,1)S(1)}, u32[]{:S(2)}, u32[]{:S(2)}) collective-permute-start(bf16[2,4,2,80,512]{4,3,2,1,0:T(8,128)(2,1)S(1)} %fusion.1), channel_id=1, source_target_pairs={{0,4},{1,3},{2,6},{3,1},{4,0},{5,7},{6,2},{7,5},{8,12},{9,11},{10,... | collective-permute-start | bytes 3932168 | tf_op jit(solution)/shard_map/ppermute | solution.py:797
  363.0 20.5 %collective-permute-start.45 = (bf16[2,2,32,512]{3,2,1,0:T(8,128)(2,1)S(1)}, bf16[2,2,32,512]{3,2,1,0:T(8,128)(2,1)S(1)}, u32[]{:S(2)}, u32[]{:S(2)}) collective-permute-start(bf16[2,2,32,512]{3,2,1,0:T(8,128)(2,1)S(1)} %pad_maximum_fusion.34), channel_id=1, source_target_pairs={{0,16},{1,17},{2,18},{3,19},{4,20},{5,21},{6,22},{7,23},{8,24},{9,... | collective-permute-start | bytes 393224 | tf_op jit(solution)/shard_map/ppermute | solution.py:797
  365.4 19.0 %collective-permute-start.42 = (bf16[4,2,32,512]{3,2,1,0:T(8,128)(2,1)S(1)}, bf16[4,2,32,512]{3,2,1,0:T(8,128)(2,1)S(1)}, u32[]{:S(2)}, u32[]{:S(2)}) collective-permute-start(bf16[4,2,32,512]{3,2,1,0:T(8,128)(2,1)S(1)} %fusion.17), channel_id=1, source_target_pairs={{0,2},{1,5},{2,0},{3,7},{4,6},{5,1},{6,4},{7,3},{8,10},{9,13},{10,... | collective-permute-start | bytes 786440 | tf_op jit(solution)/shard_map/ppermute | solution.py:797
  390.3 24.9 %collective-permute-start.49 = (bf16[2,4,2,64,512]{4,3,2,1,0:T(8,128)(2,1)}, bf16[2,4,2,64,512]{4,3,2,1,0:T(8,128)(2,1)}, u32[]{:S(2)}, u32[]{:S(2)}) collective-permute-start(bf16[2,4,2,64,512]{4,3,2,1,0:T(8,128)(2,1)} %fusion.3), channel_id=1, source_target_pairs={{0,4},{1,3},{2,6},{3,1},{4,0},{5,7},{6,2},{7,5},{8,12},{9,11},{10,... | collective-permute-start | bytes 3145736 | tf_op jit(solution)/shard_map/ppermute | solution.py:797
  391.9 22.5 %collective-permute-start.47 = (bf16[4,2,80,512]{3,2,1,0:T(8,128)(2,1)}, bf16[4,2,80,512]{3,2,1,0:T(8,128)(2,1)}, u32[]{:S(2)}, u32[]{:S(2)}) collective-permute-start(bf16[4,2,80,512]{3,2,1,0:T(8,128)(2,1)} %fusion.7), channel_id=1, source_target_pairs={{0,2},{1,5},{2,0},{3,7},{4,6},{5,1},{6,4},{7,3},{8,10},{9,13},{10,... | collective-permute-start | bytes 1966088 | tf_op jit(solution)/shard_map/ppermute | solution.py:797
  393.4 21.0 %collective-permute-start.50 = (bf16[4,2,32,512]{3,2,1,0:T(8,128)(2,1)}, bf16[4,2,32,512]{3,2,1,0:T(8,128)(2,1)S(1)}, u32[]{:S(2)}, u32[]{:S(2)}) collective-permute-start(bf16[4,2,32,512]{3,2,1,0:T(8,128)(2,1)} %bitcast.443), channel_id=1, source_target_pairs={{0,2},{1,5},{2,0},{3,7},{4,6},{5,1},{6,4},{7,3},{8,10},{9,13},{10,... | collective-permute-start | bytes 786440 | tf_op jit(solution)/shard_map/ppermute | solution.py:797
  395.2 19.2 %collective-permute-start.46 = (bf16[2,2,32,512]{3,2,1,0:T(8,128)(2,1)S(1)}, bf16[2,2,32,512]{3,2,1,0:T(8,128)(2,1)}, u32[]{:S(2)}, u32[]{:S(2)}) collective-permute-start(bf16[2,2,32,512]{3,2,1,0:T(8,128)(2,1)S(1)} %fusion.29), channel_id=1, source_target_pairs={{0,16},{1,17},{2,18},{3,19},{4,20},{5,21},{6,22},{7,23},{8,24},{9,... | collective-permute-start | bytes 393224 | tf_op jit(solution)/shard_map/ppermute | solution.py:797
  415.3 34.5 %collective-permute-start.56 = (bf16[2,4,2,32,512]{4,3,2,1,0:T(8,128)(2,1)S(1)}, bf16[2,4,2,32,512]{4,3,2,1,0:T(8,128)(2,1)}, u32[]{:S(2)}, u32[]{:S(2)}) collective-permute-start(bf16[2,4,2,32,512]{4,3,2,1,0:T(8,128)(2,1)S(1)} %pad_maximum_fusion.18.refs_0_), channel_id=1, source_target_pairs={{0,4},{1,3},{2,6},{3,1},{4,0},{5,7},{6,2},{7,5},{8,12},{9,11},{10,... | collective-permute-start | bytes 1572872 | tf_op jit(solution)/shard_map/ppermute | solution.py:797
  415.8 34.0 %collective-permute-start.57 = (bf16[2,4,2,32,512]{4,3,2,1,0:T(8,128)(2,1)S(1)}, bf16[2,4,2,32,512]{4,3,2,1,0:T(8,128)(2,1)}, u32[]{:S(2)}, u32[]{:S(2)}) collective-permute-start(bf16[2,4,2,32,512]{4,3,2,1,0:T(8,128)(2,1)S(1)} %pad_maximum_fusion.18.refs_0_), channel_id=1, source_target_pairs={{0,1},{1,0},{2,3},{3,2},{4,5},{5,4},{6,7},{7,6},{8,9},{9,8},{10,11... | collective-permute-start | bytes 1572872 | tf_op jit(solution)/shard_map/ppermute | solution.py:797
  419.9 29.9 %collective-permute-start.53 = (bf16[4,2,64,512]{3,2,1,0:T(8,128)(2,1)}, bf16[4,2,64,512]{3,2,1,0:T(8,128)(2,1)}, u32[]{:S(2)}, u32[]{:S(2)}) collective-permute-start(bf16[4,2,64,512]{3,2,1,0:T(8,128)(2,1)} %fusion.11), channel_id=1, source_target_pairs={{0,2},{1,5},{2,0},{3,7},{4,6},{5,1},{6,4},{7,3},{8,10},{9,13},{10,... | collective-permute-start | bytes 1572872 | tf_op jit(solution)/shard_map/ppermute | solution.py:797
  426.4 23.5 %collective-permute-start.55 = (bf16[2,4,2,80,512]{4,3,2,1,0:T(8,128)(2,1)}, bf16[2,4,2,80,512]{4,3,2,1,0:T(8,128)(2,1)}, u32[]{:S(2)}, u32[]{:S(2)}) collective-permute-start(bf16[2,4,2,80,512]{4,3,2,1,0:T(8,128)(2,1)} %fusion), channel_id=1, source_target_pairs={{0,4},{1,3},{2,6},{3,1},{4,0},{5,7},{6,2},{7,5},{8,12},{9,11},{10,... | collective-permute-start | bytes 3932168 | tf_op jit(solution)/shard_map/ppermute | solution.py:797
  433.0 16.8 %collective-permute-start.52 = (bf16[2,2,80,512]{3,2,1,0:T(8,128)(2,1)}, bf16[2,2,80,512]{3,2,1,0:T(8,128)(2,1)}, u32[]{:S(2)}, u32[]{:S(2)}) collective-permute-start(bf16[2,2,80,512]{3,2,1,0:T(8,128)(2,1)} %fusion.18), channel_id=1, source_target_pairs={{0,16},{1,17},{2,18},{3,19},{4,20},{5,21},{6,22},{7,23},{8,24},{9,... | collective-permute-start | bytes 983048 | tf_op jit(solution)/shard_map/ppermute | solution.py:797
  451.6 21.2 %collective-permute-start.63 = (bf16[4,2,80,512]{3,2,1,0:T(8,128)(2,1)S(1)}, bf16[4,2,80,512]{3,2,1,0:T(8,128)(2,1)S(1)}, u32[]{:S(2)}, u32[]{:S(2)}) collective-permute-start(bf16[4,2,80,512]{3,2,1,0:T(8,128)(2,1)S(1)} %fusion.5), channel_id=1, source_target_pairs={{0,2},{1,5},{2,0},{3,7},{4,6},{5,1},{6,4},{7,3},{8,10},{9,13},{10,... | collective-permute-start | bytes 1966088 | tf_op jit(solution)/shard_map/ppermute | solution.py:797
  458.7 14.9 %collective-permute-start.65 = (bf16[2,4,2,64,512]{4,3,2,1,0:T(8,128)(2,1)S(1)}, bf16[2,4,2,64,512]{4,3,2,1,0:T(8,128)(2,1)S(1)}, u32[]{:S(2)}, u32[]{:S(2)}) collective-permute-start(bf16[2,4,2,64,512]{4,3,2,1,0:T(8,128)(2,1)S(1)} %fusion.2), channel_id=1, source_target_pairs={{0,4},{1,3},{2,6},{3,1},{4,0},{5,7},{6,2},{7,5},{8,12},{9,11},{10,... | collective-permute-start | bytes 3145736 | tf_op jit(solution)/shard_map/ppermute | solution.py:797
  476.0 18.4 %collective-permute-start.72 = (bf16[4,2,64,512]{3,2,1,0:T(8,128)(2,1)}, bf16[4,2,64,512]{3,2,1,0:T(8,128)(2,1)S(1)}, u32[]{:S(2)}, u32[]{:S(2)}) collective-permute-start(bf16[4,2,64,512]{3,2,1,0:T(8,128)(2,1)} %fusion.9), channel_id=1, source_target_pairs={{0,2},{1,5},{2,0},{3,7},{4,6},{5,1},{6,4},{7,3},{8,10},{9,13},{10,... | collective-permute-start | bytes 1572872 | tf_op jit(solution)/shard_map/ppermute | solution.py:797
  481.1 13.2 %collective-permute-start.70 = (bf16[2,80,512]{2,1,0:T(8,128)(2,1)}, bf16[2,80,512]{2,1,0:T(8,128)(2,1)}, u32[]{:S(2)}, u32[]{:S(2)}) collective-permute-start(bf16[2,80,512]{2,1,0:T(8,128)(2,1)} %get-tuple-element.786), channel_id=1, source_target_pairs={{0,16},{1,17},{2,18},{3,19},{4,20},{5,21},{6,22},{7,23},{8,24},{9,... | collective-permute-start | bytes 491528 | tf_op jit(solution)/shard_map/ppermute | solution.py:797
  (145 other events, 990.6 us)

commit v10 on v9

--- a/solution.py
+++ b/solution.py
@@ -107,7 +107,7 @@
     rstd[:, at] = lax.rsqrt(group_mean(sums[:, whole]) + 1e-05)
 
 
-def forward_kernel(count, keep, parts, skip, tuned, *refs):
+def forward_kernel(count, keep, parts, skip, tuned, row, *refs):
     refs = list(refs)
     number = len(parts) - skip
     first = number > 3
@@ -120,6 +120,7 @@
     (place,) = take(1)
     x = take(2 if first else 1)
     gains, shift = take(2)
+    gains = gains.at[pl.ds(row, 1)]
     sources = take(4 if tuned else len(parts))
     (out,) = take(1)
     if keep:
@@ -246,7 +247,7 @@
     else:
         scratch += [pltpu.VMEM(*item) for item in kept + start]
     return pl.pallas_call(
-        functools.partial(forward_kernel, count, keep, parts, skip, tuned),
+        functools.partial(forward_kernel, count, keep, parts, skip, tuned, gains[1]),
         out_shape=out_shape,
         in_specs=in_smem() + in_vmem(len(stream) + 2) + hbm(len(buffers)),
         out_specs=out_specs,
@@ -254,7 +255,7 @@
         compiler_params=pltpu.CompilerParams(vmem_limit_bytes=VMEM_LIMIT),
         cost_estimate=LIGHT,
         name="block_forward",
-    )(place, *stream, gains, shift, *buffers)
+    )(place, *stream, gains[0], shift, *buffers)
 
 
 def norm_back(count, chans, slope, hid, sums, more, rstd, rstd_at, gain, grad_gain, grad_bias, store):
@@ -430,10 +431,11 @@
     rows = stream.shape[0]
 
     def body(ins, outs, made, scratch, done):
-        back_out_body(rows // ROWS, *ins, *outs, scratch, made[0])
+        gain = ins[6].at[pl.ds(gains[1], 1)]
+        back_out_body(rows // ROWS, *ins[:6], gain, *outs, scratch, made[0])
         done(0)
 
-    ins = [grad, stream, hid_two, hid_three, rstd, w_out, gains]
+    ins = [grad, stream, hid_two, hid_three, rstd, w_out, gains[0]]
     out_shape = [f32(rows, D), bf16(rows, BOT), f32(1, 2 * BOT + 2 * D)]
     return back_call("back_out", body, ins, out_shape, out_scratch(rows), parts, tuned, place)
 
@@ -446,7 +448,8 @@
         for index in range(1, len(made)):
             made[index][...] = ins[5 + index][...]
             done(index)
-        back_mid_body(rows // ROWS, *ins[:6], *outs, scratch, made[0])
+        gain = ins[4].at[pl.ds(gains[1], 1)]
+        back_mid_body(rows // ROWS, *ins[:4], gain, ins[5], *outs, scratch, made[0])
         done(0)
 
     scratch = [
@@ -456,24 +459,26 @@
         pltpu.VMEM((stats, BOT), jnp.float32),
         pltpu.VMEM((stats, BOT), jnp.float32),
     ]
-    ins = [grad, hid_one, rstd, w_mid, gains, shift, *more]
+    ins = [grad, hid_one, rstd, w_mid, gains[0], shift, *more]
     out_shape = [bf16(rows, BOT), f32(1, 2 * BOT)]
     return back_call("back_mid", body, ins, out_shape, scratch, parts, tuned, place)
 
 
 def back_between(grad, stream, dres, w_in, later, parts, tuned, place):
     rows = stream.shape[0]
+    *later, gains = later
 
     def body(ins, outs, made, scratch, done):
         dx, low, *rest = scratch
         back_in_body(rows // ROWS, *ins[:4], dx, low, made[0])
         done(0)
-        back_out_body(rows // ROWS, dx, *ins[4:], *outs, rest, made[1])
+        gain = ins[-1].at[pl.ds(gains[1], 1)]
+        back_out_body(rows // ROWS, dx, *ins[4:-1], gain, *outs, rest, made[1])
         done(1)
 
     scratch = [pltpu.VMEM((rows, D), jnp.float32), pltpu.VMEM((rows, D), jnp.bfloat16)]
     scratch += out_scratch(rows)
-    ins = [grad, stream, dres, w_in, *later]
+    ins = [grad, stream, dres, w_in, *later, gains[0]]
     out_shape = [f32(rows, D), bf16(rows, BOT), f32(1, 2 * BOT + 2 * D)]
     return back_call("back_between", body, ins, out_shape, scratch, parts, tuned, place)
 
@@ -1561,7 +1566,7 @@
     def run_block(net, index, group, buffers, state):
         keep = net == "online"
         row = index + (BLOCKS if keep else 0)
-        gain = state["gains"][row : row + 1]
+        gain = (state["gains"], row)
         stream = [state["pixels" if keep else "following"], spread]
         if index:
             stream = [state["stream"]]
@@ -1617,7 +1622,7 @@
 
     def out_inputs(index, state):
         stream, hid_one, hid_two, hid_three, rstd = state["kept%d" % index]
-        gain = state["gains"][BLOCKS + index : BLOCKS + index + 1]
+        gain = (state["gains"], BLOCKS + index)
         return [stream, hid_two, hid_three, rstd, block_weight(index, "w_out"), gain]
 
     def out_step(index, group, state):
@@ -1628,7 +1633,7 @@
 
     def mid_step(index, group, state):
         stream, hid_one, hid_two, hid_three, rstd = state["kept%d" % index]
-        gain = state["gains"][BLOCKS + index : BLOCKS + index + 1]
+        gain = (state["gains"], BLOCKS + index)
         more = [state.pop("pool")] if len(group) > 1 else []
         (low, early), dealt = back_mid(
             state["low"], hid_one, rstd, block_weight(index, "w_mid"), gain, shift, more,

time: 552 us -> 551 us (level)
    unnamed x223 -> x213, local copies, waits for them, and re-layouts: 37.7 us -> 38.3 us
  transfers between devices with their start and end apart: 85 -> 85, of which waited for: 40 -> 40; matrix products, arithmetic and copies ran while one was open for 13% -> 12% of each run, Pallas kernels for 25% -> 25%
where the time goes in v10:
time: 551 us; the launch traced here: 546 us
  waiting for transfers between devices  192 us (35%)
  Pallas kernels  158 us (29%)
  starting transfers between devices  69.5 us (13%)
  local copies, waits for them, and re-layouts  64.2 us (12%)
  other arithmetic  58.4 us (11%)
    ppermute x85, waiting for transfers between devices, send(): return lax.ppermute(array, AXES, pairs)  192 us
    ppermute x85, starting transfers between devices, send(): return lax.ppermute(array, AXES, pairs)  69.5 us
    pallas_call x4, Pallas kernels, block_forward(): pl.pallas_call(functools.partial(forward_kernel, count, keep, parts, skip...  66.4 us
    pallas_call x5, Pallas kernels, back_call(): pl.pallas_call(functools.partial(back_kernel, body, parts, tuned, counts)...  56.3 us
    unnamed x213, local copies, waits for them, and re-layouts  38.3 us
    another operation x49, other arithmetic, in_order(): return jnp.stack([first, second])  15.6 us
    convert_element_type x10, other arithmetic, low_add(): return add_up(*terms).astype(jnp.bfloat16)  14.5 us
    add x12, other arithmetic, add_up(): total = total + term.astype(jnp.float32)  12.3 us
  transfers between devices with their start and end apart: 85, of which 40 were waited for; matrix products, arithmetic and copies ran while one was open for 12% of the time, Pallas kernels for 25%

profile of v10, /device:TPU:0, one launch (start us, length us, event | category | flops | bytes accessed | tf_op | source)
XLA Modules:
  0.0 545.9 jit_solution(13226866591303966887)
XLA Ops:
  9.8 3.0 collective-permute-start.3
  12.8 2.6 collective-permute-start.4
  22.4 3.9 collective-permute-done.3
  26.4 9.9 %collective-permute-done.4 = bf16[2,144,512]{2,1,0:T(8,128)(2,1)} collective-permute-done((bf16[2,144,512]{2,1,0:T(8,128)(2,1)S(1)}, bf16[2,144,512]{2,1,0:T(8,128)(2,1)}, u32[]{:S(2)}, u32[]{:S(2)}) %collective-permute-start.4) | collective-permute-done | bytes 294944 | tf_op jit(solution)/shard_map/ppermute | solution.py:802
  42.1 4.7 collective-permute-start.8
  46.8 17.2 %collective-permute-done.7 = bf16[2,96,512]{2,1,0:T(8,128)(2,1)S(1)} collective-permute-done((bf16[2,96,512]{2,1,0:T(8,128)(2,1)S(1)}, bf16[2,96,512]{2,1,0:T(8,128)(2,1)S(1)}, u32[]{:S(2)}, u32[]{:S(2)}) %collective-permute-start.7) | collective-permute-done | bytes 196640 | tf_op jit(solution)/shard_map/ppermute | solution.py:802
  64.1 10.4 %collective-permute-done.8 = bf16[2,2,160,512]{3,2,1,0:T(8,128)(2,1)S(1)} collective-permute-done((bf16[2,2,160,512]{3,2,1,0:T(8,128)(2,1)S(1)}, bf16[2,2,160,512]{3,2,1,0:T(8,128)(2,1)S(1)}, u32[]{:S(2)}, u32[]{:S(2)}) %collective-permute-start.8) | collective-permute-done | bytes 655392 | tf_op jit(solution)/shard_map/ppermute | solution.py:802
  79.6 24.3 %collective-permute-done.11 = bf16[2,2,96,512]{3,2,1,0:T(8,128)(2,1)S(1)} collective-permute-done((bf16[2,2,96,512]{3,2,1,0:T(8,128)(2,1)S(1)}, bf16[2,2,96,512]{3,2,1,0:T(8,128)(2,1)S(1)}, u32[]{:S(2)}, u32[]{:S(2)}) %collective-permute-start.11) | collective-permute-done | bytes 393248 | tf_op jit(solution)/shard_map/ppermute | solution.py:802
  107.5 10.5 %collective-permute-done.13.refs_1_.refs_5_ = bf16[2,4,2,144,512]{4,3,2,1,0:T(8,128)(2,1)} collective-permute-done((bf16[2,4,2,144,512]{4,3,2,1,0:T(8,128)(2,1)S(1)}, bf16[2,4,2,144,512]{4,3,2,1,0:T(8,128)(2,1)}, u32[]{:S(2)}, u32[]{:S(2)}) %collective-permute-start.13) | collective-permute-done | bytes 2359328 | tf_op jit(solution)/shard_map/ppermute | solution.py:802
  128.8 25.0 %collective-permute-done.15 = bf16[2,2,160,512]{3,2,1,0:T(8,128)(2,1)} collective-permute-done((bf16[2,2,160,512]{3,2,1,0:T(8,128)(2,1)}, bf16[2,2,160,512]{3,2,1,0:T(8,128)(2,1)}, u32[]{:S(2)}, u32[]{:S(2)}) %collective-permute-start.15) | collective-permute-done | bytes 655392 | tf_op jit(solution)/shard_map/ppermute | solution.py:802
  156.4 2.5 pad_maximum_fusion.4.refs_0_
  170.9 15.7 %block_forward.4.refs_1_ = f32[384,2048]{1,0:T(8,128)} custom-call(s32[5]{0:T(128)S(1)} %stack.339.place.refs_0_, bf16[384,256]{1,0:T(8,128)(2,1)S(1)} %bitcast.412, bf16[2,256,512]{2,1,0:T(8,128)(2,1)S(1)} %add_convert_fusion.refs_2_.refs_6_, f32[4,6144]{1,0:T(4,128)S(1)} %reshape.628.refs_3_.refs_2_.refs_7_.refs_5_.refs_10_, ...), custom_call_target="tpu_custom_call" | custom-call | flops 1024 | bytes 1024 | tf_op jit(solution)/shard_map/block_forward/pallas_call | solution.py:249
  186.6 5.3 collective-permute-done.20
  204.4 15.7 %block_forward.5.stream = f32[384,2048]{1,0:T(8,128)} custom-call(s32[5]{0:T(128)S(1)} %stack.339.place.refs_0_, f32[384,2048]{1,0:T(8,128)} %block_forward.4.refs_1_, f32[4,6144]{1,0:T(4,128)S(1)} %reshape.628.refs_3_.refs_2_.refs_7_.refs_5_.refs_10_, bf16[1152,128]{1,0:T(8,128)(2,1)S(1)} %convert_element_type.412.refs_4_.refs_3_.refs_6_, ...), custom_call_target="tpu_custom_call" | custom-call | flops 1024 | bytes 1024 | tf_op jit(solution)/shard_map/block_forward/pallas_call | solution.py:249
  221.9 4.6 head_target.1.target
  230.7 10.7 %collective-permute-done.28.refs_6_.refs_1_ = bf16[2,4,2,160,512]{4,3,2,1,0:T(8,128)(2,1)} collective-permute-done((bf16[2,4,2,160,512]{4,3,2,1,0:T(8,128)(2,1)S(1)}, bf16[2,4,2,160,512]{4,3,2,1,0:T(8,128)(2,1)}, u32[]{:S(2)}, u32[]{:S(2)}) %collective-permute-start.28) | collective-permute-done | bytes 2621472 | tf_op jit(solution)/shard_map/ppermute | solution.py:802
  243.7 2.9 collective-permute-done.31.refs_8_.refs_3_
  250.5 18.1 %block_forward.6 = (f32[384,2048]{1,0:T(8,128)}, f32[384,2048]{1,0:T(8,128)}, f32[384,512]{1,0:T(8,128)S(1)}, f32[384,512]{1,0:T(8,128)S(1)}, f32[384,2048]{1,0:...) custom-call(s32[5]{0:T(128)S(1)} %stack.339.place.refs_0_, ...), custom_call_target="tpu_custom_call" | custom-call | flops 1024 | bytes 1024 | tf_op jit(solution)/shard_map/block_forward/pallas_call | solution.py:249
  272.4 6.6 %collective-permute-done.32.refs_5_ = bf16[2,4,2,144,512]{4,3,2,1,0:T(8,128)(2,1)} collective-permute-done((bf16[2,4,2,144,512]{4,3,2,1,0:T(8,128)(2,1)S(1)}, bf16[2,4,2,144,512]{4,3,2,1,0:T(8,128)(2,1)}, u32[]{:S(2)}, u32[]{:S(2)}) %collective-permute-start.32) | collective-permute-done | bytes 2359328 | tf_op jit(solution)/shard_map/ppermute | solution.py:802
  280.5 3.2 collective-permute-done.36.refs_7_
  285.1 17.0 %block_forward.7 = (f32[384,2048]{1,0:T(8,128)}, f32[384,512]{1,0:T(8,128)S(1)}, f32[384,512]{1,0:T(8,128)S(1)}, f32[384,2048]{1,0:T(8,128)}, f32[8,3072]{1,0:T(...) custom-call(s32[5]{0:T(128)S(1)} %stack.339.place.refs_0_, ...), custom_call_target="tpu_custom_call" | custom-call | flops 1024 | bytes 1024 | tf_op jit(solution)/shard_map/block_forward/pallas_call | solution.py:249
  308.7 3.4 collective-permute-done.37.refs_3_
  313.5 10.9 %head_loss.1 = (f32[1,1]{1,0:T(1,128)}, f32[384,2048]{1,0:T(8,128)}, bf16[1,2048,128]{2,1,0:T(8,128)(2,1)S(1)}, bf16[64,512]{1,0:T(8,128)(2,1)S(1)}) custom-call(s32[5]{0:T(128)S(1)} %stack.339.place.refs_0_, f32[384,2048]{1,0:T(8,128)} %get-tuple-element.550.stream, bf16[2048,128]{1,0:T(8,128)(2,1)S(1)} %bitcast.402, f32[8,128]{1,0:T(8,128)S(1)} %head_target.1.target, ...), custom_call_target="tpu_custom_call" | custom-call | flops 1024 | bytes 1024 | tf_op jit(solution)/shard_map/head_loss/pallas_call | solution.py:696
  329.0 11.1 %back_out.1 = (f32[384,2048]{1,0:T(8,128)S(1)}, bf16[384,512]{1,0:T(8,128)(2,1)S(1)}, f32[1,5120]{1,0:T(1,128)S(1)}, bf16[2,2,4,2,32,512]{5,4,3,2,1,0:T(8,128)(2...) custom-call(s32[5]{0:T(128)S(1)} %stack.339.place.refs_0_, ...), custom_call_target="tpu_custom_call" | custom-call | flops 1024 | bytes 1024 | tf_op jit(solution)/shard_map/back_out/pallas_call | solution.py:415
  342.1 2.5 collective-permute-done.39
  345.8 9.8 %back_mid.2 = (bf16[384,512]{1,0:T(8,128)(2,1)S(1)}, f32[1,1024]{1,0:T(1,128)S(1)}, bf16[2,2,4,2,80,512]{5,4,3,2,1,0:T(8,128)(2,1)S(1)}, bf16[2,4,2,80,512]{4,3,...) custom-call(s32[5]{0:T(128)S(1)} %stack.339.place.refs_0_, ...), custom_call_target="tpu_custom_call" | custom-call | flops 1024 | bytes 1024 | tf_op jit(solution)/shard_map/back_mid/pallas_call | solution.py:415
  356.0 4.7 collective-permute-done.43
  366.1 16.5 %back_between.1 = (f32[384,2048]{1,0:T(8,128)}, bf16[384,512]{1,0:T(8,128)(2,1)S(1)}, f32[1,5120]{1,0:T(1,128)S(1)}, bf16[2,2,4,2,64,512]{5,4,3,2,1,0:T(8,128)(2...) custom-call(s32[5]{0:T(128)S(1)} %stack.339.place.refs_0_, ...), custom_call_target="tpu_custom_call" | custom-call | flops 1024 | bytes 1024 | tf_op jit(solution)/shard_map/back_between/pallas_call | solution.py:415
  383.7 4.1 collective-permute-done.48
  396.0 10.6 %back_mid.3 = (bf16[384,512]{1,0:T(8,128)(2,1)S(1)}, f32[1,1024]{1,0:T(1,128)S(1)}, bf16[2,2,4,2,80,512]{5,4,3,2,1,0:T(8,128)(2,1)}, bf16[2,4,2,80,512]{4,3,2,1,...) custom-call(s32[5]{0:T(128)S(1)} %stack.339.place.refs_0_, ...), custom_call_target="tpu_custom_call" | custom-call | flops 1024 | bytes 1024 | tf_op jit(solution)/shard_map/back_mid/pallas_call | solution.py:415
  409.0 4.5 collective-permute-done.50
  416.7 2.4 fusion.11
  422.3 3.3 fusion
  429.1 3.1 collective-permute-done.51
  434.1 8.3 %back_first.1 = (bf16[2,2,4,2,64,512]{5,4,3,2,1,0:T(8,128)(2,1)}, bf16[2,4,2,64,512]{4,3,2,1,0:T(8,128)(2,1)S(1)}, bf16[4,2,64,512]{3,2,1,0:T(8,128)(2,1)S(1)}, bf16[4,2,64,512]{3,2,1,0:T(8,128)(2,1)S(1)}) custom-call(s32[5]{0:T(128)S(1)} %stack.339.place.refs_0_, bf16[384,512]{1,0:T(8,128)(2,1)S(1)} %copy-done.59, ...), custom_call_target="tpu_custom_call" | custom-call | flops 1024 | bytes 1024 | tf_op jit(solution)/shard_map/back_first/pallas_call | solution.py:415
  443.3 5.7 %collective-permute-done.52 = bf16[2,2,80,512]{3,2,1,0:T(8,128)(2,1)} collective-permute-done((bf16[2,2,80,512]{3,2,1,0:T(8,128)(2,1)}, bf16[2,2,80,512]{3,2,1,0:T(8,128)(2,1)}, u32[]{:S(2)}, u32[]{:S(2)}) %collective-permute-start.52) | collective-permute-done | bytes 327712 | tf_op jit(solution)/shard_map/ppermute | solution.py:802
  453.7 2.6 collective-permute-start.61
  462.0 4.7 collective-permute-done.61
  468.5 3.5 collective-permute-done.59
  472.8 2.4 fusion.9
  482.9 3.0 own_heads.1
  488.4 5.2 collective-permute-done.70
  496.8 3.3 collective-permute-start.74
  505.7 4.0 concatenate.90
  512.8 7.7 %directions.1 = (f32[8,128]{1,0:T(8,128)S(1)}, f32[1,115648]{1,0:T(1,128)}, f32[1,115648]{1,0:T(1,128)}, f32[1,115648]{1,0:T(1,128)S(1)}, f32[2,139456]{1,0:T(2,...) custom-call(f32[64,512]{1,0:T(8,128)S(1)} %bitcast.414, f32[160,512]{1,0:T(8,128)S(1)} %bitcast.407, ...), custom_call_target="tpu_custom_call" | custom-call | flops 1024 | bytes 1024 | tf_op jit(solution)/shard_map/directions/pallas_call | solution.py:1325
  530.0 2.7 collective-permute-start.83
  534.3 3.8 collective-permute-done.84
  538.6 4.7 update.1
  (575 shorter events, 180.4 us)
Async XLA Ops:
  9.8 16.6 %collective-permute-start.3 = (bf16[2,144,512]{2,1,0:T(8,128)(2,1)S(1)}, bf16[2,144,512]{2,1,0:T(8,128)(2,1)}, u32[]{:S(2)}, u32[]{:S(2)}) collective-permute-start(bf16[2,144,512]{2,1,0:T(8,128)(2,1)S(1)} %pad_maximum_fusion.27), channel_id=1, source_target_pairs={{0,8},{1,9},{2,10},{3,11},{4,12},{5,13},{6,14},{7,15},{8,0},{9,1},... | collective-permute-start | bytes 884744 | tf_op jit(solution)/shard_map/ppermute | solution.py:802
  12.8 23.6 %collective-permute-start.4 = (bf16[2,144,512]{2,1,0:T(8,128)(2,1)S(1)}, bf16[2,144,512]{2,1,0:T(8,128)(2,1)}, u32[]{:S(2)}, u32[]{:S(2)}) collective-permute-start(bf16[2,144,512]{2,1,0:T(8,128)(2,1)S(1)} %pad_maximum_fusion.27), channel_id=1, source_target_pairs={{0,16},{1,17},{2,18},{3,19},{4,20},{5,21},{6,22},{7,23},{8,24},{9,... | collective-permute-start | bytes 884744 | tf_op jit(solution)/shard_map/ppermute | solution.py:802
  15.3 21.0 %collective-permute-start.5 = (bf16[2,144,512]{2,1,0:T(8,128)(2,1)S(1)}, bf16[2,144,512]{2,1,0:T(8,128)(2,1)}, u32[]{:S(2)}, u32[]{:S(2)}) collective-permute-start(bf16[2,144,512]{2,1,0:T(8,128)(2,1)S(1)} %pad_maximum_fusion.27), channel_id=1, source_target_pairs={{0,24},{1,25},{2,26},{3,27},{4,28},{5,29},{6,30},{7,31},{8,16},{9,... | collective-permute-start | bytes 884744 | tf_op jit(solution)/shard_map/ppermute | solution.py:802
  18.9 20.8 %collective-permute-start.2 = (bf16[2,160,512]{2,1,0:T(8,128)(2,1)S(1)}, bf16[2,160,512]{2,1,0:T(8,128)(2,1)S(1)}, u32[]{:S(2)}, u32[]{:S(2)}) collective-permute-start(bf16[2,160,512]{2,1,0:T(8,128)(2,1)S(1)} %pad_maximum_fusion.22), channel_id=1, source_target_pairs={{0,8},{1,9},{2,10},{3,11},{4,12},{5,13},{6,14},{7,15},{8,0},{9,1},... | collective-permute-start | bytes 983048 | tf_op jit(solution)/shard_map/ppermute | solution.py:802
  22.4 17.5 %collective-permute-start.6 = (bf16[496,512]{1,0:T(8,128)(2,1)S(1)}, bf16[496,512]{1,0:T(8,128)(2,1)S(1)}, u32[]{:S(2)}, u32[]{:S(2)}) collective-permute-start(bf16[496,512]{1,0:T(8,128)(2,1)S(1)} %pad_maximum_fusion.19), channel_id=1, source_target_pairs={{0,1},{1,0},{2,3},{3,2},{4,5},{5,4},{6,7},{7,6},{8,9},{9,8},{10,11... | collective-permute-start | bytes 1523720 | tf_op jit(solution)/shard_map/ppermute | solution.py:802
  40.3 34.4 %collective-permute-start.9 = (bf16[4,2,144,512]{3,2,1,0:T(8,128)(2,1)S(1)}, bf16[4,2,144,512]{3,2,1,0:T(8,128)(2,1)S(1)}, u32[]{:S(2)}, u32[]{:S(2)}) collective-permute-start(bf16[4,2,144,512]{3,2,1,0:T(8,128)(2,1)S(1)} %bitcast.426), channel_id=1, source_target_pairs={{0,2},{1,5},{2,0},{3,7},{4,6},{5,1},{6,4},{7,3},{8,10},{9,13},{10,... | collective-permute-start | bytes 3538952 | tf_op jit(solution)/shard_map/ppermute | solution.py:802
  42.1 32.5 %collective-permute-start.8 = (bf16[2,2,160,512]{3,2,1,0:T(8,128)(2,1)S(1)}, bf16[2,2,160,512]{3,2,1,0:T(8,128)(2,1)S(1)}, u32[]{:S(2)}, u32[]{:S(2)}) collective-permute-start(bf16[2,2,160,512]{3,2,1,0:T(8,128)(2,1)S(1)} %pad_maximum_fusion.13), channel_id=1, source_target_pairs={{0,16},{1,17},{2,18},{3,19},{4,20},{5,21},{6,22},{7,23},{8,24},{9,... | collective-permute-start | bytes 1966088 | tf_op jit(solution)/shard_map/ppermute | solution.py:802
  46.8 17.2 %collective-permute-start.7 = (bf16[2,96,512]{2,1,0:T(8,128)(2,1)S(1)}, bf16[2,96,512]{2,1,0:T(8,128)(2,1)S(1)}, u32[]{:S(2)}, u32[]{:S(2)}) collective-permute-start(bf16[2,96,512]{2,1,0:T(8,128)(2,1)S(1)} %pad_maximum_fusion.32), channel_id=1, source_target_pairs={{0,8},{1,9},{2,10},{3,11},{4,12},{5,13},{6,14},{7,15},{8,0},{9,1},... | collective-permute-start | bytes 589832 | tf_op jit(solution)/shard_map/ppermute | solution.py:802
  75.0 43.1 %collective-permute-start.13 = (bf16[2,4,2,144,512]{4,3,2,1,0:T(8,128)(2,1)S(1)}, bf16[2,4,2,144,512]{4,3,2,1,0:T(8,128)(2,1)}, u32[]{:S(2)}, u32[]{:S(2)}) collective-permute-start(bf16[2,4,2,144,512]{4,3,2,1,0:T(8,128)(2,1)S(1)} %pad_maximum_fusion.2.refs_0_.refs_4_), channel_id=1, source_target_pairs={{0,4},{1,3},{2,6},{3,1},{4,0},{5,7},{6,2},{7,5},{8,12},{9,11},{10,... | collective-permute-start | bytes 7077896 | tf_op jit(solution)/shard_map/ppermute | solution.py:802
  75.6 42.5 %collective-permute-start.14 = (bf16[2,4,2,144,512]{4,3,2,1,0:T(8,128)(2,1)S(1)}, bf16[2,4,2,144,512]{4,3,2,1,0:T(8,128)(2,1)S(1)}, u32[]{:S(2)}, u32[]{:S(2)}) collective-permute-start(bf16[2,4,2,144,512]{4,3,2,1,0:T(8,128)(2,1)S(1)} %pad_maximum_fusion.2.refs_0_.refs_4_), channel_id=1, source_target_pairs={{0,1},{1,0},{2,3},{3,2},{4,5},{5,4},{6,7},{7,6},{8,9},{9,8},{10,11... | collective-permute-start | bytes 7077896 | tf_op jit(solution)/shard_map/ppermute | solution.py:802
  75.6 31.7 %collective-permute-start.12 = (bf16[4,2,160,512]{3,2,1,0:T(8,128)(2,1)S(1)}, bf16[4,2,160,512]{3,2,1,0:T(8,128)(2,1)S(1)}, u32[]{:S(2)}, u32[]{:S(2)}) collective-permute-start(bf16[4,2,160,512]{3,2,1,0:T(8,128)(2,1)S(1)} %bitcast.422), channel_id=1, source_target_pairs={{0,2},{1,5},{2,0},{3,7},{4,6},{5,1},{6,4},{7,3},{8,10},{9,13},{10,... | collective-permute-start | bytes 3932168 | tf_op jit(solution)/shard_map/ppermute | solution.py:802
  77.1 28.9 %collective-permute-start.10 = (bf16[2,400,512]{2,1,0:T(8,128)(2,1)S(1)}, bf16[2,400,512]{2,1,0:T(8,128)(2,1)S(1)}, u32[]{:S(2)}, u32[]{:S(2)}) collective-permute-start(bf16[2,400,512]{2,1,0:T(8,128)(2,1)S(1)} %pad_maximum_fusion.10), channel_id=1, source_target_pairs={{0,8},{1,9},{2,10},{3,11},{4,12},{5,13},{6,14},{7,15},{8,0},{9,1},... | collective-permute-start | bytes 2457608 | tf_op jit(solution)/shard_map/ppermute | solution.py:802
  77.2 26.6 %collective-permute-start.11 = (bf16[2,2,96,512]{3,2,1,0:T(8,128)(2,1)S(1)}, bf16[2,2,96,512]{3,2,1,0:T(8,128)(2,1)S(1)}, u32[]{:S(2)}, u32[]{:S(2)}) collective-permute-start(bf16[2,2,96,512]{3,2,1,0:T(8,128)(2,1)S(1)} %pad_maximum_fusion.20), channel_id=1, source_target_pairs={{0,16},{1,17},{2,18},{3,19},{4,20},{5,21},{6,22},{7,23},{8,24},{9,... | collective-permute-start | bytes 1179656 | tf_op jit(solution)/shard_map/ppermute | solution.py:802
  119.6 40.2 %collective-permute-start.18 = (bf16[2,4,2,160,512]{4,3,2,1,0:T(8,128)(2,1)S(1)}, bf16[2,4,2,160,512]{4,3,2,1,0:T(8,128)(2,1)}, u32[]{:S(2)}, u32[]{:S(2)}) collective-permute-start(bf16[2,4,2,160,512]{4,3,2,1,0:T(8,128)(2,1)S(1)} %pad_maximum_fusion.refs_0_.refs_5_), channel_id=1, source_target_pairs={{0,4},{1,3},{2,6},{3,1},{4,0},{5,7},{6,2},{7,5},{8,12},{9,11},{10,... | collective-permute-start | bytes 7864328 | tf_op jit(solution)/shard_map/ppermute | solution.py:802
  120.1 39.7 %collective-permute-start.19 = (bf16[2,4,2,160,512]{4,3,2,1,0:T(8,128)(2,1)S(1)}, bf16[2,4,2,160,512]{4,3,2,1,0:T(8,128)(2,1)}, u32[]{:S(2)}, u32[]{:S(2)}) collective-permute-start(bf16[2,4,2,160,512]{4,3,2,1,0:T(8,128)(2,1)S(1)} %pad_maximum_fusion.refs_0_.refs_5_), channel_id=1, source_target_pairs={{0,1},{1,0},{2,3},{3,2},{4,5},{5,4},{6,7},{7,6},{8,9},{9,8},{10,11... | collective-permute-start | bytes 7864328 | tf_op jit(solution)/shard_map/ppermute | solution.py:802
  122.1 31.7 %collective-permute-start.17 = (bf16[4,2,96,512]{3,2,1,0:T(8,128)(2,1)S(1)}, bf16[4,2,96,512]{3,2,1,0:T(8,128)(2,1)}, u32[]{:S(2)}, u32[]{:S(2)}) collective-permute-start(bf16[4,2,96,512]{3,2,1,0:T(8,128)(2,1)S(1)} %bitcast.430), channel_id=1, source_target_pairs={{0,2},{1,5},{2,0},{3,7},{4,6},{5,1},{6,4},{7,3},{8,10},{9,13},{10,... | collective-permute-start | bytes 2359304 | tf_op jit(solution)/shard_map/ppermute | solution.py:802
  122.7 31.1 %collective-permute-start.15 = (bf16[2,2,160,512]{3,2,1,0:T(8,128)(2,1)}, bf16[2,2,160,512]{3,2,1,0:T(8,128)(2,1)}, u32[]{:S(2)}, u32[]{:S(2)}) collective-permute-start(bf16[2,2,160,512]{3,2,1,0:T(8,128)(2,1)} %pad_maximum_fusion.14), channel_id=1, source_target_pairs={{0,16},{1,17},{2,18},{3,19},{4,20},{5,21},{6,22},{7,23},{8,24},{9,... | collective-permute-start | bytes 1966088 | tf_op jit(solution)/shard_map/ppermute | solution.py:802
  160.5 32.0 %collective-permute-start.22 = (bf16[4,2,160,512]{3,2,1,0:T(8,128)(2,1)}, bf16[4,2,160,512]{3,2,1,0:T(8,128)(2,1)}, u32[]{:S(2)}, u32[]{:S(2)}) collective-permute-start(bf16[4,2,160,512]{3,2,1,0:T(8,128)(2,1)} %bitcast.67), channel_id=1, source_target_pairs={{0,2},{1,5},{2,0},{3,7},{4,6},{5,1},{6,4},{7,3},{8,10},{9,13},{10,... | collective-permute-start | bytes 3932168 | tf_op jit(solution)/shard_map/ppermute | solution.py:802
  162.2 34.8 %collective-permute-start.23 = (bf16[2,4,2,96,512]{4,3,2,1,0:T(8,128)(2,1)}, bf16[2,4,2,96,512]{4,3,2,1,0:T(8,128)(2,1)}, u32[]{:S(2)}, u32[]{:S(2)}) collective-permute-start(bf16[2,4,2,96,512]{4,3,2,1,0:T(8,128)(2,1)} %pad_maximum_fusion.4.refs_0_), channel_id=1, source_target_pairs={{0,4},{1,3},{2,6},{3,1},{4,0},{5,7},{6,2},{7,5},{8,12},{9,11},{10,... | collective-permute-start | bytes 4718600 | tf_op jit(solution)/shard_map/ppermute | solution.py:802
  162.8 34.3 %collective-permute-start.24 = (bf16[2,4,2,96,512]{4,3,2,1,0:T(8,128)(2,1)}, bf16[2,4,2,96,512]{4,3,2,1,0:T(8,128)(2,1)}, u32[]{:S(2)}, u32[]{:S(2)}) collective-permute-start(bf16[2,4,2,96,512]{4,3,2,1,0:T(8,128)(2,1)} %pad_maximum_fusion.4.refs_0_), channel_id=1, source_target_pairs={{0,1},{1,0},{2,3},{3,2},{4,5},{5,4},{6,7},{7,6},{8,9},{9,8},{10,11... | collective-permute-start | bytes 4718600 | tf_op jit(solution)/shard_map/ppermute | solution.py:802
  163.2 28.8 %collective-permute-start.20 = (bf16[2,2,144,512]{3,2,1,0:T(8,128)(2,1)}, bf16[2,2,144,512]{3,2,1,0:T(8,128)(2,1)}, u32[]{:S(2)}, u32[]{:S(2)}) collective-permute-start(bf16[2,2,144,512]{3,2,1,0:T(8,128)(2,1)} %pad_maximum_fusion.17), channel_id=1, source_target_pairs={{0,16},{1,17},{2,18},{3,19},{4,20},{5,21},{6,22},{7,23},{8,24},{9,... | collective-permute-start | bytes 1769480 | tf_op jit(solution)/shard_map/ppermute | solution.py:802
  197.0 44.5 %collective-permute-start.28 = (bf16[2,4,2,160,512]{4,3,2,1,0:T(8,128)(2,1)S(1)}, bf16[2,4,2,160,512]{4,3,2,1,0:T(8,128)(2,1)}, u32[]{:S(2)}, u32[]{:S(2)}) collective-permute-start(bf16[2,4,2,160,512]{4,3,2,1,0:T(8,128)(2,1)S(1)} %pad_maximum_fusion.1.refs_5_.refs_0_), channel_id=1, source_target_pairs={{0,4},{1,3},{2,6},{3,1},{4,0},{5,7},{6,2},{7,5},{8,12},{9,11},{10,... | collective-permute-start | bytes 7864328 | tf_op jit(solution)/shard_map/ppermute | solution.py:802
  198.0 43.5 %collective-permute-start.29 = (bf16[2,4,2,160,512]{4,3,2,1,0:T(8,128)(2,1)S(1)}, bf16[2,4,2,160,512]{4,3,2,1,0:T(8,128)(2,1)}, u32[]{:S(2)}, u32[]{:S(2)}) collective-permute-start(bf16[2,4,2,160,512]{4,3,2,1,0:T(8,128)(2,1)S(1)} %pad_maximum_fusion.1.refs_5_.refs_0_), channel_id=1, source_target_pairs={{0,1},{1,0},{2,3},{3,2},{4,5},{5,4},{6,7},{7,6},{8,9},{9,8},{10,11... | collective-permute-start | bytes 7864328 | tf_op jit(solution)/shard_map/ppermute | solution.py:802
  198.0 22.0 %collective-permute-start.26 = (bf16[2,4,2,96,512]{4,3,2,1,0:T(8,128)(2,1)}, bf16[2,4,2,96,512]{4,3,2,1,0:T(8,128)(2,1)}, u32[]{:S(2)}, u32[]{:S(2)}) collective-permute-start(bf16[2,4,2,96,512]{4,3,2,1,0:T(8,128)(2,1)} %collective-permute-done.23.refs_1_), channel_id=1, source_target_pairs={{0,1},{1,0},{2,3},{3,2},{4,5},{5,4},{6,7},{7,6},{8,9},{9,8},{10,11... | collective-permute-start | bytes 4718600 | tf_op jit(solution)/shard_map/ppermute | solution.py:802
  198.5 29.2 %collective-permute-start.27 = (bf16[4,2,144,512]{3,2,1,0:T(8,128)(2,1)}, bf16[4,2,144,512]{3,2,1,0:T(8,128)(2,1)}, u32[]{:S(2)}, u32[]{:S(2)}) collective-permute-start(bf16[4,2,144,512]{3,2,1,0:T(8,128)(2,1)} %bitcast.74), channel_id=1, source_target_pairs={{0,2},{1,5},{2,0},{3,7},{4,6},{5,1},{6,4},{7,3},{8,10},{9,13},{10,... | collective-permute-start | bytes 3538952 | tf_op jit(solution)/shard_map/ppermute | solution.py:802
  199.4 27.2 %collective-permute-start.25 = (bf16[2,2,96,512]{3,2,1,0:T(8,128)(2,1)}, bf16[2,2,96,512]{3,2,1,0:T(8,128)(2,1)}, u32[]{:S(2)}, u32[]{:S(2)}) collective-permute-start(bf16[2,2,96,512]{3,2,1,0:T(8,128)(2,1)} %pad_maximum_fusion.21), channel_id=1, source_target_pairs={{0,16},{1,17},{2,18},{3,19},{4,20},{5,21},{6,22},{7,23},{8,24},{9,... | collective-permute-start | bytes 1179656 | tf_op jit(solution)/shard_map/ppermute | solution.py:802
  241.5 37.4 %collective-permute-start.32 = (bf16[2,4,2,144,512]{4,3,2,1,0:T(8,128)(2,1)S(1)}, bf16[2,4,2,144,512]{4,3,2,1,0:T(8,128)(2,1)}, u32[]{:S(2)}, u32[]{:S(2)}) collective-permute-start(bf16[2,4,2,144,512]{4,3,2,1,0:T(8,128)(2,1)S(1)} %pad_maximum_fusion.3.refs_4_), channel_id=1, source_target_pairs={{0,4},{1,3},{2,6},{3,1},{4,0},{5,7},{6,2},{7,5},{8,12},{9,11},{10,... | collective-permute-start | bytes 7077896 | tf_op jit(solution)/shard_map/ppermute | solution.py:802
  242.5 36.4 %collective-permute-start.33 = (bf16[2,4,2,144,512]{4,3,2,1,0:T(8,128)(2,1)S(1)}, bf16[2,4,2,144,512]{4,3,2,1,0:T(8,128)(2,1)}, u32[]{:S(2)}, u32[]{:S(2)}) collective-permute-start(bf16[2,4,2,144,512]{4,3,2,1,0:T(8,128)(2,1)S(1)} %pad_maximum_fusion.3.refs_4_), channel_id=1, source_target_pairs={{0,1},{1,0},{2,3},{3,2},{4,5},{5,4},{6,7},{7,6},{8,9},{9,8},{10,11... | collective-permute-start | bytes 7077896 | tf_op jit(solution)/shard_map/ppermute | solution.py:802
  243.2 27.6 %collective-permute-start.30 = (bf16[4,2,96,512]{3,2,1,0:T(8,128)(2,1)S(1)}, bf16[4,2,96,512]{3,2,1,0:T(8,128)(2,1)S(1)}, u32[]{:S(2)}, u32[]{:S(2)}) collective-permute-start(bf16[4,2,96,512]{3,2,1,0:T(8,128)(2,1)S(1)} %bitcast.432), channel_id=1, source_target_pairs={{0,2},{1,5},{2,0},{3,7},{4,6},{5,1},{6,4},{7,3},{8,10},{9,13},{10,... | collective-permute-start | bytes 2359304 | tf_op jit(solution)/shard_map/ppermute | solution.py:802
  278.9 28.1 %collective-permute-start.34 = (bf16[2,4,2,96,512]{4,3,2,1,0:T(8,128)(2,1)S(1)}, bf16[2,4,2,96,512]{4,3,2,1,0:T(8,128)(2,1)}, u32[]{:S(2)}, u32[]{:S(2)}) collective-permute-start(bf16[2,4,2,96,512]{4,3,2,1,0:T(8,128)(2,1)S(1)} %pad_maximum_fusion.5.refs_0_), channel_id=1, source_target_pairs={{0,4},{1,3},{2,6},{3,1},{4,0},{5,7},{6,2},{7,5},{8,12},{9,11},{10,... | collective-permute-start | bytes 4718600 | tf_op jit(solution)/shard_map/ppermute | solution.py:802
  279.9 27.2 %collective-permute-start.35 = (bf16[2,4,2,96,512]{4,3,2,1,0:T(8,128)(2,1)S(1)}, bf16[2,4,2,96,512]{4,3,2,1,0:T(8,128)(2,1)S(1)}, u32[]{:S(2)}, u32[]{:S(2)}) collective-permute-start(bf16[2,4,2,96,512]{4,3,2,1,0:T(8,128)(2,1)S(1)} %pad_maximum_fusion.5.refs_0_), channel_id=1, source_target_pairs={{0,1},{1,0},{2,3},{3,2},{4,5},{5,4},{6,7},{7,6},{8,9},{9,8},{10,11... | collective-permute-start | bytes 4718600 | tf_op jit(solution)/shard_map/ppermute | solution.py:802
  325.1 16.8 %collective-permute-start.38 = (bf16[32,512]{1,0:T(8,128)(2,1)S(1)}, bf16[32,512]{1,0:T(8,128)(2,1)S(1)}, u32[]{:S(2)}, u32[]{:S(2)}) collective-permute-start(bf16[32,512]{1,0:T(8,128)(2,1)S(1)} %dynamic-slice_bitcast_fusion.12), channel_id=1, source_target_pairs={{0,1},{1,0},{2,3},{3,2},{4,5},{5,4},{6,7},{7,6},{8,9},{9,8},{10,11... | collective-permute-start | bytes 98312 | tf_op jit(solution)/shard_map/ppermute | solution.py:802
  361.1 22.5 %collective-permute-start.44 = (bf16[2,4,2,80,512]{4,3,2,1,0:T(8,128)(2,1)S(1)}, bf16[2,4,2,80,512]{4,3,2,1,0:T(8,128)(2,1)S(1)}, u32[]{:S(2)}, u32[]{:S(2)}) collective-permute-start(bf16[2,4,2,80,512]{4,3,2,1,0:T(8,128)(2,1)S(1)} %fusion.1), channel_id=1, source_target_pairs={{0,4},{1,3},{2,6},{3,1},{4,0},{5,7},{6,2},{7,5},{8,12},{9,11},{10,... | collective-permute-start | bytes 3932168 | tf_op jit(solution)/shard_map/ppermute | solution.py:802
  362.3 20.4 %collective-permute-start.45 = (bf16[2,2,32,512]{3,2,1,0:T(8,128)(2,1)S(1)}, bf16[2,2,32,512]{3,2,1,0:T(8,128)(2,1)S(1)}, u32[]{:S(2)}, u32[]{:S(2)}) collective-permute-start(bf16[2,2,32,512]{3,2,1,0:T(8,128)(2,1)S(1)} %pad_maximum_fusion.34), channel_id=1, source_target_pairs={{0,16},{1,17},{2,18},{3,19},{4,20},{5,21},{6,22},{7,23},{8,24},{9,... | collective-permute-start | bytes 393224 | tf_op jit(solution)/shard_map/ppermute | solution.py:802
  364.6 19.0 %collective-permute-start.42 = (bf16[4,2,32,512]{3,2,1,0:T(8,128)(2,1)S(1)}, bf16[4,2,32,512]{3,2,1,0:T(8,128)(2,1)S(1)}, u32[]{:S(2)}, u32[]{:S(2)}) collective-permute-start(bf16[4,2,32,512]{3,2,1,0:T(8,128)(2,1)S(1)} %fusion.17), channel_id=1, source_target_pairs={{0,2},{1,5},{2,0},{3,7},{4,6},{5,1},{6,4},{7,3},{8,10},{9,13},{10,... | collective-permute-start | bytes 786440 | tf_op jit(solution)/shard_map/ppermute | solution.py:802
  389.5 24.9 %collective-permute-start.49 = (bf16[2,4,2,64,512]{4,3,2,1,0:T(8,128)(2,1)}, bf16[2,4,2,64,512]{4,3,2,1,0:T(8,128)(2,1)}, u32[]{:S(2)}, u32[]{:S(2)}) collective-permute-start(bf16[2,4,2,64,512]{4,3,2,1,0:T(8,128)(2,1)} %fusion.3), channel_id=1, source_target_pairs={{0,4},{1,3},{2,6},{3,1},{4,0},{5,7},{6,2},{7,5},{8,12},{9,11},{10,... | collective-permute-start | bytes 3145736 | tf_op jit(solution)/shard_map/ppermute | solution.py:802
  391.1 22.5 %collective-permute-start.47 = (bf16[4,2,80,512]{3,2,1,0:T(8,128)(2,1)}, bf16[4,2,80,512]{3,2,1,0:T(8,128)(2,1)}, u32[]{:S(2)}, u32[]{:S(2)}) collective-permute-start(bf16[4,2,80,512]{3,2,1,0:T(8,128)(2,1)} %fusion.7), channel_id=1, source_target_pairs={{0,2},{1,5},{2,0},{3,7},{4,6},{5,1},{6,4},{7,3},{8,10},{9,13},{10,... | collective-permute-start | bytes 1966088 | tf_op jit(solution)/shard_map/ppermute | solution.py:802
  392.5 21.0 %collective-permute-start.50 = (bf16[4,2,32,512]{3,2,1,0:T(8,128)(2,1)}, bf16[4,2,32,512]{3,2,1,0:T(8,128)(2,1)S(1)}, u32[]{:S(2)}, u32[]{:S(2)}) collective-permute-start(bf16[4,2,32,512]{3,2,1,0:T(8,128)(2,1)} %bitcast.443), channel_id=1, source_target_pairs={{0,2},{1,5},{2,0},{3,7},{4,6},{5,1},{6,4},{7,3},{8,10},{9,13},{10,... | collective-permute-start | bytes 786440 | tf_op jit(solution)/shard_map/ppermute | solution.py:802
  394.4 19.2 %collective-permute-start.46 = (bf16[2,2,32,512]{3,2,1,0:T(8,128)(2,1)S(1)}, bf16[2,2,32,512]{3,2,1,0:T(8,128)(2,1)}, u32[]{:S(2)}, u32[]{:S(2)}) collective-permute-start(bf16[2,2,32,512]{3,2,1,0:T(8,128)(2,1)S(1)} %fusion.29), channel_id=1, source_target_pairs={{0,16},{1,17},{2,18},{3,19},{4,20},{5,21},{6,22},{7,23},{8,24},{9,... | collective-permute-start | bytes 393224 | tf_op jit(solution)/shard_map/ppermute | solution.py:802
  414.5 34.5 %collective-permute-start.56 = (bf16[2,4,2,32,512]{4,3,2,1,0:T(8,128)(2,1)S(1)}, bf16[2,4,2,32,512]{4,3,2,1,0:T(8,128)(2,1)}, u32[]{:S(2)}, u32[]{:S(2)}) collective-permute-start(bf16[2,4,2,32,512]{4,3,2,1,0:T(8,128)(2,1)S(1)} %pad_maximum_fusion.18.refs_0_), channel_id=1, source_target_pairs={{0,4},{1,3},{2,6},{3,1},{4,0},{5,7},{6,2},{7,5},{8,12},{9,11},{10,... | collective-permute-start | bytes 1572872 | tf_op jit(solution)/shard_map/ppermute | solution.py:802
  415.0 34.0 %collective-permute-start.57 = (bf16[2,4,2,32,512]{4,3,2,1,0:T(8,128)(2,1)S(1)}, bf16[2,4,2,32,512]{4,3,2,1,0:T(8,128)(2,1)}, u32[]{:S(2)}, u32[]{:S(2)}) collective-permute-start(bf16[2,4,2,32,512]{4,3,2,1,0:T(8,128)(2,1)S(1)} %pad_maximum_fusion.18.refs_0_), channel_id=1, source_target_pairs={{0,1},{1,0},{2,3},{3,2},{4,5},{5,4},{6,7},{7,6},{8,9},{9,8},{10,11... | collective-permute-start | bytes 1572872 | tf_op jit(solution)/shard_map/ppermute | solution.py:802
  419.1 29.9 %collective-permute-start.53 = (bf16[4,2,64,512]{3,2,1,0:T(8,128)(2,1)}, bf16[4,2,64,512]{3,2,1,0:T(8,128)(2,1)}, u32[]{:S(2)}, u32[]{:S(2)}) collective-permute-start(bf16[4,2,64,512]{3,2,1,0:T(8,128)(2,1)} %fusion.11), channel_id=1, source_target_pairs={{0,2},{1,5},{2,0},{3,7},{4,6},{5,1},{6,4},{7,3},{8,10},{9,13},{10,... | collective-permute-start | bytes 1572872 | tf_op jit(solution)/shard_map/ppermute | solution.py:802
  425.5 23.5 %collective-permute-start.55 = (bf16[2,4,2,80,512]{4,3,2,1,0:T(8,128)(2,1)}, bf16[2,4,2,80,512]{4,3,2,1,0:T(8,128)(2,1)}, u32[]{:S(2)}, u32[]{:S(2)}) collective-permute-start(bf16[2,4,2,80,512]{4,3,2,1,0:T(8,128)(2,1)} %fusion), channel_id=1, source_target_pairs={{0,4},{1,3},{2,6},{3,1},{4,0},{5,7},{6,2},{7,5},{8,12},{9,11},{10,... | collective-permute-start | bytes 3932168 | tf_op jit(solution)/shard_map/ppermute | solution.py:802
  432.2 16.8 %collective-permute-start.52 = (bf16[2,2,80,512]{3,2,1,0:T(8,128)(2,1)}, bf16[2,2,80,512]{3,2,1,0:T(8,128)(2,1)}, u32[]{:S(2)}, u32[]{:S(2)}) collective-permute-start(bf16[2,2,80,512]{3,2,1,0:T(8,128)(2,1)} %fusion.18), channel_id=1, source_target_pairs={{0,16},{1,17},{2,18},{3,19},{4,20},{5,21},{6,22},{7,23},{8,24},{9,... | collective-permute-start | bytes 983048 | tf_op jit(solution)/shard_map/ppermute | solution.py:802
  450.8 21.2 %collective-permute-start.63 = (bf16[4,2,80,512]{3,2,1,0:T(8,128)(2,1)S(1)}, bf16[4,2,80,512]{3,2,1,0:T(8,128)(2,1)S(1)}, u32[]{:S(2)}, u32[]{:S(2)}) collective-permute-start(bf16[4,2,80,512]{3,2,1,0:T(8,128)(2,1)S(1)} %fusion.5), channel_id=1, source_target_pairs={{0,2},{1,5},{2,0},{3,7},{4,6},{5,1},{6,4},{7,3},{8,10},{9,13},{10,... | collective-permute-start | bytes 1966088 | tf_op jit(solution)/shard_map/ppermute | solution.py:802
  457.9 14.9 %collective-permute-start.65 = (bf16[2,4,2,64,512]{4,3,2,1,0:T(8,128)(2,1)S(1)}, bf16[2,4,2,64,512]{4,3,2,1,0:T(8,128)(2,1)S(1)}, u32[]{:S(2)}, u32[]{:S(2)}) collective-permute-start(bf16[2,4,2,64,512]{4,3,2,1,0:T(8,128)(2,1)S(1)} %fusion.2), channel_id=1, source_target_pairs={{0,4},{1,3},{2,6},{3,1},{4,0},{5,7},{6,2},{7,5},{8,12},{9,11},{10,... | collective-permute-start | bytes 3145736 | tf_op jit(solution)/shard_map/ppermute | solution.py:802
  475.2 18.4 %collective-permute-start.72 = (bf16[4,2,64,512]{3,2,1,0:T(8,128)(2,1)}, bf16[4,2,64,512]{3,2,1,0:T(8,128)(2,1)S(1)}, u32[]{:S(2)}, u32[]{:S(2)}) collective-permute-start(bf16[4,2,64,512]{3,2,1,0:T(8,128)(2,1)} %fusion.9), channel_id=1, source_target_pairs={{0,2},{1,5},{2,0},{3,7},{4,6},{5,1},{6,4},{7,3},{8,10},{9,13},{10,... | collective-permute-start | bytes 1572872 | tf_op jit(solution)/shard_map/ppermute | solution.py:802
  480.3 13.3 %collective-permute-start.70 = (bf16[2,80,512]{2,1,0:T(8,128)(2,1)}, bf16[2,80,512]{2,1,0:T(8,128)(2,1)}, u32[]{:S(2)}, u32[]{:S(2)}) collective-permute-start(bf16[2,80,512]{2,1,0:T(8,128)(2,1)} %get-tuple-element.786), channel_id=1, source_target_pairs={{0,16},{1,17},{2,18},{3,19},{4,20},{5,21},{6,22},{7,23},{8,24},{9,... | collective-permute-start | bytes 491528 | tf_op jit(solution)/shard_map/ppermute | solution.py:802
  (140 other events, 997.5 us)
